TPU v7x, 32 devices: a whole 2x2x4 slice. The times are simulated.
32 devices in a mesh: rep: 2 (over x), sp: 16 (over z, y, core).
Axes of the slice: x: 2, y: 2, z: 4, core: 2. Of those that a mesh axis runs over, the one named last changes fastest.
Arguments:
- volume: bfloat16 [128, 16, 16, 128], P(('rep', 'sp')), parts along dimension 0, may hold values from -6 to 6
- first_kernel: bfloat16 [3, 3, 3, 128, 128], replicated, may hold values from -0.15625 to 0.15625
- second_kernel: bfloat16 [3, 3, 3, 128, 256], replicated, may hold values from -0.15625 to 0.15625
- deep_kernel: bfloat16 [3, 3, 3, 256, 512], P(None, None, None, None, 'sp'), may hold values from -0.109375 to 0.109375
- deeper_kernel: bfloat16 [3, 3, 3, 512, 512], P(None, None, None, None, 'sp'), may hold values from -0.078125 to 0.078125
- rise_kernel: bfloat16 [2, 2, 2, 512, 256], replicated, may hold values from -0.375 to 0.375
- decode_kernel: bfloat16 [3, 3, 3, 512, 256], P(None, None, None, 'sp'), may hold values from -0.078125 to 0.078125
- final_kernel: bfloat16 [2, 2, 2, 256, 128], replicated, may hold values from -0.5 to 0.5
Outputs:
- segmented: bfloat16 [128, 16, 16, 128], P(('rep', 'sp')), parts along dimension 0
There are 2 independent parts, one for each index of `rep`. A program takes and returns all parts, laid end to end along the dimension named above; an argument that names none is the same for every part. Nothing has to cross between parts.
All inputs are finite; a program needn't handle non-finite values.
Results may differ from a plain program's by a relative error of at most 0.015.
Values may be sent and summed in bfloat16 or wider, within the bound.
No kernel may reach another device: no remote copies, remote signals or barrier semaphores. Data moves between devices by JAX's collectives and lax.ppermute only.
A program may use at most 64 MiB of HBM per device.

v0:
```python
import functools

import jax
import jax.numpy as jnp
import numpy as np
from jax import lax
from jax.experimental import pallas as pl
from jax.experimental.pallas import tpu as pltpu
from jax.sharding import PartitionSpec as P

GROUP = 4
MIB = 1024 * 1024


def call(kernel, outs, scratch, args, flops, vmem_mib, scalars=0):
    spaces = [
        pltpu.SMEM if i < scalars else pltpu.VMEM
        for i in range(len(args))
    ]
    return pl.pallas_call(
        kernel,
        out_shape=outs,
        in_specs=[pl.BlockSpec(memory_space=space) for space in spaces],
        out_specs=jax.tree.map(lambda _: pl.BlockSpec(memory_space=pltpu.VMEM), outs),
        scratch_shapes=scratch,
        compiler_params=pltpu.CompilerParams(vmem_limit_bytes=vmem_mib * MIB),
        cost_estimate=pl.CostEstimate(
            flops=flops,
            bytes_accessed=sum(a.size * a.dtype.itemsize for a in args),
            transcendentals=0,
        ),
    )(*args)


def dot(left, right, dims=((1,), (0,))):
    return lax.dot_general(left, right, (dims, ((), ())), preferred_element_type=jnp.float32)


def round_once(values):
    return values.astype(jnp.bfloat16).astype(jnp.float32)


def fill_patches(framed, patches, slices):
    for b in range(3):
        for c in range(3):
            tap = framed[:, b : b + 8, 7 + c : 15 + c, :].reshape(slices * 64, 128)
            col = (b * 3 + c) * 128
            patches[:, col : col + 128] = tap.astype(jnp.bfloat16)


def shift_slice(shifted, s, values):
    row = lax.broadcasted_iota(jnp.int32, (256, 128), 0) & 15
    here = values.reshape(256, 128).astype(jnp.float32)
    before = jnp.where(row == 0, 0.0, pltpu.roll(here, 1, 0))
    after = jnp.where(row == 15, 0.0, pltpu.roll(here, 255, 0))
    shifted[s, 0] = jnp.zeros((16, 384), jnp.bfloat16)
    shifted[s, 17] = jnp.zeros((16, 384), jnp.bfloat16)
    for c, tap in enumerate((before, here, after)):
        tap = tap.astype(jnp.bfloat16).reshape(16, 16, 128)
        shifted[s, 1:17, :, 128 * c : 128 * c + 128] = tap


def depth_pair(shifted, slices, weights, steps):
    left = jnp.concatenate(
        [shifted[s, b : b + 16].reshape(256, 384) for s in slices for b in range(3)], axis=1
    )
    none = jnp.zeros((1152, 128), jnp.bfloat16)
    right = [
        jnp.concatenate(
            [weights[j] if j < 3 else none, weights[j - 1] if j > 0 else none], axis=1
        )
        for j in steps
    ]
    return dot(left, jnp.concatenate(right, axis=0))


def depth_one(shifted, s, weights):
    left = jnp.concatenate([shifted[s, b : b + 16].reshape(256, 384) for b in range(3)], axis=1)
    return dot(left, weights)


def own_stage(volume, weights, out, shifted):
    for s in range(4):
        shift_slice(shifted, s, volume[s])
    out[0, :, :128] = jnp.zeros((256, 128), jnp.float32)
    out[0, :, 128:] = depth_one(shifted, 0, weights[2])
    out[1] = depth_pair(shifted, (0, 1, 2), weights, (1, 2, 3))
    out[2] = depth_pair(shifted, (1, 2, 3), weights, (0, 1, 2))
    out[3, :, :128] = depth_one(shifted, 3, weights[0])
    out[3, :, 128:] = jnp.zeros((256, 128), jnp.float32)


def stem_stage(
    ends, low, high, own, weights, second, order, out, shifted, halves, framed, patches, quarters
):
    for s in range(3):
        shift_slice(shifted, s, low[s])
        shift_slice(shifted, 3 + s, high[s])
    framed[...] = jnp.zeros(framed.shape, jnp.float32)
    for m in range(4):
        if m == 0:
            first = own[0] + depth_pair(shifted, (0, 1, 2), weights, (0, 1, 2))
        elif m == 3:
            first = own[3] + depth_pair(shifted, (3, 4, 5), weights, (1, 2, 3))
        elif m == 1:
            near = own[1, :, :128] + depth_one(shifted, 2, weights[0])
            first = jnp.concatenate([near, own[1, :, 128:]], axis=1)
        else:
            far = own[2, :, 128:] + depth_one(shifted, 3, weights[2])
            first = jnp.concatenate([own[2, :, :128], far], axis=1)
        first = round_once(jnp.maximum(first, 0.0))
        pair = (first[:, :128] + first[:, 128:]).reshape(8, 32, 128)
        halves[...] = (pair[:, :16] + pair[:, 16:]).reshape(128, 128)
        pooled = halves[pl.ds(0, 64, stride=2), :] + halves[pl.ds(1, 64, stride=2), :]
        pooled = round_once(pooled * 0.125)
        if m == 0:
            pooled = jnp.where(ends[0] == 0, 0.0, pooled)
        if m == 3:
            pooled = jnp.where(ends[1] == 0, 0.0, pooled)
        framed[m, 1:9, 8:16, :] = pooled.reshape(8, 8, 128)
    fill_patches(framed, patches, 4)
    skip = dot(patches[0:128], second[0])
    skip += dot(patches[64:192], second[1])
    skip += dot(patches[128:256], second[2])
    skip = jnp.maximum(skip, 0.0).astype(jnp.bfloat16)
    wide = skip.astype(jnp.float32)
    pair = (wide[:64] + wide[64:]).reshape(4, 16, 256)
    pair = (pair[:, :8] + pair[:, 8:]).reshape(32, 256)
    for k in range(2):
        quarters[k] = pair[:, 128 * k : 128 * k + 128]
    pooled = jnp.concatenate(
        [
            quarters[k, pl.ds(0, 16, stride=2), :] + quarters[k, pl.ds(1, 16, stride=2), :]
            for k in range(2)
        ],
        axis=1,
    )
    pooled = (pooled * 0.125).astype(jnp.bfloat16)
    sorted_skip = dot(skip, order[...])
    for r in range(GROUP):
        near, far = sorted_skip[:64, 64 * r : 64 * r + 64], sorted_skip[64:, 64 * r : 64 * r + 64]
        block = jnp.concatenate([near, far], axis=1)
        block = jnp.concatenate([block[:32], block[32:]], axis=1).astype(jnp.bfloat16)
        out[r, 0:16, :] = pooled
        out[r, 16:48, :] = block


def relay_stage(plane, near, out):
    lower = lax.broadcasted_iota(jnp.int32, (16, 128), 1) < 64

    def edge(block, far):
        sides = []
        for k in range(2):
            half = block[:, 128 * k : 128 * k + 128]
            top, bottom = half[:16], half[16:]
            if far:
                top = pltpu.roll(top, 64, 1)
            else:
                bottom = pltpu.roll(bottom, 64, 1)
            sides.append(jnp.where(lower, top, bottom))
        return jnp.concatenate(sides, axis=1)

    first = edge(near[0, 16:48, :].astype(jnp.float32), False)
    last = edge(near[GROUP - 1, 16:48, :].astype(jnp.float32), True)
    pooled = [near[r, 0:16, :] for r in range(GROUP)]
    for p in range(out.shape[0]):
        for r in range(GROUP):
            out[p, 16 * r : 16 * r + 16, :] = pooled[r]
        out[p, 64:80, :] = jnp.where(plane[0] < p, last, first).astype(jnp.bfloat16)


def spread_taps(weights, values, dims, chans, voxels):
    lane = lax.broadcasted_iota(jnp.int32, (chans, voxels), 1)

    def moved(term, tap, step, place, last):
        if tap == 1:
            return term
        keep = place > 0 if tap == 0 else place < last
        return jnp.where(keep, pltpu.roll(term, ((1 - tap) * step) % voxels, 1), 0.0)

    total = None
    for a in range(3):
        products = dot(weights[a * 9 * chans : (a + 1) * 9 * chans, :], values, dims)
        plane = None
        for b in range(3):
            line = None
            for c in range(3):
                at = (b * 3 + c) * chans
                term = moved(products[at : at + chans], c, 1, lane & 3, 3)
                line = term if line is None else line + term
            line = moved(line, b, 4, (lane >> 2) & 3, 3)
            plane = line if plane is None else plane + line
        plane = moved(plane, a, 16, lane >> 4, voxels // 16 - 1)
        total = plane if total is None else total + plane
    return jnp.maximum(total, 0.0)


def deep_stage(pooled, weights, out):
    n, chans, voxels = out.shape
    values = jnp.concatenate([pooled[p, 0:64, :] for p in range(n // GROUP)], axis=0)
    deep = spread_taps(weights, values, ((1,), (1,)), chans, voxels).astype(jnp.bfloat16)
    for dest in range(n):
        out[dest] = deep


def deeper_stage(deep, weights, out):
    n, chans, _ = out.shape
    voxels = deep.shape[1]
    deeper = spread_taps(weights, deep[...], ((1,), (0,)), chans, voxels)
    lane = lax.broadcasted_iota(jnp.int32, (chans, 128), 1)
    planes = n // GROUP
    for p in range(planes):
        part = pltpu.roll(deeper, (16 - 64 * p) % voxels, 1)[:, :128]
        if p == 0:
            part = jnp.where(lane < 16, 0.0, part)
        if p == planes - 1:
            part = jnp.where(lane >= 80, 0.0, part)
        part = part.astype(jnp.bfloat16)
        for r in range(GROUP):
            out[GROUP * p + r] = part


def decode_stage(
    plane, deeper, rise, near, relayed, decode, out, framed, patches, risen
):
    planes = relayed.shape[0]
    framed[...] = jnp.zeros(framed.shape, jnp.float32)
    spread = round_once(dot(deeper[...].astype(jnp.float32).T.astype(jnp.bfloat16), rise[...]))
    for pair in range(4):
        both = spread[:, 128 * pair : 128 * pair + 128]
        risen[2 * pair] = both
        risen[2 * pair + 1] = pltpu.roll(both, 64, 1)
    upper = lax.broadcasted_iota(jnp.int32, (64, 128), 1) >= 64
    for s in range(10):
        d, a = (s + 1) // 2, (s + 1) % 2
        for h in range(4):
            for b in range(2):
                for c in range(2):
                    framed[s, 1 + 2 * h + b, pl.ds(8 + c, 4, stride=2), :] = risen[
                        4 * a + 2 * b + c, 16 * d + 4 * h : 16 * d + 4 * h + 4, :
                    ]
        if s == 0 or s == 9:
            other = jnp.maximum(plane[0] - 1, 0) if s == 0 else jnp.minimum(plane[0] + 1, planes - 1)
            edge = relayed[other, 64:80, :].astype(jnp.float32)
            edge = jnp.where(other == plane[0], 0.0, edge)
            parts = []
            for k in range(2):
                half = edge[:, 128 * k : 128 * k + 128]
                parts += [pltpu.roll(half, 64, 1), half]
            skip = jnp.concatenate(parts, axis=0)
        else:
            both = near[(s - 1) // 2, 16:48, :].astype(jnp.float32)
            skip = jnp.concatenate([both[:, :128], both[:, 128:]], axis=0)
            if (s - 1) % 2 == 0:
                skip = pltpu.roll(skip, 64, 1)
        joined = framed[s, 1:9, 8:16, :].reshape(64, 128)
        framed[s, 1:9, 8:16, :] = jnp.where(upper, skip, joined).reshape(8, 8, 128)
    fill_patches(framed, patches, 10)
    blocks = decode.shape[0]
    step = 128 // blocks
    partial = None
    for a in range(3):
        right = [
            decode[z, tap * step : (tap + 1) * step, :]
            for tap in range(9 * a, 9 * a + 9)
            for z in range(blocks)
        ]
        term = dot(patches[64 * a : 64 * a + 512], jnp.concatenate(right, axis=0))
        partial = term if partial is None else partial + term
    out[...] = partial.astype(jnp.bfloat16)


def final_stage(partials, weights, out, spaced):
    decoded = partials[0].astype(jnp.float32)
    for g in range(1, GROUP):
        decoded += partials[g].astype(jnp.float32)
    decoded = jnp.maximum(decoded, 0.0).astype(jnp.bfloat16)
    for a in range(2):
        for b in range(2):
            for c in range(2):
                values = dot(decoded, weights[4 * a + 2 * b + c])
                for d in range(2):
                    for h in range(8):
                        at = ((2 * d + a) * 16 + 2 * h + b) * 16 + c
                        spaced[pl.ds(at, 8, stride=2), :] = values[64 * d + 8 * h : 64 * d + 8 * h + 8]
    out[...] = spaced[...].astype(jnp.bfloat16)


ALL = ("z", "r")


def exchange(payload, axis):
    return lax.all_to_all(payload, axis, split_axis=0, concat_axis=0, tiled=True)


def body(
    volume,
    first_kernel,
    second_kernel,
    deep_kernel,
    deeper_kernel,
    rise_kernel,
    decode_kernel,
    final_kernel,
):
    n = lax.axis_size(ALL)
    place = lax.axis_index(ALL)
    planes = n // GROUP
    plane, rank = lax.axis_index("z"), lax.axis_index("r")
    chans = deep_kernel.shape[4]
    voxels = 16 * n
    bf16 = functools.partial(jax.ShapeDtypeStruct, dtype=jnp.bfloat16)

    decode_part = lax.all_gather(decode_kernel.reshape(27 * chans, 256), "z", axis=0)
    if chans % 16:
        decode_part = decode_part.reshape(planes, 27, chans, 256).transpose(1, 0, 2, 3)
        decode_part = decode_part.reshape(1, 27 * 128, 256)

    forward = [(i, i + 1) for i in range(n - 1)]
    backward = [(target, source) for source, target in forward]
    low = lax.ppermute(volume[1:], ALL, forward)
    high = lax.ppermute(volume[:3], ALL, backward)

    taps = first_kernel.reshape(3, 1152, 128)
    own = call(
        own_stage,
        jax.ShapeDtypeStruct((4, 256, 256), jnp.float32),
        [pltpu.VMEM((4, 18, 16, 384), jnp.bfloat16)],
        (volume, taps),
        2 * 1024 * 2304 * 256,
        24,
    )
    lane = np.arange(256)
    source = (lane // 64 + GROUP * (lane % 64 // chans)) * chans + lane % chans
    order = jnp.asarray(np.arange(256)[:, None] == source[None, :], jnp.bfloat16)
    ends = jnp.stack([place, n - 1 - place]).astype(jnp.int32)
    sends = call(
        stem_stage,
        bf16((GROUP, 48, 256)),
        [
            pltpu.VMEM((6, 18, 16, 384), jnp.bfloat16),
            pltpu.VMEM((128, 128), jnp.float32),
            pltpu.VMEM((4, 10, 24, 128), jnp.float32),
            pltpu.VMEM((256, 1152), jnp.bfloat16),
            pltpu.VMEM((2, 32, 128), jnp.float32),
        ],
        (ends, low, high, own, taps, second_kernel.reshape(3, 1152, 256), order),
        2 * 1024 * 2304 * 256,
        24,
        scalars=1,
    )
    near = exchange(sends, "r")
    plane_ref = plane.astype(jnp.int32).reshape(1)
    relays = call(
        relay_stage, bf16((planes, 80, 256)), [], (plane_ref, near), 0, 16, scalars=1
    )
    relayed = exchange(relays, "z")

    deep = call(
        deep_stage,
        bf16((n, chans, voxels)),
        [],
        (relayed, deep_kernel.transpose(0, 1, 2, 4, 3).reshape(27 * chans, 256)),
        2 * 27 * chans * 256 * voxels,
        16,
    )
    deep_whole = exchange(deep, ALL).reshape(n * chans, voxels)

    deeper = call(
        deeper_stage,
        bf16((n, chans, 128)),
        [],
        (deep_whole, deeper_kernel.transpose(0, 1, 2, 4, 3).reshape(27 * chans, n * chans)),
        2 * 27 * chans * n * chans * voxels,
        16,
    )
    deeper_near = exchange(deeper, ALL).reshape(n * chans, 128)

    mine = lax.dynamic_slice_in_dim(order, 64 * rank, 64, axis=1)
    rise_part = jnp.einsum("pio,os->ips", rise_kernel.reshape(8, n * chans, 256), mine)
    rise_part = rise_part.reshape(n * chans, 512)
    partial = call(
        decode_stage,
        bf16((512, 256)),
        [
            pltpu.VMEM((10, 10, 24, 128), jnp.float32),
            pltpu.VMEM((640, 1152), jnp.bfloat16),
            pltpu.VMEM((8, 128, 128), jnp.float32),
        ],
        (plane_ref, deeper_near, rise_part, near, relayed, decode_part),
        2 * 512 * 3456 * 256,
        24,
        scalars=1,
    )
    partials = exchange(partial.reshape(GROUP, 128, 256), "r")
    out = call(
        final_stage,
        bf16((1024, 128)),
        [pltpu.VMEM((1024, 128), jnp.float32)],
        (partials, final_kernel.reshape(8, 256, 128)),
        2 * 128 * 256 * 1024,
        16,
    )
    return out.reshape(4, 16, 16, 128)


def solution(mesh):
    reps, n = mesh.devices.shape
    grid = jax.sharding.Mesh(mesh.devices.reshape(reps, n // GROUP, GROUP), ("rep",) + ALL)
    return jax.shard_map(
        body,
        mesh=grid,
        in_specs=(
            P(("rep",) + ALL, None, None, None),
            P(),
            P(),
            P(None, None, None, None, ALL),
            P(None, None, None, None, ALL),
            P(),
            P(None, None, None, ALL, None),
            P(),
        ),
        out_specs=P(("rep",) + ALL, None, None, None),
        check_vma=False,
    )
```

profile of v0, /device:TPU:1, one launch (start us, length us, event | category | flops | bytes accessed | tf_op | source)
XLA Modules:
  0.0 94.6 jit_solution(15487864609318667276)
XLA Ops:
  6.5 0.0 copy-start
  6.5 0.0 all-gather.2.cloned.1.call-start
  6.5 0.7 all-gather.2.cloned.1.call-update
  7.3 1.1 %fusion.4 = (bf16[3,16,16,128]{3,2,1,0:T(8,128)(2,1)S(1)}, bf16[3,16,16,128]{3,2,1,0:T(8,128)(2,1)S(1)}) fusion(bf16[4,16,16,128]{3,2,1,0:T(8,128)(2,1)} %volume.1), kind=kLoop, calls=%fused_computation.5 | loop fusion | bytes 786432 | tf_op jit(solution)/shard_map/slice | solution.py:322
  8.3 4.6 %collective-permute-start = (bf16[3,16,16,128]{3,2,1,0:T(8,128)(2,1)S(1)}, bf16[3,16,16,128]{3,2,1,0:T(8,128)(2,1)S(1)}, u32[]{:S(2)}, u32[]{:S(2)}) collective-permute-start(bf16[3,16,16,128]{3,2,1,0:T(8,128)(2,1)S(1)} %get-tuple-element.6), channel_id=1, source_target_pairs={{0,1},{1,2},{2,3},{3,4},{4,5},{5,6},{6,7},{7,8},{8,9},{9,10},{10,1... | collective-permute-start | bytes 589832 | tf_op jit(solution)/shard_map/ppermute | solution.py:321
  12.9 1.9 %collective-permute-start.1 = (bf16[3,16,16,128]{3,2,1,0:T(8,128)(2,1)S(1)}, bf16[3,16,16,128]{3,2,1,0:T(8,128)(2,1)S(1)}, u32[]{:S(2)}, u32[]{:S(2)}) collective-permute-start(bf16[3,16,16,128]{3,2,1,0:T(8,128)(2,1)S(1)} %get-tuple-element.5), channel_id=1, source_target_pairs={{1,0},{2,1},{3,2},{4,3},{5,4},{6,5},{7,6},{8,7},{9,8},{10,9},{11,1... | collective-permute-start | bytes 589832 | tf_op jit(solution)/shard_map/ppermute | solution.py:322
  14.8 0.1 pad_add_fusion.ends
  14.9 0.9 %copy-done.2 = bf16[4,16,16,128]{3,2,1,0:T(8,128)(2,1)S(1)} copy-done((bf16[4,16,16,128]{3,2,1,0:T(8,128)(2,1)S(1)}, bf16[4,16,16,128]{3,2,1,0:T(8,128)(2,1)}, u32[]{:S(2)}) %copy-start.2) | copy-done | bytes 262168
  15.8 1.2 %copy-done.8 = bf16[3,3,3,128,128]{4,3,2,1,0:T(8,128)(2,1)S(1)} copy-done((bf16[3,3,3,128,128]{4,3,2,1,0:T(8,128)(2,1)S(1)}, bf16[3,3,3,128,128]{4,3,2,1,0:T(8,128)(2,1)}, u32[]{:S(2)}) %copy-start.8) | copy-done | bytes 884760
  17.0 1.4 %shard_map.91.own = f32[4,256,256]{2,1,0:T(8,128)S(1)} custom-call(bf16[4,16,16,128]{3,2,1,0:T(8,128)(2,1)S(1)} %copy-done.2, bf16[3,1152,128]{2,1,0:T(8,128)(2,1)S(1)} %bitcast.32), custom_call_target="tpu_custom_call" | custom-call | flops 1207959552 | bytes 1146880 | tf_op jit(solution)/shard_map/pallas_call | solution.py:20
  18.4 0.0 collective-permute-done.low
  18.4 1.4 %collective-permute-done.1.high = bf16[3,16,16,128]{3,2,1,0:T(8,128)(2,1)S(1)} collective-permute-done((bf16[3,16,16,128]{3,2,1,0:T(8,128)(2,1)S(1)}, bf16[3,16,16,128]{3,2,1,0:T(8,128)(2,1)S(1)}, u32[]{:S(2)}, u32[]{:S(2)}) %collective-permute-start.1) | collective-permute-done | bytes 196640 | tf_op jit(solution)/shard_map/ppermute | solution.py:322
  19.9 0.0 copy-done.5
  19.9 0.0 copy-done.6
  19.9 2.8 %shard_map.92 = bf16[4,48,256]{2,1,0:T(8,128)(2,1)S(1)} custom-call(s32[2]{0:T(128)S(1)} %pad_add_fusion.ends, bf16[3,16,16,128]{3,2,1,0:T(8,128)(2,1)S(1)} %collective-permute-done.low, bf16[3,16,16,128]{3,2,1,0:T(8,128)(2,1)S(1)} %collective-permute-done.1.high, f32[4,256,256]{2,1,0:T(8,128)S(1)} %shard_map.91.own, bf16[3,1152,128]{2,1,0:T(8,128)(2,1)S(1)} %bitcast.33, ...), custom_call_target="tpu_custom_call" | custom-call | flops 1207959552 | bytes 4227080 | tf_op jit(solution)/shard_map/pallas_call | solution.py:20
  22.7 0.0 copy-start.1
  22.7 7.5 %all_to_all.25.near = bf16[4,48,256]{2,1,0:T(8,128)(2,1)S(1)} all-to-all(bf16[4,48,256]{2,1,0:T(8,128)(2,1)S(1)} %shard_map.92), channel_id=1, replica_groups=mesh['rep'=2,'z'=4,'r'=4] {'r'}, dimensions={0} | all-to-all | bytes 196608 | tf_op jit(solution)/shard_map/all_to_all | solution.py:293
  30.2 0.1 shard_map.93
  30.3 16.1 %all_to_all.26.pooled.relayed = bf16[4,80,256]{2,1,0:T(8,128)(2,1)S(1)} all-to-all(bf16[4,80,256]{2,1,0:T(8,128)(2,1)S(1)} %shard_map.93), channel_id=1, replica_groups=mesh['rep'=2,'z'=4,'r'=4] {'z'}, dimensions={0} | all-to-all | bytes 327680 | tf_op jit(solution)/shard_map/all_to_all | solution.py:293
  46.4 1.3 %shard_map.94 = bf16[16,32,256]{2,1,0:T(8,128)(2,1)} custom-call(bf16[4,80,256]{2,1,0:T(8,128)(2,1)S(1)} %all_to_all.26.pooled.relayed, bf16[864,256]{1,0:T(8,128)(2,1)S(1)} %bitcast.29), custom_call_target="tpu_custom_call" | custom-call | flops 113246208 | bytes 606208 | tf_op jit(solution)/shard_map/pallas_call | solution.py:20
  47.7 4.1 %all-to-all-start.2 = ((bf16[16,32,256]{2,1,0:T(8,128)(2,1)}), bf16[16,32,256]{2,1,0:T(8,128)(2,1)S(1)}, u32[]{:S(2)}, u32[]{:S(2)}) async-start(bf16[16,32,256]{2,1,0:T(8,128)(2,1)} %shard_map.94), calls=%async_computation.2 | async-start | bytes 524288 | tf_op jit(solution)/shard_map/all_to_all | solution.py:293
  51.7 9.6 %all-to-all-done.2 = bf16[16,32,256]{2,1,0:T(8,128)(2,1)S(1)} async-done(((bf16[16,32,256]{2,1,0:T(8,128)(2,1)}), bf16[16,32,256]{2,1,0:T(8,128)(2,1)S(1)}, u32[]{:S(2)}, u32[]{:S(2)}) %all-to-all-start.2) | async-done | bytes 262176 | tf_op jit(solution)/shard_map/all_to_all | solution.py:293
  61.3 1.4 %shard_map.95 = bf16[16,32,128]{2,1,0:T(8,128)(2,1)} custom-call(bf16[512,256]{1,0:T(8,128)(2,1)S(1)} %bitcast.26, bf16[864,512]{1,0:T(8,128)(2,1)S(1)} %bitcast.27), custom_call_target="tpu_custom_call" | custom-call | flops 226492416 | bytes 1146880 | tf_op jit(solution)/shard_map/pallas_call | solution.py:20
  62.6 4.6 %all-to-all-start.3 = ((bf16[16,32,128]{2,1,0:T(8,128)(2,1)}), bf16[16,32,128]{2,1,0:T(8,128)(2,1)}, u32[]{:S(2)}, u32[]{:S(2)}) async-start(bf16[16,32,128]{2,1,0:T(8,128)(2,1)} %shard_map.95), calls=%async_computation.3 | async-start | bytes 262144 | tf_op jit(solution)/shard_map/all_to_all | solution.py:293
  67.2 1.7 %fusion = bf16[64,8,512]{2,0,1:T(8,128)(2,1)S(1)} fusion(bf16[8,512,256]{2,1,0:T(8,128)(2,1)S(1)} %bitcast.25, bf16[256,256]{1,0:T(8,128)(2,1)} %constant.19.clone.order, s32[]{:T(128)S(6)} %select_n.3), kind=kOutput, calls=%fused_computation | convolution fusion | flops 134217728 | bytes 2686980 | tf_op jit(solution)/shard_map/pio,os->ips/dot_general | solution.py:380
  68.9 0.2 copy.15.rise
  69.1 0.0 copy-start.3
  69.1 5.1 %all-to-all-done.3 = bf16[16,32,128]{2,1,0:T(8,128)(2,1)} async-done(((bf16[16,32,128]{2,1,0:T(8,128)(2,1)}), bf16[16,32,128]{2,1,0:T(8,128)(2,1)}, u32[]{:S(2)}, u32[]{:S(2)}) %all-to-all-start.3) | async-done | bytes 131104 | tf_op jit(solution)/shard_map/all_to_all | solution.py:293
  74.3 1.5 %copy-done.7 = bf16[4,864,256]{2,1,0:T(8,128)(2,1)S(1)} copy-done((bf16[4,864,256]{2,1,0:T(8,128)(2,1)S(1)}, bf16[4,864,256]{2,1,0:T(8,128)(2,1)}, u32[]{:S(2)}) %copy-start.7) | copy-done | bytes 1769496
  75.7 2.5 %shard_map.96 = bf16[512,256]{1,0:T(8,128)(2,1)S(1)} custom-call(s32[1]{0:T(128)} %bitcast.plane, bf16[512,128]{1,0:T(8,128)(2,1)} %bitcast.10.deeper, bf16[512,512]{1,0:T(8,128)(2,1)S(1)} %copy.15.rise, bf16[4,48,256]{2,1,0:T(8,128)(2,1)S(1)} %all_to_all.25.near, bf16[4,80,256]{2,1,0:T(8,128)(2,1)S(1)} %all_to_all.26.pooled.relayed, ...), custom_call_target="tpu_custom_call" | custom-call | flops 905969664 | bytes 2686980 | tf_op jit(solution)/shard_map/pallas_call | solution.py:20
  78.2 8.6 %all_to_all.27.partials = bf16[4,128,256]{2,1,0:T(8,128)(2,1)S(1)} all-to-all(bf16[4,128,256]{2,1,0:T(8,128)(2,1)S(1)} %bitcast.30), channel_id=1, replica_groups=mesh['rep'=2,'z'=4,'r'=4] {'r'}, dimensions={0} | all-to-all | bytes 524288 | tf_op jit(solution)/shard_map/all_to_all | solution.py:293
  86.7 1.1 %shard_map.97 = bf16[1024,128]{1,0:T(8,128)(2,1)} custom-call(bf16[4,128,256]{2,1,0:T(8,128)(2,1)S(1)} %all_to_all.27.partials, bf16[8,256,128]{2,1,0:T(8,128)(2,1)S(1)} %bitcast.28), custom_call_target="tpu_custom_call" | custom-call | flops 67108864 | bytes 786432 | tf_op jit(solution)/shard_map/pallas_call | solution.py:20
  (11 shorter events, 0.0 us)
Async XLA Ops:
  6.5 60.7 %copy-start = (bf16[2,2,2,512,256]{4,3,2,1,0:T(8,128)(2,1)S(1)}, bf16[2,2,2,512,256]{4,3,2,1,0:T(8,128)(2,1)}, u32[]{:S(2)}) copy-start(bf16[2,2,2,512,256]{4,3,2,1,0:T(8,128)(2,1)} %param.14) | copy-start | bytes 6291460
  6.5 67.7 %all-gather.2.cloned.1.call-start = ((), (), s32[]{:S(2)}) async-start(), calls=%async_computation.5 | async-start | bytes 2211840 | tf_op jit(solution)/shard_map/all_gather | solution.py:314
  8.3 10.1 %collective-permute-start = (bf16[3,16,16,128]{3,2,1,0:T(8,128)(2,1)S(1)}, bf16[3,16,16,128]{3,2,1,0:T(8,128)(2,1)S(1)}, u32[]{:S(2)}, u32[]{:S(2)}) collective-permute-start(bf16[3,16,16,128]{3,2,1,0:T(8,128)(2,1)S(1)} %get-tuple-element.6), channel_id=1, source_target_pairs={{0,1},{1,2},{2,3},{3,4},{4,5},{5,6},{6,7},{7,8},{8,9},{9,10},{10,1... | collective-permute-start | bytes 589832 | tf_op jit(solution)/shard_map/ppermute | solution.py:321
  12.9 7.0 %collective-permute-start.1 = (bf16[3,16,16,128]{3,2,1,0:T(8,128)(2,1)S(1)}, bf16[3,16,16,128]{3,2,1,0:T(8,128)(2,1)S(1)}, u32[]{:S(2)}, u32[]{:S(2)}) collective-permute-start(bf16[3,16,16,128]{3,2,1,0:T(8,128)(2,1)S(1)} %get-tuple-element.5), channel_id=1, source_target_pairs={{1,0},{2,1},{3,2},{4,3},{5,4},{6,5},{7,6},{8,7},{9,8},{10,9},{11,1... | collective-permute-start | bytes 589832 | tf_op jit(solution)/shard_map/ppermute | solution.py:322
  14.9 1.0 %copy-start.2 = (bf16[4,16,16,128]{3,2,1,0:T(8,128)(2,1)S(1)}, bf16[4,16,16,128]{3,2,1,0:T(8,128)(2,1)}, u32[]{:S(2)}) copy-start(bf16[4,16,16,128]{3,2,1,0:T(8,128)(2,1)} %volume.1) | copy-start | bytes 786436
  15.8 1.2 %copy-start.8 = (bf16[3,3,3,128,128]{4,3,2,1,0:T(8,128)(2,1)S(1)}, bf16[3,3,3,128,128]{4,3,2,1,0:T(8,128)(2,1)}, u32[]{:S(2)}) copy-start(bf16[3,3,3,128,128]{4,3,2,1,0:T(8,128)(2,1)} %param.10) | copy-start | bytes 2654212
  17.0 2.9 %copy-start.5 = (bf16[256,256]{1,0:T(8,128)(2,1)S(1)}, bf16[256,256]{1,0:T(8,128)(2,1)}, u32[]{:S(2)}) copy-start(bf16[256,256]{1,0:T(8,128)(2,1)} %constant.19.clone.order) | copy-start | bytes 393220
  17.0 2.9 %copy-start.6 = (bf16[3,3,3,128,256]{4,3,2,1,0:T(8,128)(2,1)S(1)}, bf16[3,3,3,128,256]{4,3,2,1,0:T(8,128)(2,1)}, u32[]{:S(2)}) copy-start(bf16[3,3,3,128,256]{4,3,2,1,0:T(8,128)(2,1)} %param.11) | copy-start | bytes 5308420
  19.9 26.5 %copy-start.4 = (bf16[3,3,3,256,32]{3,4,2,1,0:T(8,128)(2,1)S(1)}, bf16[3,3,3,256,32]{3,4,2,1,0:T(8,128)(2,1)}, u32[]{:S(2)}) copy-start(bf16[3,3,3,256,32]{3,4,2,1,0:T(8,128)(2,1)} %param.12) | copy-start | bytes 1327108
  22.7 38.6 %copy-start.1 = (bf16[3,3,3,512,32]{3,4,2,1,0:T(8,128)(2,1)S(1)}, bf16[3,3,3,512,32]{3,4,2,1,0:T(8,128)(2,1)}, u32[]{:S(2)}) copy-start(bf16[3,3,3,512,32]{3,4,2,1,0:T(8,128)(2,1)} %param.13) | copy-start | bytes 2654212
  47.7 13.6 %all-to-all-start.2 = ((bf16[16,32,256]{2,1,0:T(8,128)(2,1)}), bf16[16,32,256]{2,1,0:T(8,128)(2,1)S(1)}, u32[]{:S(2)}, u32[]{:S(2)}) async-start(bf16[16,32,256]{2,1,0:T(8,128)(2,1)} %shard_map.94), calls=%async_computation.2 | async-start | bytes 524288 | tf_op jit(solution)/shard_map/all_to_all | solution.py:293
  62.6 11.6 %all-to-all-start.3 = ((bf16[16,32,128]{2,1,0:T(8,128)(2,1)}), bf16[16,32,128]{2,1,0:T(8,128)(2,1)}, u32[]{:S(2)}, u32[]{:S(2)}) async-start(bf16[16,32,128]{2,1,0:T(8,128)(2,1)} %shard_map.95), calls=%async_computation.3 | async-start | bytes 262144 | tf_op jit(solution)/shard_map/all_to_all | solution.py:293
  69.1 17.6 %copy-start.3 = (bf16[2,2,2,256,128]{4,3,2,1,0:T(8,128)(2,1)S(1)}, bf16[2,2,2,256,128]{4,3,2,1,0:T(8,128)(2,1)}, u32[]{:S(2)}) copy-start(bf16[2,2,2,256,128]{4,3,2,1,0:T(8,128)(2,1)} %param.16) | copy-start | bytes 1572868
  74.3 1.5 %copy-start.7 = (bf16[4,864,256]{2,1,0:T(8,128)(2,1)S(1)}, bf16[4,864,256]{2,1,0:T(8,128)(2,1)}, u32[]{:S(2)}) copy-start(bf16[4,864,256]{2,1,0:T(8,128)(2,1)} %all-gather.2.cloned.1.call-done.decode) | copy-start | bytes 5308420
Sparse Core Ops, SparseCore 0:
  8.9 45.8 all-gather.1
where the time goes:
time: 96.3 us; the launch traced here: 94.6 us
  blocking collectives  32.1 us (33%)
  waiting for transfers between devices  16.8 us (17%)
  starting transfers between devices  15.1 us (16%)
  between operations  13.5 us (14%)
  Pallas kernels  10.5 us (11%)
  local copies, waits for them, and re-layouts  4.88 us (5%)
  matrix products  1.68 us (2%)
    all_to_all x3, blocking collectives, exchange(): lax.all_to_all(payload, axis, split_axis=0, concat_axis=0, tiled=True)  32.1 us
    all_to_all x2, waiting for transfers between devices, exchange(): lax.all_to_all(payload, axis, split_axis=0, concat_axis=0, tiled=True)  14.7 us
    pallas_call x7, Pallas kernels, call(): pl.pallas_call(kernel, out_shape=outs, in_specs=[pl.BlockSpec(memory_spac...  10.5 us
    all_to_all x2, starting transfers between devices, exchange(): lax.all_to_all(payload, axis, split_axis=0, concat_axis=0, tiled=True)  8.62 us
    ppermute x1, starting transfers between devices, body(): low = lax.ppermute(volume[1:], ALL, forward)  4.55 us
    unnamed x18, local copies, waits for them, and re-layouts  3.62 us
  transfers between devices with their start and end apart: 5, of which 3 were waited for; matrix products, arithmetic and copies ran while one was open for 3% of the time, Pallas kernels for 7%

commit v1 on v0

--- a/solution.py
+++ b/solution.py
@@ -91,7 +91,9 @@
 
 
 def stem_stage(
-    ends, low, high, own, weights, second, order, out, shifted, halves, framed, patches, quarters
+    ends, low, high, own, weights, second, order,
+    pooled_out, skip_out,
+    shifted, halves, framed, patches, quarters,
 ):
     for s in range(3):
         shift_slice(shifted, s, low[s])
@@ -136,37 +138,36 @@
         axis=1,
     )
     pooled = (pooled * 0.125).astype(jnp.bfloat16)
+    for p in range(pooled_out.shape[0]):
+        pooled_out[p] = pooled
     sorted_skip = dot(skip, order[...])
     for r in range(GROUP):
         near, far = sorted_skip[:64, 64 * r : 64 * r + 64], sorted_skip[64:, 64 * r : 64 * r + 64]
         block = jnp.concatenate([near, far], axis=1)
         block = jnp.concatenate([block[:32], block[32:]], axis=1).astype(jnp.bfloat16)
-        out[r, 0:16, :] = pooled
-        out[r, 16:48, :] = block
-
-
-def relay_stage(plane, near, out):
+        skip_out[r] = block
+
+
+def relay_stage(pooled, skips, out):
+    planes = pooled.shape[0]
+    for r in range(GROUP):
+        for p in range(planes):
+            out[r, 16 * p : 16 * p + 16, :] = pooled[p]
+        out[r, 16 * planes :, :] = skips[r]
+
+
+def edge_slice(block, far):
     lower = lax.broadcasted_iota(jnp.int32, (16, 128), 1) < 64
-
-    def edge(block, far):
-        sides = []
-        for k in range(2):
-            half = block[:, 128 * k : 128 * k + 128]
-            top, bottom = half[:16], half[16:]
-            if far:
-                top = pltpu.roll(top, 64, 1)
-            else:
-                bottom = pltpu.roll(bottom, 64, 1)
-            sides.append(jnp.where(lower, top, bottom))
-        return jnp.concatenate(sides, axis=1)
-
-    first = edge(near[0, 16:48, :].astype(jnp.float32), False)
-    last = edge(near[GROUP - 1, 16:48, :].astype(jnp.float32), True)
-    pooled = [near[r, 0:16, :] for r in range(GROUP)]
-    for p in range(out.shape[0]):
-        for r in range(GROUP):
-            out[p, 16 * r : 16 * r + 16, :] = pooled[r]
-        out[p, 64:80, :] = jnp.where(plane[0] < p, last, first).astype(jnp.bfloat16)
+    sides = []
+    for k in range(2):
+        half = block[:, 128 * k : 128 * k + 128].astype(jnp.float32)
+        top, bottom = half[:16], half[16:]
+        if far:
+            top = pltpu.roll(top, 64, 1)
+        else:
+            bottom = pltpu.roll(bottom, 64, 1)
+        sides.append(jnp.where(lower, top, bottom))
+    return jnp.concatenate(sides, axis=1).astype(jnp.bfloat16)
 
 
 def spread_taps(weights, values, dims, chans, voxels):
@@ -195,12 +196,15 @@
     return jnp.maximum(total, 0.0)
 
 
-def deep_stage(pooled, weights, out):
+def deep_stage(near, weights, out, first, last):
     n, chans, voxels = out.shape
-    values = jnp.concatenate([pooled[p, 0:64, :] for p in range(n // GROUP)], axis=0)
+    values = [near[r, 16 * p : 16 * p + 16, :] for p in range(n // GROUP) for r in range(GROUP)]
+    values = jnp.concatenate(values, axis=0)
     deep = spread_taps(weights, values, ((1,), (1,)), chans, voxels).astype(jnp.bfloat16)
     for dest in range(n):
         out[dest] = deep
+    first[...] = edge_slice(near[0, voxels // GROUP :, :], False)
+    last[...] = edge_slice(near[GROUP - 1, voxels // GROUP :, :], True)
 
 
 def deeper_stage(deep, weights, out):
@@ -221,9 +225,8 @@
 
 
 def decode_stage(
-    plane, deeper, rise, near, relayed, decode, out, framed, patches, risen
+    deeper, rise, near, low, high, decode, out, framed, patches, risen
 ):
-    planes = relayed.shape[0]
     framed[...] = jnp.zeros(framed.shape, jnp.float32)
     spread = round_once(dot(deeper[...].astype(jnp.float32).T.astype(jnp.bfloat16), rise[...]))
     for pair in range(4):
@@ -240,16 +243,14 @@
                         4 * a + 2 * b + c, 16 * d + 4 * h : 16 * d + 4 * h + 4, :
                     ]
         if s == 0 or s == 9:
-            other = jnp.maximum(plane[0] - 1, 0) if s == 0 else jnp.minimum(plane[0] + 1, planes - 1)
-            edge = relayed[other, 64:80, :].astype(jnp.float32)
-            edge = jnp.where(other == plane[0], 0.0, edge)
+            edge = (low if s == 0 else high)[...].astype(jnp.float32)
             parts = []
             for k in range(2):
                 half = edge[:, 128 * k : 128 * k + 128]
                 parts += [pltpu.roll(half, 64, 1), half]
             skip = jnp.concatenate(parts, axis=0)
         else:
-            both = near[(s - 1) // 2, 16:48, :].astype(jnp.float32)
+            both = near[(s - 1) // 2, near.shape[1] - 32 :, :].astype(jnp.float32)
             skip = jnp.concatenate([both[:, :128], both[:, 128:]], axis=0)
             if (s - 1) % 2 == 0:
                 skip = pltpu.roll(skip, 64, 1)
@@ -306,7 +307,7 @@
     n = lax.axis_size(ALL)
     place = lax.axis_index(ALL)
     planes = n // GROUP
-    plane, rank = lax.axis_index("z"), lax.axis_index("r")
+    rank = lax.axis_index("r")
     chans = deep_kernel.shape[4]
     voxels = 16 * n
     bf16 = functools.partial(jax.ShapeDtypeStruct, dtype=jnp.bfloat16)
@@ -334,9 +335,9 @@
     source = (lane // 64 + GROUP * (lane % 64 // chans)) * chans + lane % chans
     order = jnp.asarray(np.arange(256)[:, None] == source[None, :], jnp.bfloat16)
     ends = jnp.stack([place, n - 1 - place]).astype(jnp.int32)
-    sends = call(
+    pooled_two, skips = call(
         stem_stage,
-        bf16((GROUP, 48, 256)),
+        (bf16((planes, 16, 256)), bf16((GROUP, 32, 256))),
         [
             pltpu.VMEM((6, 18, 16, 384), jnp.bfloat16),
             pltpu.VMEM((128, 128), jnp.float32),
@@ -349,21 +350,22 @@
         24,
         scalars=1,
     )
-    near = exchange(sends, "r")
-    plane_ref = plane.astype(jnp.int32).reshape(1)
+    pooled_line = exchange(pooled_two, "z")
     relays = call(
-        relay_stage, bf16((planes, 80, 256)), [], (plane_ref, near), 0, 16, scalars=1
-    )
-    relayed = exchange(relays, "z")
-
-    deep = call(
+        relay_stage, bf16((GROUP, 16 * planes + 32, 256)), [], (pooled_line, skips), 0, 16
+    )
+    near = exchange(relays, "r")
+
+    deep, first, last = call(
         deep_stage,
-        bf16((n, chans, voxels)),
+        (bf16((n, chans, voxels)), bf16((16, 256)), bf16((16, 256))),
         [],
-        (relayed, deep_kernel.transpose(0, 1, 2, 4, 3).reshape(27 * chans, 256)),
+        (near, deep_kernel.transpose(0, 1, 2, 4, 3).reshape(27 * chans, 256)),
         2 * 27 * chans * 256 * voxels,
         16,
     )
+    skip_low = lax.ppermute(last, "z", [(p, p + 1) for p in range(planes - 1)])
+    skip_high = lax.ppermute(first, "z", [(p + 1, p) for p in range(planes - 1)])
     deep_whole = exchange(deep, ALL).reshape(n * chans, voxels)
 
     deeper = call(
@@ -387,10 +389,9 @@
             pltpu.VMEM((640, 1152), jnp.bfloat16),
             pltpu.VMEM((8, 128, 128), jnp.float32),
         ],
-        (plane_ref, deeper_near, rise_part, near, relayed, decode_part),
+        (deeper_near, rise_part, near, skip_low, skip_high, decode_part),
         2 * 512 * 3456 * 256,
         24,
-        scalars=1,
     )
     partials = exchange(partial.reshape(GROUP, 128, 256), "r")
     out = call(

time: 96.3 us -> 90.9 us (0.944)
  blocking collectives: 32.1 us -> 26.6 us
  starting transfers between devices: 15.1 us -> 19.2 us
  waiting for transfers between devices: 16.8 us -> 13.8 us
  Pallas kernels: 10.5 us -> 8.12 us
  local copies, waits for them, and re-layouts: 4.88 us -> 6.23 us
    all_to_all x3, blocking collectives: 32.1 us -> 26.6 us  [exchange(): lax.all_to_all(payload, axis, split_axis=0, concat_axis=0, tiled=True)]
    ppermute x0 -> x2, starting transfers between devices: none -> 4.57 us  [the longest x1 3.28 us: body(): skip_low = lax.ppermute(last, 'z', [(p, p + 1) for p in range(planes - 1)])]
    all_to_all x2, waiting for transfers between devices: 14.7 us -> 11.7 us  [exchange(): lax.all_to_all(payload, axis, split_axis=0, concat_axis=0, tiled=True)]
    pallas_call x7, Pallas kernels: 10.5 us -> 8.12 us  [call(): pl.pallas_call(kernel, out_shape=outs, in_specs=[pl.BlockSpec(memory_spac...]
    unnamed x18 -> x22, local copies, waits for them, and re-layouts: 3.62 us -> 4.97 us
  transfers between devices with their start and end apart: 5 -> 7, of which waited for: 3 -> 3; matrix products, arithmetic and copies ran while one was open for 3% -> 3% of each run, Pallas kernels for 7% -> 6%
where the time goes in v1:
time: 90.9 us; the launch traced here: 89.3 us
  blocking collectives  26.6 us (29%)
  starting transfers between devices  19.2 us (21%)
  waiting for transfers between devices  13.8 us (15%)
  between operations  13.6 us (15%)
  Pallas kernels  8.12 us (9%)
  local copies, waits for them, and re-layouts  6.23 us (7%)
  matrix products  1.67 us (2%)
    all_to_all x3, blocking collectives, exchange(): lax.all_to_all(payload, axis, split_axis=0, concat_axis=0, tiled=True)  26.6 us
    all_to_all x2, waiting for transfers between devices, exchange(): lax.all_to_all(payload, axis, split_axis=0, concat_axis=0, tiled=True)  11.7 us
    all_to_all x2, starting transfers between devices, exchange(): lax.all_to_all(payload, axis, split_axis=0, concat_axis=0, tiled=True)  8.13 us
    pallas_call x7, Pallas kernels, call(): pl.pallas_call(kernel, out_shape=outs, in_specs=[pl.BlockSpec(memory_spac...  8.12 us
    unnamed x22, local copies, waits for them, and re-layouts  4.97 us
    ppermute x1, starting transfers between devices, body(): low = lax.ppermute(volume[1:], ALL, forward)  4.55 us
    ppermute x1, starting transfers between devices, body(): skip_low = lax.ppermute(last, 'z', [(p, p + 1) for p in range(planes - 1)])  3.28 us
    ppermute x1, starting transfers between devices, body(): high = lax.ppermute(volume[:3], ALL, backward)  1.92 us
  transfers between devices with their start and end apart: 7, of which 3 were waited for; matrix products, arithmetic and copies ran while one was open for 3% of the time, Pallas kernels for 6%

profile of v1, /device:TPU:1, one launch (start us, length us, event | category | flops | bytes accessed | tf_op | source)
XLA Modules:
  0.0 89.3 jit_solution(15578491929426055523)
XLA Ops:
  6.5 0.7 all-gather.2.cloned.1.call-update
  7.3 1.1 %fusion.4 = (bf16[3,16,16,128]{3,2,1,0:T(8,128)(2,1)S(1)}, bf16[3,16,16,128]{3,2,1,0:T(8,128)(2,1)S(1)}) fusion(bf16[4,16,16,128]{3,2,1,0:T(8,128)(2,1)} %volume.1), kind=kLoop, calls=%fused_computation.5 | loop fusion | bytes 786432 | tf_op jit(solution)/shard_map/slice | solution.py:323
  8.3 4.6 %collective-permute-start = (bf16[3,16,16,128]{3,2,1,0:T(8,128)(2,1)S(1)}, bf16[3,16,16,128]{3,2,1,0:T(8,128)(2,1)S(1)}, u32[]{:S(2)}, u32[]{:S(2)}) collective-permute-start(bf16[3,16,16,128]{3,2,1,0:T(8,128)(2,1)S(1)} %get-tuple-element.16), channel_id=1, source_target_pairs={{0,1},{1,2},{2,3},{3,4},{4,5},{5,6},{6,7},{7,8},{8,9},{9,10},{10,1... | collective-permute-start | bytes 589832 | tf_op jit(solution)/shard_map/ppermute | solution.py:322
  12.9 1.9 %collective-permute-start.1 = (bf16[3,16,16,128]{3,2,1,0:T(8,128)(2,1)S(1)}, bf16[3,16,16,128]{3,2,1,0:T(8,128)(2,1)S(1)}, u32[]{:S(2)}, u32[]{:S(2)}) collective-permute-start(bf16[3,16,16,128]{3,2,1,0:T(8,128)(2,1)S(1)} %get-tuple-element.15), channel_id=1, source_target_pairs={{1,0},{2,1},{3,2},{4,3},{5,4},{6,5},{7,6},{8,7},{9,8},{10,9},{11,1... | collective-permute-start | bytes 589832 | tf_op jit(solution)/shard_map/ppermute | solution.py:323
  14.8 0.1 pad_add_fusion.ends
  14.9 0.9 %copy-done.2 = bf16[4,16,16,128]{3,2,1,0:T(8,128)(2,1)S(1)} copy-done((bf16[4,16,16,128]{3,2,1,0:T(8,128)(2,1)S(1)}, bf16[4,16,16,128]{3,2,1,0:T(8,128)(2,1)}, u32[]{:S(2)}) %copy-start.2) | copy-done | bytes 262168
  15.8 1.2 %copy-done.10 = bf16[3,3,3,128,128]{4,3,2,1,0:T(8,128)(2,1)S(1)} copy-done((bf16[3,3,3,128,128]{4,3,2,1,0:T(8,128)(2,1)S(1)}, bf16[3,3,3,128,128]{4,3,2,1,0:T(8,128)(2,1)}, u32[]{:S(2)}) %copy-start.10) | copy-done | bytes 884760
  17.0 1.4 %shard_map.91.own = f32[4,256,256]{2,1,0:T(8,128)S(1)} custom-call(bf16[4,16,16,128]{3,2,1,0:T(8,128)(2,1)S(1)} %copy-done.2, bf16[3,1152,128]{2,1,0:T(8,128)(2,1)S(1)} %bitcast.32), custom_call_target="tpu_custom_call" | custom-call | flops 1207959552 | bytes 1146880 | tf_op jit(solution)/shard_map/pallas_call | solution.py:20
  18.4 1.4 %collective-permute-done.1.high = bf16[3,16,16,128]{3,2,1,0:T(8,128)(2,1)S(1)} collective-permute-done((bf16[3,16,16,128]{3,2,1,0:T(8,128)(2,1)S(1)}, bf16[3,16,16,128]{3,2,1,0:T(8,128)(2,1)S(1)}, u32[]{:S(2)}, u32[]{:S(2)}) %collective-permute-start.1) | collective-permute-done | bytes 196640 | tf_op jit(solution)/shard_map/ppermute | solution.py:323
  19.9 2.8 %shard_map.92 = (bf16[4,16,256]{2,1,0:T(8,128)(2,1)S(1)}, bf16[4,32,256]{2,1,0:T(8,128)(2,1)S(1)}) custom-call(s32[2]{0:T(128)S(1)} %pad_add_fusion.ends, bf16[3,16,16,128]{3,2,1,0:T(8,128)(2,1)S(1)} %collective-permute-done.low, bf16[3,16,16,128]{3,2,1,0:T(8,128)(2,1)S(1)} %collective-permute-done.1.high, f32[4,256,256]{2,1,0:T(8,128)S(1)} %shard_map.91.own, ...), custom_call_target="tpu_custom_call" | custom-call | flops 1207959552 | bytes 4227080 | tf_op jit(solution)/shard_map/pallas_call | solution.py:20
  22.7 10.1 %all_to_all.25.pooled = bf16[4,16,256]{2,1,0:T(8,128)(2,1)S(1)} all-to-all(bf16[4,16,256]{2,1,0:T(8,128)(2,1)S(1)} %get-tuple-element.10), channel_id=1, replica_groups=mesh['rep'=2,'z'=4,'r'=4] {'z'}, dimensions={0} | all-to-all | bytes 65536 | tf_op jit(solution)/shard_map/all_to_all | solution.py:294
  32.8 8.0 %all_to_all.26.near = bf16[4,96,256]{2,1,0:T(8,128)(2,1)S(1)} all-to-all(bf16[4,96,256]{2,1,0:T(8,128)(2,1)S(1)} %shard_map.93), channel_id=1, replica_groups=mesh['rep'=2,'z'=4,'r'=4] {'r'}, dimensions={0} | all-to-all | bytes 393216 | tf_op jit(solution)/shard_map/all_to_all | solution.py:294
  40.8 0.6 shard_map.94
  41.4 0.0 copy-start.6
  41.4 0.7 copy-done.6
  42.1 3.9 %all-to-all-start.2 = ((bf16[16,32,256]{2,1,0:T(8,128)(2,1)}), bf16[16,32,256]{2,1,0:T(8,128)(2,1)S(1)}, u32[]{:S(2)}, u32[]{:S(2)}) async-start(bf16[16,32,256]{2,1,0:T(8,128)(2,1)} %copy-done.6), calls=%async_computation.2 | async-start | bytes 524288 | tf_op jit(solution)/shard_map/all_to_all | solution.py:294
  46.0 3.3 %collective-permute-start.2 = (bf16[16,256]{1,0:T(8,128)(2,1)S(1)}, bf16[16,256]{1,0:T(8,128)(2,1)S(1)}, u32[]{:S(2)}, u32[]{:S(2)}) collective-permute-start(bf16[16,256]{1,0:T(8,128)(2,1)S(1)} %get-tuple-element.13), channel_id=1, source_target_pairs={{0,4},{4,8},{8,12},{1,5},{5,9},{9,13},{2,6},{6,10},{10,14},{3,7},{... | collective-permute-start | bytes 24584 | tf_op jit(solution)/shard_map/ppermute | solution.py:367
  49.3 1.3 %collective-permute-start.3 = (bf16[16,256]{1,0:T(8,128)(2,1)S(1)}, bf16[16,256]{1,0:T(8,128)(2,1)S(1)}, u32[]{:S(2)}, u32[]{:S(2)}) collective-permute-start(bf16[16,256]{1,0:T(8,128)(2,1)S(1)} %get-tuple-element.14), channel_id=1, source_target_pairs={{4,0},{8,4},{12,8},{5,1},{9,5},{13,9},{6,2},{10,6},{14,10},{7,3},{... | collective-permute-start | bytes 24584 | tf_op jit(solution)/shard_map/ppermute | solution.py:368
  50.6 6.7 %all-to-all-done.2 = bf16[16,32,256]{2,1,0:T(8,128)(2,1)S(1)} async-done(((bf16[16,32,256]{2,1,0:T(8,128)(2,1)}), bf16[16,32,256]{2,1,0:T(8,128)(2,1)S(1)}, u32[]{:S(2)}, u32[]{:S(2)}) %all-to-all-start.2) | async-done | bytes 262176 | tf_op jit(solution)/shard_map/all_to_all | solution.py:294
  57.2 0.7 shard_map.95
  57.9 0.0 copy-start.3
  58.0 0.6 copy-done.3
  58.6 4.3 %all-to-all-start.3 = ((bf16[16,32,128]{2,1,0:T(8,128)(2,1)}), bf16[16,32,128]{2,1,0:T(8,128)(2,1)S(1)}, u32[]{:S(2)}, u32[]{:S(2)}) async-start(bf16[16,32,128]{2,1,0:T(8,128)(2,1)} %copy-done.3), calls=%async_computation.3 | async-start | bytes 262144 | tf_op jit(solution)/shard_map/all_to_all | solution.py:294
  62.9 1.7 %fusion = bf16[64,8,512]{2,0,1:T(8,128)(2,1)S(1)} fusion(bf16[8,512,256]{2,1,0:T(8,128)(2,1)S(1)} %bitcast.24, bf16[256,256]{1,0:T(8,128)(2,1)} %constant.19.clone.order, s32[]{:T(128)S(6)} %select_n.3), kind=kOutput, calls=%fused_computation | convolution fusion | flops 134217728 | bytes 2686980 | tf_op jit(solution)/shard_map/pio,os->ips/dot_general | solution.py:382
  64.5 0.2 copy.15.rise
  64.8 0.0 copy-start.4
  64.8 0.0 collective-permute-done.3.high
  64.8 5.0 %all-to-all-done.3 = bf16[16,32,128]{2,1,0:T(8,128)(2,1)S(1)} async-done(((bf16[16,32,128]{2,1,0:T(8,128)(2,1)}), bf16[16,32,128]{2,1,0:T(8,128)(2,1)S(1)}, u32[]{:S(2)}, u32[]{:S(2)}) %all-to-all-start.3) | async-done | bytes 131104 | tf_op jit(solution)/shard_map/all_to_all | solution.py:294
  69.8 1.5 %copy-done.9 = bf16[4,864,256]{2,1,0:T(8,128)(2,1)S(1)} copy-done((bf16[4,864,256]{2,1,0:T(8,128)(2,1)S(1)}, bf16[4,864,256]{2,1,0:T(8,128)(2,1)}, u32[]{:S(2)}) %copy-start.9) | copy-done | bytes 1769496
  71.3 1.6 %shard_map.96 = bf16[512,256]{1,0:T(8,128)(2,1)S(1)} custom-call(bf16[512,128]{1,0:T(8,128)(2,1)S(1)} %bitcast.30, bf16[512,512]{1,0:T(8,128)(2,1)S(1)} %copy.15.rise, bf16[4,96,256]{2,1,0:T(8,128)(2,1)S(1)} %all_to_all.26.near, bf16[16,256]{1,0:T(8,128)(2,1)S(1)} %collective-permute-done.2.low, bf16[16,256]{1,0:T(8,128)(2,1)S(1)} %collective-permute-done.3.high, ...), custom_call_target="tpu_custom_call" | custom-call | flops 905969664 | bytes 2637824 | tf_op jit(solution)/shard_map/pallas_call | solution.py:20
  72.8 8.6 %all_to_all.27.partials = bf16[4,128,256]{2,1,0:T(8,128)(2,1)S(1)} all-to-all(bf16[4,128,256]{2,1,0:T(8,128)(2,1)S(1)} %bitcast.29), channel_id=1, replica_groups=mesh['rep'=2,'z'=4,'r'=4] {'r'}, dimensions={0} | all-to-all | bytes 524288 | tf_op jit(solution)/shard_map/all_to_all | solution.py:294
  81.4 1.1 %shard_map.97 = bf16[1024,128]{1,0:T(8,128)(2,1)} custom-call(bf16[4,128,256]{2,1,0:T(8,128)(2,1)S(1)} %all_to_all.27.partials, bf16[8,256,128]{2,1,0:T(8,128)(2,1)S(1)} %bitcast.27), custom_call_target="tpu_custom_call" | custom-call | flops 67108864 | bytes 786432 | tf_op jit(solution)/shard_map/pallas_call | solution.py:20
  (19 shorter events, 0.0 us)
Async XLA Ops:
  6.5 56.3 %copy-start = (bf16[2,2,2,512,256]{4,3,2,1,0:T(8,128)(2,1)S(1)}, bf16[2,2,2,512,256]{4,3,2,1,0:T(8,128)(2,1)}, u32[]{:S(2)}) copy-start(bf16[2,2,2,512,256]{4,3,2,1,0:T(8,128)(2,1)} %param.14) | copy-start | bytes 6291460
  6.5 63.3 %all-gather.2.cloned.1.call-start = ((), (), s32[]{:S(2)}) async-start(), calls=%async_computation.5 | async-start | bytes 2211840 | tf_op jit(solution)/shard_map/all_gather | solution.py:315
  8.3 10.1 %collective-permute-start = (bf16[3,16,16,128]{3,2,1,0:T(8,128)(2,1)S(1)}, bf16[3,16,16,128]{3,2,1,0:T(8,128)(2,1)S(1)}, u32[]{:S(2)}, u32[]{:S(2)}) collective-permute-start(bf16[3,16,16,128]{3,2,1,0:T(8,128)(2,1)S(1)} %get-tuple-element.16), channel_id=1, source_target_pairs={{0,1},{1,2},{2,3},{3,4},{4,5},{5,6},{6,7},{7,8},{8,9},{9,10},{10,1... | collective-permute-start | bytes 589832 | tf_op jit(solution)/shard_map/ppermute | solution.py:322
  12.9 7.0 %collective-permute-start.1 = (bf16[3,16,16,128]{3,2,1,0:T(8,128)(2,1)S(1)}, bf16[3,16,16,128]{3,2,1,0:T(8,128)(2,1)S(1)}, u32[]{:S(2)}, u32[]{:S(2)}) collective-permute-start(bf16[3,16,16,128]{3,2,1,0:T(8,128)(2,1)S(1)} %get-tuple-element.15), channel_id=1, source_target_pairs={{1,0},{2,1},{3,2},{4,3},{5,4},{6,5},{7,6},{8,7},{9,8},{10,9},{11,1... | collective-permute-start | bytes 589832 | tf_op jit(solution)/shard_map/ppermute | solution.py:323
  14.9 1.0 %copy-start.2 = (bf16[4,16,16,128]{3,2,1,0:T(8,128)(2,1)S(1)}, bf16[4,16,16,128]{3,2,1,0:T(8,128)(2,1)}, u32[]{:S(2)}) copy-start(bf16[4,16,16,128]{3,2,1,0:T(8,128)(2,1)} %volume.1) | copy-start | bytes 786436
  15.8 1.2 %copy-start.10 = (bf16[3,3,3,128,128]{4,3,2,1,0:T(8,128)(2,1)S(1)}, bf16[3,3,3,128,128]{4,3,2,1,0:T(8,128)(2,1)}, u32[]{:S(2)}) copy-start(bf16[3,3,3,128,128]{4,3,2,1,0:T(8,128)(2,1)} %param.10) | copy-start | bytes 2654212
  17.0 2.9 %copy-start.7 = (bf16[256,256]{1,0:T(8,128)(2,1)S(1)}, bf16[256,256]{1,0:T(8,128)(2,1)}, u32[]{:S(2)}) copy-start(bf16[256,256]{1,0:T(8,128)(2,1)} %constant.19.clone.order) | copy-start | bytes 393220
  17.0 2.9 %copy-start.8 = (bf16[3,3,3,128,256]{4,3,2,1,0:T(8,128)(2,1)S(1)}, bf16[3,3,3,128,256]{4,3,2,1,0:T(8,128)(2,1)}, u32[]{:S(2)}) copy-start(bf16[3,3,3,128,256]{4,3,2,1,0:T(8,128)(2,1)} %param.11) | copy-start | bytes 5308420
  19.9 21.0 %copy-start.5 = (bf16[3,3,3,256,32]{3,4,2,1,0:T(8,128)(2,1)S(1)}, bf16[3,3,3,256,32]{3,4,2,1,0:T(8,128)(2,1)}, u32[]{:S(2)}) copy-start(bf16[3,3,3,256,32]{3,4,2,1,0:T(8,128)(2,1)} %param.12) | copy-start | bytes 1327108
  19.9 37.4 %copy-start.1 = (bf16[3,3,3,512,32]{3,4,2,1,0:T(8,128)(2,1)S(1)}, bf16[3,3,3,512,32]{3,4,2,1,0:T(8,128)(2,1)}, u32[]{:S(2)}) copy-start(bf16[3,3,3,512,32]{3,4,2,1,0:T(8,128)(2,1)} %param.13) | copy-start | bytes 2654212
  41.4 0.7 copy-start.6
  42.1 15.1 %all-to-all-start.2 = ((bf16[16,32,256]{2,1,0:T(8,128)(2,1)}), bf16[16,32,256]{2,1,0:T(8,128)(2,1)S(1)}, u32[]{:S(2)}, u32[]{:S(2)}) async-start(bf16[16,32,256]{2,1,0:T(8,128)(2,1)} %copy-done.6), calls=%async_computation.2 | async-start | bytes 524288 | tf_op jit(solution)/shard_map/all_to_all | solution.py:294
  46.0 18.8 %collective-permute-start.2 = (bf16[16,256]{1,0:T(8,128)(2,1)S(1)}, bf16[16,256]{1,0:T(8,128)(2,1)S(1)}, u32[]{:S(2)}, u32[]{:S(2)}) collective-permute-start(bf16[16,256]{1,0:T(8,128)(2,1)S(1)} %get-tuple-element.13), channel_id=1, source_target_pairs={{0,4},{4,8},{8,12},{1,5},{5,9},{9,13},{2,6},{6,10},{10,14},{3,7},{... | collective-permute-start | bytes 24584 | tf_op jit(solution)/shard_map/ppermute | solution.py:367
  49.3 15.5 %collective-permute-start.3 = (bf16[16,256]{1,0:T(8,128)(2,1)S(1)}, bf16[16,256]{1,0:T(8,128)(2,1)S(1)}, u32[]{:S(2)}, u32[]{:S(2)}) collective-permute-start(bf16[16,256]{1,0:T(8,128)(2,1)S(1)} %get-tuple-element.14), channel_id=1, source_target_pairs={{4,0},{8,4},{12,8},{5,1},{9,5},{13,9},{6,2},{10,6},{14,10},{7,3},{... | collective-permute-start | bytes 24584 | tf_op jit(solution)/shard_map/ppermute | solution.py:368
  57.9 0.7 copy-start.3
  58.6 11.2 %all-to-all-start.3 = ((bf16[16,32,128]{2,1,0:T(8,128)(2,1)}), bf16[16,32,128]{2,1,0:T(8,128)(2,1)S(1)}, u32[]{:S(2)}, u32[]{:S(2)}) async-start(bf16[16,32,128]{2,1,0:T(8,128)(2,1)} %copy-done.3), calls=%async_computation.3 | async-start | bytes 262144 | tf_op jit(solution)/shard_map/all_to_all | solution.py:294
  64.8 16.6 %copy-start.4 = (bf16[2,2,2,256,128]{4,3,2,1,0:T(8,128)(2,1)S(1)}, bf16[2,2,2,256,128]{4,3,2,1,0:T(8,128)(2,1)}, u32[]{:S(2)}) copy-start(bf16[2,2,2,256,128]{4,3,2,1,0:T(8,128)(2,1)} %param.16) | copy-start | bytes 1572868
  69.8 1.5 %copy-start.9 = (bf16[4,864,256]{2,1,0:T(8,128)(2,1)S(1)}, bf16[4,864,256]{2,1,0:T(8,128)(2,1)}, u32[]{:S(2)}) copy-start(bf16[4,864,256]{2,1,0:T(8,128)(2,1)} %all-gather.2.cloned.1.call-done.decode) | copy-start | bytes 5308420
Sparse Core Ops, SparseCore 0:
  8.9 45.1 all-gather.1

commit v2 on v1

--- a/solution.py
+++ b/solution.py
@@ -12,11 +12,9 @@
 MIB = 1024 * 1024
 
 
-def call(kernel, outs, scratch, args, flops, vmem_mib, scalars=0):
-    spaces = [
-        pltpu.SMEM if i < scalars else pltpu.VMEM
-        for i in range(len(args))
-    ]
+def call(kernel, outs, scratch, args, flops, vmem_mib, scalars=0, unread=0):
+    spaces = [pltpu.SMEM] * scalars + [pltpu.VMEM] * (len(args) - scalars - unread)
+    spaces += [pl.ANY] * unread
     return pl.pallas_call(
         kernel,
         out_shape=outs,
@@ -26,7 +24,7 @@
         compiler_params=pltpu.CompilerParams(vmem_limit_bytes=vmem_mib * MIB),
         cost_estimate=pl.CostEstimate(
             flops=flops,
-            bytes_accessed=sum(a.size * a.dtype.itemsize for a in args),
+            bytes_accessed=sum(a.size * a.dtype.itemsize for a in args[: len(args) - unread]),
             transcendentals=0,
         ),
     )(*args)
@@ -77,6 +75,12 @@
 def depth_one(shifted, s, weights):
     left = jnp.concatenate([shifted[s, b : b + 16].reshape(256, 384) for b in range(3)], axis=1)
     return dot(left, weights)
+
+
+def front_stage(volume, tail, head, whole):
+    tail[...] = volume[1:]
+    head[...] = volume[:3]
+    whole[...] = volume[...]
 
 
 def own_stage(volume, weights, out, shifted):
@@ -224,6 +228,17 @@
             out[GROUP * p + r] = part
 
 
+def rise_stage(rank, chans, rise, _, out):
+    lane = lax.broadcasted_iota(jnp.int32, (256, 64), 1)
+    row = lax.broadcasted_iota(jnp.int32, (256, 64), 0)
+    source = (rank[0] + GROUP * (lane // chans)) * chans + lane % chans
+    mine = jnp.where(row == source, 1.0, 0.0).astype(jnp.bfloat16)
+    for pair in range(4):
+        both = [dot(rise[2 * pair + k], mine) for k in range(2)]
+        both = jnp.concatenate(both, axis=1).astype(jnp.bfloat16)
+        out[:, 128 * pair : 128 * pair + 128] = both
+
+
 def decode_stage(
     deeper, rise, near, low, high, decode, out, framed, patches, risen
 ):
@@ -319,8 +334,16 @@
 
     forward = [(i, i + 1) for i in range(n - 1)]
     backward = [(target, source) for source, target in forward]
-    low = lax.ppermute(volume[1:], ALL, forward)
-    high = lax.ppermute(volume[:3], ALL, backward)
+    tail, head, volume = call(
+        front_stage,
+        (bf16((3, 16, 16, 128)), bf16((3, 16, 16, 128)), bf16((4, 16, 16, 128))),
+        [],
+        (volume,),
+        3 * 10**9,
+        16,
+    )
+    low = lax.ppermute(tail, ALL, forward)
+    high = lax.ppermute(head, ALL, backward)
 
     taps = first_kernel.reshape(3, 1152, 128)
     own = call(
@@ -378,9 +401,16 @@
     )
     deeper_near = exchange(deeper, ALL).reshape(n * chans, 128)
 
-    mine = lax.dynamic_slice_in_dim(order, 64 * rank, 64, axis=1)
-    rise_part = jnp.einsum("pio,os->ips", rise_kernel.reshape(8, n * chans, 256), mine)
-    rise_part = rise_part.reshape(n * chans, 512)
+    rise_part = call(
+        lambda rank_ref, *refs: rise_stage(rank_ref, chans, *refs),
+        bf16((n * chans, 512)),
+        [],
+        (rank.astype(jnp.int32).reshape(1), rise_kernel.reshape(8, n * chans, 256), decode_part[0, :16]),
+        2 * 8 * n * chans * 256 * 64,
+        16,
+        scalars=1,
+        unread=1,
+    )
     partial = call(
         decode_stage,
         bf16((512, 256)),

time: 90.9 us -> 92.3 us (1.015)
  blocking collectives: 26.6 us -> 43 us
  waiting for transfers between devices: 13.8 us -> 5.87 us
  starting transfers between devices: 19.2 us -> 15.5 us
  local copies, waits for them, and re-layouts: 6.23 us -> 3.15 us
  matrix products: 1.67 us -> 0 us
  Pallas kernels: 8.12 us -> 9.68 us
    all_to_all x3 -> x4, blocking collectives: 26.6 us -> 43 us  [exchange(): lax.all_to_all(payload, axis, split_axis=0, concat_axis=0, tiled=True)]
    all_to_all x2 -> x1, waiting for transfers between devices: 11.7 us -> 0.01 us  [exchange(): lax.all_to_all(payload, axis, split_axis=0, concat_axis=0, tiled=True)]
    all_to_all x2 -> x1, starting transfers between devices: 8.13 us -> 4.27 us  [exchange(): lax.all_to_all(payload, axis, split_axis=0, concat_axis=0, tiled=True)]
    unnamed x22 -> x18, local copies, waits for them, and re-layouts: 4.97 us -> 2.45 us
    ppermute x2, waiting for transfers between devices: 1.43 us -> 3.55 us  [the longest x1 3.54 us: body(): high = lax.ppermute(head, ALL, backward)]
    dot_general x1 -> x0, matrix products: 1.67 us -> none  [body(): jnp.einsum('pio,os->ips', rise_kernel.reshape(8, n * chans, 256), mine)]
    ppermute x1, waiting for transfers between devices: 0.01 us -> 1.58 us  [body(): lax.ppermute(first, 'z', [(p + 1, p) for p in range(planes - 1)])]
    pallas_call x7 -> x9, Pallas kernels: 8.12 us -> 9.68 us  [call(): pl.pallas_call(kernel, out_shape=outs, in_specs=[pl.BlockSpec(memory_spac...]
  transfers between devices with their start and end apart: 7 -> 6, of which waited for: 3 -> 2; matrix products, arithmetic and copies ran while one was open for 3% -> 1% of each run, Pallas kernels for 6% -> 8%
where the time goes in v2:
time: 92.3 us; the launch traced here: 90.8 us
  blocking collectives  43 us (47%)
  starting transfers between devices  15.5 us (17%)
  between operations  13.5 us (15%)
  Pallas kernels  9.68 us (10%)
  waiting for transfers between devices  5.87 us (6%)
  local copies, waits for them, and re-layouts  3.15 us (3%)
    all_to_all x4, blocking collectives, exchange(): lax.all_to_all(payload, axis, split_axis=0, concat_axis=0, tiled=True)  43 us
    pallas_call x9, Pallas kernels, call(): pl.pallas_call(kernel, out_shape=outs, in_specs=[pl.BlockSpec(memory_spac...  9.68 us
    ppermute x1, starting transfers between devices, body(): low = lax.ppermute(tail, ALL, forward)  4.67 us
    all_to_all x1, starting transfers between devices, exchange(): lax.all_to_all(payload, axis, split_axis=0, concat_axis=0, tiled=True)  4.27 us
    ppermute x1, waiting for transfers between devices, body(): high = lax.ppermute(head, ALL, backward)  3.54 us
    ppermute x1, starting transfers between devices, body(): skip_low = lax.ppermute(last, 'z', [(p, p + 1) for p in range(planes - 1)])  3.3 us
    unnamed x18, local copies, waits for them, and re-layouts  2.45 us
    ppermute x1, starting transfers between devices, body(): high = lax.ppermute(head, ALL, backward)  1.92 us
  transfers between devices with their start and end apart: 6, of which 2 were waited for; matrix products, arithmetic and copies ran while one was open for 1% of the time, Pallas kernels for 8%

profile of v2, /device:TPU:1, one launch (start us, length us, event | category | flops | bytes accessed | tf_op | source)
XLA Modules:
  0.0 90.8 jit_solution(15861831558789638326)
XLA Ops:
  6.5 0.0 all-gather.2.cloned.1.call-start
  6.5 0.7 all-gather.2.cloned.1.call-update
  7.3 0.0 copy-start.7
  7.3 0.9 %copy-done.7 = bf16[4,16,16,128]{3,2,1,0:T(8,128)(2,1)S(1)} copy-done((bf16[4,16,16,128]{3,2,1,0:T(8,128)(2,1)S(1)}, bf16[4,16,16,128]{3,2,1,0:T(8,128)(2,1)}, u32[]{:S(2)}) %copy-start.7) | copy-done | bytes 262168
  8.2 0.1 shard_map.91
  8.3 4.7 %collective-permute-start = (bf16[3,16,16,128]{3,2,1,0:T(8,128)(2,1)S(1)}, bf16[3,16,16,128]{3,2,1,0:T(8,128)(2,1)S(1)}, u32[]{:S(2)}, u32[]{:S(2)}) collective-permute-start(bf16[3,16,16,128]{3,2,1,0:T(8,128)(2,1)S(1)} %get-tuple-element.13), channel_id=1, source_target_pairs={{0,1},{1,2},{2,3},{3,4},{4,5},{5,6},{6,7},{7,8},{8,9},{9,10},{10,1... | collective-permute-start | bytes 589832 | tf_op jit(solution)/shard_map/ppermute | solution.py:345
  13.0 1.9 %collective-permute-start.1 = (bf16[3,16,16,128]{3,2,1,0:T(8,128)(2,1)S(1)}, bf16[3,16,16,128]{3,2,1,0:T(8,128)(2,1)S(1)}, u32[]{:S(2)}, u32[]{:S(2)}) collective-permute-start(bf16[3,16,16,128]{3,2,1,0:T(8,128)(2,1)S(1)} %get-tuple-element.14), channel_id=1, source_target_pairs={{1,0},{2,1},{3,2},{4,3},{5,4},{6,5},{7,6},{8,7},{9,8},{10,9},{11,1... | collective-permute-start | bytes 589832 | tf_op jit(solution)/shard_map/ppermute | solution.py:346
  14.9 0.1 pad_add_fusion.ends
  15.0 1.4 %shard_map.92.own = f32[4,256,256]{2,1,0:T(8,128)S(1)} custom-call(bf16[4,16,16,128]{3,2,1,0:T(8,128)(2,1)S(1)} %get-tuple-element.15.volume, bf16[3,1152,128]{2,1,0:T(8,128)(2,1)S(1)} %bitcast.28), custom_call_target="tpu_custom_call" | custom-call | flops 1207959552 | bytes 1146880 | tf_op jit(solution)/shard_map/pallas_call | solution.py:18
  16.4 0.0 collective-permute-done.low
  16.4 3.5 %collective-permute-done.1.high = bf16[3,16,16,128]{3,2,1,0:T(8,128)(2,1)S(1)} collective-permute-done((bf16[3,16,16,128]{3,2,1,0:T(8,128)(2,1)S(1)}, bf16[3,16,16,128]{3,2,1,0:T(8,128)(2,1)S(1)}, u32[]{:S(2)}, u32[]{:S(2)}) %collective-permute-start.1) | collective-permute-done | bytes 196640 | tf_op jit(solution)/shard_map/ppermute | solution.py:346
  20.0 2.8 %shard_map.93 = (bf16[4,16,256]{2,1,0:T(8,128)(2,1)S(1)}, bf16[4,32,256]{2,1,0:T(8,128)(2,1)S(1)}) custom-call(s32[2]{0:T(128)S(1)} %pad_add_fusion.ends, bf16[3,16,16,128]{3,2,1,0:T(8,128)(2,1)S(1)} %collective-permute-done.low, bf16[3,16,16,128]{3,2,1,0:T(8,128)(2,1)S(1)} %collective-permute-done.1.high, f32[4,256,256]{2,1,0:T(8,128)S(1)} %shard_map.92.own, ...), custom_call_target="tpu_custom_call" | custom-call | flops 1207959552 | bytes 4227080 | tf_op jit(solution)/shard_map/pallas_call | solution.py:18
  22.8 0.0 copy-start
  22.8 10.1 %all_to_all.25.pooled = bf16[4,16,256]{2,1,0:T(8,128)(2,1)S(1)} all-to-all(bf16[4,16,256]{2,1,0:T(8,128)(2,1)S(1)} %get-tuple-element.16), channel_id=1, replica_groups=mesh['rep'=2,'z'=4,'r'=4] {'z'}, dimensions={0} | all-to-all | bytes 65536 | tf_op jit(solution)/shard_map/all_to_all | solution.py:309
  33.0 7.5 %all_to_all.26.near = bf16[4,96,256]{2,1,0:T(8,128)(2,1)S(1)} all-to-all(bf16[4,96,256]{2,1,0:T(8,128)(2,1)S(1)} %shard_map.94), channel_id=1, replica_groups=mesh['rep'=2,'z'=4,'r'=4] {'r'}, dimensions={0} | all-to-all | bytes 393216 | tf_op jit(solution)/shard_map/all_to_all | solution.py:309
  40.5 0.6 shard_map.95
  41.1 16.1 %all_to_all.27 = bf16[16,32,256]{2,1,0:T(8,128)(2,1)S(1)} all-to-all(bf16[16,32,256]{2,1,0:T(8,128)(2,1)S(1)} %get-tuple-element.18), channel_id=1, replica_groups=mesh['rep'=2,'z'=4,'r'=4] {'z','r'}, dimensions={0} | all-to-all | bytes 524288 | tf_op jit(solution)/shard_map/all_to_all | solution.py:309
  57.2 1.4 %shard_map.96 = bf16[16,32,128]{2,1,0:T(8,128)(2,1)} custom-call(bf16[512,256]{1,0:T(8,128)(2,1)S(1)} %bitcast.21, bf16[864,512]{1,0:T(8,128)(2,1)S(1)} %bitcast.22), custom_call_target="tpu_custom_call" | custom-call | flops 226492416 | bytes 1146880 | tf_op jit(solution)/shard_map/pallas_call | solution.py:18
  58.5 4.3 %all-to-all-start.3 = ((bf16[16,32,128]{2,1,0:T(8,128)(2,1)}), bf16[16,32,128]{2,1,0:T(8,128)(2,1)S(1)}, u32[]{:S(2)}, u32[]{:S(2)}) async-start(bf16[16,32,128]{2,1,0:T(8,128)(2,1)} %shard_map.96), calls=%async_computation.3 | async-start | bytes 262144 | tf_op jit(solution)/shard_map/all_to_all | solution.py:309
  62.8 3.3 %collective-permute-start.2 = (bf16[16,256]{1,0:T(8,128)(2,1)S(1)}, bf16[16,256]{1,0:T(8,128)(2,1)S(1)}, u32[]{:S(2)}, u32[]{:S(2)}) collective-permute-start(bf16[16,256]{1,0:T(8,128)(2,1)S(1)} %get-tuple-element.19), channel_id=1, source_target_pairs={{0,4},{4,8},{8,12},{1,5},{5,9},{9,13},{2,6},{6,10},{10,14},{3,7},{... | collective-permute-start | bytes 24584 | tf_op jit(solution)/shard_map/ppermute | solution.py:390
  66.1 1.3 %collective-permute-start.3 = (bf16[16,256]{1,0:T(8,128)(2,1)S(1)}, bf16[16,256]{1,0:T(8,128)(2,1)S(1)}, u32[]{:S(2)}, u32[]{:S(2)}) collective-permute-start(bf16[16,256]{1,0:T(8,128)(2,1)S(1)} %get-tuple-element.20), channel_id=1, source_target_pairs={{4,0},{8,4},{12,8},{5,1},{9,5},{13,9},{6,2},{10,6},{14,10},{7,3},{... | collective-permute-start | bytes 24584 | tf_op jit(solution)/shard_map/ppermute | solution.py:391
  67.4 0.0 all-gather.2.cloned.1.call-done.decode
  67.4 0.7 slice_bitcast_fusion.refs_1_
  68.1 0.8 shard_map.97.rise
  68.9 0.0 collective-permute-done.2.low
  68.9 1.6 %collective-permute-done.3.high = bf16[16,256]{1,0:T(8,128)(2,1)S(1)} collective-permute-done((bf16[16,256]{1,0:T(8,128)(2,1)S(1)}, bf16[16,256]{1,0:T(8,128)(2,1)S(1)}, u32[]{:S(2)}, u32[]{:S(2)}) %collective-permute-start.3) | collective-permute-done | bytes 8224 | tf_op jit(solution)/shard_map/ppermute | solution.py:391
  70.5 0.0 all-to-all-done.3
  70.5 1.5 %copy-done.4 = bf16[4,864,256]{2,1,0:T(8,128)(2,1)S(1)} copy-done((bf16[4,864,256]{2,1,0:T(8,128)(2,1)S(1)}, bf16[4,864,256]{2,1,0:T(8,128)(2,1)}, u32[]{:S(2)}) %copy-start.4) | copy-done | bytes 1769496
  72.0 1.6 %shard_map.98 = bf16[512,256]{1,0:T(8,128)(2,1)S(1)} custom-call(bf16[512,128]{1,0:T(8,128)(2,1)S(1)} %bitcast.26, bf16[512,512]{1,0:T(8,128)(2,1)S(1)} %shard_map.97.rise, bf16[4,96,256]{2,1,0:T(8,128)(2,1)S(1)} %all_to_all.26.near, bf16[16,256]{1,0:T(8,128)(2,1)S(1)} %collective-permute-done.2.low, bf16[16,256]{1,0:T(8,128)(2,1)S(1)} %collective-permute-done.3.high, ...), custom_call_target="tpu_custom_call" | custom-call | flops 905969664 | bytes 2637824 | tf_op jit(solution)/shard_map/pallas_call | solution.py:18
  73.6 9.3 %all_to_all.28.partials = bf16[4,128,256]{2,1,0:T(8,128)(2,1)S(1)} all-to-all(bf16[4,128,256]{2,1,0:T(8,128)(2,1)S(1)} %bitcast.25), channel_id=1, replica_groups=mesh['rep'=2,'z'=4,'r'=4] {'r'}, dimensions={0} | all-to-all | bytes 524288 | tf_op jit(solution)/shard_map/all_to_all | solution.py:309
  82.9 0.0 copy-done.2
  82.9 1.1 %shard_map.99 = bf16[1024,128]{1,0:T(8,128)(2,1)} custom-call(bf16[4,128,256]{2,1,0:T(8,128)(2,1)S(1)} %all_to_all.28.partials, bf16[8,256,128]{2,1,0:T(8,128)(2,1)S(1)} %bitcast.23), custom_call_target="tpu_custom_call" | custom-call | flops 67108864 | bytes 786432 | tf_op jit(solution)/shard_map/pallas_call | solution.py:18
  (14 shorter events, 0.0 us)
Async XLA Ops:
  6.5 60.9 %all-gather.2.cloned.1.call-start = ((), (), s32[]{:S(2)}) async-start(), calls=%async_computation.5 | async-start | bytes 2211840 | tf_op jit(solution)/shard_map/all_gather | solution.py:330
  7.3 1.0 %copy-start.7 = (bf16[4,16,16,128]{3,2,1,0:T(8,128)(2,1)S(1)}, bf16[4,16,16,128]{3,2,1,0:T(8,128)(2,1)}, u32[]{:S(2)}) copy-start(bf16[4,16,16,128]{3,2,1,0:T(8,128)(2,1)} %volume.1) | copy-start | bytes 786436
  8.2 6.8 %copy-start.6 = (bf16[3,3,3,128,128]{4,3,2,1,0:T(8,128)(2,1)S(1)}, bf16[3,3,3,128,128]{4,3,2,1,0:T(8,128)(2,1)}, u32[]{:S(2)}) copy-start(bf16[3,3,3,128,128]{4,3,2,1,0:T(8,128)(2,1)} %param.10) | copy-start | bytes 2654212
  8.3 8.1 %collective-permute-start = (bf16[3,16,16,128]{3,2,1,0:T(8,128)(2,1)S(1)}, bf16[3,16,16,128]{3,2,1,0:T(8,128)(2,1)S(1)}, u32[]{:S(2)}, u32[]{:S(2)}) collective-permute-start(bf16[3,16,16,128]{3,2,1,0:T(8,128)(2,1)S(1)} %get-tuple-element.13), channel_id=1, source_target_pairs={{0,1},{1,2},{2,3},{3,4},{4,5},{5,6},{6,7},{7,8},{8,9},{9,10},{10,1... | collective-permute-start | bytes 589832 | tf_op jit(solution)/shard_map/ppermute | solution.py:345
  13.0 7.0 %collective-permute-start.1 = (bf16[3,16,16,128]{3,2,1,0:T(8,128)(2,1)S(1)}, bf16[3,16,16,128]{3,2,1,0:T(8,128)(2,1)S(1)}, u32[]{:S(2)}, u32[]{:S(2)}) collective-permute-start(bf16[3,16,16,128]{3,2,1,0:T(8,128)(2,1)S(1)} %get-tuple-element.14), channel_id=1, source_target_pairs={{1,0},{2,1},{3,2},{4,3},{5,4},{6,5},{7,6},{8,7},{9,8},{10,9},{11,1... | collective-permute-start | bytes 589832 | tf_op jit(solution)/shard_map/ppermute | solution.py:346
  15.0 5.0 %copy-start.5 = (bf16[3,3,3,128,256]{4,3,2,1,0:T(8,128)(2,1)S(1)}, bf16[3,3,3,128,256]{4,3,2,1,0:T(8,128)(2,1)}, u32[]{:S(2)}) copy-start(bf16[3,3,3,128,256]{4,3,2,1,0:T(8,128)(2,1)} %param.11) | copy-start | bytes 5308420
  15.0 5.0 %copy-start.8 = (bf16[256,256]{1,0:T(8,128)(2,1)S(1)}, bf16[256,256]{1,0:T(8,128)(2,1)}, u32[]{:S(2)}) copy-start(bf16[256,256]{1,0:T(8,128)(2,1)} %constant.13.clone.order) | copy-start | bytes 393220
  20.0 20.5 %copy-start.3 = (bf16[3,3,3,256,32]{3,4,2,1,0:T(8,128)(2,1)S(1)}, bf16[3,3,3,256,32]{3,4,2,1,0:T(8,128)(2,1)}, u32[]{:S(2)}) copy-start(bf16[3,3,3,256,32]{3,4,2,1,0:T(8,128)(2,1)} %param.12) | copy-start | bytes 1327108
  20.0 37.2 %copy-start.1 = (bf16[3,3,3,512,32]{3,4,2,1,0:T(8,128)(2,1)S(1)}, bf16[3,3,3,512,32]{3,4,2,1,0:T(8,128)(2,1)}, u32[]{:S(2)}) copy-start(bf16[3,3,3,512,32]{3,4,2,1,0:T(8,128)(2,1)} %param.13) | copy-start | bytes 2654212
  22.8 45.3 %copy-start = (bf16[2,2,2,512,256]{4,3,2,1,0:T(8,128)(2,1)S(1)}, bf16[2,2,2,512,256]{4,3,2,1,0:T(8,128)(2,1)}, u32[]{:S(2)}) copy-start(bf16[2,2,2,512,256]{4,3,2,1,0:T(8,128)(2,1)} %param.14) | copy-start | bytes 6291460
  58.5 12.0 %all-to-all-start.3 = ((bf16[16,32,128]{2,1,0:T(8,128)(2,1)}), bf16[16,32,128]{2,1,0:T(8,128)(2,1)S(1)}, u32[]{:S(2)}, u32[]{:S(2)}) async-start(bf16[16,32,128]{2,1,0:T(8,128)(2,1)} %shard_map.96), calls=%async_computation.3 | async-start | bytes 262144 | tf_op jit(solution)/shard_map/all_to_all | solution.py:309
  62.8 6.1 %collective-permute-start.2 = (bf16[16,256]{1,0:T(8,128)(2,1)S(1)}, bf16[16,256]{1,0:T(8,128)(2,1)S(1)}, u32[]{:S(2)}, u32[]{:S(2)}) collective-permute-start(bf16[16,256]{1,0:T(8,128)(2,1)S(1)} %get-tuple-element.19), channel_id=1, source_target_pairs={{0,4},{4,8},{8,12},{1,5},{5,9},{9,13},{2,6},{6,10},{10,14},{3,7},{... | collective-permute-start | bytes 24584 | tf_op jit(solution)/shard_map/ppermute | solution.py:390
  66.1 4.4 %collective-permute-start.3 = (bf16[16,256]{1,0:T(8,128)(2,1)S(1)}, bf16[16,256]{1,0:T(8,128)(2,1)S(1)}, u32[]{:S(2)}, u32[]{:S(2)}) collective-permute-start(bf16[16,256]{1,0:T(8,128)(2,1)S(1)} %get-tuple-element.20), channel_id=1, source_target_pairs={{4,0},{8,4},{12,8},{5,1},{9,5},{13,9},{6,2},{10,6},{14,10},{7,3},{... | collective-permute-start | bytes 24584 | tf_op jit(solution)/shard_map/ppermute | solution.py:391
  70.5 1.5 %copy-start.4 = (bf16[4,864,256]{2,1,0:T(8,128)(2,1)S(1)}, bf16[4,864,256]{2,1,0:T(8,128)(2,1)}, u32[]{:S(2)}) copy-start(bf16[4,864,256]{2,1,0:T(8,128)(2,1)} %all-gather.2.cloned.1.call-done.decode) | copy-start | bytes 5308420
  72.0 10.9 %copy-start.2 = (bf16[2,2,2,256,128]{4,3,2,1,0:T(8,128)(2,1)S(1)}, bf16[2,2,2,256,128]{4,3,2,1,0:T(8,128)(2,1)}, u32[]{:S(2)}) copy-start(bf16[2,2,2,256,128]{4,3,2,1,0:T(8,128)(2,1)} %param.16) | copy-start | bytes 1572868
Sparse Core Ops, SparseCore 0:
  8.9 47.5 all-gather.1

commit v3 on v2

--- a/solution.py
+++ b/solution.py
@@ -12,19 +12,22 @@
 MIB = 1024 * 1024
 
 
-def call(kernel, outs, scratch, args, flops, vmem_mib, scalars=0, unread=0):
-    spaces = [pltpu.SMEM] * scalars + [pltpu.VMEM] * (len(args) - scalars - unread)
-    spaces += [pl.ANY] * unread
+def call(kernel, outs, scratch, args, flops, vmem_mib, scalars=0, far=0, far_outs=0):
+    spaces = [pltpu.SMEM] * scalars + [pltpu.VMEM] * (len(args) - scalars - far)
+    spaces += [pl.ANY] * far
+    several = isinstance(outs, tuple)
+    out_spaces = [pltpu.VMEM] * ((len(outs) if several else 1) - far_outs) + [pl.ANY] * far_outs
+    out_specs = [pl.BlockSpec(memory_space=space) for space in out_spaces]
     return pl.pallas_call(
         kernel,
         out_shape=outs,
         in_specs=[pl.BlockSpec(memory_space=space) for space in spaces],
-        out_specs=jax.tree.map(lambda _: pl.BlockSpec(memory_space=pltpu.VMEM), outs),
+        out_specs=out_specs if several else out_specs[0],
         scratch_shapes=scratch,
         compiler_params=pltpu.CompilerParams(vmem_limit_bytes=vmem_mib * MIB),
         cost_estimate=pl.CostEstimate(
             flops=flops,
-            bytes_accessed=sum(a.size * a.dtype.itemsize for a in args[: len(args) - unread]),
+            bytes_accessed=sum(a.size * a.dtype.itemsize for a in args[: len(args) - far]),
             transcendentals=0,
         ),
     )(*args)
@@ -77,10 +80,15 @@
     return dot(left, weights)
 
 
-def front_stage(volume, tail, head, whole):
+def front_stage(rep, volume, decode, tail, head, whole, block, done):
+    rows = block.shape[0]
+    at = pl.multiple_of(jnp.where(rows == decode.shape[0], 0, rep[0] * rows), 16)
+    copy = pltpu.make_async_copy(decode.at[pl.ds(at, rows)], block, done)
+    copy.start()
     tail[...] = volume[1:]
     head[...] = volume[:3]
     whole[...] = volume[...]
+    copy.wait()
 
 
 def own_stage(volume, weights, out, shifted):
@@ -211,7 +219,7 @@
     last[...] = edge_slice(near[GROUP - 1, voxels // GROUP :, :], True)
 
 
-def deeper_stage(deep, weights, out):
+def deeper_stage(deep, weights, _, __, out):
     n, chans, _ = out.shape
     voxels = deep.shape[1]
     deeper = spread_taps(weights, deep[...], ((1,), (0,)), chans, voxels)
@@ -228,7 +236,9 @@
             out[GROUP * p + r] = part
 
 
-def rise_stage(rank, chans, rise, _, out):
+def rise_stage(rank, chans, rise, decode, out, weights, done):
+    copy = pltpu.make_async_copy(decode, weights, done)
+    copy.start()
     lane = lax.broadcasted_iota(jnp.int32, (256, 64), 1)
     row = lax.broadcasted_iota(jnp.int32, (256, 64), 0)
     source = (rank[0] + GROUP * (lane // chans)) * chans + lane % chans
@@ -237,6 +247,7 @@
         both = [dot(rise[2 * pair + k], mine) for k in range(2)]
         both = jnp.concatenate(both, axis=1).astype(jnp.bfloat16)
         out[:, 128 * pair : 128 * pair + 128] = both
+    copy.wait()
 
 
 def decode_stage(
@@ -272,14 +283,15 @@
         joined = framed[s, 1:9, 8:16, :].reshape(64, 128)
         framed[s, 1:9, 8:16, :] = jnp.where(upper, skip, joined).reshape(8, 8, 128)
     fill_patches(framed, patches, 10)
-    blocks = decode.shape[0]
+    _, blocks, rows, _ = decode.shape
     step = 128 // blocks
     partial = None
     for a in range(3):
         right = [
-            decode[z, tap * step : (tap + 1) * step, :]
+            decode[row // rows, z, row % rows : row % rows + 16, :]
             for tap in range(9 * a, 9 * a + 9)
             for z in range(blocks)
+            for row in range(tap * step, (tap + 1) * step, 16)
         ]
         term = dot(patches[64 * a : 64 * a + 512], jnp.concatenate(right, axis=0))
         partial = term if partial is None else partial + term
@@ -327,21 +339,39 @@
     voxels = 16 * n
     bf16 = functools.partial(jax.ShapeDtypeStruct, dtype=jnp.bfloat16)
 
-    decode_part = lax.all_gather(decode_kernel.reshape(27 * chans, 256), "z", axis=0)
-    if chans % 16:
+    shares = 2 if lax.axis_size("rep") == 2 and 27 * chans % 32 == 0 else 1
+    rows = 27 * chans // shares
+    tail, head, volume, block = call(
+        front_stage,
+        (
+            bf16((3, 16, 16, 128)),
+            bf16((3, 16, 16, 128)),
+            bf16((4, 16, 16, 128)),
+            bf16((rows, 256)),
+        ),
+        [pltpu.SemaphoreType.DMA],
+        (
+            lax.axis_index("rep").astype(jnp.int32).reshape(1),
+            volume,
+            decode_kernel.reshape(27 * chans, 256),
+        ),
+        3 * 10**9,
+        16,
+        scalars=1,
+        far=1,
+        far_outs=1,
+    )
+    decode_part = lax.all_gather(block, "z", axis=0)
+    if shares == 2:
+        decode_part = lax.all_gather(decode_part, "rep", axis=0)
+    elif chans % 16:
         decode_part = decode_part.reshape(planes, 27, chans, 256).transpose(1, 0, 2, 3)
-        decode_part = decode_part.reshape(1, 27 * 128, 256)
+        decode_part = decode_part.reshape(1, 1, 27 * 128, 256)
+    else:
+        decode_part = decode_part[None]
 
     forward = [(i, i + 1) for i in range(n - 1)]
     backward = [(target, source) for source, target in forward]
-    tail, head, volume = call(
-        front_stage,
-        (bf16((3, 16, 16, 128)), bf16((3, 16, 16, 128)), bf16((4, 16, 16, 128))),
-        [],
-        (volume,),
-        3 * 10**9,
-        16,
-    )
     low = lax.ppermute(tail, ALL, forward)
     high = lax.ppermute(head, ALL, backward)
 
@@ -395,21 +425,27 @@
         deeper_stage,
         bf16((n, chans, 128)),
         [],
-        (deep_whole, deeper_kernel.transpose(0, 1, 2, 4, 3).reshape(27 * chans, n * chans)),
+        (
+            deep_whole,
+            deeper_kernel.transpose(0, 1, 2, 4, 3).reshape(27 * chans, n * chans),
+            skip_low,
+            skip_high,
+        ),
         2 * 27 * chans * n * chans * voxels,
         16,
+        far=2,
     )
     deeper_near = exchange(deeper, ALL).reshape(n * chans, 128)
 
-    rise_part = call(
+    rise_part, decode_part = call(
         lambda rank_ref, *refs: rise_stage(rank_ref, chans, *refs),
-        bf16((n * chans, 512)),
-        [],
-        (rank.astype(jnp.int32).reshape(1), rise_kernel.reshape(8, n * chans, 256), decode_part[0, :16]),
+        (bf16((n * chans, 512)), bf16(decode_part.shape)),
+        [pltpu.SemaphoreType.DMA],
+        (rank.astype(jnp.int32).reshape(1), rise_kernel.reshape(8, n * chans, 256), decode_part),
         2 * 8 * n * chans * 256 * 64,
         16,
         scalars=1,
-        unread=1,
+        far=1,
     )
     partial = call(
         decode_stage,

time: 92.3 us -> 109 us (1.18)
  starting transfers between devices: 15.5 us -> 21.5 us
  waiting for transfers between devices: 5.87 us -> 11.8 us
  local copies, waits for them, and re-layouts: 3.15 us -> 7.53 us
    all_to_all x4 -> x3, blocking collectives: 43 us -> 23.4 us  [exchange(): lax.all_to_all(payload, axis, split_axis=0, concat_axis=0, tiled=True)]
    all_gather x0 -> x1, blocking collectives: none -> 19.5 us  [body(): decode_part = lax.all_gather(block, 'z', axis=0)]
    unnamed x18 -> x28, local copies, waits for them, and re-layouts: 2.45 us -> 7.53 us
    all_to_all x1 -> x2, waiting for transfers between devices: 0.01 us -> 4.73 us  [exchange(): lax.all_to_all(payload, axis, split_axis=0, concat_axis=0, tiled=True)]
    all_to_all x1 -> x2, starting transfers between devices: 4.27 us -> 8.34 us  [exchange(): lax.all_to_all(payload, axis, split_axis=0, concat_axis=0, tiled=True)]
    ppermute x1, starting transfers between devices: 4.67 us -> 6.68 us  [body(): low = lax.ppermute(tail, ALL, forward)]
    ppermute x1, waiting for transfers between devices: 1.58 us -> 2.93 us  [body(): lax.ppermute(first, 'z', [(p + 1, p) for p in range(planes - 1)])]
  transfers between devices with their start and end apart: 6 -> 7, of which waited for: 2 -> 5; matrix products, arithmetic and copies ran while one was open for 1% -> 0% of each run, Pallas kernels for 8% -> 6%
where the time goes in v3:
time: 109 us; the launch traced here: 107 us
  blocking collectives  42.9 us (39%)
  starting transfers between devices  21.5 us (20%)
  between operations  13.6 us (12%)
  waiting for transfers between devices  11.8 us (11%)
  Pallas kernels  9.66 us (9%)
  local copies, waits for them, and re-layouts  7.53 us (7%)
    all_to_all x3, blocking collectives, exchange(): lax.all_to_all(payload, axis, split_axis=0, concat_axis=0, tiled=True)  23.4 us
    all_gather x1, blocking collectives, body(): decode_part = lax.all_gather(block, 'z', axis=0)  19.5 us
    pallas_call x9, Pallas kernels, call(): pl.pallas_call(kernel, out_shape=outs, in_specs=[pl.BlockSpec(memory_spac...  9.66 us
    all_to_all x2, starting transfers between devices, exchange(): lax.all_to_all(payload, axis, split_axis=0, concat_axis=0, tiled=True)  8.34 us
    unnamed x28, local copies, waits for them, and re-layouts  7.53 us
    ppermute x1, starting transfers between devices, body(): low = lax.ppermute(tail, ALL, forward)  6.68 us
    all_to_all x2, waiting for transfers between devices, exchange(): lax.all_to_all(payload, axis, split_axis=0, concat_axis=0, tiled=True)  4.73 us
    ppermute x1, waiting for transfers between devices, body(): high = lax.ppermute(head, ALL, backward)  3.95 us
  transfers between devices with their start and end apart: 7, of which 5 were waited for; matrix products, arithmetic and copies ran while one was open for 0% of the time, Pallas kernels for 6%

profile of v3, /device:TPU:1, one launch (start us, length us, event | category | flops | bytes accessed | tf_op | source)
XLA Modules:
  0.0 107.2 jit_solution(12415423473660527063)
XLA Ops:
  6.5 1.0 copy-done.11
  7.6 0.9 copy-done.12
  8.5 0.3 shard_map.91
  8.9 19.5 %all-gather = bf16[1728,256]{1,0:T(8,128)(2,1)} all-gather(bf16[432,256]{1,0:T(8,128)(2,1)S(1)} %get-tuple-element.24), channel_id=2, replica_groups=mesh['rep'=2,'z'=4,'r'=4] {'z'}, dimensions={0}, use_global_device_ids=true | all-gather | bytes 1105920 | tf_op jit(solution)/shard_map/all_gather | solution.py:364
  28.4 0.0 all-gather.4.cloned.1.call-update
  28.4 6.7 %collective-permute-start = (bf16[3,16,16,128]{3,2,1,0:T(8,128)(2,1)S(1)}, bf16[3,16,16,128]{3,2,1,0:T(8,128)(2,1)S(1)}, u32[]{:S(2)}, u32[]{:S(2)}) collective-permute-start(bf16[3,16,16,128]{3,2,1,0:T(8,128)(2,1)S(1)} %get-tuple-element.16), channel_id=1, source_target_pairs={{0,1},{1,2},{2,3},{3,4},{4,5},{5,6},{6,7},{7,8},{8,9},{9,10},{10,1... | collective-permute-start | bytes 589832 | tf_op jit(solution)/shard_map/ppermute | solution.py:375
  35.1 1.9 %collective-permute-start.1 = (bf16[3,16,16,128]{3,2,1,0:T(8,128)(2,1)S(1)}, bf16[3,16,16,128]{3,2,1,0:T(8,128)(2,1)S(1)}, u32[]{:S(2)}, u32[]{:S(2)}) collective-permute-start(bf16[3,16,16,128]{3,2,1,0:T(8,128)(2,1)S(1)} %get-tuple-element.17), channel_id=1, source_target_pairs={{1,0},{2,1},{3,2},{4,3},{5,4},{6,5},{7,6},{8,7},{9,8},{10,9},{11,1... | collective-permute-start | bytes 589832 | tf_op jit(solution)/shard_map/ppermute | solution.py:376
  37.0 0.1 pad_add_fusion.ends
  37.1 1.4 %shard_map.92.own = f32[4,256,256]{2,1,0:T(8,128)S(1)} custom-call(bf16[4,16,16,128]{3,2,1,0:T(8,128)(2,1)S(1)} %get-tuple-element.18.volume, bf16[3,1152,128]{2,1,0:T(8,128)(2,1)S(1)} %bitcast.30), custom_call_target="tpu_custom_call" | custom-call | flops 1207959552 | bytes 1146880 | tf_op jit(solution)/shard_map/pallas_call | solution.py:21
  38.5 3.9 %collective-permute-done.1.high = bf16[3,16,16,128]{3,2,1,0:T(8,128)(2,1)S(1)} collective-permute-done((bf16[3,16,16,128]{3,2,1,0:T(8,128)(2,1)S(1)}, bf16[3,16,16,128]{3,2,1,0:T(8,128)(2,1)S(1)}, u32[]{:S(2)}, u32[]{:S(2)}) %collective-permute-start.1) | collective-permute-done | bytes 196640 | tf_op jit(solution)/shard_map/ppermute | solution.py:376
  42.5 2.8 %shard_map.93 = (bf16[4,16,256]{2,1,0:T(8,128)(2,1)S(1)}, bf16[4,32,256]{2,1,0:T(8,128)(2,1)S(1)}) custom-call(s32[2]{0:T(128)S(1)} %pad_add_fusion.ends, bf16[3,16,16,128]{3,2,1,0:T(8,128)(2,1)S(1)} %collective-permute-done.low, bf16[3,16,16,128]{3,2,1,0:T(8,128)(2,1)S(1)} %collective-permute-done.1.high, f32[4,256,256]{2,1,0:T(8,128)S(1)} %shard_map.92.own, ...), custom_call_target="tpu_custom_call" | custom-call | flops 1207959552 | bytes 4227080 | tf_op jit(solution)/shard_map/pallas_call | solution.py:21
  45.3 7.3 %all_to_all.25.pooled = bf16[4,16,256]{2,1,0:T(8,128)(2,1)S(1)} all-to-all(bf16[4,16,256]{2,1,0:T(8,128)(2,1)S(1)} %get-tuple-element.19), channel_id=1, replica_groups=mesh['rep'=2,'z'=4,'r'=4] {'z'}, dimensions={0} | all-to-all | bytes 65536 | tf_op jit(solution)/shard_map/all_to_all | solution.py:321
  52.6 7.6 %all_to_all.26.near = bf16[4,96,256]{2,1,0:T(8,128)(2,1)S(1)} all-to-all(bf16[4,96,256]{2,1,0:T(8,128)(2,1)S(1)} %shard_map.94), channel_id=1, replica_groups=mesh['rep'=2,'z'=4,'r'=4] {'r'}, dimensions={0} | all-to-all | bytes 393216 | tf_op jit(solution)/shard_map/all_to_all | solution.py:321
  60.2 0.6 shard_map.95
  60.8 0.7 copy-done.6
  61.5 3.8 %all-to-all-start.2 = ((bf16[16,32,256]{2,1,0:T(8,128)(2,1)}), bf16[16,32,256]{2,1,0:T(8,128)(2,1)S(1)}, u32[]{:S(2)}, u32[]{:S(2)}) async-start(bf16[16,32,256]{2,1,0:T(8,128)(2,1)} %copy-done.6), calls=%async_computation.2 | async-start | bytes 524288 | tf_op jit(solution)/shard_map/all_to_all | solution.py:321
  65.3 3.3 %collective-permute-start.2 = (bf16[16,256]{1,0:T(8,128)(2,1)S(1)}, bf16[16,256]{1,0:T(8,128)(2,1)S(1)}, u32[]{:S(2)}, u32[]{:S(2)}) collective-permute-start(bf16[16,256]{1,0:T(8,128)(2,1)S(1)} %get-tuple-element.22), channel_id=1, source_target_pairs={{0,4},{4,8},{8,12},{1,5},{5,9},{9,13},{2,6},{6,10},{10,14},{3,7},{... | collective-permute-start | bytes 24584 | tf_op jit(solution)/shard_map/ppermute | solution.py:420
  68.6 1.3 %collective-permute-start.3 = (bf16[16,256]{1,0:T(8,128)(2,1)S(1)}, bf16[16,256]{1,0:T(8,128)(2,1)S(1)}, u32[]{:S(2)}, u32[]{:S(2)}) collective-permute-start(bf16[16,256]{1,0:T(8,128)(2,1)S(1)} %get-tuple-element.23), channel_id=1, source_target_pairs={{4,0},{8,4},{12,8},{5,1},{9,5},{13,9},{6,2},{10,6},{14,10},{7,3},{... | collective-permute-start | bytes 24584 | tf_op jit(solution)/shard_map/ppermute | solution.py:421
  69.9 0.2 collective-permute-done.2._.low
  70.1 2.9 %collective-permute-done.3.__.high = bf16[16,256]{1,0:T(8,128)(2,1)S(1)} collective-permute-done((bf16[16,256]{1,0:T(8,128)(2,1)S(1)}, bf16[16,256]{1,0:T(8,128)(2,1)S(1)}, u32[]{:S(2)}, u32[]{:S(2)}) %collective-permute-start.3) | collective-permute-done | bytes 8224 | tf_op jit(solution)/shard_map/ppermute | solution.py:421
  73.1 1.8 %all-to-all-done.2 = bf16[16,32,256]{2,1,0:T(8,128)(2,1)S(1)} async-done(((bf16[16,32,256]{2,1,0:T(8,128)(2,1)}), bf16[16,32,256]{2,1,0:T(8,128)(2,1)S(1)}, u32[]{:S(2)}, u32[]{:S(2)}) %all-to-all-start.2) | async-done | bytes 262176 | tf_op jit(solution)/shard_map/all_to_all | solution.py:321
  74.9 0.7 shard_map.96
  75.6 0.6 copy-done.3
  76.2 4.6 %all-to-all-start.3 = ((bf16[16,32,128]{2,1,0:T(8,128)(2,1)}), bf16[16,32,128]{2,1,0:T(8,128)(2,1)S(1)}, u32[]{:S(2)}, u32[]{:S(2)}) async-start(bf16[16,32,128]{2,1,0:T(8,128)(2,1)} %copy-done.3), calls=%async_computation.3 | async-start | bytes 262144 | tf_op jit(solution)/shard_map/all_to_all | solution.py:321
  80.8 1.5 %copy-done.1 = bf16[8,432,256]{2,1,0:T(8,128)(2,1)S(1)} copy-done((bf16[8,432,256]{2,1,0:T(8,128)(2,1)S(1)}, bf16[8,432,256]{2,1,0:T(8,128)(2,1)}, u32[]{:S(2)}) %copy-start.1) | copy-done | bytes 1769496
  82.3 1.2 %shard_map.97 = (bf16[512,512]{1,0:T(8,128)(2,1)S(1)}, bf16[2,4,432,256]{3,2,1,0:T(8,128)(2,1)S(1)}) custom-call(s32[1]{0:T(128)} %bitcast.12.rank_ref, bf16[8,512,256]{2,1,0:T(8,128)(2,1)S(1)} %bitcast.21, bf16[2,4,432,256]{3,2,1,0:T(8,128)(2,1)S(1)} %bitcast.22), custom_call_target="tpu_custom_call" | custom-call | flops 134217728 | bytes 2097156 | tf_op jit(solution)/shard_map/pallas_call | solution.py:21
  83.5 1.2 %copy-done.8 = bf16[2,4,432,256]{3,2,1,0:T(8,128)(2,1)} copy-done((bf16[2,4,432,256]{3,2,1,0:T(8,128)(2,1)}, bf16[2,4,432,256]{3,2,1,0:T(8,128)(2,1)S(1)}, u32[]{:S(2)}) %copy-start.8) | copy-done | bytes 1769496
  84.7 2.9 %all-to-all-done.3 = bf16[16,32,128]{2,1,0:T(8,128)(2,1)S(1)} async-done(((bf16[16,32,128]{2,1,0:T(8,128)(2,1)}), bf16[16,32,128]{2,1,0:T(8,128)(2,1)S(1)}, u32[]{:S(2)}, u32[]{:S(2)}) %all-to-all-start.3) | async-done | bytes 131104 | tf_op jit(solution)/shard_map/all_to_all | solution.py:321
  87.7 1.5 %copy-done.9 = bf16[2,4,432,256]{3,2,1,0:T(8,128)(2,1)S(1)} copy-done((bf16[2,4,432,256]{3,2,1,0:T(8,128)(2,1)S(1)}, bf16[2,4,432,256]{3,2,1,0:T(8,128)(2,1)}, u32[]{:S(2)}) %copy-start.9) | copy-done | bytes 1769496
  89.2 1.5 %shard_map.98 = bf16[512,256]{1,0:T(8,128)(2,1)S(1)} custom-call(bf16[512,128]{1,0:T(8,128)(2,1)S(1)} %bitcast.28, bf16[512,512]{1,0:T(8,128)(2,1)S(1)} %get-tuple-element.25.rise, bf16[4,96,256]{2,1,0:T(8,128)(2,1)S(1)} %all_to_all.26.near, bf16[16,256]{1,0:T(8,128)(2,1)S(1)} %collective-permute-done.2._.low, ...), custom_call_target="tpu_custom_call" | custom-call | flops 905969664 | bytes 2637824 | tf_op jit(solution)/shard_map/pallas_call | solution.py:21
  90.7 8.6 %all_to_all.27.partials = bf16[4,128,256]{2,1,0:T(8,128)(2,1)S(1)} all-to-all(bf16[4,128,256]{2,1,0:T(8,128)(2,1)S(1)} %bitcast.27), channel_id=1, replica_groups=mesh['rep'=2,'z'=4,'r'=4] {'r'}, dimensions={0} | all-to-all | bytes 524288 | tf_op jit(solution)/shard_map/all_to_all | solution.py:321
  99.3 1.1 shard_map.99
  (25 shorter events, 0.1 us)
Async XLA Ops:
  6.5 74.3 %all-gather.4.cloned.1.call-start = ((), (), s32[]{:S(2)}) async-start(), calls=%async_computation.5 | async-start | bytes 2654208 | tf_op jit(solution)/shard_map/all_gather | solution.py:366
  6.5 1.0 copy-start.11
  7.6 0.9 copy-start.12
  8.9 28.2 %copy-start.10 = (bf16[3,3,3,128,128]{4,3,2,1,0:T(8,128)(2,1)S(1)}, bf16[3,3,3,128,128]{4,3,2,1,0:T(8,128)(2,1)}, u32[]{:S(2)}) copy-start(bf16[3,3,3,128,128]{4,3,2,1,0:T(8,128)(2,1)} %param.10) | copy-start | bytes 2654212
  28.4 10.1 %collective-permute-start = (bf16[3,16,16,128]{3,2,1,0:T(8,128)(2,1)S(1)}, bf16[3,16,16,128]{3,2,1,0:T(8,128)(2,1)S(1)}, u32[]{:S(2)}, u32[]{:S(2)}) collective-permute-start(bf16[3,16,16,128]{3,2,1,0:T(8,128)(2,1)S(1)} %get-tuple-element.16), channel_id=1, source_target_pairs={{0,1},{1,2},{2,3},{3,4},{4,5},{5,6},{6,7},{7,8},{8,9},{9,10},{10,1... | collective-permute-start | bytes 589832 | tf_op jit(solution)/shard_map/ppermute | solution.py:375
  35.1 7.4 %collective-permute-start.1 = (bf16[3,16,16,128]{3,2,1,0:T(8,128)(2,1)S(1)}, bf16[3,16,16,128]{3,2,1,0:T(8,128)(2,1)S(1)}, u32[]{:S(2)}, u32[]{:S(2)}) collective-permute-start(bf16[3,16,16,128]{3,2,1,0:T(8,128)(2,1)S(1)} %get-tuple-element.17), channel_id=1, source_target_pairs={{1,0},{2,1},{3,2},{4,3},{5,4},{6,5},{7,6},{8,7},{9,8},{10,9},{11,1... | collective-permute-start | bytes 589832 | tf_op jit(solution)/shard_map/ppermute | solution.py:376
  37.1 5.4 %copy-start.7 = (bf16[3,3,3,128,256]{4,3,2,1,0:T(8,128)(2,1)S(1)}, bf16[3,3,3,128,256]{4,3,2,1,0:T(8,128)(2,1)}, u32[]{:S(2)}) copy-start(bf16[3,3,3,128,256]{4,3,2,1,0:T(8,128)(2,1)} %param.11) | copy-start | bytes 5308420
  37.1 5.4 %copy-start.13 = (bf16[256,256]{1,0:T(8,128)(2,1)S(1)}, bf16[256,256]{1,0:T(8,128)(2,1)}, u32[]{:S(2)}) copy-start(bf16[256,256]{1,0:T(8,128)(2,1)} %constant.19.clone.order) | copy-start | bytes 393220
  42.5 17.8 %copy-start.5 = (bf16[3,3,3,256,32]{3,4,2,1,0:T(8,128)(2,1)S(1)}, bf16[3,3,3,256,32]{3,4,2,1,0:T(8,128)(2,1)}, u32[]{:S(2)}) copy-start(bf16[3,3,3,256,32]{3,4,2,1,0:T(8,128)(2,1)} %param.12) | copy-start | bytes 1327108
  42.5 32.4 %copy-start.2 = (bf16[3,3,3,512,32]{3,4,2,1,0:T(8,128)(2,1)S(1)}, bf16[3,3,3,512,32]{3,4,2,1,0:T(8,128)(2,1)}, u32[]{:S(2)}) copy-start(bf16[3,3,3,512,32]{3,4,2,1,0:T(8,128)(2,1)} %param.13) | copy-start | bytes 2654212
  45.3 35.5 %copy-start = (bf16[2,2,2,512,256]{4,3,2,1,0:T(8,128)(2,1)S(1)}, bf16[2,2,2,512,256]{4,3,2,1,0:T(8,128)(2,1)}, u32[]{:S(2)}) copy-start(bf16[2,2,2,512,256]{4,3,2,1,0:T(8,128)(2,1)} %param.14) | copy-start | bytes 6291460
  60.8 0.7 copy-start.6
  61.5 13.3 %all-to-all-start.2 = ((bf16[16,32,256]{2,1,0:T(8,128)(2,1)}), bf16[16,32,256]{2,1,0:T(8,128)(2,1)S(1)}, u32[]{:S(2)}, u32[]{:S(2)}) async-start(bf16[16,32,256]{2,1,0:T(8,128)(2,1)} %copy-done.6), calls=%async_computation.2 | async-start | bytes 524288 | tf_op jit(solution)/shard_map/all_to_all | solution.py:321
  65.3 4.8 %collective-permute-start.2 = (bf16[16,256]{1,0:T(8,128)(2,1)S(1)}, bf16[16,256]{1,0:T(8,128)(2,1)S(1)}, u32[]{:S(2)}, u32[]{:S(2)}) collective-permute-start(bf16[16,256]{1,0:T(8,128)(2,1)S(1)} %get-tuple-element.22), channel_id=1, source_target_pairs={{0,4},{4,8},{8,12},{1,5},{5,9},{9,13},{2,6},{6,10},{10,14},{3,7},{... | collective-permute-start | bytes 24584 | tf_op jit(solution)/shard_map/ppermute | solution.py:420
  68.6 4.4 %collective-permute-start.3 = (bf16[16,256]{1,0:T(8,128)(2,1)S(1)}, bf16[16,256]{1,0:T(8,128)(2,1)S(1)}, u32[]{:S(2)}, u32[]{:S(2)}) collective-permute-start(bf16[16,256]{1,0:T(8,128)(2,1)S(1)} %get-tuple-element.23), channel_id=1, source_target_pairs={{4,0},{8,4},{12,8},{5,1},{9,5},{13,9},{6,2},{10,6},{14,10},{7,3},{... | collective-permute-start | bytes 24584 | tf_op jit(solution)/shard_map/ppermute | solution.py:421
  75.6 0.7 copy-start.3
  76.2 11.4 %all-to-all-start.3 = ((bf16[16,32,128]{2,1,0:T(8,128)(2,1)}), bf16[16,32,128]{2,1,0:T(8,128)(2,1)S(1)}, u32[]{:S(2)}, u32[]{:S(2)}) async-start(bf16[16,32,128]{2,1,0:T(8,128)(2,1)} %copy-done.3), calls=%async_computation.3 | async-start | bytes 262144 | tf_op jit(solution)/shard_map/all_to_all | solution.py:321
  80.8 1.5 %copy-start.1 = (bf16[8,432,256]{2,1,0:T(8,128)(2,1)S(1)}, bf16[8,432,256]{2,1,0:T(8,128)(2,1)}, u32[]{:S(2)}) copy-start(bf16[8,432,256]{2,1,0:T(8,128)(2,1)} %all-gather.4.cloned.1.call-done) | copy-start | bytes 5308420
  83.5 1.2 %copy-start.8 = (bf16[2,4,432,256]{3,2,1,0:T(8,128)(2,1)}, bf16[2,4,432,256]{3,2,1,0:T(8,128)(2,1)S(1)}, u32[]{:S(2)}) copy-start(bf16[2,4,432,256]{3,2,1,0:T(8,128)(2,1)S(1)} %get-tuple-element.26.decode) | copy-start | bytes 5308420
  87.7 1.5 %copy-start.9 = (bf16[2,4,432,256]{3,2,1,0:T(8,128)(2,1)S(1)}, bf16[2,4,432,256]{3,2,1,0:T(8,128)(2,1)}, u32[]{:S(2)}) copy-start(bf16[2,4,432,256]{3,2,1,0:T(8,128)(2,1)} %copy-done.8) | copy-start | bytes 5308420
  89.1 10.1 %copy-start.4 = (bf16[2,2,2,256,128]{4,3,2,1,0:T(8,128)(2,1)S(1)}, bf16[2,2,2,256,128]{4,3,2,1,0:T(8,128)(2,1)}, u32[]{:S(2)}) copy-start(bf16[2,2,2,256,128]{4,3,2,1,0:T(8,128)(2,1)} %param.16) | copy-start | bytes 1572868
Sparse Core Ops, SparseCore 0:
  28.5 31.6 all-gather.3

commit v4 on v2

--- a/solution.py
+++ b/solution.py
@@ -77,9 +77,10 @@
     return dot(left, weights)
 
 
-def front_stage(volume, tail, head, whole):
-    tail[...] = volume[1:]
-    head[...] = volume[:3]
+def front_stage(odd, volume, off_chip, on_chip, whole):
+    for s in range(3):
+        off_chip[s] = jnp.where(odd[0] == 0, volume[s], volume[s + 1])
+        on_chip[s] = jnp.where(odd[0] == 0, volume[s + 1], volume[s])
     whole[...] = volume[...]
 
 
@@ -95,13 +96,14 @@
 
 
 def stem_stage(
-    ends, low, high, own, weights, second, order,
+    ends, off_chip, on_chip, own, weights, second, order,
     pooled_out, skip_out,
     shifted, halves, framed, patches, quarters,
 ):
     for s in range(3):
-        shift_slice(shifted, s, low[s])
-        shift_slice(shifted, 3 + s, high[s])
+        even = ends[2] == 0
+        shift_slice(shifted, s, jnp.where(even, off_chip[s], on_chip[s]))
+        shift_slice(shifted, 3 + s, jnp.where(even, on_chip[s], off_chip[s]))
     framed[...] = jnp.zeros(framed.shape, jnp.float32)
     for m in range(4):
         if m == 0:
@@ -201,17 +203,17 @@
 
 
 def deep_stage(near, weights, out, first, last):
-    n, chans, voxels = out.shape
+    chans, voxels = out.shape
+    n = voxels // 16
     values = [near[r, 16 * p : 16 * p + 16, :] for p in range(n // GROUP) for r in range(GROUP)]
     values = jnp.concatenate(values, axis=0)
     deep = spread_taps(weights, values, ((1,), (1,)), chans, voxels).astype(jnp.bfloat16)
-    for dest in range(n):
-        out[dest] = deep
+    out[...] = deep
     first[...] = edge_slice(near[0, voxels // GROUP :, :], False)
     last[...] = edge_slice(near[GROUP - 1, voxels // GROUP :, :], True)
 
 
-def deeper_stage(deep, weights, out):
+def deeper_stage(deep, weights, _, __, out):
     n, chans, _ = out.shape
     voxels = deep.shape[1]
     deeper = spread_taps(weights, deep[...], ((1,), (0,)), chans, voxels)
@@ -228,7 +230,7 @@
             out[GROUP * p + r] = part
 
 
-def rise_stage(rank, chans, rise, _, out):
+def rise_stage(rank, chans, rise, out):
     lane = lax.broadcasted_iota(jnp.int32, (256, 64), 1)
     row = lax.broadcasted_iota(jnp.int32, (256, 64), 0)
     source = (rank[0] + GROUP * (lane // chans)) * chans + lane % chans
@@ -332,18 +334,19 @@
         decode_part = decode_part.reshape(planes, 27, chans, 256).transpose(1, 0, 2, 3)
         decode_part = decode_part.reshape(1, 27 * 128, 256)
 
-    forward = [(i, i + 1) for i in range(n - 1)]
-    backward = [(target, source) for source, target in forward]
-    tail, head, volume = call(
+    odd = (place % 2).astype(jnp.int32)
+    off_chip, on_chip, volume = call(
         front_stage,
         (bf16((3, 16, 16, 128)), bf16((3, 16, 16, 128)), bf16((4, 16, 16, 128))),
         [],
-        (volume,),
+        (odd.reshape(1), volume),
         3 * 10**9,
         16,
-    )
-    low = lax.ppermute(tail, ALL, forward)
-    high = lax.ppermute(head, ALL, backward)
+        scalars=1,
+    )
+    pairs = [(i, i + 1) for i in range(1, n - 1, 2)]
+    off_chip = lax.ppermute(off_chip, ALL, pairs + [(j, i) for i, j in pairs])
+    on_chip = lax.ppermute(on_chip, ALL, [(i, i ^ 1) for i in range(n)])
 
     taps = first_kernel.reshape(3, 1152, 128)
     own = call(
@@ -357,7 +360,7 @@
     lane = np.arange(256)
     source = (lane // 64 + GROUP * (lane % 64 // chans)) * chans + lane % chans
     order = jnp.asarray(np.arange(256)[:, None] == source[None, :], jnp.bfloat16)
-    ends = jnp.stack([place, n - 1 - place]).astype(jnp.int32)
+    ends = jnp.stack([place, n - 1 - place, odd]).astype(jnp.int32)
     pooled_two, skips = call(
         stem_stage,
         (bf16((planes, 16, 256)), bf16((GROUP, 32, 256))),
@@ -368,7 +371,7 @@
             pltpu.VMEM((256, 1152), jnp.bfloat16),
             pltpu.VMEM((2, 32, 128), jnp.float32),
         ],
-        (ends, low, high, own, taps, second_kernel.reshape(3, 1152, 256), order),
+        (ends, off_chip, on_chip, own, taps, second_kernel.reshape(3, 1152, 256), order),
         2 * 1024 * 2304 * 256,
         24,
         scalars=1,
@@ -381,7 +384,7 @@
 
     deep, first, last = call(
         deep_stage,
-        (bf16((n, chans, voxels)), bf16((16, 256)), bf16((16, 256))),
+        (bf16((chans, voxels)), bf16((16, 256)), bf16((16, 256))),
         [],
         (near, deep_kernel.transpose(0, 1, 2, 4, 3).reshape(27 * chans, 256)),
         2 * 27 * chans * 256 * voxels,
@@ -389,15 +392,21 @@
     )
     skip_low = lax.ppermute(last, "z", [(p, p + 1) for p in range(planes - 1)])
     skip_high = lax.ppermute(first, "z", [(p + 1, p) for p in range(planes - 1)])
-    deep_whole = exchange(deep, ALL).reshape(n * chans, voxels)
+    deep_whole = lax.all_gather(deep, ALL, axis=0).reshape(n * chans, voxels)
 
     deeper = call(
         deeper_stage,
         bf16((n, chans, 128)),
         [],
-        (deep_whole, deeper_kernel.transpose(0, 1, 2, 4, 3).reshape(27 * chans, n * chans)),
+        (
+            deep_whole,
+            deeper_kernel.transpose(0, 1, 2, 4, 3).reshape(27 * chans, n * chans),
+            skip_low,
+            skip_high,
+        ),
         2 * 27 * chans * n * chans * voxels,
         16,
+        unread=2,
     )
     deeper_near = exchange(deeper, ALL).reshape(n * chans, 128)
 
@@ -405,11 +414,10 @@
         lambda rank_ref, *refs: rise_stage(rank_ref, chans, *refs),
         bf16((n * chans, 512)),
         [],
-        (rank.astype(jnp.int32).reshape(1), rise_kernel.reshape(8, n * chans, 256), decode_part[0, :16]),
+        (rank.astype(jnp.int32).reshape(1), rise_kernel.reshape(8, n * chans, 256)),
         2 * 8 * n * chans * 256 * 64,
         16,
         scalars=1,
-        unread=1,
     )
     partial = call(
         decode_stage,

time: 92.3 us -> 98.3 us (1.065)
  blocking collectives: 43 us -> 49 us
  waiting for transfers between devices: 5.87 us -> 9.99 us
  starting transfers between devices: 15.5 us -> 12.2 us
    all_gather x0 -> x1, blocking collectives: none -> 22 us  [body(): deep_whole = lax.all_gather(deep, ALL, axis=0).reshape(n * chans, voxels)]
    all_to_all x4 -> x3, blocking collectives: 43 us -> 27 us  [exchange(): lax.all_to_all(payload, axis, split_axis=0, concat_axis=0, tiled=True)]
    all_to_all x1, waiting for transfers between devices: 0.01 us -> 6.15 us  [exchange(): lax.all_to_all(payload, axis, split_axis=0, concat_axis=0, tiled=True)]
    ppermute x2, starting transfers between devices: 6.59 us -> 4.74 us  [the longest x1 4.67 us: body(): off_chip = lax.ppermute(off_chip, ALL, pairs + [(j, i) for i, j in pairs])]
    ppermute x1, waiting for transfers between devices: 1.58 us -> 0.01 us  [body(): lax.ppermute(first, 'z', [(p + 1, p) for p in range(planes - 1)])]
  transfers between devices with their start and end apart: 6 -> 6, of which waited for: 2 -> 2; matrix products, arithmetic and copies ran while one was open for 1% -> 0% of each run, Pallas kernels for 8% -> 7%
where the time goes in v4:
time: 98.3 us; the launch traced here: 96.9 us
  blocking collectives  49 us (50%)
  between operations  13.5 us (14%)
  starting transfers between devices  12.2 us (12%)
  waiting for transfers between devices  9.99 us (10%)
  Pallas kernels  9.67 us (10%)
  local copies, waits for them, and re-layouts  2.45 us (2%)
    all_to_all x3, blocking collectives, exchange(): lax.all_to_all(payload, axis, split_axis=0, concat_axis=0, tiled=True)  27 us
    all_gather x1, blocking collectives, body(): deep_whole = lax.all_gather(deep, ALL, axis=0).reshape(n * chans, voxels)  22 us
    pallas_call x9, Pallas kernels, call(): pl.pallas_call(kernel, out_shape=outs, in_specs=[pl.BlockSpec(memory_spac...  9.67 us
    all_to_all x1, waiting for transfers between devices, exchange(): lax.all_to_all(payload, axis, split_axis=0, concat_axis=0, tiled=True)  6.15 us
    ppermute x1, starting transfers between devices, body(): off_chip = lax.ppermute(off_chip, ALL, pairs + [(j, i) for i, j in pairs])  4.67 us
    all_to_all x1, starting transfers between devices, exchange(): lax.all_to_all(payload, axis, split_axis=0, concat_axis=0, tiled=True)  3.47 us
    ppermute x1, waiting for transfers between devices, body(): off_chip = lax.ppermute(off_chip, ALL, pairs + [(j, i) for i, j in pairs])  3.11 us
    ppermute x1, starting transfers between devices, body(): skip_low = lax.ppermute(last, 'z', [(p, p + 1) for p in range(planes - 1)])  2.68 us
  transfers between devices with their start and end apart: 6, of which 2 were waited for; matrix products, arithmetic and copies ran while one was open for 0% of the time, Pallas kernels for 7%

profile of v4, /device:TPU:1, one launch (start us, length us, event | category | flops | bytes accessed | tf_op | source)
XLA Modules:
  0.0 96.9 jit_solution(1161729713671623523)
XLA Ops:
  6.5 0.0 all-gather.3.cloned.1.call-start
  6.5 0.7 all-gather.3.cloned.1.call-update
  7.3 0.9 copy-done.7
  8.2 0.1 shard_map.91
  8.3 4.7 %collective-permute-start = (bf16[3,16,16,128]{3,2,1,0:T(8,128)(2,1)S(1)}, bf16[3,16,16,128]{3,2,1,0:T(8,128)(2,1)S(1)}, u32[]{:S(2)}, u32[]{:S(2)}) collective-permute-start(bf16[3,16,16,128]{3,2,1,0:T(8,128)(2,1)S(1)} %get-tuple-element.13), channel_id=1, source_target_pairs={{1,2},{3,4},{5,6},{7,8},{9,10},{11,12},{13,14},{2,1},{4,3},{6,5},{... | collective-permute-start | bytes 589832 | tf_op jit(solution)/shard_map/ppermute | solution.py:348
  13.0 0.1 collective-permute-start.1
  13.1 0.1 pad_add_fusion.ends
  13.2 1.4 %shard_map.92.own = f32[4,256,256]{2,1,0:T(8,128)S(1)} custom-call(bf16[4,16,16,128]{3,2,1,0:T(8,128)(2,1)S(1)} %get-tuple-element.15.volume, bf16[3,1152,128]{2,1,0:T(8,128)(2,1)S(1)} %bitcast.25), custom_call_target="tpu_custom_call" | custom-call | flops 1207959552 | bytes 1146880 | tf_op jit(solution)/shard_map/pallas_call | solution.py:18
  14.6 3.1 %collective-permute-done.off_chip = bf16[3,16,16,128]{3,2,1,0:T(8,128)(2,1)S(1)} collective-permute-done((bf16[3,16,16,128]{3,2,1,0:T(8,128)(2,1)S(1)}, bf16[3,16,16,128]{3,2,1,0:T(8,128)(2,1)S(1)}, u32[]{:S(2)}, u32[]{:S(2)}) %collective-permute-start) | collective-permute-done | bytes 196640 | tf_op jit(solution)/shard_map/ppermute | solution.py:348
  17.7 0.0 collective-permute-done.1.on_chip
  17.7 0.0 copy-done.4
  17.7 0.0 copy-start.1
  17.7 2.8 %shard_map.93 = (bf16[4,16,256]{2,1,0:T(8,128)(2,1)S(1)}, bf16[4,32,256]{2,1,0:T(8,128)(2,1)S(1)}) custom-call(s32[3]{0:T(128)S(1)} %pad_add_fusion.ends, bf16[3,16,16,128]{3,2,1,0:T(8,128)(2,1)S(1)} %collective-permute-done.off_chip, bf16[3,16,16,128]{3,2,1,0:T(8,128)(2,1)S(1)} %collective-permute-done.1.on_chip, f32[4,256,256]{2,1,0:T(8,128)S(1)} %shard_map.92.own, ...), custom_call_target="tpu_custom_call" | custom-call | flops 1207959552 | bytes 4227084 | tf_op jit(solution)/shard_map/pallas_call | solution.py:18
  20.6 0.0 copy-start
  20.6 10.0 %all_to_all.20.pooled = bf16[4,16,256]{2,1,0:T(8,128)(2,1)S(1)} all-to-all(bf16[4,16,256]{2,1,0:T(8,128)(2,1)S(1)} %get-tuple-element.16), channel_id=1, replica_groups=mesh['rep'=2,'z'=4,'r'=4] {'z'}, dimensions={0} | all-to-all | bytes 65536 | tf_op jit(solution)/shard_map/all_to_all | solution.py:311
  30.6 8.5 %all_to_all.21.near = bf16[4,96,256]{2,1,0:T(8,128)(2,1)S(1)} all-to-all(bf16[4,96,256]{2,1,0:T(8,128)(2,1)S(1)} %shard_map.94), channel_id=1, replica_groups=mesh['rep'=2,'z'=4,'r'=4] {'r'}, dimensions={0} | all-to-all | bytes 393216 | tf_op jit(solution)/shard_map/all_to_all | solution.py:311
  39.0 0.6 shard_map.95
  39.6 2.7 %collective-permute-start.2 = (bf16[16,256]{1,0:T(8,128)(2,1)S(1)}, bf16[16,256]{1,0:T(8,128)(2,1)S(1)}, u32[]{:S(2)}, u32[]{:S(2)}) collective-permute-start(bf16[16,256]{1,0:T(8,128)(2,1)S(1)} %get-tuple-element.19), channel_id=1, source_target_pairs={{0,4},{4,8},{8,12},{1,5},{5,9},{9,13},{2,6},{6,10},{10,14},{3,7},{... | collective-permute-start | bytes 24584 | tf_op jit(solution)/shard_map/ppermute | solution.py:393
  42.3 1.3 %collective-permute-start.3 = (bf16[16,256]{1,0:T(8,128)(2,1)S(1)}, bf16[16,256]{1,0:T(8,128)(2,1)S(1)}, u32[]{:S(2)}, u32[]{:S(2)}) collective-permute-start(bf16[16,256]{1,0:T(8,128)(2,1)S(1)} %get-tuple-element.20), channel_id=1, source_target_pairs={{4,0},{8,4},{12,8},{5,1},{9,5},{13,9},{6,2},{10,6},{14,10},{7,3},{... | collective-permute-start | bytes 24584 | tf_op jit(solution)/shard_map/ppermute | solution.py:394
  43.6 22.0 %all-gather.deep = bf16[512,256]{1,0:T(8,128)(2,1)S(1)} all-gather(bf16[32,256]{1,0:T(8,128)(2,1)S(1)} %get-tuple-element.18), channel_id=2, replica_groups=mesh['rep'=2,'z'=4,'r'=4] {'z','r'}, dimensions={0}, use_global_device_ids=true | all-gather | bytes 278528 | tf_op jit(solution)/shard_map/all_gather | solution.py:395
  65.6 0.0 collective-permute-done.2._.low
  65.6 0.0 collective-permute-done.3.__.high
  65.6 1.4 %shard_map.96 = bf16[16,32,128]{2,1,0:T(8,128)(2,1)} custom-call(bf16[512,256]{1,0:T(8,128)(2,1)S(1)} %all-gather.deep, bf16[864,512]{1,0:T(8,128)(2,1)S(1)} %bitcast.19, bf16[16,256]{1,0:T(8,128)(2,1)S(1)} %collective-permute-done.2._.low, bf16[16,256]{1,0:T(8,128)(2,1)S(1)} %collective-permute-done.3.__.high), custom_call_target="tpu_custom_call" | custom-call | flops 226492416 | bytes 1146880 | tf_op jit(solution)/shard_map/pallas_call | solution.py:18
  67.0 3.5 %all-to-all-start.2 = ((bf16[16,32,128]{2,1,0:T(8,128)(2,1)}), bf16[16,32,128]{2,1,0:T(8,128)(2,1)S(1)}, u32[]{:S(2)}, u32[]{:S(2)}) async-start(bf16[16,32,128]{2,1,0:T(8,128)(2,1)} %shard_map.96), calls=%async_computation.2 | async-start | bytes 262144 | tf_op jit(solution)/shard_map/all_to_all | solution.py:311
  70.4 0.0 copy-done
  70.4 0.8 shard_map.97.rise
  71.2 6.2 %all-to-all-done.2 = bf16[16,32,128]{2,1,0:T(8,128)(2,1)S(1)} async-done(((bf16[16,32,128]{2,1,0:T(8,128)(2,1)}), bf16[16,32,128]{2,1,0:T(8,128)(2,1)S(1)}, u32[]{:S(2)}, u32[]{:S(2)}) %all-to-all-start.2) | async-done | bytes 131104 | tf_op jit(solution)/shard_map/all_to_all | solution.py:311
  77.4 1.5 %copy-done.5 = bf16[4,864,256]{2,1,0:T(8,128)(2,1)S(1)} copy-done((bf16[4,864,256]{2,1,0:T(8,128)(2,1)S(1)}, bf16[4,864,256]{2,1,0:T(8,128)(2,1)}, u32[]{:S(2)}) %copy-start.5) | copy-done | bytes 1769496
  78.9 1.6 %shard_map.98 = bf16[512,256]{1,0:T(8,128)(2,1)S(1)} custom-call(bf16[512,128]{1,0:T(8,128)(2,1)S(1)} %bitcast.23, bf16[512,512]{1,0:T(8,128)(2,1)S(1)} %shard_map.97.rise, bf16[4,96,256]{2,1,0:T(8,128)(2,1)S(1)} %all_to_all.21.near, bf16[16,256]{1,0:T(8,128)(2,1)S(1)} %collective-permute-done.2._.low, bf16[16,256]{1,0:T(8,128)(2,1)S(1)} %collective-permute-done.3.__.high, ...), custom_call_target="tpu_custom_call" | custom-call | flops 905969664 | bytes 2637824 | tf_op jit(solution)/shard_map/pallas_call | solution.py:18
  80.4 8.6 %all_to_all.22.partials = bf16[4,128,256]{2,1,0:T(8,128)(2,1)S(1)} all-to-all(bf16[4,128,256]{2,1,0:T(8,128)(2,1)S(1)} %bitcast.22), channel_id=1, replica_groups=mesh['rep'=2,'z'=4,'r'=4] {'r'}, dimensions={0} | all-to-all | bytes 524288 | tf_op jit(solution)/shard_map/all_to_all | solution.py:311
  89.0 0.0 copy-done.2
  89.0 1.1 %shard_map.99 = bf16[1024,128]{1,0:T(8,128)(2,1)} custom-call(bf16[4,128,256]{2,1,0:T(8,128)(2,1)S(1)} %all_to_all.22.partials, bf16[8,256,128]{2,1,0:T(8,128)(2,1)S(1)} %bitcast.20), custom_call_target="tpu_custom_call" | custom-call | flops 67108864 | bytes 786432 | tf_op jit(solution)/shard_map/pallas_call | solution.py:18
  (13 shorter events, 0.0 us)
Async XLA Ops:
  6.5 70.8 %all-gather.3.cloned.1.call-start = ((), (), s32[]{:S(2)}) async-start(), calls=%async_computation.4 | async-start | bytes 2211840 | tf_op jit(solution)/shard_map/all_gather | solution.py:332
  7.3 1.0 copy-start.7
  8.2 4.9 %copy-start.6 = (bf16[3,3,3,128,128]{4,3,2,1,0:T(8,128)(2,1)S(1)}, bf16[3,3,3,128,128]{4,3,2,1,0:T(8,128)(2,1)}, u32[]{:S(2)}) copy-start(bf16[3,3,3,128,128]{4,3,2,1,0:T(8,128)(2,1)} %param.10) | copy-start | bytes 2654212
  8.3 9.4 %collective-permute-start = (bf16[3,16,16,128]{3,2,1,0:T(8,128)(2,1)S(1)}, bf16[3,16,16,128]{3,2,1,0:T(8,128)(2,1)S(1)}, u32[]{:S(2)}, u32[]{:S(2)}) collective-permute-start(bf16[3,16,16,128]{3,2,1,0:T(8,128)(2,1)S(1)} %get-tuple-element.13), channel_id=1, source_target_pairs={{1,2},{3,4},{5,6},{7,8},{9,10},{11,12},{13,14},{2,1},{4,3},{6,5},{... | collective-permute-start | bytes 589832 | tf_op jit(solution)/shard_map/ppermute | solution.py:348
  13.0 4.7 %collective-permute-start.1 = (bf16[3,16,16,128]{3,2,1,0:T(8,128)(2,1)S(1)}, bf16[3,16,16,128]{3,2,1,0:T(8,128)(2,1)S(1)}, u32[]{:S(2)}, u32[]{:S(2)}) collective-permute-start(bf16[3,16,16,128]{3,2,1,0:T(8,128)(2,1)S(1)} %get-tuple-element.14), channel_id=1, source_target_pairs={{0,1},{1,0},{2,3},{3,2},{4,5},{5,4},{6,7},{7,6},{8,9},{9,8},{10,11... | collective-permute-start | bytes 589832 | tf_op jit(solution)/shard_map/ppermute | solution.py:349
  13.2 4.5 %copy-start.4 = (bf16[3,3,3,128,256]{4,3,2,1,0:T(8,128)(2,1)S(1)}, bf16[3,3,3,128,256]{4,3,2,1,0:T(8,128)(2,1)}, u32[]{:S(2)}) copy-start(bf16[3,3,3,128,256]{4,3,2,1,0:T(8,128)(2,1)} %param.11) | copy-start | bytes 5308420
  13.2 4.5 %copy-start.8 = (bf16[256,256]{1,0:T(8,128)(2,1)S(1)}, bf16[256,256]{1,0:T(8,128)(2,1)}, u32[]{:S(2)}) copy-start(bf16[256,256]{1,0:T(8,128)(2,1)} %constant.26.clone.order) | copy-start | bytes 393220
  17.7 21.3 %copy-start.3 = (bf16[3,3,3,256,32]{3,4,2,1,0:T(8,128)(2,1)S(1)}, bf16[3,3,3,256,32]{3,4,2,1,0:T(8,128)(2,1)}, u32[]{:S(2)}) copy-start(bf16[3,3,3,256,32]{3,4,2,1,0:T(8,128)(2,1)} %param.12) | copy-start | bytes 1327108
  17.7 47.9 %copy-start.1 = (bf16[3,3,3,512,32]{3,4,2,1,0:T(8,128)(2,1)S(1)}, bf16[3,3,3,512,32]{3,4,2,1,0:T(8,128)(2,1)}, u32[]{:S(2)}) copy-start(bf16[3,3,3,512,32]{3,4,2,1,0:T(8,128)(2,1)} %param.13) | copy-start | bytes 2654212
  20.6 49.9 %copy-start = (bf16[2,2,2,512,256]{4,3,2,1,0:T(8,128)(2,1)S(1)}, bf16[2,2,2,512,256]{4,3,2,1,0:T(8,128)(2,1)}, u32[]{:S(2)}) copy-start(bf16[2,2,2,512,256]{4,3,2,1,0:T(8,128)(2,1)} %param.14) | copy-start | bytes 6291460
  39.6 26.0 %collective-permute-start.2 = (bf16[16,256]{1,0:T(8,128)(2,1)S(1)}, bf16[16,256]{1,0:T(8,128)(2,1)S(1)}, u32[]{:S(2)}, u32[]{:S(2)}) collective-permute-start(bf16[16,256]{1,0:T(8,128)(2,1)S(1)} %get-tuple-element.19), channel_id=1, source_target_pairs={{0,4},{4,8},{8,12},{1,5},{5,9},{9,13},{2,6},{6,10},{10,14},{3,7},{... | collective-permute-start | bytes 24584 | tf_op jit(solution)/shard_map/ppermute | solution.py:393
  42.3 23.3 %collective-permute-start.3 = (bf16[16,256]{1,0:T(8,128)(2,1)S(1)}, bf16[16,256]{1,0:T(8,128)(2,1)S(1)}, u32[]{:S(2)}, u32[]{:S(2)}) collective-permute-start(bf16[16,256]{1,0:T(8,128)(2,1)S(1)} %get-tuple-element.20), channel_id=1, source_target_pairs={{4,0},{8,4},{12,8},{5,1},{9,5},{13,9},{6,2},{10,6},{14,10},{7,3},{... | collective-permute-start | bytes 24584 | tf_op jit(solution)/shard_map/ppermute | solution.py:394
  67.0 10.4 %all-to-all-start.2 = ((bf16[16,32,128]{2,1,0:T(8,128)(2,1)}), bf16[16,32,128]{2,1,0:T(8,128)(2,1)S(1)}, u32[]{:S(2)}, u32[]{:S(2)}) async-start(bf16[16,32,128]{2,1,0:T(8,128)(2,1)} %shard_map.96), calls=%async_computation.2 | async-start | bytes 262144 | tf_op jit(solution)/shard_map/all_to_all | solution.py:311
  77.4 1.5 %copy-start.5 = (bf16[4,864,256]{2,1,0:T(8,128)(2,1)S(1)}, bf16[4,864,256]{2,1,0:T(8,128)(2,1)}, u32[]{:S(2)}) copy-start(bf16[4,864,256]{2,1,0:T(8,128)(2,1)} %all-gather.3.cloned.1.call-done.decode) | copy-start | bytes 5308420
  78.9 10.1 %copy-start.2 = (bf16[2,2,2,256,128]{4,3,2,1,0:T(8,128)(2,1)S(1)}, bf16[2,2,2,256,128]{4,3,2,1,0:T(8,128)(2,1)}, u32[]{:S(2)}) copy-start(bf16[2,2,2,256,128]{4,3,2,1,0:T(8,128)(2,1)} %param.16) | copy-start | bytes 1572868
Sparse Core Ops, SparseCore 0:
  8.9 43.7 all-gather.2

commit v5 on v4

--- a/solution.py
+++ b/solution.py
@@ -95,11 +95,9 @@
     out[3, :, 128:] = jnp.zeros((256, 128), jnp.float32)
 
 
-def stem_stage(
-    ends, off_chip, on_chip, own, weights, second, order,
-    pooled_out, skip_out,
-    shifted, halves, framed, patches, quarters,
-):
+def stem_stage(ends, off_chip, on_chip, own, weights, second, order, *refs):
+    pooled_out, skip_outs = refs[0], refs[1 : 1 + GROUP]
+    shifted, halves, framed, patches, quarters, blocks = refs[1 + GROUP :]
     for s in range(3):
         even = ends[2] == 0
         shift_slice(shifted, s, jnp.where(even, off_chip[s], on_chip[s]))
@@ -151,15 +149,9 @@
         near, far = sorted_skip[:64, 64 * r : 64 * r + 64], sorted_skip[64:, 64 * r : 64 * r + 64]
         block = jnp.concatenate([near, far], axis=1)
         block = jnp.concatenate([block[:32], block[32:]], axis=1).astype(jnp.bfloat16)
-        skip_out[r] = block
-
-
-def relay_stage(pooled, skips, out):
-    planes = pooled.shape[0]
-    for r in range(GROUP):
-        for p in range(planes):
-            out[r, 16 * p : 16 * p + 16, :] = pooled[p]
-        out[r, 16 * planes :, :] = skips[r]
+        blocks[r] = block
+    for k in range(GROUP):
+        skip_outs[k][...] = blocks[ends[3] ^ k]
 
 
 def edge_slice(block, far):
@@ -202,18 +194,27 @@
     return jnp.maximum(total, 0.0)
 
 
-def deep_stage(near, weights, out, first, last):
-    chans, voxels = out.shape
-    n = voxels // 16
-    values = [near[r, 16 * p : 16 * p + 16, :] for p in range(n // GROUP) for r in range(GROUP)]
-    values = jnp.concatenate(values, axis=0)
-    deep = spread_taps(weights, values, ((1,), (1,)), chans, voxels).astype(jnp.bfloat16)
-    out[...] = deep
-    first[...] = edge_slice(near[0, voxels // GROUP :, :], False)
-    last[...] = edge_slice(near[GROUP - 1, voxels // GROUP :, :], True)
-
-
-def deeper_stage(deep, weights, _, __, out):
+def by_rank(rank, near, blocks):
+    for k in range(GROUP):
+        blocks[rank[0] ^ k] = near[k][...]
+
+
+def edge_stage(rank, *refs):
+    near, (first, last, blocks) = refs[:GROUP], refs[GROUP:]
+    by_rank(rank, near, blocks)
+    first[...] = edge_slice(blocks[0], False)
+    last[...] = edge_slice(blocks[GROUP - 1], True)
+
+
+def deep_stage(pooled, weights, out):
+    n, chans, voxels = out.shape
+    deep = spread_taps(weights, pooled[...], ((1,), (1,)), chans, voxels).astype(jnp.bfloat16)
+    for dest in range(n):
+        out[dest] = deep
+
+
+def deeper_stage(deep, weights, *refs):
+    out = refs[-1]
     n, chans, _ = out.shape
     voxels = deep.shape[1]
     deeper = spread_taps(weights, deep[...], ((1,), (0,)), chans, voxels)
@@ -241,9 +242,9 @@
         out[:, 128 * pair : 128 * pair + 128] = both
 
 
-def decode_stage(
-    deeper, rise, near, low, high, decode, out, framed, patches, risen
-):
+def decode_stage(rank, deeper, rise, low, high, decode, *refs):
+    near, (out, framed, patches, risen, blocks) = refs[:GROUP], refs[GROUP:]
+    by_rank(rank, near, blocks)
     framed[...] = jnp.zeros(framed.shape, jnp.float32)
     spread = round_once(dot(deeper[...].astype(jnp.float32).T.astype(jnp.bfloat16), rise[...]))
     for pair in range(4):
@@ -267,7 +268,7 @@
                 parts += [pltpu.roll(half, 64, 1), half]
             skip = jnp.concatenate(parts, axis=0)
         else:
-            both = near[(s - 1) // 2, near.shape[1] - 32 :, :].astype(jnp.float32)
+            both = blocks[(s - 1) // 2].astype(jnp.float32)
             skip = jnp.concatenate([both[:, :128], both[:, 128:]], axis=0)
             if (s - 1) % 2 == 0:
                 skip = pltpu.roll(skip, 64, 1)
@@ -360,39 +361,62 @@
     lane = np.arange(256)
     source = (lane // 64 + GROUP * (lane % 64 // chans)) * chans + lane % chans
     order = jnp.asarray(np.arange(256)[:, None] == source[None, :], jnp.bfloat16)
-    ends = jnp.stack([place, n - 1 - place, odd]).astype(jnp.int32)
-    pooled_two, skips = call(
+    ends = jnp.stack([place, n - 1 - place, odd, rank]).astype(jnp.int32)
+    pooled_two, *skips = call(
         stem_stage,
-        (bf16((planes, 16, 256)), bf16((GROUP, 32, 256))),
+        (bf16((n, 16, 256)),) + (bf16((32, 256)),) * GROUP,
         [
             pltpu.VMEM((6, 18, 16, 384), jnp.bfloat16),
             pltpu.VMEM((128, 128), jnp.float32),
             pltpu.VMEM((4, 10, 24, 128), jnp.float32),
             pltpu.VMEM((256, 1152), jnp.bfloat16),
             pltpu.VMEM((2, 32, 128), jnp.float32),
+            pltpu.VMEM((GROUP, 32, 256), jnp.bfloat16),
         ],
         (ends, off_chip, on_chip, own, taps, second_kernel.reshape(3, 1152, 256), order),
         2 * 1024 * 2304 * 256,
         24,
         scalars=1,
     )
-    pooled_line = exchange(pooled_two, "z")
-    relays = call(
-        relay_stage, bf16((GROUP, 16 * planes + 32, 256)), [], (pooled_line, skips), 0, 16
-    )
-    near = exchange(relays, "r")
-
-    deep, first, last = call(
+    pooled_whole = exchange(pooled_two, ALL)
+    near = [skips[0]] + [
+        lax.ppermute(skips[k], "r", [(r, r ^ k) for r in range(GROUP)]) for k in range(1, GROUP)
+    ]
+    rank_ref = rank.astype(jnp.int32).reshape(1)
+    blocks = pltpu.VMEM((GROUP, 32, 256), jnp.bfloat16)
+
+    deep = call(
         deep_stage,
-        (bf16((chans, voxels)), bf16((16, 256)), bf16((16, 256))),
+        bf16((n, chans, voxels)),
         [],
-        (near, deep_kernel.transpose(0, 1, 2, 4, 3).reshape(27 * chans, 256)),
+        (
+            pooled_whole.reshape(voxels, 256),
+            deep_kernel.transpose(0, 1, 2, 4, 3).reshape(27 * chans, 256),
+        ),
         2 * 27 * chans * 256 * voxels,
         16,
+    )
+    first, last = call(
+        edge_stage,
+        (bf16((16, 256)), bf16((16, 256))),
+        [blocks],
+        (rank_ref, *near),
+        0,
+        16,
+        scalars=1,
     )
     skip_low = lax.ppermute(last, "z", [(p, p + 1) for p in range(planes - 1)])
     skip_high = lax.ppermute(first, "z", [(p + 1, p) for p in range(planes - 1)])
-    deep_whole = lax.all_gather(deep, ALL, axis=0).reshape(n * chans, voxels)
+    rise_part = call(
+        lambda rank_ref, *refs: rise_stage(rank_ref, chans, *refs),
+        bf16((n * chans, 512)),
+        [],
+        (rank_ref, rise_kernel.reshape(8, n * chans, 256)),
+        2 * 8 * n * chans * 256 * 64,
+        16,
+        scalars=1,
+    )
+    deep_whole = exchange(deep, ALL).reshape(n * chans, voxels)
 
     deeper = call(
         deeper_stage,
@@ -403,22 +427,14 @@
             deeper_kernel.transpose(0, 1, 2, 4, 3).reshape(27 * chans, n * chans),
             skip_low,
             skip_high,
+            rise_part,
         ),
         2 * 27 * chans * n * chans * voxels,
         16,
-        unread=2,
+        unread=3,
     )
     deeper_near = exchange(deeper, ALL).reshape(n * chans, 128)
 
-    rise_part = call(
-        lambda rank_ref, *refs: rise_stage(rank_ref, chans, *refs),
-        bf16((n * chans, 512)),
-        [],
-        (rank.astype(jnp.int32).reshape(1), rise_kernel.reshape(8, n * chans, 256)),
-        2 * 8 * n * chans * 256 * 64,
-        16,
-        scalars=1,
-    )
     partial = call(
         decode_stage,
         bf16((512, 256)),
@@ -426,10 +442,12 @@
             pltpu.VMEM((10, 10, 24, 128), jnp.float32),
             pltpu.VMEM((640, 1152), jnp.bfloat16),
             pltpu.VMEM((8, 128, 128), jnp.float32),
+            blocks,
         ],
-        (deeper_near, rise_part, near, skip_low, skip_high, decode_part),
+        (rank_ref, deeper_near, rise_part, skip_low, skip_high, decode_part, *near),
         2 * 512 * 3456 * 256,
         24,
+        scalars=1,
     )
     partials = exchange(partial.reshape(GROUP, 128, 256), "r")
     out = call(

time: 98.3 us -> 91 us (0.926)
  blocking collectives: 49 us -> 36.7 us
  starting transfers between devices: 12.2 us -> 15.4 us
  local copies, waits for them, and re-layouts: 2.45 us -> 3.62 us
    all_gather x1 -> x0, blocking collectives: 22 us -> none  [body(): deep_whole = lax.all_gather(deep, ALL, axis=0).reshape(n * chans, voxels)]
    all_to_all x3, blocking collectives: 27 us -> 36.7 us  [exchange(): lax.all_to_all(payload, axis, split_axis=0, concat_axis=0, tiled=True)]
    all_to_all x1, waiting for transfers between devices: 6.15 us -> 0.45 us  [exchange(): lax.all_to_all(payload, axis, split_axis=0, concat_axis=0, tiled=True)]
    ppermute x0 -> x3, waiting for transfers between devices: none -> 3.21 us  [body(): lax.ppermute(skips[k], 'r', [(r, r ^ k) for r in range(GROUP)])]
    ppermute x1, waiting for transfers between devices: 0.01 us -> 2.81 us  [body(): lax.ppermute(first, 'z', [(p + 1, p) for p in range(planes - 1)])]
    ppermute x0 -> x3, starting transfers between devices: none -> 2.14 us  [body(): lax.ppermute(skips[k], 'r', [(r, r ^ k) for r in range(GROUP)])]
    unnamed x18 -> x20, local copies, waits for them, and re-layouts: 2.45 us -> 3.62 us
    all_to_all x1, starting transfers between devices: 3.47 us -> 4.54 us  [exchange(): lax.all_to_all(payload, axis, split_axis=0, concat_axis=0, tiled=True)]
  transfers between devices with their start and end apart: 6 -> 9, of which waited for: 2 -> 5; matrix products, arithmetic and copies ran while one was open for 0% -> 0% of each run, Pallas kernels for 7% -> 8%
where the time goes in v5:
time: 91 us; the launch traced here: 89.5 us
  blocking collectives  36.7 us (40%)
  starting transfers between devices  15.4 us (17%)
  between operations  13.5 us (15%)
  waiting for transfers between devices  10.3 us (11%)
  Pallas kernels  9.91 us (11%)
  local copies, waits for them, and re-layouts  3.62 us (4%)
    all_to_all x3, blocking collectives, exchange(): lax.all_to_all(payload, axis, split_axis=0, concat_axis=0, tiled=True)  36.7 us
    pallas_call x9, Pallas kernels, call(): pl.pallas_call(kernel, out_shape=outs, in_specs=[pl.BlockSpec(memory_spac...  9.91 us
    ppermute x1, starting transfers between devices, body(): off_chip = lax.ppermute(off_chip, ALL, pairs + [(j, i) for i, j in pairs])  4.67 us
    all_to_all x1, starting transfers between devices, exchange(): lax.all_to_all(payload, axis, split_axis=0, concat_axis=0, tiled=True)  4.54 us
    unnamed x20, local copies, waits for them, and re-layouts  3.62 us
    ppermute x3, waiting for transfers between devices, body(): lax.ppermute(skips[k], 'r', [(r, r ^ k) for r in range(GROUP)])  3.21 us
    ppermute x1, waiting for transfers between devices, body(): off_chip = lax.ppermute(off_chip, ALL, pairs + [(j, i) for i, j in pairs])  3.1 us
    ppermute x1, waiting for transfers between devices, body(): lax.ppermute(first, 'z', [(p + 1, p) for p in range(planes - 1)])  2.81 us
  transfers between devices with their start and end apart: 9, of which 5 were waited for; matrix products, arithmetic and copies ran while one was open for 0% of the time, Pallas kernels for 8%

profile of v5, /device:TPU:1, one launch (start us, length us, event | category | flops | bytes accessed | tf_op | source)
XLA Modules:
  0.0 89.5 jit_solution(14010532750683629163)
XLA Ops:
  6.5 0.7 all-gather.2.cloned.1.call-update
  7.3 0.9 %copy-done.8 = bf16[4,16,16,128]{3,2,1,0:T(8,128)(2,1)S(1)} copy-done((bf16[4,16,16,128]{3,2,1,0:T(8,128)(2,1)S(1)}, bf16[4,16,16,128]{3,2,1,0:T(8,128)(2,1)}, u32[]{:S(2)}) %copy-start.8) | copy-done | bytes 262168
  8.2 0.1 shard_map.91
  8.3 4.7 %collective-permute-start = (bf16[3,16,16,128]{3,2,1,0:T(8,128)(2,1)S(1)}, bf16[3,16,16,128]{3,2,1,0:T(8,128)(2,1)S(1)}, u32[]{:S(2)}, u32[]{:S(2)}) collective-permute-start(bf16[3,16,16,128]{3,2,1,0:T(8,128)(2,1)S(1)} %get-tuple-element.15), channel_id=1, source_target_pairs={{1,2},{3,4},{5,6},{7,8},{9,10},{11,12},{13,14},{2,1},{4,3},{6,5},{... | collective-permute-start | bytes 589832 | tf_op jit(solution)/shard_map/ppermute | solution.py:349
  13.0 0.1 collective-permute-start.1
  13.1 0.1 pad_add_fusion.ends
  13.2 0.0 copy-start.9
  13.2 1.4 %shard_map.92.own = f32[4,256,256]{2,1,0:T(8,128)S(1)} custom-call(bf16[4,16,16,128]{3,2,1,0:T(8,128)(2,1)S(1)} %get-tuple-element.17.volume, bf16[3,1152,128]{2,1,0:T(8,128)(2,1)S(1)} %bitcast.29), custom_call_target="tpu_custom_call" | custom-call | flops 1207959552 | bytes 1146880 | tf_op jit(solution)/shard_map/pallas_call | solution.py:18
  14.6 3.1 %collective-permute-done.off_chip = bf16[3,16,16,128]{3,2,1,0:T(8,128)(2,1)S(1)} collective-permute-done((bf16[3,16,16,128]{3,2,1,0:T(8,128)(2,1)S(1)}, bf16[3,16,16,128]{3,2,1,0:T(8,128)(2,1)S(1)}, u32[]{:S(2)}, u32[]{:S(2)}) %collective-permute-start) | collective-permute-done | bytes 196640 | tf_op jit(solution)/shard_map/ppermute | solution.py:349
  17.7 0.0 copy-start.3
  17.7 2.9 %shard_map.93 = (bf16[16,16,256]{2,1,0:T(8,128)(2,1)S(1)}, bf16[32,256]{1,0:T(8,128)(2,1)S(1)}, bf16[32,256]{1,0:T(8,128)(2,1)S(1)}, bf16[32,256]{1,0:T(8,128)(2,1)S(1)}, bf16[32,256]{1,0:T(8,128)(2,1)S(1)}) custom-call(s32[4]{0:T(128)S(1)} %pad_add_fusion.ends, bf16[3,16,16,128]{3,2,1,0:T(8,128)(2,1)S(1)} %collective-permute-done.off_chip, ...), custom_call_target="tpu_custom_call" | custom-call | flops 1207959552 | bytes 4227088 | tf_op jit(solution)/shard_map/pallas_call | solution.py:18
  20.7 15.3 %all_to_all.20 = bf16[16,16,256]{2,1,0:T(8,128)(2,1)S(1)} all-to-all(bf16[16,16,256]{2,1,0:T(8,128)(2,1)S(1)} %get-tuple-element.18), channel_id=1, replica_groups=mesh['rep'=2,'z'=4,'r'=4] {'z','r'}, dimensions={0} | all-to-all | bytes 262144 | tf_op jit(solution)/shard_map/all_to_all | solution.py:312
  35.9 1.3 %shard_map.94 = bf16[16,32,256]{2,1,0:T(8,128)(2,1)} custom-call(bf16[256,256]{1,0:T(8,128)(2,1)S(1)} %bitcast.23, bf16[864,256]{1,0:T(8,128)(2,1)S(1)} %bitcast.25), custom_call_target="tpu_custom_call" | custom-call | flops 113246208 | bytes 573440 | tf_op jit(solution)/shard_map/pallas_call | solution.py:18
  37.2 4.5 %all-to-all-start.1 = ((bf16[16,32,256]{2,1,0:T(8,128)(2,1)}), bf16[16,32,256]{2,1,0:T(8,128)(2,1)S(1)}, u32[]{:S(2)}, u32[]{:S(2)}) async-start(bf16[16,32,256]{2,1,0:T(8,128)(2,1)} %shard_map.94), calls=%async_computation.1 | async-start | bytes 524288 | tf_op jit(solution)/shard_map/all_to_all | solution.py:312
  41.8 0.3 collective-permute-start.2
  42.0 1.5 %collective-permute-start.3 = (bf16[32,256]{1,0:T(8,128)(2,1)S(1)}, bf16[32,256]{1,0:T(8,128)(2,1)S(1)}, u32[]{:S(2)}, u32[]{:S(2)}) collective-permute-start(bf16[32,256]{1,0:T(8,128)(2,1)S(1)} %get-tuple-element.21), channel_id=1, source_target_pairs={{0,2},{1,3},{2,0},{3,1},{4,6},{5,7},{6,4},{7,5},{8,10},{9,11},{10,... | collective-permute-start | bytes 49160 | tf_op jit(solution)/shard_map/ppermute | solution.py:383
  43.5 0.4 collective-permute-start.4
  43.9 1.3 %collective-permute-done.3.refs_2_ = bf16[32,256]{1,0:T(8,128)(2,1)S(1)} collective-permute-done((bf16[32,256]{1,0:T(8,128)(2,1)S(1)}, bf16[32,256]{1,0:T(8,128)(2,1)S(1)}, u32[]{:S(2)}, u32[]{:S(2)}) %collective-permute-start.3) | collective-permute-done | bytes 16416 | tf_op jit(solution)/shard_map/ppermute | solution.py:383
  45.2 1.9 %collective-permute-done.4.refs_3_ = bf16[32,256]{1,0:T(8,128)(2,1)S(1)} collective-permute-done((bf16[32,256]{1,0:T(8,128)(2,1)S(1)}, bf16[32,256]{1,0:T(8,128)(2,1)S(1)}, u32[]{:S(2)}, u32[]{:S(2)}) %collective-permute-start.4) | collective-permute-done | bytes 16416 | tf_op jit(solution)/shard_map/ppermute | solution.py:383
  47.1 0.1 shard_map.95
  47.2 2.7 %collective-permute-start.5 = (bf16[16,256]{1,0:T(8,128)(2,1)S(1)}, bf16[16,256]{1,0:T(8,128)(2,1)S(1)}, u32[]{:S(2)}, u32[]{:S(2)}) collective-permute-start(bf16[16,256]{1,0:T(8,128)(2,1)S(1)} %get-tuple-element.23), channel_id=1, source_target_pairs={{0,4},{4,8},{8,12},{1,5},{5,9},{9,13},{2,6},{6,10},{10,14},{3,7},{... | collective-permute-start | bytes 24584 | tf_op jit(solution)/shard_map/ppermute | solution.py:408
  49.9 1.3 %collective-permute-start.6 = (bf16[16,256]{1,0:T(8,128)(2,1)S(1)}, bf16[16,256]{1,0:T(8,128)(2,1)S(1)}, u32[]{:S(2)}, u32[]{:S(2)}) collective-permute-start(bf16[16,256]{1,0:T(8,128)(2,1)S(1)} %get-tuple-element.24), channel_id=1, source_target_pairs={{4,0},{8,4},{12,8},{5,1},{9,5},{13,9},{6,2},{10,6},{14,10},{7,3},{... | collective-permute-start | bytes 24584 | tf_op jit(solution)/shard_map/ppermute | solution.py:409
  51.2 0.8 shard_map.96.refs_2_.rise
  52.0 2.8 %collective-permute-done.6.refs_1_.high = bf16[16,256]{1,0:T(8,128)(2,1)S(1)} collective-permute-done((bf16[16,256]{1,0:T(8,128)(2,1)S(1)}, bf16[16,256]{1,0:T(8,128)(2,1)S(1)}, u32[]{:S(2)}, u32[]{:S(2)}) %collective-permute-start.6) | collective-permute-done | bytes 8224 | tf_op jit(solution)/shard_map/ppermute | solution.py:409
  54.8 0.4 all-to-all-done.1
  55.3 1.2 %copy-done.1 = bf16[3,3,3,512,32]{3,4,2,1,0:T(8,128)(2,1)S(1)} copy-done((bf16[3,3,3,512,32]{3,4,2,1,0:T(8,128)(2,1)S(1)}, bf16[3,3,3,512,32]{3,4,2,1,0:T(8,128)(2,1)}, u32[]{:S(2)}) %copy-start.1) | copy-done | bytes 884760
  56.5 0.7 shard_map.97
  57.2 12.9 %all_to_all.21 = bf16[16,32,128]{2,1,0:T(8,128)(2,1)S(1)} all-to-all(bf16[16,32,128]{2,1,0:T(8,128)(2,1)S(1)} %shard_map.97), channel_id=1, replica_groups=mesh['rep'=2,'z'=4,'r'=4] {'z','r'}, dimensions={0} | all-to-all | bytes 262144 | tf_op jit(solution)/shard_map/all_to_all | solution.py:312
  70.0 1.5 %copy-done.5 = bf16[4,864,256]{2,1,0:T(8,128)(2,1)S(1)} copy-done((bf16[4,864,256]{2,1,0:T(8,128)(2,1)S(1)}, bf16[4,864,256]{2,1,0:T(8,128)(2,1)}, u32[]{:S(2)}) %copy-start.5) | copy-done | bytes 1769496
  71.5 1.6 %shard_map.98 = bf16[512,256]{1,0:T(8,128)(2,1)S(1)} custom-call(s32[1]{0:T(128)} %bitcast.rank.rank_ref, bf16[512,128]{1,0:T(8,128)(2,1)S(1)} %bitcast.27, bf16[512,512]{1,0:T(8,128)(2,1)S(1)} %shard_map.96.refs_2_.rise, bf16[16,256]{1,0:T(8,128)(2,1)S(1)} %collective-permute-done.5.refs_0_.low, bf16[16,256]{1,0:T(8,128)(2,1)S(1)} %collective-permute-done.6.refs_1_.high, ...), custom_call_target="tpu_custom_call" | custom-call | flops 905969664 | bytes 2506756 | tf_op jit(solution)/shard_map/pallas_call | solution.py:18
  73.1 8.6 %all_to_all.22.partials = bf16[4,128,256]{2,1,0:T(8,128)(2,1)S(1)} all-to-all(bf16[4,128,256]{2,1,0:T(8,128)(2,1)S(1)} %bitcast.26), channel_id=1, replica_groups=mesh['rep'=2,'z'=4,'r'=4] {'r'}, dimensions={0} | all-to-all | bytes 524288 | tf_op jit(solution)/shard_map/all_to_all | solution.py:312
  81.6 1.1 %shard_map.99 = bf16[1024,128]{1,0:T(8,128)(2,1)} custom-call(bf16[4,128,256]{2,1,0:T(8,128)(2,1)S(1)} %all_to_all.22.partials, bf16[8,256,128]{2,1,0:T(8,128)(2,1)S(1)} %bitcast.24), custom_call_target="tpu_custom_call" | custom-call | flops 67108864 | bytes 786432 | tf_op jit(solution)/shard_map/pallas_call | solution.py:18
  (20 shorter events, 0.0 us)
Async XLA Ops:
  6.5 63.5 %all-gather.2.cloned.1.call-start = ((), (), s32[]{:S(2)}) async-start(), calls=%async_computation.4 | async-start | bytes 2211840 | tf_op jit(solution)/shard_map/all_gather | solution.py:333
  7.3 1.0 %copy-start.8 = (bf16[4,16,16,128]{3,2,1,0:T(8,128)(2,1)S(1)}, bf16[4,16,16,128]{3,2,1,0:T(8,128)(2,1)}, u32[]{:S(2)}) copy-start(bf16[4,16,16,128]{3,2,1,0:T(8,128)(2,1)} %volume.1) | copy-start | bytes 786436
  8.2 4.9 %copy-start.6 = (bf16[3,3,3,128,128]{4,3,2,1,0:T(8,128)(2,1)S(1)}, bf16[3,3,3,128,128]{4,3,2,1,0:T(8,128)(2,1)}, u32[]{:S(2)}) copy-start(bf16[3,3,3,128,128]{4,3,2,1,0:T(8,128)(2,1)} %param.10) | copy-start | bytes 2654212
  8.3 9.4 %collective-permute-start = (bf16[3,16,16,128]{3,2,1,0:T(8,128)(2,1)S(1)}, bf16[3,16,16,128]{3,2,1,0:T(8,128)(2,1)S(1)}, u32[]{:S(2)}, u32[]{:S(2)}) collective-permute-start(bf16[3,16,16,128]{3,2,1,0:T(8,128)(2,1)S(1)} %get-tuple-element.15), channel_id=1, source_target_pairs={{1,2},{3,4},{5,6},{7,8},{9,10},{11,12},{13,14},{2,1},{4,3},{6,5},{... | collective-permute-start | bytes 589832 | tf_op jit(solution)/shard_map/ppermute | solution.py:349
  13.0 4.7 %collective-permute-start.1 = (bf16[3,16,16,128]{3,2,1,0:T(8,128)(2,1)S(1)}, bf16[3,16,16,128]{3,2,1,0:T(8,128)(2,1)S(1)}, u32[]{:S(2)}, u32[]{:S(2)}) collective-permute-start(bf16[3,16,16,128]{3,2,1,0:T(8,128)(2,1)S(1)} %get-tuple-element.16), channel_id=1, source_target_pairs={{0,1},{1,0},{2,3},{3,2},{4,5},{5,4},{6,7},{7,6},{8,9},{9,8},{10,11... | collective-permute-start | bytes 589832 | tf_op jit(solution)/shard_map/ppermute | solution.py:350
  13.2 4.5 %copy-start.4 = (bf16[3,3,3,128,256]{4,3,2,1,0:T(8,128)(2,1)S(1)}, bf16[3,3,3,128,256]{4,3,2,1,0:T(8,128)(2,1)}, u32[]{:S(2)}) copy-start(bf16[3,3,3,128,256]{4,3,2,1,0:T(8,128)(2,1)} %param.11) | copy-start | bytes 5308420
  13.2 4.5 %copy-start.7 = (bf16[3,3,3,128,128]{4,3,2,1,0:T(8,128)(2,1)S(1)}, bf16[3,3,3,128,128]{4,3,2,1,0:T(8,128)(2,1)}, u32[]{:S(2)}) copy-start(bf16[3,3,3,128,128]{4,3,2,1,0:T(8,128)(2,1)} %param.10) | copy-start | bytes 2654212
  13.2 4.5 %copy-start.9 = (bf16[256,256]{1,0:T(8,128)(2,1)S(1)}, bf16[256,256]{1,0:T(8,128)(2,1)}, u32[]{:S(2)}) copy-start(bf16[256,256]{1,0:T(8,128)(2,1)} %constant.26.clone.order) | copy-start | bytes 393220
  17.7 18.2 %copy-start.3 = (bf16[3,3,3,256,32]{3,4,2,1,0:T(8,128)(2,1)S(1)}, bf16[3,3,3,256,32]{3,4,2,1,0:T(8,128)(2,1)}, u32[]{:S(2)}) copy-start(bf16[3,3,3,256,32]{3,4,2,1,0:T(8,128)(2,1)} %param.12) | copy-start | bytes 1327108
  17.7 33.5 %copy-start = (bf16[2,2,2,512,256]{4,3,2,1,0:T(8,128)(2,1)S(1)}, bf16[2,2,2,512,256]{4,3,2,1,0:T(8,128)(2,1)}, u32[]{:S(2)}) copy-start(bf16[2,2,2,512,256]{4,3,2,1,0:T(8,128)(2,1)} %param.14) | copy-start | bytes 6291460
  37.2 18.1 %all-to-all-start.1 = ((bf16[16,32,256]{2,1,0:T(8,128)(2,1)}), bf16[16,32,256]{2,1,0:T(8,128)(2,1)S(1)}, u32[]{:S(2)}, u32[]{:S(2)}) async-start(bf16[16,32,256]{2,1,0:T(8,128)(2,1)} %shard_map.94), calls=%async_computation.1 | async-start | bytes 524288 | tf_op jit(solution)/shard_map/all_to_all | solution.py:312
  41.8 2.1 %collective-permute-start.2 = (bf16[32,256]{1,0:T(8,128)(2,1)S(1)}, bf16[32,256]{1,0:T(8,128)(2,1)S(1)}, u32[]{:S(2)}, u32[]{:S(2)}) collective-permute-start(bf16[32,256]{1,0:T(8,128)(2,1)S(1)} %get-tuple-element.20), channel_id=1, source_target_pairs={{0,1},{1,0},{2,3},{3,2},{4,5},{5,4},{6,7},{7,6},{8,9},{9,8},{10,11... | collective-permute-start | bytes 49160 | tf_op jit(solution)/shard_map/ppermute | solution.py:383
  42.0 3.2 %collective-permute-start.3 = (bf16[32,256]{1,0:T(8,128)(2,1)S(1)}, bf16[32,256]{1,0:T(8,128)(2,1)S(1)}, u32[]{:S(2)}, u32[]{:S(2)}) collective-permute-start(bf16[32,256]{1,0:T(8,128)(2,1)S(1)} %get-tuple-element.21), channel_id=1, source_target_pairs={{0,2},{1,3},{2,0},{3,1},{4,6},{5,7},{6,4},{7,5},{8,10},{9,11},{10,... | collective-permute-start | bytes 49160 | tf_op jit(solution)/shard_map/ppermute | solution.py:383
  43.5 3.6 %collective-permute-start.4 = (bf16[32,256]{1,0:T(8,128)(2,1)S(1)}, bf16[32,256]{1,0:T(8,128)(2,1)S(1)}, u32[]{:S(2)}, u32[]{:S(2)}) collective-permute-start(bf16[32,256]{1,0:T(8,128)(2,1)S(1)} %get-tuple-element.22), channel_id=1, source_target_pairs={{0,3},{1,2},{2,1},{3,0},{4,7},{5,6},{6,5},{7,4},{8,11},{9,10},{10,... | collective-permute-start | bytes 49160 | tf_op jit(solution)/shard_map/ppermute | solution.py:383
  47.2 4.8 %collective-permute-start.5 = (bf16[16,256]{1,0:T(8,128)(2,1)S(1)}, bf16[16,256]{1,0:T(8,128)(2,1)S(1)}, u32[]{:S(2)}, u32[]{:S(2)}) collective-permute-start(bf16[16,256]{1,0:T(8,128)(2,1)S(1)} %get-tuple-element.23), channel_id=1, source_target_pairs={{0,4},{4,8},{8,12},{1,5},{5,9},{9,13},{2,6},{6,10},{10,14},{3,7},{... | collective-permute-start | bytes 24584 | tf_op jit(solution)/shard_map/ppermute | solution.py:408
  49.9 4.9 %collective-permute-start.6 = (bf16[16,256]{1,0:T(8,128)(2,1)S(1)}, bf16[16,256]{1,0:T(8,128)(2,1)S(1)}, u32[]{:S(2)}, u32[]{:S(2)}) collective-permute-start(bf16[16,256]{1,0:T(8,128)(2,1)S(1)} %get-tuple-element.24), channel_id=1, source_target_pairs={{4,0},{8,4},{12,8},{5,1},{9,5},{13,9},{6,2},{10,6},{14,10},{7,3},{... | collective-permute-start | bytes 24584 | tf_op jit(solution)/shard_map/ppermute | solution.py:409
  55.3 1.2 %copy-start.1 = (bf16[3,3,3,512,32]{3,4,2,1,0:T(8,128)(2,1)S(1)}, bf16[3,3,3,512,32]{3,4,2,1,0:T(8,128)(2,1)}, u32[]{:S(2)}) copy-start(bf16[3,3,3,512,32]{3,4,2,1,0:T(8,128)(2,1)} %param.13) | copy-start | bytes 2654212
  70.0 1.5 %copy-start.5 = (bf16[4,864,256]{2,1,0:T(8,128)(2,1)S(1)}, bf16[4,864,256]{2,1,0:T(8,128)(2,1)}, u32[]{:S(2)}) copy-start(bf16[4,864,256]{2,1,0:T(8,128)(2,1)} %all-gather.2.cloned.1.call-done.decode) | copy-start | bytes 5308420
  71.5 10.1 %copy-start.2 = (bf16[2,2,2,256,128]{4,3,2,1,0:T(8,128)(2,1)S(1)}, bf16[2,2,2,256,128]{4,3,2,1,0:T(8,128)(2,1)}, u32[]{:S(2)}) copy-start(bf16[2,2,2,256,128]{4,3,2,1,0:T(8,128)(2,1)} %param.16) | copy-start | bytes 1572868
Sparse Core Ops, SparseCore 0:
  8.9 51.0 all-gather.1

commit v6 on v5

--- a/solution.py
+++ b/solution.py
@@ -206,7 +206,8 @@
     last[...] = edge_slice(blocks[GROUP - 1], True)
 
 
-def deep_stage(pooled, weights, out):
+def deep_stage(pooled, weights, *refs):
+    out = refs[-1]
     n, chans, voxels = out.shape
     deep = spread_taps(weights, pooled[...], ((1,), (1,)), chans, voxels).astype(jnp.bfloat16)
     for dest in range(n):
@@ -392,9 +393,11 @@
         (
             pooled_whole.reshape(voxels, 256),
             deep_kernel.transpose(0, 1, 2, 4, 3).reshape(27 * chans, 256),
+            *near[1:],
         ),
         2 * 27 * chans * 256 * voxels,
         16,
+        unread=GROUP - 1,
     )
     first, last = call(
         edge_stage,

time: 91 us -> 91.8 us (level)
  blocking collectives: 36.7 us -> 21.1 us
  waiting for transfers between devices: 10.3 us -> 19.2 us
  starting transfers between devices: 15.4 us -> 22.3 us
    all_to_all x3 -> x2, blocking collectives: 36.7 us -> 21.1 us  [exchange(): lax.all_to_all(payload, axis, split_axis=0, concat_axis=0, tiled=True)]
    all_to_all x1 -> x2, waiting for transfers between devices: 0.45 us -> 8.31 us  [exchange(): lax.all_to_all(payload, axis, split_axis=0, concat_axis=0, tiled=True)]
    all_to_all x1 -> x2, starting transfers between devices: 4.54 us -> 10.8 us  [exchange(): lax.all_to_all(payload, axis, split_axis=0, concat_axis=0, tiled=True)]
    ppermute x1, waiting for transfers between devices: 0.01 us -> 3.93 us  [body(): skip_low = lax.ppermute(last, 'z', [(p, p + 1) for p in range(planes - 1)])]
    ppermute x1, waiting for transfers between devices: 2.81 us -> 0.01 us  [body(): lax.ppermute(first, 'z', [(p + 1, p) for p in range(planes - 1)])]
  transfers between devices with their start and end apart: 9 -> 10, of which waited for: 5 -> 6; matrix products, arithmetic and copies ran while one was open for 0% -> 0% of each run, Pallas kernels for 8% -> 9%
where the time goes in v6:
time: 91.8 us; the launch traced here: 90.3 us
  starting transfers between devices  22.3 us (24%)
  blocking collectives  21.1 us (23%)
  waiting for transfers between devices  19.2 us (21%)
  between operations  13.5 us (15%)
  Pallas kernels  10.4 us (11%)
  local copies, waits for them, and re-layouts  3.62 us (4%)
    all_to_all x2, blocking collectives, exchange(): lax.all_to_all(payload, axis, split_axis=0, concat_axis=0, tiled=True)  21.1 us
    all_to_all x2, starting transfers between devices, exchange(): lax.all_to_all(payload, axis, split_axis=0, concat_axis=0, tiled=True)  10.8 us
    pallas_call x9, Pallas kernels, call(): pl.pallas_call(kernel, out_shape=outs, in_specs=[pl.BlockSpec(memory_spac...  10.4 us
    all_to_all x2, waiting for transfers between devices, exchange(): lax.all_to_all(payload, axis, split_axis=0, concat_axis=0, tiled=True)  8.31 us
    ppermute x1, starting transfers between devices, body(): off_chip = lax.ppermute(off_chip, ALL, pairs + [(j, i) for i, j in pairs])  4.67 us
    ppermute x1, waiting for transfers between devices, body(): skip_low = lax.ppermute(last, 'z', [(p, p + 1) for p in range(planes - 1)])  3.93 us
    unnamed x20, local copies, waits for them, and re-layouts  3.62 us
    ppermute x1, starting transfers between devices, body(): skip_low = lax.ppermute(last, 'z', [(p, p + 1) for p in range(planes - 1)])  3.28 us
  transfers between devices with their start and end apart: 10, of which 6 were waited for; matrix products, arithmetic and copies ran while one was open for 0% of the time, Pallas kernels for 9%

profile of v6, /device:TPU:1, one launch (start us, length us, event | category | flops | bytes accessed | tf_op | source)
XLA Modules:
  0.0 90.3 jit_solution(15578438475816340289)
XLA Ops:
  6.5 0.7 all-gather.2.cloned.1.call-update
  7.3 0.9 %copy-done.8 = bf16[4,16,16,128]{3,2,1,0:T(8,128)(2,1)S(1)} copy-done((bf16[4,16,16,128]{3,2,1,0:T(8,128)(2,1)S(1)}, bf16[4,16,16,128]{3,2,1,0:T(8,128)(2,1)}, u32[]{:S(2)}) %copy-start.8) | copy-done | bytes 262168
  8.2 0.1 shard_map.91
  8.3 4.7 %collective-permute-start = (bf16[3,16,16,128]{3,2,1,0:T(8,128)(2,1)S(1)}, bf16[3,16,16,128]{3,2,1,0:T(8,128)(2,1)S(1)}, u32[]{:S(2)}, u32[]{:S(2)}) collective-permute-start(bf16[3,16,16,128]{3,2,1,0:T(8,128)(2,1)S(1)} %get-tuple-element.15), channel_id=1, source_target_pairs={{1,2},{3,4},{5,6},{7,8},{9,10},{11,12},{13,14},{2,1},{4,3},{6,5},{... | collective-permute-start | bytes 589832 | tf_op jit(solution)/shard_map/ppermute | solution.py:350
  13.0 0.1 collective-permute-start.1
  13.1 0.1 pad_add_fusion.ends
  13.2 0.0 copy-start.9
  13.2 1.4 %shard_map.92.own = f32[4,256,256]{2,1,0:T(8,128)S(1)} custom-call(bf16[4,16,16,128]{3,2,1,0:T(8,128)(2,1)S(1)} %get-tuple-element.17.volume, bf16[3,1152,128]{2,1,0:T(8,128)(2,1)S(1)} %bitcast.29), custom_call_target="tpu_custom_call" | custom-call | flops 1207959552 | bytes 1146880 | tf_op jit(solution)/shard_map/pallas_call | solution.py:18
  14.6 3.1 %collective-permute-done.off_chip = bf16[3,16,16,128]{3,2,1,0:T(8,128)(2,1)S(1)} collective-permute-done((bf16[3,16,16,128]{3,2,1,0:T(8,128)(2,1)S(1)}, bf16[3,16,16,128]{3,2,1,0:T(8,128)(2,1)S(1)}, u32[]{:S(2)}, u32[]{:S(2)}) %collective-permute-start) | collective-permute-done | bytes 196640 | tf_op jit(solution)/shard_map/ppermute | solution.py:350
  17.7 3.4 %shard_map.93 = (bf16[16,16,256]{2,1,0:T(8,128)(2,1)}, bf16[32,256]{1,0:T(8,128)(2,1)S(1)}, bf16[32,256]{1,0:T(8,128)(2,1)S(1)}, bf16[32,256]{1,0:T(8,128)(2,1)S(1)}, bf16[32,256]{1,0:T(8,128)(2,1)S(1)}) custom-call(s32[4]{0:T(128)S(1)} %pad_add_fusion.ends, bf16[3,16,16,128]{3,2,1,0:T(8,128)(2,1)S(1)} %collective-permute-done.off_chip, ...), custom_call_target="tpu_custom_call" | custom-call | flops 1207959552 | bytes 4227088 | tf_op jit(solution)/shard_map/pallas_call | solution.py:18
  21.1 6.2 %all-to-all-start = ((bf16[16,16,256]{2,1,0:T(8,128)(2,1)}), bf16[16,16,256]{2,1,0:T(8,128)(2,1)S(1)}, u32[]{:S(2)}, u32[]{:S(2)}) async-start(bf16[16,16,256]{2,1,0:T(8,128)(2,1)} %get-tuple-element.18), calls=%async_computation | async-start | bytes 262144 | tf_op jit(solution)/shard_map/all_to_all | solution.py:313
  27.3 0.2 collective-permute-start.2
  27.5 1.6 %collective-permute-start.3 = (bf16[32,256]{1,0:T(8,128)(2,1)S(1)}, bf16[32,256]{1,0:T(8,128)(2,1)S(1)}, u32[]{:S(2)}, u32[]{:S(2)}) collective-permute-start(bf16[32,256]{1,0:T(8,128)(2,1)S(1)} %get-tuple-element.20), channel_id=1, source_target_pairs={{0,2},{1,3},{2,0},{3,1},{4,6},{5,7},{6,4},{7,5},{8,10},{9,11},{10,... | collective-permute-start | bytes 49160 | tf_op jit(solution)/shard_map/ppermute | solution.py:384
  29.1 0.4 collective-permute-start.4
  29.5 1.1 %collective-permute-done.3.refs_1_.refs_2_ = bf16[32,256]{1,0:T(8,128)(2,1)S(1)} collective-permute-done((bf16[32,256]{1,0:T(8,128)(2,1)S(1)}, bf16[32,256]{1,0:T(8,128)(2,1)S(1)}, u32[]{:S(2)}, u32[]{:S(2)}) %collective-permute-start.3) | collective-permute-done | bytes 16416 | tf_op jit(solution)/shard_map/ppermute | solution.py:384
  30.6 2.0 %collective-permute-done.4.refs_2_.refs_3_ = bf16[32,256]{1,0:T(8,128)(2,1)S(1)} collective-permute-done((bf16[32,256]{1,0:T(8,128)(2,1)S(1)}, bf16[32,256]{1,0:T(8,128)(2,1)S(1)}, u32[]{:S(2)}, u32[]{:S(2)}) %collective-permute-start.4) | collective-permute-done | bytes 16416 | tf_op jit(solution)/shard_map/ppermute | solution.py:384
  32.7 4.2 %all-to-all-done = bf16[16,16,256]{2,1,0:T(8,128)(2,1)S(1)} async-done(((bf16[16,16,256]{2,1,0:T(8,128)(2,1)}), bf16[16,16,256]{2,1,0:T(8,128)(2,1)S(1)}, u32[]{:S(2)}, u32[]{:S(2)}) %all-to-all-start) | async-done | bytes 131104 | tf_op jit(solution)/shard_map/all_to_all | solution.py:313
  36.9 1.3 %shard_map.94 = bf16[16,32,256]{2,1,0:T(8,128)(2,1)} custom-call(bf16[256,256]{1,0:T(8,128)(2,1)S(1)} %bitcast.23, bf16[864,256]{1,0:T(8,128)(2,1)S(1)} %bitcast.25, bf16[32,256]{1,0:T(8,128)(2,1)S(1)} %collective-permute-done.2.refs_0_.refs_1_, bf16[32,256]{1,0:T(8,128)(2,1)S(1)} %collective-permute-done.3.refs_1_.refs_2_, ...), custom_call_target="tpu_custom_call" | custom-call | flops 113246208 | bytes 573440 | tf_op jit(solution)/shard_map/pallas_call | solution.py:18
  38.1 4.7 %all-to-all-start.1 = ((bf16[16,32,256]{2,1,0:T(8,128)(2,1)}), bf16[16,32,256]{2,1,0:T(8,128)(2,1)S(1)}, u32[]{:S(2)}, u32[]{:S(2)}) async-start(bf16[16,32,256]{2,1,0:T(8,128)(2,1)} %shard_map.94), calls=%async_computation.1 | async-start | bytes 524288 | tf_op jit(solution)/shard_map/all_to_all | solution.py:313
  42.8 0.1 shard_map.95
  42.9 3.3 %collective-permute-start.5 = (bf16[16,256]{1,0:T(8,128)(2,1)S(1)}, bf16[16,256]{1,0:T(8,128)(2,1)S(1)}, u32[]{:S(2)}, u32[]{:S(2)}) collective-permute-start(bf16[16,256]{1,0:T(8,128)(2,1)S(1)} %get-tuple-element.23), channel_id=1, source_target_pairs={{0,4},{4,8},{8,12},{1,5},{5,9},{9,13},{2,6},{6,10},{10,14},{3,7},{... | collective-permute-start | bytes 24584 | tf_op jit(solution)/shard_map/ppermute | solution.py:411
  46.2 1.3 %collective-permute-start.6 = (bf16[16,256]{1,0:T(8,128)(2,1)S(1)}, bf16[16,256]{1,0:T(8,128)(2,1)S(1)}, u32[]{:S(2)}, u32[]{:S(2)}) collective-permute-start(bf16[16,256]{1,0:T(8,128)(2,1)S(1)} %get-tuple-element.24), channel_id=1, source_target_pairs={{4,0},{8,4},{12,8},{5,1},{9,5},{13,9},{6,2},{10,6},{14,10},{7,3},{... | collective-permute-start | bytes 24584 | tf_op jit(solution)/shard_map/ppermute | solution.py:412
  47.5 0.8 shard_map.96.refs_2_.rise
  48.3 3.9 %collective-permute-done.5.refs_0_.low = bf16[16,256]{1,0:T(8,128)(2,1)S(1)} collective-permute-done((bf16[16,256]{1,0:T(8,128)(2,1)S(1)}, bf16[16,256]{1,0:T(8,128)(2,1)S(1)}, u32[]{:S(2)}, u32[]{:S(2)}) %collective-permute-start.5) | collective-permute-done | bytes 8224 | tf_op jit(solution)/shard_map/ppermute | solution.py:411
  52.2 4.1 %all-to-all-done.1 = bf16[16,32,256]{2,1,0:T(8,128)(2,1)S(1)} async-done(((bf16[16,32,256]{2,1,0:T(8,128)(2,1)}), bf16[16,32,256]{2,1,0:T(8,128)(2,1)S(1)}, u32[]{:S(2)}, u32[]{:S(2)}) %all-to-all-start.1) | async-done | bytes 262176 | tf_op jit(solution)/shard_map/all_to_all | solution.py:313
  56.3 1.2 %copy-done.1 = bf16[3,3,3,512,32]{3,4,2,1,0:T(8,128)(2,1)S(1)} copy-done((bf16[3,3,3,512,32]{3,4,2,1,0:T(8,128)(2,1)S(1)}, bf16[3,3,3,512,32]{3,4,2,1,0:T(8,128)(2,1)}, u32[]{:S(2)}) %copy-start.1) | copy-done | bytes 884760
  57.5 0.7 shard_map.97
  58.2 12.6 %all_to_all.20 = bf16[16,32,128]{2,1,0:T(8,128)(2,1)S(1)} all-to-all(bf16[16,32,128]{2,1,0:T(8,128)(2,1)S(1)} %shard_map.97), channel_id=1, replica_groups=mesh['rep'=2,'z'=4,'r'=4] {'z','r'}, dimensions={0} | all-to-all | bytes 262144 | tf_op jit(solution)/shard_map/all_to_all | solution.py:313
  70.8 1.5 %copy-done.5 = bf16[4,864,256]{2,1,0:T(8,128)(2,1)S(1)} copy-done((bf16[4,864,256]{2,1,0:T(8,128)(2,1)S(1)}, bf16[4,864,256]{2,1,0:T(8,128)(2,1)}, u32[]{:S(2)}) %copy-start.5) | copy-done | bytes 1769496
  72.2 1.6 %shard_map.98 = bf16[512,256]{1,0:T(8,128)(2,1)S(1)} custom-call(s32[1]{0:T(128)} %bitcast.rank.rank_ref, bf16[512,128]{1,0:T(8,128)(2,1)S(1)} %bitcast.27, bf16[512,512]{1,0:T(8,128)(2,1)S(1)} %shard_map.96.refs_2_.rise, bf16[16,256]{1,0:T(8,128)(2,1)S(1)} %collective-permute-done.5.refs_0_.low, bf16[16,256]{1,0:T(8,128)(2,1)S(1)} %collective-permute-done.6.refs_1_.high, ...), custom_call_target="tpu_custom_call" | custom-call | flops 905969664 | bytes 2506756 | tf_op jit(solution)/shard_map/pallas_call | solution.py:18
  73.8 8.6 %all_to_all.21.partials = bf16[4,128,256]{2,1,0:T(8,128)(2,1)S(1)} all-to-all(bf16[4,128,256]{2,1,0:T(8,128)(2,1)S(1)} %bitcast.26), channel_id=1, replica_groups=mesh['rep'=2,'z'=4,'r'=4] {'r'}, dimensions={0} | all-to-all | bytes 524288 | tf_op jit(solution)/shard_map/all_to_all | solution.py:313
  82.4 1.1 %shard_map.99 = bf16[1024,128]{1,0:T(8,128)(2,1)} custom-call(bf16[4,128,256]{2,1,0:T(8,128)(2,1)S(1)} %all_to_all.21.partials, bf16[8,256,128]{2,1,0:T(8,128)(2,1)S(1)} %bitcast.24), custom_call_target="tpu_custom_call" | custom-call | flops 67108864 | bytes 786432 | tf_op jit(solution)/shard_map/pallas_call | solution.py:18
  (21 shorter events, 0.0 us)
Async XLA Ops:
  6.5 64.2 %all-gather.2.cloned.1.call-start = ((), (), s32[]{:S(2)}) async-start(), calls=%async_computation.4 | async-start | bytes 2211840 | tf_op jit(solution)/shard_map/all_gather | solution.py:334
  7.3 1.0 %copy-start.8 = (bf16[4,16,16,128]{3,2,1,0:T(8,128)(2,1)S(1)}, bf16[4,16,16,128]{3,2,1,0:T(8,128)(2,1)}, u32[]{:S(2)}) copy-start(bf16[4,16,16,128]{3,2,1,0:T(8,128)(2,1)} %volume.1) | copy-start | bytes 786436
  8.2 4.9 %copy-start.6 = (bf16[3,3,3,128,128]{4,3,2,1,0:T(8,128)(2,1)S(1)}, bf16[3,3,3,128,128]{4,3,2,1,0:T(8,128)(2,1)}, u32[]{:S(2)}) copy-start(bf16[3,3,3,128,128]{4,3,2,1,0:T(8,128)(2,1)} %param.10) | copy-start | bytes 2654212
  8.3 9.4 %collective-permute-start = (bf16[3,16,16,128]{3,2,1,0:T(8,128)(2,1)S(1)}, bf16[3,16,16,128]{3,2,1,0:T(8,128)(2,1)S(1)}, u32[]{:S(2)}, u32[]{:S(2)}) collective-permute-start(bf16[3,16,16,128]{3,2,1,0:T(8,128)(2,1)S(1)} %get-tuple-element.15), channel_id=1, source_target_pairs={{1,2},{3,4},{5,6},{7,8},{9,10},{11,12},{13,14},{2,1},{4,3},{6,5},{... | collective-permute-start | bytes 589832 | tf_op jit(solution)/shard_map/ppermute | solution.py:350
  13.0 4.7 %collective-permute-start.1 = (bf16[3,16,16,128]{3,2,1,0:T(8,128)(2,1)S(1)}, bf16[3,16,16,128]{3,2,1,0:T(8,128)(2,1)S(1)}, u32[]{:S(2)}, u32[]{:S(2)}) collective-permute-start(bf16[3,16,16,128]{3,2,1,0:T(8,128)(2,1)S(1)} %get-tuple-element.16), channel_id=1, source_target_pairs={{0,1},{1,0},{2,3},{3,2},{4,5},{5,4},{6,7},{7,6},{8,9},{9,8},{10,11... | collective-permute-start | bytes 589832 | tf_op jit(solution)/shard_map/ppermute | solution.py:351
  13.2 4.5 %copy-start.4 = (bf16[3,3,3,128,256]{4,3,2,1,0:T(8,128)(2,1)S(1)}, bf16[3,3,3,128,256]{4,3,2,1,0:T(8,128)(2,1)}, u32[]{:S(2)}) copy-start(bf16[3,3,3,128,256]{4,3,2,1,0:T(8,128)(2,1)} %param.11) | copy-start | bytes 5308420
  13.2 4.5 %copy-start.7 = (bf16[3,3,3,128,128]{4,3,2,1,0:T(8,128)(2,1)S(1)}, bf16[3,3,3,128,128]{4,3,2,1,0:T(8,128)(2,1)}, u32[]{:S(2)}) copy-start(bf16[3,3,3,128,128]{4,3,2,1,0:T(8,128)(2,1)} %param.10) | copy-start | bytes 2654212
  13.2 4.5 %copy-start.9 = (bf16[256,256]{1,0:T(8,128)(2,1)S(1)}, bf16[256,256]{1,0:T(8,128)(2,1)}, u32[]{:S(2)}) copy-start(bf16[256,256]{1,0:T(8,128)(2,1)} %constant.26.clone.order) | copy-start | bytes 393220
  17.7 19.2 %copy-start.3 = (bf16[3,3,3,256,32]{3,4,2,1,0:T(8,128)(2,1)S(1)}, bf16[3,3,3,256,32]{3,4,2,1,0:T(8,128)(2,1)}, u32[]{:S(2)}) copy-start(bf16[3,3,3,256,32]{3,4,2,1,0:T(8,128)(2,1)} %param.12) | copy-start | bytes 1327108
  17.7 29.8 %copy-start = (bf16[2,2,2,512,256]{4,3,2,1,0:T(8,128)(2,1)S(1)}, bf16[2,2,2,512,256]{4,3,2,1,0:T(8,128)(2,1)}, u32[]{:S(2)}) copy-start(bf16[2,2,2,512,256]{4,3,2,1,0:T(8,128)(2,1)} %param.14) | copy-start | bytes 6291460
  21.1 15.7 %all-to-all-start = ((bf16[16,16,256]{2,1,0:T(8,128)(2,1)}), bf16[16,16,256]{2,1,0:T(8,128)(2,1)S(1)}, u32[]{:S(2)}, u32[]{:S(2)}) async-start(bf16[16,16,256]{2,1,0:T(8,128)(2,1)} %get-tuple-element.18), calls=%async_computation | async-start | bytes 262144 | tf_op jit(solution)/shard_map/all_to_all | solution.py:313
  27.3 2.1 %collective-permute-start.2 = (bf16[32,256]{1,0:T(8,128)(2,1)S(1)}, bf16[32,256]{1,0:T(8,128)(2,1)S(1)}, u32[]{:S(2)}, u32[]{:S(2)}) collective-permute-start(bf16[32,256]{1,0:T(8,128)(2,1)S(1)} %get-tuple-element.19), channel_id=1, source_target_pairs={{0,1},{1,0},{2,3},{3,2},{4,5},{5,4},{6,7},{7,6},{8,9},{9,8},{10,11... | collective-permute-start | bytes 49160 | tf_op jit(solution)/shard_map/ppermute | solution.py:384
  27.5 3.1 %collective-permute-start.3 = (bf16[32,256]{1,0:T(8,128)(2,1)S(1)}, bf16[32,256]{1,0:T(8,128)(2,1)S(1)}, u32[]{:S(2)}, u32[]{:S(2)}) collective-permute-start(bf16[32,256]{1,0:T(8,128)(2,1)S(1)} %get-tuple-element.20), channel_id=1, source_target_pairs={{0,2},{1,3},{2,0},{3,1},{4,6},{5,7},{6,4},{7,5},{8,10},{9,11},{10,... | collective-permute-start | bytes 49160 | tf_op jit(solution)/shard_map/ppermute | solution.py:384
  29.1 3.6 %collective-permute-start.4 = (bf16[32,256]{1,0:T(8,128)(2,1)S(1)}, bf16[32,256]{1,0:T(8,128)(2,1)S(1)}, u32[]{:S(2)}, u32[]{:S(2)}) collective-permute-start(bf16[32,256]{1,0:T(8,128)(2,1)S(1)} %get-tuple-element.21), channel_id=1, source_target_pairs={{0,3},{1,2},{2,1},{3,0},{4,7},{5,6},{6,5},{7,4},{8,11},{9,10},{10,... | collective-permute-start | bytes 49160 | tf_op jit(solution)/shard_map/ppermute | solution.py:384
  38.1 18.2 %all-to-all-start.1 = ((bf16[16,32,256]{2,1,0:T(8,128)(2,1)}), bf16[16,32,256]{2,1,0:T(8,128)(2,1)S(1)}, u32[]{:S(2)}, u32[]{:S(2)}) async-start(bf16[16,32,256]{2,1,0:T(8,128)(2,1)} %shard_map.94), calls=%async_computation.1 | async-start | bytes 524288 | tf_op jit(solution)/shard_map/all_to_all | solution.py:313
  42.9 9.3 %collective-permute-start.5 = (bf16[16,256]{1,0:T(8,128)(2,1)S(1)}, bf16[16,256]{1,0:T(8,128)(2,1)S(1)}, u32[]{:S(2)}, u32[]{:S(2)}) collective-permute-start(bf16[16,256]{1,0:T(8,128)(2,1)S(1)} %get-tuple-element.23), channel_id=1, source_target_pairs={{0,4},{4,8},{8,12},{1,5},{5,9},{9,13},{2,6},{6,10},{10,14},{3,7},{... | collective-permute-start | bytes 24584 | tf_op jit(solution)/shard_map/ppermute | solution.py:411
  46.2 6.0 %collective-permute-start.6 = (bf16[16,256]{1,0:T(8,128)(2,1)S(1)}, bf16[16,256]{1,0:T(8,128)(2,1)S(1)}, u32[]{:S(2)}, u32[]{:S(2)}) collective-permute-start(bf16[16,256]{1,0:T(8,128)(2,1)S(1)} %get-tuple-element.24), channel_id=1, source_target_pairs={{4,0},{8,4},{12,8},{5,1},{9,5},{13,9},{6,2},{10,6},{14,10},{7,3},{... | collective-permute-start | bytes 24584 | tf_op jit(solution)/shard_map/ppermute | solution.py:412
  56.3 1.2 %copy-start.1 = (bf16[3,3,3,512,32]{3,4,2,1,0:T(8,128)(2,1)S(1)}, bf16[3,3,3,512,32]{3,4,2,1,0:T(8,128)(2,1)}, u32[]{:S(2)}) copy-start(bf16[3,3,3,512,32]{3,4,2,1,0:T(8,128)(2,1)} %param.13) | copy-start | bytes 2654212
  70.8 1.5 %copy-start.5 = (bf16[4,864,256]{2,1,0:T(8,128)(2,1)S(1)}, bf16[4,864,256]{2,1,0:T(8,128)(2,1)}, u32[]{:S(2)}) copy-start(bf16[4,864,256]{2,1,0:T(8,128)(2,1)} %all-gather.2.cloned.1.call-done.decode) | copy-start | bytes 5308420
  72.2 10.1 %copy-start.2 = (bf16[2,2,2,256,128]{4,3,2,1,0:T(8,128)(2,1)S(1)}, bf16[2,2,2,256,128]{4,3,2,1,0:T(8,128)(2,1)}, u32[]{:S(2)}) copy-start(bf16[2,2,2,256,128]{4,3,2,1,0:T(8,128)(2,1)} %param.16) | copy-start | bytes 1572868
Sparse Core Ops, SparseCore 0:
  8.9 50.9 all-gather.1

commit v7 on v6

--- a/solution.py
+++ b/solution.py
@@ -12,14 +12,16 @@
 MIB = 1024 * 1024
 
 
-def call(kernel, outs, scratch, args, flops, vmem_mib, scalars=0, unread=0):
+def call(kernel, outs, scratch, args, flops, vmem_mib, scalars=0, unread=0, far_outs=0):
     spaces = [pltpu.SMEM] * scalars + [pltpu.VMEM] * (len(args) - scalars - unread)
     spaces += [pl.ANY] * unread
     return pl.pallas_call(
         kernel,
         out_shape=outs,
         in_specs=[pl.BlockSpec(memory_space=space) for space in spaces],
-        out_specs=jax.tree.map(lambda _: pl.BlockSpec(memory_space=pltpu.VMEM), outs),
+        out_specs=jax.tree.map(
+            lambda _: pl.BlockSpec(memory_space=pl.ANY if far_outs else pltpu.VMEM), outs
+        ),
         scratch_shapes=scratch,
         compiler_params=pltpu.CompilerParams(vmem_limit_bytes=vmem_mib * MIB),
         cost_estimate=pl.CostEstimate(
@@ -82,6 +84,22 @@
         off_chip[s] = jnp.where(odd[0] == 0, volume[s], volume[s + 1])
         on_chip[s] = jnp.where(odd[0] == 0, volume[s + 1], volume[s])
     whole[...] = volume[...]
+
+
+def share_stage(place, decode, _, out, done):
+    step, rows = decode.shape[0] - out.shape[0], out.shape[0]
+    at = pl.multiple_of(place[1] * step, 16)
+    copy = pltpu.make_async_copy(decode.at[pl.ds(at, rows)], out, done)
+    copy.start()
+    copy.wait()
+
+
+def pick_stage(place, line, _, out, done):
+    rows = out.shape[1]
+    at = pl.multiple_of(place[1] * (line.shape[1] - rows), 16)
+    copy = pltpu.make_async_copy(line.at[:, pl.ds(at, rows)], out, done)
+    copy.start()
+    copy.wait()
 
 
 def own_stage(volume, weights, out, shifted):
@@ -165,7 +183,7 @@
         else:
             bottom = pltpu.roll(bottom, 64, 1)
         sides.append(jnp.where(lower, top, bottom))
-    return jnp.concatenate(sides, axis=1).astype(jnp.bfloat16)
+    return jnp.concatenate(sides, axis=1)
 
 
 def spread_taps(weights, values, dims, chans, voxels):
@@ -199,11 +217,14 @@
         blocks[rank[0] ^ k] = near[k][...]
 
 
-def edge_stage(rank, *refs):
-    near, (first, last, blocks) = refs[:GROUP], refs[GROUP:]
-    by_rank(rank, near, blocks)
-    first[...] = edge_slice(blocks[0], False)
-    last[...] = edge_slice(blocks[GROUP - 1], True)
+def edge_stage(place, *refs):
+    near, (near_swap, far_swap, blocks) = refs[:GROUP], refs[GROUP:]
+    by_rank(place, near, blocks)
+    first = edge_slice(blocks[0], False)
+    last = edge_slice(blocks[GROUP - 1], True)
+    even = place[2] == 0
+    near_swap[...] = jnp.where(even, last, first).astype(jnp.bfloat16)
+    far_swap[...] = jnp.where(even, first, last).astype(jnp.bfloat16)
 
 
 def deep_stage(pooled, weights, *refs):
@@ -243,9 +264,10 @@
         out[:, 128 * pair : 128 * pair + 128] = both
 
 
-def decode_stage(rank, deeper, rise, low, high, decode, *refs):
-    near, (out, framed, patches, risen, blocks) = refs[:GROUP], refs[GROUP:]
-    by_rank(rank, near, blocks)
+def decode_stage(place, deeper, rise, near_swap, far_swap, *refs):
+    near, (*decode, out, framed, patches, risen, blocks) = refs[:GROUP], refs[GROUP:]
+    by_rank(place, near, blocks)
+    even = place[2] == 0
     framed[...] = jnp.zeros(framed.shape, jnp.float32)
     spread = round_once(dot(deeper[...].astype(jnp.float32).T.astype(jnp.bfloat16), rise[...]))
     for pair in range(4):
@@ -262,7 +284,8 @@
                         4 * a + 2 * b + c, 16 * d + 4 * h : 16 * d + 4 * h + 4, :
                     ]
         if s == 0 or s == 9:
-            edge = (low if s == 0 else high)[...].astype(jnp.float32)
+            sides = near_swap[...].astype(jnp.float32), far_swap[...].astype(jnp.float32)
+            edge = jnp.where(even, sides[s == 0], sides[s == 9])
             parts = []
             for k in range(2):
                 half = edge[:, 128 * k : 128 * k + 128]
@@ -276,18 +299,31 @@
         joined = framed[s, 1:9, 8:16, :].reshape(64, 128)
         framed[s, 1:9, 8:16, :] = jnp.where(upper, skip, joined).reshape(8, 8, 128)
     fill_patches(framed, patches, 10)
-    blocks = decode.shape[0]
-    step = 128 // blocks
-    partial = None
-    for a in range(3):
-        right = [
-            decode[z, tap * step : (tap + 1) * step, :]
-            for tap in range(9 * a, 9 * a + 9)
-            for z in range(blocks)
-        ]
-        term = dot(patches[64 * a : 64 * a + 512], jnp.concatenate(right, axis=0))
-        partial = term if partial is None else partial + term
-    out[...] = partial.astype(jnp.bfloat16)
+    def multiply(rep):
+        if rep == 0:
+            parts = decode
+        else:
+            parts = decode[::-1]
+        split = parts[0].shape[1]
+        count = decode[0].shape[0]
+        step = 128 // count
+        partial = None
+        for a in range(3):
+            right = [
+                parts[0][z, row : row + 16, :] if row < split else parts[1][z, row - split : row - split + 16, :]
+                for tap in range(9 * a, 9 * a + 9)
+                for z in range(count)
+                for row in range(tap * step, (tap + 1) * step, 16)
+            ]
+            term = dot(patches[64 * a : 64 * a + 512], jnp.concatenate(right, axis=0))
+            partial = term if partial is None else partial + term
+        out[...] = partial.astype(jnp.bfloat16)
+
+    if len(decode) == 1:
+        multiply(0)
+    else:
+        pl.when(place[1] == 0)(lambda: multiply(0))
+        pl.when(place[1] == 1)(lambda: multiply(1))
 
 
 def final_stage(partials, weights, out, spaced):
@@ -331,11 +367,8 @@
     voxels = 16 * n
     bf16 = functools.partial(jax.ShapeDtypeStruct, dtype=jnp.bfloat16)
 
-    decode_part = lax.all_gather(decode_kernel.reshape(27 * chans, 256), "z", axis=0)
-    if chans % 16:
-        decode_part = decode_part.reshape(planes, 27, chans, 256).transpose(1, 0, 2, 3)
-        decode_part = decode_part.reshape(1, 27 * 128, 256)
-
+    rep = lax.axis_index("rep")
+    marks = jnp.stack([rank, rep, lax.axis_index("z") % 2]).astype(jnp.int32)
     odd = (place % 2).astype(jnp.int32)
     off_chip, on_chip, volume = call(
         front_stage,
@@ -346,6 +379,22 @@
         16,
         scalars=1,
     )
+    decode_block = decode_kernel.reshape(27 * chans, 256)
+    shared = lax.axis_size("rep") == 2 and chans == 32
+    if shared:
+        decode_block = call(
+            share_stage,
+            bf16((528, 256)),
+            [pltpu.SemaphoreType.DMA],
+            (marks, decode_block, volume),
+            0,
+            16,
+            scalars=1,
+            unread=2,
+            far_outs=1,
+        )
+    line = lax.all_gather(decode_block, "z", axis=0)
+
     pairs = [(i, i + 1) for i in range(1, n - 1, 2)]
     off_chip = lax.ppermute(off_chip, ALL, pairs + [(j, i) for i, j in pairs])
     on_chip = lax.ppermute(on_chip, ALL, [(i, i ^ 1) for i in range(n)])
@@ -383,7 +432,6 @@
     near = [skips[0]] + [
         lax.ppermute(skips[k], "r", [(r, r ^ k) for r in range(GROUP)]) for k in range(1, GROUP)
     ]
-    rank_ref = rank.astype(jnp.int32).reshape(1)
     blocks = pltpu.VMEM((GROUP, 32, 256), jnp.bfloat16)
 
     deep = call(
@@ -399,22 +447,42 @@
         16,
         unread=GROUP - 1,
     )
-    first, last = call(
+    if shared:
+        piece = call(
+            pick_stage,
+            bf16((planes, 336, 256)),
+            [pltpu.SemaphoreType.DMA],
+            (marks, line, deep),
+            0,
+            16,
+            scalars=1,
+            unread=2,
+            far_outs=1,
+        )
+        weights = (line, lax.ppermute(piece, "rep", [(0, 1), (1, 0)]))
+    elif chans % 16:
+        weights = line.reshape(planes, 27, chans, 256).transpose(1, 0, 2, 3)
+        weights = (weights.reshape(1, 27 * 128, 256),)
+    else:
+        weights = (line,)
+    swaps = call(
         edge_stage,
         (bf16((16, 256)), bf16((16, 256))),
         [blocks],
-        (rank_ref, *near),
+        (marks, *near),
         0,
         16,
         scalars=1,
     )
-    skip_low = lax.ppermute(last, "z", [(p, p + 1) for p in range(planes - 1)])
-    skip_high = lax.ppermute(first, "z", [(p + 1, p) for p in range(planes - 1)])
+    near_pairs = [(p, p + 1) for p in range(0, planes - 1, 2)]
+    far_pairs = [(p, p + 1) for p in range(1, planes - 1, 2)]
+    near_swap = lax.ppermute(swaps[0], "z", near_pairs + [(j, i) for i, j in near_pairs])
+    far_swap = lax.ppermute(swaps[1], "z", far_pairs + [(j, i) for i, j in far_pairs])
     rise_part = call(
         lambda rank_ref, *refs: rise_stage(rank_ref, chans, *refs),
         bf16((n * chans, 512)),
         [],
-        (rank_ref, rise_kernel.reshape(8, n * chans, 256)),
+        (marks, rise_kernel.reshape(8, n * chans, 256)),
         2 * 8 * n * chans * 256 * 64,
         16,
         scalars=1,
@@ -428,8 +496,8 @@
         (
             deep_whole,
             deeper_kernel.transpose(0, 1, 2, 4, 3).reshape(27 * chans, n * chans),
-            skip_low,
-            skip_high,
+            near_swap,
+            far_swap,
             rise_part,
         ),
         2 * 27 * chans * n * chans * voxels,
@@ -447,7 +515,7 @@
             pltpu.VMEM((8, 128, 128), jnp.float32),
             blocks,
         ],
-        (rank_ref, deeper_near, rise_part, skip_low, skip_high, decode_part, *near),
+        (marks, deeper_near, rise_part, near_swap, far_swap, *near, *weights),
         2 * 512 * 3456 * 256,
         24,
         scalars=1,

time: 91.8 us -> 90.5 us (0.986)
  waiting for transfers between devices: 19.2 us -> 11.7 us
  Pallas kernels: 10.4 us -> 15.4 us
  blocking collectives: 21.1 us -> 22.7 us
  starting transfers between devices: 22.3 us -> 21.2 us
    pallas_call x9 -> x11, Pallas kernels: 10.4 us -> 15.4 us  [call(): pl.pallas_call(kernel, out_shape=outs, in_specs=[pl.BlockSpec(memory_spac...]
    ppermute x2 -> x3, waiting for transfers between devices: 3.93 us -> 0.01 us  [the longest x1 0.01 us: body(): lax.ppermute(swaps[1], 'z', far_pairs + [(j, i) for i, j in far_pairs])]
    all_to_all x2, waiting for transfers between devices: 8.31 us -> 5.37 us  [exchange(): lax.all_to_all(payload, axis, split_axis=0, concat_axis=0, tiled=True)]
    all_to_all x2, blocking collectives: 21.1 us -> 22.7 us  [exchange(): lax.all_to_all(payload, axis, split_axis=0, concat_axis=0, tiled=True)]
    ppermute x2 -> x3, starting transfers between devices: 4.57 us -> 3.35 us  [the longest x1 1.39 us: body(): lax.ppermute(swaps[0], 'z', near_pairs + [(j, i) for i, j in near_pairs])]
    unnamed x20 -> x22, local copies, waits for them, and re-layouts: 3.62 us -> 4.21 us
  transfers between devices with their start and end apart: 10 -> 11, of which waited for: 6 -> 5; matrix products, arithmetic and copies ran while one was open for 0% -> 0% of each run, Pallas kernels for 9% -> 11%
where the time goes in v7:
time: 90.5 us; the launch traced here: 89 us
  blocking collectives  22.7 us (25%)
  starting transfers between devices  21.2 us (23%)
  Pallas kernels  15.4 us (17%)
  between operations  13.6 us (15%)
  waiting for transfers between devices  11.7 us (13%)
  local copies, waits for them, and re-layouts  4.21 us (5%)
    all_to_all x2, blocking collectives, exchange(): lax.all_to_all(payload, axis, split_axis=0, concat_axis=0, tiled=True)  22.7 us
    pallas_call x11, Pallas kernels, call(): pl.pallas_call(kernel, out_shape=outs, in_specs=[pl.BlockSpec(memory_spac...  15.4 us
    all_to_all x2, starting transfers between devices, exchange(): lax.all_to_all(payload, axis, split_axis=0, concat_axis=0, tiled=True)  11 us
    all_to_all x2, waiting for transfers between devices, exchange(): lax.all_to_all(payload, axis, split_axis=0, concat_axis=0, tiled=True)  5.37 us
    ppermute x1, starting transfers between devices, body(): off_chip = lax.ppermute(off_chip, ALL, pairs + [(j, i) for i, j in pairs])  4.57 us
    unnamed x22, local copies, waits for them, and re-layouts  4.21 us
    ppermute x3, waiting for transfers between devices, body(): lax.ppermute(skips[k], 'r', [(r, r ^ k) for r in range(GROUP)])  3.19 us
    ppermute x1, waiting for transfers between devices, body(): off_chip = lax.ppermute(off_chip, ALL, pairs + [(j, i) for i, j in pairs])  3.11 us
  transfers between devices with their start and end apart: 11, of which 5 were waited for; matrix products, arithmetic and copies ran while one was open for 0% of the time, Pallas kernels for 11%

profile of v7, /device:TPU:1, one launch (start us, length us, event | category | flops | bytes accessed | tf_op | source)
XLA Modules:
  0.0 89.0 jit_solution(12125142710811285058)
XLA Ops:
  6.5 0.9 %copy-done.9 = bf16[4,16,16,128]{3,2,1,0:T(8,128)(2,1)S(1)} copy-done((bf16[4,16,16,128]{3,2,1,0:T(8,128)(2,1)S(1)}, bf16[4,16,16,128]{3,2,1,0:T(8,128)(2,1)}, u32[]{:S(2)}) %copy-start.9) | copy-done | bytes 262168
  7.5 0.1 shard_map.91
  7.6 0.1 pad_add_fusion.place.rank_ref
  7.7 0.8 copy-done.5
  8.5 1.3 %shard_map.98 = bf16[528,256]{1,0:T(8,128)(2,1)} custom-call(s32[3]{0:T(128)S(1)} %pad_add_fusion.place.rank_ref, bf16[864,256]{1,0:T(8,128)(2,1)S(1)} %bitcast.30, bf16[4,16,16,128]{3,2,1,0:T(8,128)(2,1)S(1)} %get-tuple-element.17.volume._), custom_call_target="tpu_custom_call" | custom-call | bytes 12 | tf_op jit(solution)/shard_map/pallas_call | solution.py:18
  9.8 4.6 %collective-permute-start = (bf16[3,16,16,128]{3,2,1,0:T(8,128)(2,1)S(1)}, bf16[3,16,16,128]{3,2,1,0:T(8,128)(2,1)S(1)}, u32[]{:S(2)}, u32[]{:S(2)}) collective-permute-start(bf16[3,16,16,128]{3,2,1,0:T(8,128)(2,1)S(1)} %get-tuple-element.15), channel_id=1, source_target_pairs={{1,2},{3,4},{5,6},{7,8},{9,10},{11,12},{13,14},{2,1},{4,3},{6,5},{... | collective-permute-start | bytes 589832 | tf_op jit(solution)/shard_map/ppermute | solution.py:399
  14.5 1.4 %shard_map.92.own = f32[4,256,256]{2,1,0:T(8,128)S(1)} custom-call(bf16[4,16,16,128]{3,2,1,0:T(8,128)(2,1)S(1)} %get-tuple-element.17.volume._, bf16[3,1152,128]{2,1,0:T(8,128)(2,1)S(1)} %bitcast.35), custom_call_target="tpu_custom_call" | custom-call | flops 1207959552 | bytes 1146880 | tf_op jit(solution)/shard_map/pallas_call | solution.py:18
  16.0 3.1 %collective-permute-done.off_chip = bf16[3,16,16,128]{3,2,1,0:T(8,128)(2,1)S(1)} collective-permute-done((bf16[3,16,16,128]{3,2,1,0:T(8,128)(2,1)S(1)}, bf16[3,16,16,128]{3,2,1,0:T(8,128)(2,1)S(1)}, u32[]{:S(2)}, u32[]{:S(2)}) %collective-permute-start) | collective-permute-done | bytes 196640 | tf_op jit(solution)/shard_map/ppermute | solution.py:399
  19.1 3.3 %shard_map.93 = (bf16[16,16,256]{2,1,0:T(8,128)(2,1)}, bf16[32,256]{1,0:T(8,128)(2,1)S(1)}, bf16[32,256]{1,0:T(8,128)(2,1)S(1)}, bf16[32,256]{1,0:T(8,128)(2,1)S(1)}, bf16[32,256]{1,0:T(8,128)(2,1)S(1)}) custom-call(s32[4]{0:T(128)S(1)} %pad_add_fusion.1.ends, bf16[3,16,16,128]{3,2,1,0:T(8,128)(2,1)S(1)} %collective-permute-done.off_chip, ...), custom_call_target="tpu_custom_call" | custom-call | flops 1207959552 | bytes 4227088 | tf_op jit(solution)/shard_map/pallas_call | solution.py:18
  22.4 6.2 %all-to-all-start = ((bf16[16,16,256]{2,1,0:T(8,128)(2,1)}), bf16[16,16,256]{2,1,0:T(8,128)(2,1)S(1)}, u32[]{:S(2)}, u32[]{:S(2)}) async-start(bf16[16,16,256]{2,1,0:T(8,128)(2,1)} %get-tuple-element.18), calls=%async_computation | async-start | bytes 262144 | tf_op jit(solution)/shard_map/all_to_all | solution.py:349
  28.6 0.2 collective-permute-start.2
  28.8 1.6 %collective-permute-start.3 = (bf16[32,256]{1,0:T(8,128)(2,1)S(1)}, bf16[32,256]{1,0:T(8,128)(2,1)S(1)}, u32[]{:S(2)}, u32[]{:S(2)}) collective-permute-start(bf16[32,256]{1,0:T(8,128)(2,1)S(1)} %get-tuple-element.20), channel_id=1, source_target_pairs={{0,2},{1,3},{2,0},{3,1},{4,6},{5,7},{6,4},{7,5},{8,10},{9,11},{10,... | collective-permute-start | bytes 49160 | tf_op jit(solution)/shard_map/ppermute | solution.py:433
  30.4 0.4 collective-permute-start.4
  30.8 1.1 %collective-permute-done.3.refs_1_.refs_2_ = bf16[32,256]{1,0:T(8,128)(2,1)S(1)} collective-permute-done((bf16[32,256]{1,0:T(8,128)(2,1)S(1)}, bf16[32,256]{1,0:T(8,128)(2,1)S(1)}, u32[]{:S(2)}, u32[]{:S(2)}) %collective-permute-start.3) | collective-permute-done | bytes 16416 | tf_op jit(solution)/shard_map/ppermute | solution.py:433
  31.9 2.1 %collective-permute-done.4.refs_2_.refs_3_ = bf16[32,256]{1,0:T(8,128)(2,1)S(1)} collective-permute-done((bf16[32,256]{1,0:T(8,128)(2,1)S(1)}, bf16[32,256]{1,0:T(8,128)(2,1)S(1)}, u32[]{:S(2)}, u32[]{:S(2)}) %collective-permute-start.4) | collective-permute-done | bytes 16416 | tf_op jit(solution)/shard_map/ppermute | solution.py:433
  34.0 3.9 %all-to-all-done = bf16[16,16,256]{2,1,0:T(8,128)(2,1)S(1)} async-done(((bf16[16,16,256]{2,1,0:T(8,128)(2,1)}), bf16[16,16,256]{2,1,0:T(8,128)(2,1)S(1)}, u32[]{:S(2)}, u32[]{:S(2)}) %all-to-all-start) | async-done | bytes 131104 | tf_op jit(solution)/shard_map/all_to_all | solution.py:349
  37.9 1.3 %shard_map.94._ = bf16[16,32,256]{2,1,0:T(8,128)(2,1)} custom-call(bf16[256,256]{1,0:T(8,128)(2,1)S(1)} %bitcast.28, bf16[864,256]{1,0:T(8,128)(2,1)S(1)} %bitcast.31, bf16[32,256]{1,0:T(8,128)(2,1)S(1)} %collective-permute-done.2.refs_0_.refs_1_, bf16[32,256]{1,0:T(8,128)(2,1)S(1)} %collective-permute-done.3.refs_1_.refs_2_, ...), custom_call_target="tpu_custom_call" | custom-call | flops 113246208 | bytes 573440 | tf_op jit(solution)/shard_map/pallas_call | solution.py:18
  39.2 4.8 %all-to-all-start.1 = ((bf16[16,32,256]{2,1,0:T(8,128)(2,1)}), bf16[16,32,256]{2,1,0:T(8,128)(2,1)S(1)}, u32[]{:S(2)}, u32[]{:S(2)}) async-start(bf16[16,32,256]{2,1,0:T(8,128)(2,1)} %shard_map.94._), calls=%async_computation.1 | async-start | bytes 524288 | tf_op jit(solution)/shard_map/all_to_all | solution.py:349
  44.1 1.2 %copy-done.1 = bf16[2112,256]{1,0:T(8,128)(2,1)S(1)} copy-done((bf16[2112,256]{1,0:T(8,128)(2,1)S(1)}, bf16[2112,256]{1,0:T(8,128)(2,1)}, u32[]{:S(2)}) %copy-start.1) | copy-done | bytes 1081368
  45.3 1.4 %shard_map.99 = bf16[4,336,256]{2,1,0:T(8,128)(2,1)} custom-call(s32[3]{0:T(128)S(1)} %pad_add_fusion.place.rank_ref, bf16[4,528,256]{2,1,0:T(8,128)(2,1)S(1)} %bitcast.24, bf16[16,32,256]{2,1,0:T(8,128)(2,1)} %shard_map.94._), custom_call_target="tpu_custom_call" | custom-call | bytes 12 | tf_op jit(solution)/shard_map/pallas_call | solution.py:18
  46.7 1.3 %collective-permute-start.7 = (bf16[4,336,256]{2,1,0:T(8,128)(2,1)}, bf16[4,336,256]{2,1,0:T(8,128)(2,1)}, u32[]{:S(2)}, u32[]{:S(2)}) collective-permute-start(bf16[4,336,256]{2,1,0:T(8,128)(2,1)} %shard_map.99), channel_id=1, source_target_pairs={{0,16},{16,0},{1,17},{17,1},{2,18},{18,2},{3,19},{19,3},{4,20},{20... | collective-permute-start | bytes 2064392 | tf_op jit(solution)/shard_map/ppermute | solution.py:462
  48.0 0.6 shard_map.95
  48.6 1.4 %collective-permute-start.5 = (bf16[16,256]{1,0:T(8,128)(2,1)S(1)}, bf16[16,256]{1,0:T(8,128)(2,1)S(1)}, u32[]{:S(2)}, u32[]{:S(2)}) collective-permute-start(bf16[16,256]{1,0:T(8,128)(2,1)S(1)} %get-tuple-element.23), channel_id=1, source_target_pairs={{0,4},{8,12},{4,0},{12,8},{1,5},{9,13},{5,1},{13,9},{2,6},{10,14},... | collective-permute-start | bytes 24584 | tf_op jit(solution)/shard_map/ppermute | solution.py:479
  50.0 0.6 collective-permute-start.6
  50.7 1.3 %shard_map.96.refs_2_.rise = bf16[512,512]{1,0:T(8,128)(2,1)S(1)} custom-call(s32[3]{0:T(128)S(1)} %pad_add_fusion.place.rank_ref, bf16[8,512,256]{2,1,0:T(8,128)(2,1)S(1)} %bitcast.23), custom_call_target="tpu_custom_call" | custom-call | flops 134217728 | bytes 2097164 | tf_op jit(solution)/shard_map/pallas_call | solution.py:18
  52.1 1.5 %all-to-all-done.1 = bf16[16,32,256]{2,1,0:T(8,128)(2,1)S(1)} async-done(((bf16[16,32,256]{2,1,0:T(8,128)(2,1)}), bf16[16,32,256]{2,1,0:T(8,128)(2,1)S(1)}, u32[]{:S(2)}, u32[]{:S(2)}) %all-to-all-start.1) | async-done | bytes 262176 | tf_op jit(solution)/shard_map/all_to_all | solution.py:349
  53.5 1.2 %copy-done.3 = bf16[3,3,3,512,32]{3,4,2,1,0:T(8,128)(2,1)S(1)} copy-done((bf16[3,3,3,512,32]{3,4,2,1,0:T(8,128)(2,1)S(1)}, bf16[3,3,3,512,32]{3,4,2,1,0:T(8,128)(2,1)}, u32[]{:S(2)}) %copy-start.3) | copy-done | bytes 884760
  54.7 0.7 shard_map.97
  55.4 14.2 %all_to_all.20 = bf16[16,32,128]{2,1,0:T(8,128)(2,1)S(1)} all-to-all(bf16[16,32,128]{2,1,0:T(8,128)(2,1)S(1)} %shard_map.97), channel_id=1, replica_groups=mesh['rep'=2,'z'=4,'r'=4] {'z','r'}, dimensions={0} | all-to-all | bytes 262144 | tf_op jit(solution)/shard_map/all_to_all | solution.py:349
  69.6 2.9 %shard_map.100 = bf16[512,256]{1,0:T(8,128)(2,1)S(1)} custom-call(s32[3]{0:T(128)S(1)} %pad_add_fusion.place.rank_ref, bf16[512,128]{1,0:T(8,128)(2,1)S(1)} %bitcast.33, bf16[512,512]{1,0:T(8,128)(2,1)S(1)} %shard_map.96.refs_2_.rise, bf16[16,256]{1,0:T(8,128)(2,1)S(1)} %collective-permute-done.5.refs_0_.near_swap, ...), custom_call_target="tpu_custom_call" | custom-call | flops 905969664 | bytes 2506764 | tf_op jit(solution)/shard_map/pallas_call | solution.py:18
  72.5 8.6 %all_to_all.21.partials = bf16[4,128,256]{2,1,0:T(8,128)(2,1)S(1)} all-to-all(bf16[4,128,256]{2,1,0:T(8,128)(2,1)S(1)} %bitcast.32), channel_id=1, replica_groups=mesh['rep'=2,'z'=4,'r'=4] {'r'}, dimensions={0} | all-to-all | bytes 524288 | tf_op jit(solution)/shard_map/all_to_all | solution.py:349
  81.1 1.1 %shard_map.101 = bf16[1024,128]{1,0:T(8,128)(2,1)} custom-call(bf16[4,128,256]{2,1,0:T(8,128)(2,1)S(1)} %all_to_all.21.partials, bf16[8,256,128]{2,1,0:T(8,128)(2,1)S(1)} %bitcast.29), custom_call_target="tpu_custom_call" | custom-call | flops 67108864 | bytes 786432 | tf_op jit(solution)/shard_map/pallas_call | solution.py:18
  (28 shorter events, 0.2 us)
Async XLA Ops:
  6.5 37.5 %all-gather.3.cloned.1.call-start = ((), (), s32[]{:S(2)}) async-start(), calls=%async_computation.4 | async-start | bytes 1351680 | tf_op jit(solution)/shard_map/all_gather | solution.py:396
  6.5 0.9 %copy-start.9 = (bf16[4,16,16,128]{3,2,1,0:T(8,128)(2,1)S(1)}, bf16[4,16,16,128]{3,2,1,0:T(8,128)(2,1)}, u32[]{:S(2)}) copy-start(bf16[4,16,16,128]{3,2,1,0:T(8,128)(2,1)} %volume.1) | copy-start | bytes 786436
  7.5 1.0 %copy-start.5 = (bf16[3,3,3,32,256]{4,3,2,1,0:T(8,128)(2,1)S(1)}, bf16[3,3,3,32,256]{4,3,2,1,0:T(8,128)(2,1)}, u32[]{:S(2)}) copy-start(bf16[3,3,3,32,256]{4,3,2,1,0:T(8,128)(2,1)} %param.15) | copy-start | bytes 1327108
  7.5 7.0 %copy-start.8 = (bf16[3,3,3,128,128]{4,3,2,1,0:T(8,128)(2,1)S(1)}, bf16[3,3,3,128,128]{4,3,2,1,0:T(8,128)(2,1)}, u32[]{:S(2)}) copy-start(bf16[3,3,3,128,128]{4,3,2,1,0:T(8,128)(2,1)} %param.10) | copy-start | bytes 2654212
  9.8 9.3 %collective-permute-start = (bf16[3,16,16,128]{3,2,1,0:T(8,128)(2,1)S(1)}, bf16[3,16,16,128]{3,2,1,0:T(8,128)(2,1)S(1)}, u32[]{:S(2)}, u32[]{:S(2)}) collective-permute-start(bf16[3,16,16,128]{3,2,1,0:T(8,128)(2,1)S(1)} %get-tuple-element.15), channel_id=1, source_target_pairs={{1,2},{3,4},{5,6},{7,8},{9,10},{11,12},{13,14},{2,1},{4,3},{6,5},{... | collective-permute-start | bytes 589832 | tf_op jit(solution)/shard_map/ppermute | solution.py:399
  14.4 4.7 %collective-permute-start.1 = (bf16[3,16,16,128]{3,2,1,0:T(8,128)(2,1)S(1)}, bf16[3,16,16,128]{3,2,1,0:T(8,128)(2,1)S(1)}, u32[]{:S(2)}, u32[]{:S(2)}) collective-permute-start(bf16[3,16,16,128]{3,2,1,0:T(8,128)(2,1)S(1)} %get-tuple-element.16), channel_id=1, source_target_pairs={{0,1},{1,0},{2,3},{3,2},{4,5},{5,4},{6,7},{7,6},{8,9},{9,8},{10,11... | collective-permute-start | bytes 589832 | tf_op jit(solution)/shard_map/ppermute | solution.py:400
  14.5 4.5 %copy-start.7 = (bf16[3,3,3,128,256]{4,3,2,1,0:T(8,128)(2,1)S(1)}, bf16[3,3,3,128,256]{4,3,2,1,0:T(8,128)(2,1)}, u32[]{:S(2)}) copy-start(bf16[3,3,3,128,256]{4,3,2,1,0:T(8,128)(2,1)} %param.11) | copy-start | bytes 5308420
  14.5 4.5 %copy-start.10 = (bf16[256,256]{1,0:T(8,128)(2,1)S(1)}, bf16[256,256]{1,0:T(8,128)(2,1)}, u32[]{:S(2)}) copy-start(bf16[256,256]{1,0:T(8,128)(2,1)} %constant.36.clone.order) | copy-start | bytes 393220
  19.1 18.8 %copy-start.6 = (bf16[3,3,3,256,32]{3,4,2,1,0:T(8,128)(2,1)S(1)}, bf16[3,3,3,256,32]{3,4,2,1,0:T(8,128)(2,1)}, u32[]{:S(2)}) copy-start(bf16[3,3,3,256,32]{3,4,2,1,0:T(8,128)(2,1)} %param.12) | copy-start | bytes 1327108
  22.4 15.5 %all-to-all-start = ((bf16[16,16,256]{2,1,0:T(8,128)(2,1)}), bf16[16,16,256]{2,1,0:T(8,128)(2,1)S(1)}, u32[]{:S(2)}, u32[]{:S(2)}) async-start(bf16[16,16,256]{2,1,0:T(8,128)(2,1)} %get-tuple-element.18), calls=%async_computation | async-start | bytes 262144 | tf_op jit(solution)/shard_map/all_to_all | solution.py:349
  28.6 22.1 %copy-start = (bf16[2,2,2,512,256]{4,3,2,1,0:T(8,128)(2,1)S(1)}, bf16[2,2,2,512,256]{4,3,2,1,0:T(8,128)(2,1)}, u32[]{:S(2)}) copy-start(bf16[2,2,2,512,256]{4,3,2,1,0:T(8,128)(2,1)} %param.14) | copy-start | bytes 6291460
  28.6 2.2 %collective-permute-start.2 = (bf16[32,256]{1,0:T(8,128)(2,1)S(1)}, bf16[32,256]{1,0:T(8,128)(2,1)S(1)}, u32[]{:S(2)}, u32[]{:S(2)}) collective-permute-start(bf16[32,256]{1,0:T(8,128)(2,1)S(1)} %get-tuple-element.19), channel_id=1, source_target_pairs={{0,1},{1,0},{2,3},{3,2},{4,5},{5,4},{6,7},{7,6},{8,9},{9,8},{10,11... | collective-permute-start | bytes 49160 | tf_op jit(solution)/shard_map/ppermute | solution.py:433
  28.8 3.2 %collective-permute-start.3 = (bf16[32,256]{1,0:T(8,128)(2,1)S(1)}, bf16[32,256]{1,0:T(8,128)(2,1)S(1)}, u32[]{:S(2)}, u32[]{:S(2)}) collective-permute-start(bf16[32,256]{1,0:T(8,128)(2,1)S(1)} %get-tuple-element.20), channel_id=1, source_target_pairs={{0,2},{1,3},{2,0},{3,1},{4,6},{5,7},{6,4},{7,5},{8,10},{9,11},{10,... | collective-permute-start | bytes 49160 | tf_op jit(solution)/shard_map/ppermute | solution.py:433
  30.4 3.6 %collective-permute-start.4 = (bf16[32,256]{1,0:T(8,128)(2,1)S(1)}, bf16[32,256]{1,0:T(8,128)(2,1)S(1)}, u32[]{:S(2)}, u32[]{:S(2)}) collective-permute-start(bf16[32,256]{1,0:T(8,128)(2,1)S(1)} %get-tuple-element.21), channel_id=1, source_target_pairs={{0,3},{1,2},{2,1},{3,0},{4,7},{5,6},{6,5},{7,4},{8,11},{9,10},{10,... | collective-permute-start | bytes 49160 | tf_op jit(solution)/shard_map/ppermute | solution.py:433
  39.2 14.3 %all-to-all-start.1 = ((bf16[16,32,256]{2,1,0:T(8,128)(2,1)}), bf16[16,32,256]{2,1,0:T(8,128)(2,1)S(1)}, u32[]{:S(2)}, u32[]{:S(2)}) async-start(bf16[16,32,256]{2,1,0:T(8,128)(2,1)} %shard_map.94._), calls=%async_computation.1 | async-start | bytes 524288 | tf_op jit(solution)/shard_map/all_to_all | solution.py:349
  44.1 1.2 %copy-start.1 = (bf16[2112,256]{1,0:T(8,128)(2,1)S(1)}, bf16[2112,256]{1,0:T(8,128)(2,1)}, u32[]{:S(2)}) copy-start(bf16[2112,256]{1,0:T(8,128)(2,1)} %all-gather.3.cloned.1.call-done) | copy-start | bytes 3244036
  46.7 22.9 %collective-permute-start.7 = (bf16[4,336,256]{2,1,0:T(8,128)(2,1)}, bf16[4,336,256]{2,1,0:T(8,128)(2,1)}, u32[]{:S(2)}, u32[]{:S(2)}) collective-permute-start(bf16[4,336,256]{2,1,0:T(8,128)(2,1)} %shard_map.99), channel_id=1, source_target_pairs={{0,16},{16,0},{1,17},{17,1},{2,18},{18,2},{3,19},{19,3},{4,20},{20... | collective-permute-start | bytes 2064392 | tf_op jit(solution)/shard_map/ppermute | solution.py:462
  48.6 3.4 %collective-permute-start.5 = (bf16[16,256]{1,0:T(8,128)(2,1)S(1)}, bf16[16,256]{1,0:T(8,128)(2,1)S(1)}, u32[]{:S(2)}, u32[]{:S(2)}) collective-permute-start(bf16[16,256]{1,0:T(8,128)(2,1)S(1)} %get-tuple-element.23), channel_id=1, source_target_pairs={{0,4},{8,12},{4,0},{12,8},{1,5},{9,13},{5,1},{13,9},{2,6},{10,14},... | collective-permute-start | bytes 24584 | tf_op jit(solution)/shard_map/ppermute | solution.py:479
  50.0 2.0 %collective-permute-start.6 = (bf16[16,256]{1,0:T(8,128)(2,1)S(1)}, bf16[16,256]{1,0:T(8,128)(2,1)S(1)}, u32[]{:S(2)}, u32[]{:S(2)}) collective-permute-start(bf16[16,256]{1,0:T(8,128)(2,1)S(1)} %get-tuple-element.24), channel_id=1, source_target_pairs={{4,8},{8,4},{5,9},{9,5},{6,10},{10,6},{7,11},{11,7},{20,24},{24,20... | collective-permute-start | bytes 24584 | tf_op jit(solution)/shard_map/ppermute | solution.py:480
  52.0 17.6 %copy-start.2 = (bf16[2112,256]{1,0:T(8,128)(2,1)S(1)}, bf16[2112,256]{1,0:T(8,128)(2,1)}, u32[]{:S(2)}) copy-start(bf16[2112,256]{1,0:T(8,128)(2,1)} %all-gather.3.cloned.1.call-done) | copy-start | bytes 3244036
  53.5 1.2 %copy-start.3 = (bf16[3,3,3,512,32]{3,4,2,1,0:T(8,128)(2,1)S(1)}, bf16[3,3,3,512,32]{3,4,2,1,0:T(8,128)(2,1)}, u32[]{:S(2)}) copy-start(bf16[3,3,3,512,32]{3,4,2,1,0:T(8,128)(2,1)} %param.13) | copy-start | bytes 2654212
  69.6 11.5 %copy-start.4 = (bf16[2,2,2,256,128]{4,3,2,1,0:T(8,128)(2,1)S(1)}, bf16[2,2,2,256,128]{4,3,2,1,0:T(8,128)(2,1)}, u32[]{:S(2)}) copy-start(bf16[2,2,2,256,128]{4,3,2,1,0:T(8,128)(2,1)} %param.16) | copy-start | bytes 1572868
Sparse Core Ops, SparseCore 0:
  9.9 33.9 all-gather.2

commit v8 on v7

--- a/solution.py
+++ b/solution.py
@@ -12,16 +12,14 @@
 MIB = 1024 * 1024
 
 
-def call(kernel, outs, scratch, args, flops, vmem_mib, scalars=0, unread=0, far_outs=0):
+def call(kernel, outs, scratch, args, flops, vmem_mib, scalars=0, unread=0):
     spaces = [pltpu.SMEM] * scalars + [pltpu.VMEM] * (len(args) - scalars - unread)
     spaces += [pl.ANY] * unread
     return pl.pallas_call(
         kernel,
         out_shape=outs,
         in_specs=[pl.BlockSpec(memory_space=space) for space in spaces],
-        out_specs=jax.tree.map(
-            lambda _: pl.BlockSpec(memory_space=pl.ANY if far_outs else pltpu.VMEM), outs
-        ),
+        out_specs=jax.tree.map(lambda _: pl.BlockSpec(memory_space=pltpu.VMEM), outs),
         scratch_shapes=scratch,
         compiler_params=pltpu.CompilerParams(vmem_limit_bytes=vmem_mib * MIB),
         cost_estimate=pl.CostEstimate(
@@ -86,22 +84,6 @@
     whole[...] = volume[...]
 
 
-def share_stage(place, decode, _, out, done):
-    step, rows = decode.shape[0] - out.shape[0], out.shape[0]
-    at = pl.multiple_of(place[1] * step, 16)
-    copy = pltpu.make_async_copy(decode.at[pl.ds(at, rows)], out, done)
-    copy.start()
-    copy.wait()
-
-
-def pick_stage(place, line, _, out, done):
-    rows = out.shape[1]
-    at = pl.multiple_of(place[1] * (line.shape[1] - rows), 16)
-    copy = pltpu.make_async_copy(line.at[:, pl.ds(at, rows)], out, done)
-    copy.start()
-    copy.wait()
-
-
 def own_stage(volume, weights, out, shifted):
     for s in range(4):
         shift_slice(shifted, s, volume[s])
@@ -113,7 +95,7 @@
     out[3, :, 128:] = jnp.zeros((256, 128), jnp.float32)
 
 
-def stem_stage(ends, off_chip, on_chip, own, weights, second, order, *refs):
+def stem_stage(ends, off_chip, on_chip, own, weights, second, order, _, *refs):
     pooled_out, skip_outs = refs[0], refs[1 : 1 + GROUP]
     shifted, halves, framed, patches, quarters, blocks = refs[1 + GROUP :]
     for s in range(3):
@@ -299,18 +281,22 @@
         joined = framed[s, 1:9, 8:16, :].reshape(64, 128)
         framed[s, 1:9, 8:16, :] = jnp.where(upper, skip, joined).reshape(8, 8, 128)
     fill_patches(framed, patches, 10)
+    def rows_at(rep, z, row):
+        if rep == 0 and row >= 528:
+            return decode[1][z, row - 528 : row - 512, :]
+        if rep == 1 and row < 336:
+            return decode[1][z, row : row + 16, :]
+        if rep == 1 and row >= 528:
+            row -= 528
+        return decode[0][z, row : row + 16, :]
+
     def multiply(rep):
-        if rep == 0:
-            parts = decode
-        else:
-            parts = decode[::-1]
-        split = parts[0].shape[1]
         count = decode[0].shape[0]
         step = 128 // count
         partial = None
         for a in range(3):
             right = [
-                parts[0][z, row : row + 16, :] if row < split else parts[1][z, row - split : row - split + 16, :]
+                rows_at(rep, z, row)
                 for tap in range(9 * a, 9 * a + 9)
                 for z in range(count)
                 for row in range(tap * step, (tap + 1) * step, 16)
@@ -320,7 +306,7 @@
         out[...] = partial.astype(jnp.bfloat16)
 
     if len(decode) == 1:
-        multiply(0)
+        multiply(None)
     else:
         pl.when(place[1] == 0)(lambda: multiply(0))
         pl.when(place[1] == 1)(lambda: multiply(1))
@@ -382,17 +368,8 @@
     decode_block = decode_kernel.reshape(27 * chans, 256)
     shared = lax.axis_size("rep") == 2 and chans == 32
     if shared:
-        decode_block = call(
-            share_stage,
-            bf16((528, 256)),
-            [pltpu.SemaphoreType.DMA],
-            (marks, decode_block, volume),
-            0,
-            16,
-            scalars=1,
-            unread=2,
-            far_outs=1,
-        )
+        own_rows = lax.dynamic_slice_in_dim(decode_block, 528 * rep, 336, axis=0)
+        decode_block = jnp.concatenate([own_rows, decode_block[336:528]], axis=0)
     line = lax.all_gather(decode_block, "z", axis=0)
 
     pairs = [(i, i + 1) for i in range(1, n - 1, 2)]
@@ -412,6 +389,15 @@
     source = (lane // 64 + GROUP * (lane % 64 // chans)) * chans + lane % chans
     order = jnp.asarray(np.arange(256)[:, None] == source[None, :], jnp.bfloat16)
     ends = jnp.stack([place, n - 1 - place, odd, rank]).astype(jnp.int32)
+    rise_part = call(
+        lambda rank_ref, *refs: rise_stage(rank_ref, chans, *refs),
+        bf16((n * chans, 512)),
+        [],
+        (marks, rise_kernel.reshape(8, n * chans, 256)),
+        2 * 8 * n * chans * 256 * 64,
+        16,
+        scalars=1,
+    )
     pooled_two, *skips = call(
         stem_stage,
         (bf16((n, 16, 256)),) + (bf16((32, 256)),) * GROUP,
@@ -423,10 +409,11 @@
             pltpu.VMEM((2, 32, 128), jnp.float32),
             pltpu.VMEM((GROUP, 32, 256), jnp.bfloat16),
         ],
-        (ends, off_chip, on_chip, own, taps, second_kernel.reshape(3, 1152, 256), order),
+        (ends, off_chip, on_chip, own, taps, second_kernel.reshape(3, 1152, 256), order, rise_part),
         2 * 1024 * 2304 * 256,
         24,
         scalars=1,
+        unread=1,
     )
     pooled_whole = exchange(pooled_two, ALL)
     near = [skips[0]] + [
@@ -448,18 +435,7 @@
         unread=GROUP - 1,
     )
     if shared:
-        piece = call(
-            pick_stage,
-            bf16((planes, 336, 256)),
-            [pltpu.SemaphoreType.DMA],
-            (marks, line, deep),
-            0,
-            16,
-            scalars=1,
-            unread=2,
-            far_outs=1,
-        )
-        weights = (line, lax.ppermute(piece, "rep", [(0, 1), (1, 0)]))
+        weights = (line, lax.ppermute(line[:, :336], "rep", [(0, 1), (1, 0)]))
     elif chans % 16:
         weights = line.reshape(planes, 27, chans, 256).transpose(1, 0, 2, 3)
         weights = (weights.reshape(1, 27 * 128, 256),)
@@ -478,15 +454,6 @@
     far_pairs = [(p, p + 1) for p in range(1, planes - 1, 2)]
     near_swap = lax.ppermute(swaps[0], "z", near_pairs + [(j, i) for i, j in near_pairs])
     far_swap = lax.ppermute(swaps[1], "z", far_pairs + [(j, i) for i, j in far_pairs])
-    rise_part = call(
-        lambda rank_ref, *refs: rise_stage(rank_ref, chans, *refs),
-        bf16((n * chans, 512)),
-        [],
-        (marks, rise_kernel.reshape(8, n * chans, 256)),
-        2 * 8 * n * chans * 256 * 64,
-        16,
-        scalars=1,
-    )
     deep_whole = exchange(deep, ALL).reshape(n * chans, voxels)
 
     deeper = call(
@@ -498,11 +465,10 @@
             deeper_kernel.transpose(0, 1, 2, 4, 3).reshape(27 * chans, n * chans),
             near_swap,
             far_swap,
-            rise_part,
         ),
         2 * 27 * chans * n * chans * voxels,
         16,
-        unread=3,
+        unread=2,
     )
     deeper_near = exchange(deeper, ALL).reshape(n * chans, 128)
 

time: 90.5 us -> 91.4 us (level)
  Pallas kernels: 15.4 us -> 14 us
  local copies, waits for them, and re-layouts: 4.21 us -> 5.61 us
    slice x0 -> x2, local copies, waits for them, and re-layouts: none -> 3 us  [the longest x1 2.1 us: body(): weights = (line, lax.ppermute(line[:, :336], 'rep', [(0, 1), (1, 0)]))]
    unnamed x22, local copies, waits for them, and re-layouts: 4.21 us -> 1.69 us
    pallas_call x11 -> x9, Pallas kernels: 15.4 us -> 14 us  [call(): pl.pallas_call(kernel, out_shape=outs, in_specs=[pl.BlockSpec(memory_spac...]
    ppermute x1, waiting for transfers between devices: 3.11 us -> 1.98 us  [body(): off_chip = lax.ppermute(off_chip, ALL, pairs + [(j, i) for i, j in pairs])]
    ppermute x1, waiting for transfers between devices: 0.01 us -> 1.12 us  [body(): lax.ppermute(swaps[0], 'z', near_pairs + [(j, i) for i, j in near_pairs])]
    dynamic_slice x0 -> x1, local copies, waits for them, and re-layouts: none -> 0.93 us  [body(): own_rows = lax.dynamic_slice_in_dim(decode_block, 528 * rep, 336, axis=0)]
  transfers between devices with their start and end apart: 11 -> 11, of which waited for: 5 -> 6; matrix products, arithmetic and copies ran while one was open for 0% -> 3% of each run, Pallas kernels for 11% -> 11%
where the time goes in v8:
time: 91.4 us; the launch traced here: 89.9 us
  blocking collectives  22.1 us (24%)
  starting transfers between devices  21.2 us (23%)
  Pallas kernels  14 us (15%)
  between operations  13.5 us (15%)
  waiting for transfers between devices  12.6 us (14%)
  local copies, waits for them, and re-layouts  5.61 us (6%)
    all_to_all x2, blocking collectives, exchange(): lax.all_to_all(payload, axis, split_axis=0, concat_axis=0, tiled=True)  22.1 us
    pallas_call x9, Pallas kernels, call(): pl.pallas_call(kernel, out_shape=outs, in_specs=[pl.BlockSpec(memory_spac...  14 us
    all_to_all x2, starting transfers between devices, exchange(): lax.all_to_all(payload, axis, split_axis=0, concat_axis=0, tiled=True)  11.1 us
    all_to_all x2, waiting for transfers between devices, exchange(): lax.all_to_all(payload, axis, split_axis=0, concat_axis=0, tiled=True)  6.25 us
    ppermute x1, starting transfers between devices, body(): off_chip = lax.ppermute(off_chip, ALL, pairs + [(j, i) for i, j in pairs])  4.66 us
    ppermute x3, waiting for transfers between devices, body(): lax.ppermute(skips[k], 'r', [(r, r ^ k) for r in range(GROUP)])  3.24 us
    ppermute x3, starting transfers between devices, body(): lax.ppermute(skips[k], 'r', [(r, r ^ k) for r in range(GROUP)])  2.14 us
    slice x1, local copies, waits for them, and re-layouts, body(): weights = (line, lax.ppermute(line[:, :336], 'rep', [(0, 1), (1, 0)]))  2.1 us
  transfers between devices with their start and end apart: 11, of which 6 were waited for; matrix products, arithmetic and copies ran while one was open for 3% of the time, Pallas kernels for 11%

profile of v8, /device:TPU:1, one launch (start us, length us, event | category | flops | bytes accessed | tf_op | source)
XLA Modules:
  0.0 89.9 jit_solution(2941054446937397210)
XLA Ops:
  6.5 0.9 %slice.8 = bf16[192,256]{1,0:T(8,128)(2,1)S(1)} slice(bf16[864,256]{1,0:T(8,128)(2,1)} %bitcast.36), slice={[336:528], [0:256]} | slice | bytes 196608 | tf_op jit(solution)/shard_map/slice | solution.py:372
  7.4 0.9 %constant_dynamic-slice_fusion = bf16[336,256]{1,0:T(8,128)(2,1)S(1)} fusion(bf16[864,256]{1,0:T(8,128)(2,1)} %bitcast.37, s32[]{:T(128)S(6)} %select_n.16), kind=kLoop, calls=%fused_computation.3 | loop fusion | bytes 344068 | tf_op jit(solution)/shard_map/dynamic_slice | solution.py:371
  8.4 0.7 pad_maximum_fusion
  9.2 0.9 %copy-done.8 = bf16[4,16,16,128]{3,2,1,0:T(8,128)(2,1)S(1)} copy-done((bf16[4,16,16,128]{3,2,1,0:T(8,128)(2,1)S(1)}, bf16[4,16,16,128]{3,2,1,0:T(8,128)(2,1)}, u32[]{:S(2)}) %copy-start.8) | copy-done | bytes 262168
  10.1 0.8 shard_map.91
  10.9 0.7 copy-done.9
  11.6 4.7 %collective-permute-start = (bf16[3,16,16,128]{3,2,1,0:T(8,128)(2,1)}, bf16[3,16,16,128]{3,2,1,0:T(8,128)(2,1)}, u32[]{:S(2)}, u32[]{:S(2)}) collective-permute-start(bf16[3,16,16,128]{3,2,1,0:T(8,128)(2,1)} %get-tuple-element.15), channel_id=1, source_target_pairs={{1,2},{3,4},{5,6},{7,8},{9,10},{11,12},{13,14},{2,1},{4,3},{6,5},{... | collective-permute-start | bytes 589832 | tf_op jit(solution)/shard_map/ppermute | solution.py:376
  16.5 1.3 %shard_map.93._.rise = bf16[512,512]{1,0:T(8,128)(2,1)S(1)} custom-call(s32[3]{0:T(128)S(1)} %pad_add_fusion.rank_ref.place, bf16[8,512,256]{2,1,0:T(8,128)(2,1)S(1)} %bitcast.23), custom_call_target="tpu_custom_call" | custom-call | flops 134217728 | bytes 2097164 | tf_op jit(solution)/shard_map/pallas_call | solution.py:18
  17.9 1.4 %shard_map.92.own = f32[4,256,256]{2,1,0:T(8,128)S(1)} custom-call(bf16[4,16,16,128]{3,2,1,0:T(8,128)(2,1)S(1)} %copy-done.10, bf16[3,1152,128]{2,1,0:T(8,128)(2,1)S(1)} %bitcast.26), custom_call_target="tpu_custom_call" | custom-call | flops 1207959552 | bytes 1146880 | tf_op jit(solution)/shard_map/pallas_call | solution.py:18
  19.3 2.0 %collective-permute-done.off_chip = bf16[3,16,16,128]{3,2,1,0:T(8,128)(2,1)} collective-permute-done((bf16[3,16,16,128]{3,2,1,0:T(8,128)(2,1)}, bf16[3,16,16,128]{3,2,1,0:T(8,128)(2,1)}, u32[]{:S(2)}, u32[]{:S(2)}) %collective-permute-start) | collective-permute-done | bytes 196640 | tf_op jit(solution)/shard_map/ppermute | solution.py:376
  21.3 3.9 %shard_map.94 = (bf16[16,16,256]{2,1,0:T(8,128)(2,1)}, bf16[32,256]{1,0:T(8,128)(2,1)S(1)}, bf16[32,256]{1,0:T(8,128)(2,1)S(1)}, bf16[32,256]{1,0:T(8,128)(2,1)S(1)}, bf16[32,256]{1,0:T(8,128)(2,1)S(1)}) custom-call(s32[4]{0:T(128)S(1)} %pad_add_fusion.1.ends, bf16[3,16,16,128]{3,2,1,0:T(8,128)(2,1)} %collective-permute-done.off_chip, ...), custom_call_target="tpu_custom_call" | custom-call | flops 1207959552 | bytes 4227088 | tf_op jit(solution)/shard_map/pallas_call | solution.py:18
  25.2 6.3 %all-to-all-start = ((bf16[16,16,256]{2,1,0:T(8,128)(2,1)}), bf16[16,16,256]{2,1,0:T(8,128)(2,1)S(1)}, u32[]{:S(2)}, u32[]{:S(2)}) async-start(bf16[16,16,256]{2,1,0:T(8,128)(2,1)} %get-tuple-element.18), calls=%async_computation | async-start | bytes 262144 | tf_op jit(solution)/shard_map/all_to_all | solution.py:335
  31.5 0.2 collective-permute-start.2
  31.7 1.6 %collective-permute-start.3 = (bf16[32,256]{1,0:T(8,128)(2,1)S(1)}, bf16[32,256]{1,0:T(8,128)(2,1)S(1)}, u32[]{:S(2)}, u32[]{:S(2)}) collective-permute-start(bf16[32,256]{1,0:T(8,128)(2,1)S(1)} %get-tuple-element.20), channel_id=1, source_target_pairs={{0,2},{1,3},{2,0},{3,1},{4,6},{5,7},{6,4},{7,5},{8,10},{9,11},{10,... | collective-permute-start | bytes 49160 | tf_op jit(solution)/shard_map/ppermute | solution.py:420
  33.3 0.4 collective-permute-start.4
  33.7 1.1 %collective-permute-done.3.refs_1_.refs_2_ = bf16[32,256]{1,0:T(8,128)(2,1)S(1)} collective-permute-done((bf16[32,256]{1,0:T(8,128)(2,1)S(1)}, bf16[32,256]{1,0:T(8,128)(2,1)S(1)}, u32[]{:S(2)}, u32[]{:S(2)}) %collective-permute-start.3) | collective-permute-done | bytes 16416 | tf_op jit(solution)/shard_map/ppermute | solution.py:420
  34.8 2.1 %collective-permute-done.4.refs_2_.refs_3_ = bf16[32,256]{1,0:T(8,128)(2,1)S(1)} collective-permute-done((bf16[32,256]{1,0:T(8,128)(2,1)S(1)}, bf16[32,256]{1,0:T(8,128)(2,1)S(1)}, u32[]{:S(2)}, u32[]{:S(2)}) %collective-permute-start.4) | collective-permute-done | bytes 16416 | tf_op jit(solution)/shard_map/ppermute | solution.py:420
  36.9 3.9 %all-to-all-done = bf16[16,16,256]{2,1,0:T(8,128)(2,1)S(1)} async-done(((bf16[16,16,256]{2,1,0:T(8,128)(2,1)}), bf16[16,16,256]{2,1,0:T(8,128)(2,1)S(1)}, u32[]{:S(2)}, u32[]{:S(2)}) %all-to-all-start) | async-done | bytes 131104 | tf_op jit(solution)/shard_map/all_to_all | solution.py:335
  40.8 1.3 %shard_map.95 = bf16[16,32,256]{2,1,0:T(8,128)(2,1)} custom-call(bf16[256,256]{1,0:T(8,128)(2,1)S(1)} %bitcast.29, bf16[864,256]{1,0:T(8,128)(2,1)S(1)} %bitcast.31, bf16[32,256]{1,0:T(8,128)(2,1)S(1)} %collective-permute-done.2.refs_0_.refs_1_, bf16[32,256]{1,0:T(8,128)(2,1)S(1)} %collective-permute-done.3.refs_1_.refs_2_, ...), custom_call_target="tpu_custom_call" | custom-call | flops 113246208 | bytes 573440 | tf_op jit(solution)/shard_map/pallas_call | solution.py:18
  42.0 4.7 %all-to-all-start.1 = ((bf16[16,32,256]{2,1,0:T(8,128)(2,1)}), bf16[16,32,256]{2,1,0:T(8,128)(2,1)S(1)}, u32[]{:S(2)}, u32[]{:S(2)}) async-start(bf16[16,32,256]{2,1,0:T(8,128)(2,1)} %shard_map.95), calls=%async_computation.1 | async-start | bytes 524288 | tf_op jit(solution)/shard_map/all_to_all | solution.py:335
  46.8 2.1 %slice.9 = bf16[4,336,256]{2,1,0:T(8,128)(2,1)} slice(bf16[4,528,256]{2,1,0:T(8,128)(2,1)} %bitcast.32), slice={[0:4], [0:336], [0:256]} | slice | bytes 1376256 | tf_op jit(solution)/shard_map/slice | solution.py:438
  48.9 1.2 %collective-permute-start.7 = (bf16[4,336,256]{2,1,0:T(8,128)(2,1)}, bf16[4,336,256]{2,1,0:T(8,128)(2,1)}, u32[]{:S(2)}, u32[]{:S(2)}) collective-permute-start(bf16[4,336,256]{2,1,0:T(8,128)(2,1)} %slice.9), channel_id=1, source_target_pairs={{0,16},{16,0},{1,17},{17,1},{2,18},{18,2},{3,19},{19,3},{4,20},{20... | collective-permute-start | bytes 2064392 | tf_op jit(solution)/shard_map/ppermute | solution.py:438
  50.1 0.6 shard_map.96
  50.7 1.4 %collective-permute-start.5 = (bf16[16,256]{1,0:T(8,128)(2,1)S(1)}, bf16[16,256]{1,0:T(8,128)(2,1)S(1)}, u32[]{:S(2)}, u32[]{:S(2)}) collective-permute-start(bf16[16,256]{1,0:T(8,128)(2,1)S(1)} %get-tuple-element.23), channel_id=1, source_target_pairs={{0,4},{8,12},{4,0},{12,8},{1,5},{9,13},{5,1},{13,9},{2,6},{10,14},... | collective-permute-start | bytes 24584 | tf_op jit(solution)/shard_map/ppermute | solution.py:455
  52.1 0.6 collective-permute-start.6
  52.8 1.1 %collective-permute-done.5.refs_0_.near_swap = bf16[16,256]{1,0:T(8,128)(2,1)S(1)} collective-permute-done((bf16[16,256]{1,0:T(8,128)(2,1)S(1)}, bf16[16,256]{1,0:T(8,128)(2,1)S(1)}, u32[]{:S(2)}, u32[]{:S(2)}) %collective-permute-start.5) | collective-permute-done | bytes 8224 | tf_op jit(solution)/shard_map/ppermute | solution.py:455
  53.9 2.4 %all-to-all-done.1 = bf16[16,32,256]{2,1,0:T(8,128)(2,1)S(1)} async-done(((bf16[16,32,256]{2,1,0:T(8,128)(2,1)}), bf16[16,32,256]{2,1,0:T(8,128)(2,1)S(1)}, u32[]{:S(2)}, u32[]{:S(2)}) %all-to-all-start.1) | async-done | bytes 262176 | tf_op jit(solution)/shard_map/all_to_all | solution.py:335
  56.3 0.7 shard_map.97
  57.0 13.5 %all_to_all.20 = bf16[16,32,128]{2,1,0:T(8,128)(2,1)S(1)} all-to-all(bf16[16,32,128]{2,1,0:T(8,128)(2,1)S(1)} %shard_map.97), channel_id=1, replica_groups=mesh['rep'=2,'z'=4,'r'=4] {'z','r'}, dimensions={0} | all-to-all | bytes 262144 | tf_op jit(solution)/shard_map/all_to_all | solution.py:335
  70.5 2.9 %shard_map.98 = bf16[512,256]{1,0:T(8,128)(2,1)S(1)} custom-call(s32[3]{0:T(128)S(1)} %pad_add_fusion.rank_ref.place, bf16[512,128]{1,0:T(8,128)(2,1)S(1)} %bitcast.35, bf16[512,512]{1,0:T(8,128)(2,1)S(1)} %shard_map.93._.rise, bf16[16,256]{1,0:T(8,128)(2,1)S(1)} %collective-permute-done.5.refs_0_.near_swap, ...), custom_call_target="tpu_custom_call" | custom-call | flops 905969664 | bytes 2506764 | tf_op jit(solution)/shard_map/pallas_call | solution.py:18
  73.4 8.6 %all_to_all.21.partials = bf16[4,128,256]{2,1,0:T(8,128)(2,1)S(1)} all-to-all(bf16[4,128,256]{2,1,0:T(8,128)(2,1)S(1)} %bitcast.34), channel_id=1, replica_groups=mesh['rep'=2,'z'=4,'r'=4] {'r'}, dimensions={0} | all-to-all | bytes 524288 | tf_op jit(solution)/shard_map/all_to_all | solution.py:335
  82.0 1.1 %shard_map.99 = bf16[1024,128]{1,0:T(8,128)(2,1)} custom-call(bf16[4,128,256]{2,1,0:T(8,128)(2,1)S(1)} %all_to_all.21.partials, bf16[8,256,128]{2,1,0:T(8,128)(2,1)S(1)} %bitcast.30), custom_call_target="tpu_custom_call" | custom-call | flops 67108864 | bytes 786432 | tf_op jit(solution)/shard_map/pallas_call | solution.py:18
  (30 shorter events, 0.3 us)
Async XLA Ops:
  6.5 40.2 %all-gather.3.cloned.1.call-start = ((), (), s32[]{:S(2)}) async-start(), calls=%async_computation.4 | async-start | bytes 1351680 | tf_op jit(solution)/shard_map/all_gather | solution.py:373
  9.1 1.0 %copy-start.8 = (bf16[4,16,16,128]{3,2,1,0:T(8,128)(2,1)S(1)}, bf16[4,16,16,128]{3,2,1,0:T(8,128)(2,1)}, u32[]{:S(2)}) copy-start(bf16[4,16,16,128]{3,2,1,0:T(8,128)(2,1)} %volume.1) | copy-start | bytes 786436
  10.1 6.4 %copy-start = (bf16[2,2,2,512,256]{4,3,2,1,0:T(8,128)(2,1)S(1)}, bf16[2,2,2,512,256]{4,3,2,1,0:T(8,128)(2,1)}, u32[]{:S(2)}) copy-start(bf16[2,2,2,512,256]{4,3,2,1,0:T(8,128)(2,1)} %param.14) | copy-start | bytes 6291460
  10.9 0.7 copy-start.9
  11.6 6.3 %copy-start.2 = (bf16[3,3,3,128,128]{4,3,2,1,0:T(8,128)(2,1)S(1)}, bf16[3,3,3,128,128]{4,3,2,1,0:T(8,128)(2,1)}, u32[]{:S(2)}) copy-start(bf16[3,3,3,128,128]{4,3,2,1,0:T(8,128)(2,1)} %param.10) | copy-start | bytes 2654212
  11.6 9.7 %collective-permute-start = (bf16[3,16,16,128]{3,2,1,0:T(8,128)(2,1)}, bf16[3,16,16,128]{3,2,1,0:T(8,128)(2,1)}, u32[]{:S(2)}, u32[]{:S(2)}) collective-permute-start(bf16[3,16,16,128]{3,2,1,0:T(8,128)(2,1)} %get-tuple-element.15), channel_id=1, source_target_pairs={{1,2},{3,4},{5,6},{7,8},{9,10},{11,12},{13,14},{2,1},{4,3},{6,5},{... | collective-permute-start | bytes 589832 | tf_op jit(solution)/shard_map/ppermute | solution.py:376
  16.3 5.0 %collective-permute-start.1 = (bf16[3,16,16,128]{3,2,1,0:T(8,128)(2,1)}, bf16[3,16,16,128]{3,2,1,0:T(8,128)(2,1)}, u32[]{:S(2)}, u32[]{:S(2)}) collective-permute-start(bf16[3,16,16,128]{3,2,1,0:T(8,128)(2,1)} %get-tuple-element.16), channel_id=1, source_target_pairs={{0,1},{1,0},{2,3},{3,2},{4,5},{5,4},{6,7},{7,6},{8,9},{9,8},{10,11... | collective-permute-start | bytes 589832 | tf_op jit(solution)/shard_map/ppermute | solution.py:377
  16.4 1.5 %copy-start.10 = (bf16[4,16,16,128]{3,2,1,0:T(8,128)(2,1)S(1)}, bf16[4,16,16,128]{3,2,1,0:T(8,128)(2,1)}, u32[]{:S(2)}) copy-start(bf16[4,16,16,128]{3,2,1,0:T(8,128)(2,1)} %copy-done.9) | copy-start | bytes 786436
  17.9 3.4 %copy-start.1 = (bf16[3,3,3,128,256]{4,3,2,1,0:T(8,128)(2,1)S(1)}, bf16[3,3,3,128,256]{4,3,2,1,0:T(8,128)(2,1)}, u32[]{:S(2)}) copy-start(bf16[3,3,3,128,256]{4,3,2,1,0:T(8,128)(2,1)} %param.11) | copy-start | bytes 5308420
  17.9 3.4 %copy-start.7 = (bf16[256,256]{1,0:T(8,128)(2,1)S(1)}, bf16[256,256]{1,0:T(8,128)(2,1)}, u32[]{:S(2)}) copy-start(bf16[256,256]{1,0:T(8,128)(2,1)} %constant.41.clone.order) | copy-start | bytes 393220
  21.3 19.4 %copy-start.5 = (bf16[3,3,3,256,32]{3,4,2,1,0:T(8,128)(2,1)S(1)}, bf16[3,3,3,256,32]{3,4,2,1,0:T(8,128)(2,1)}, u32[]{:S(2)}) copy-start(bf16[3,3,3,256,32]{3,4,2,1,0:T(8,128)(2,1)} %param.12) | copy-start | bytes 1327108
  25.2 31.1 %copy-start.3 = (bf16[3,3,3,512,32]{3,4,2,1,0:T(8,128)(2,1)S(1)}, bf16[3,3,3,512,32]{3,4,2,1,0:T(8,128)(2,1)}, u32[]{:S(2)}) copy-start(bf16[3,3,3,512,32]{3,4,2,1,0:T(8,128)(2,1)} %param.13) | copy-start | bytes 2654212
  25.2 15.6 %all-to-all-start = ((bf16[16,16,256]{2,1,0:T(8,128)(2,1)}), bf16[16,16,256]{2,1,0:T(8,128)(2,1)S(1)}, u32[]{:S(2)}, u32[]{:S(2)}) async-start(bf16[16,16,256]{2,1,0:T(8,128)(2,1)} %get-tuple-element.18), calls=%async_computation | async-start | bytes 262144 | tf_op jit(solution)/shard_map/all_to_all | solution.py:335
  31.5 2.1 %collective-permute-start.2 = (bf16[32,256]{1,0:T(8,128)(2,1)S(1)}, bf16[32,256]{1,0:T(8,128)(2,1)S(1)}, u32[]{:S(2)}, u32[]{:S(2)}) collective-permute-start(bf16[32,256]{1,0:T(8,128)(2,1)S(1)} %get-tuple-element.19), channel_id=1, source_target_pairs={{0,1},{1,0},{2,3},{3,2},{4,5},{5,4},{6,7},{7,6},{8,9},{9,8},{10,11... | collective-permute-start | bytes 49160 | tf_op jit(solution)/shard_map/ppermute | solution.py:420
  31.7 3.1 %collective-permute-start.3 = (bf16[32,256]{1,0:T(8,128)(2,1)S(1)}, bf16[32,256]{1,0:T(8,128)(2,1)S(1)}, u32[]{:S(2)}, u32[]{:S(2)}) collective-permute-start(bf16[32,256]{1,0:T(8,128)(2,1)S(1)} %get-tuple-element.20), channel_id=1, source_target_pairs={{0,2},{1,3},{2,0},{3,1},{4,6},{5,7},{6,4},{7,5},{8,10},{9,11},{10,... | collective-permute-start | bytes 49160 | tf_op jit(solution)/shard_map/ppermute | solution.py:420
  33.3 3.6 %collective-permute-start.4 = (bf16[32,256]{1,0:T(8,128)(2,1)S(1)}, bf16[32,256]{1,0:T(8,128)(2,1)S(1)}, u32[]{:S(2)}, u32[]{:S(2)}) collective-permute-start(bf16[32,256]{1,0:T(8,128)(2,1)S(1)} %get-tuple-element.21), channel_id=1, source_target_pairs={{0,3},{1,2},{2,1},{3,0},{4,7},{5,6},{6,5},{7,4},{8,11},{9,10},{10,... | collective-permute-start | bytes 49160 | tf_op jit(solution)/shard_map/ppermute | solution.py:420
  42.0 14.2 %all-to-all-start.1 = ((bf16[16,32,256]{2,1,0:T(8,128)(2,1)}), bf16[16,32,256]{2,1,0:T(8,128)(2,1)S(1)}, u32[]{:S(2)}, u32[]{:S(2)}) async-start(bf16[16,32,256]{2,1,0:T(8,128)(2,1)} %shard_map.95), calls=%async_computation.1 | async-start | bytes 524288 | tf_op jit(solution)/shard_map/all_to_all | solution.py:335
  46.8 23.7 %copy-start.6 = (bf16[2112,256]{1,0:T(8,128)(2,1)S(1)}, bf16[2112,256]{1,0:T(8,128)(2,1)}, u32[]{:S(2)}) copy-start(bf16[2112,256]{1,0:T(8,128)(2,1)} %all-gather.3.cloned.1.call-done) | copy-start | bytes 3244036
  48.9 21.6 %collective-permute-start.7 = (bf16[4,336,256]{2,1,0:T(8,128)(2,1)}, bf16[4,336,256]{2,1,0:T(8,128)(2,1)}, u32[]{:S(2)}, u32[]{:S(2)}) collective-permute-start(bf16[4,336,256]{2,1,0:T(8,128)(2,1)} %slice.9), channel_id=1, source_target_pairs={{0,16},{16,0},{1,17},{17,1},{2,18},{18,2},{3,19},{19,3},{4,20},{20... | collective-permute-start | bytes 2064392 | tf_op jit(solution)/shard_map/ppermute | solution.py:438
  50.7 3.1 %collective-permute-start.5 = (bf16[16,256]{1,0:T(8,128)(2,1)S(1)}, bf16[16,256]{1,0:T(8,128)(2,1)S(1)}, u32[]{:S(2)}, u32[]{:S(2)}) collective-permute-start(bf16[16,256]{1,0:T(8,128)(2,1)S(1)} %get-tuple-element.23), channel_id=1, source_target_pairs={{0,4},{8,12},{4,0},{12,8},{1,5},{9,13},{5,1},{13,9},{2,6},{10,14},... | collective-permute-start | bytes 24584 | tf_op jit(solution)/shard_map/ppermute | solution.py:455
  52.1 1.8 %collective-permute-start.6 = (bf16[16,256]{1,0:T(8,128)(2,1)S(1)}, bf16[16,256]{1,0:T(8,128)(2,1)S(1)}, u32[]{:S(2)}, u32[]{:S(2)}) collective-permute-start(bf16[16,256]{1,0:T(8,128)(2,1)S(1)} %get-tuple-element.24), channel_id=1, source_target_pairs={{4,8},{8,4},{5,9},{9,5},{6,10},{10,6},{7,11},{11,7},{20,24},{24,20... | collective-permute-start | bytes 24584 | tf_op jit(solution)/shard_map/ppermute | solution.py:456
  70.5 11.5 %copy-start.4 = (bf16[2,2,2,256,128]{4,3,2,1,0:T(8,128)(2,1)S(1)}, bf16[2,2,2,256,128]{4,3,2,1,0:T(8,128)(2,1)}, u32[]{:S(2)}) copy-start(bf16[2,2,2,256,128]{4,3,2,1,0:T(8,128)(2,1)} %param.16) | copy-start | bytes 1572868
Sparse Core Ops, SparseCore 0:
  9.2 33.9 all-gather.2

commit v9 on v8

--- a/solution.py
+++ b/solution.py
@@ -77,11 +77,25 @@
     return dot(left, weights)
 
 
-def front_stage(odd, volume, off_chip, on_chip, whole):
-    for s in range(3):
-        off_chip[s] = jnp.where(odd[0] == 0, volume[s], volume[s + 1])
-        on_chip[s] = jnp.where(odd[0] == 0, volume[s + 1], volume[s])
-    whole[...] = volume[...]
+def front_stage(marks, volume, decode, off_chip, on_chip, *refs):
+    block, done = refs if len(refs) == 2 else (None, refs[0])
+    odd, rep = marks[4], marks[1]
+    pairs = [
+        (volume.at[pl.ds(odd, 3)], off_chip),
+        (volume.at[pl.ds(1 - odd, 3)], on_chip),
+    ]
+    if block is not None:
+        pairs += [
+            (decode.at[pl.ds(pl.multiple_of(528 * rep, 16), 336)], block.at[pl.ds(0, 336)]),
+            (decode.at[pl.ds(336, 192)], block.at[pl.ds(336, 192)]),
+        ]
+    copies = [
+        pltpu.make_async_copy(source, target, done.at[i]) for i, (source, target) in enumerate(pairs)
+    ]
+    for copy in copies:
+        copy.start()
+    for copy in copies:
+        copy.wait()
 
 
 def own_stage(volume, weights, out, shifted):
@@ -95,11 +109,11 @@
     out[3, :, 128:] = jnp.zeros((256, 128), jnp.float32)
 
 
-def stem_stage(ends, off_chip, on_chip, own, weights, second, order, _, *refs):
+def stem_stage(marks, off_chip, on_chip, own, weights, second, order, _, *refs):
     pooled_out, skip_outs = refs[0], refs[1 : 1 + GROUP]
     shifted, halves, framed, patches, quarters, blocks = refs[1 + GROUP :]
     for s in range(3):
-        even = ends[2] == 0
+        even = marks[4] == 0
         shift_slice(shifted, s, jnp.where(even, off_chip[s], on_chip[s]))
         shift_slice(shifted, 3 + s, jnp.where(even, on_chip[s], off_chip[s]))
     framed[...] = jnp.zeros(framed.shape, jnp.float32)
@@ -120,9 +134,9 @@
         pooled = halves[pl.ds(0, 64, stride=2), :] + halves[pl.ds(1, 64, stride=2), :]
         pooled = round_once(pooled * 0.125)
         if m == 0:
-            pooled = jnp.where(ends[0] == 0, 0.0, pooled)
+            pooled = jnp.where(marks[5] == 0, 0.0, pooled)
         if m == 3:
-            pooled = jnp.where(ends[1] == 0, 0.0, pooled)
+            pooled = jnp.where(marks[6] == 0, 0.0, pooled)
         framed[m, 1:9, 8:16, :] = pooled.reshape(8, 8, 128)
     fill_patches(framed, patches, 4)
     skip = dot(patches[0:128], second[0])
@@ -149,9 +163,11 @@
         near, far = sorted_skip[:64, 64 * r : 64 * r + 64], sorted_skip[64:, 64 * r : 64 * r + 64]
         block = jnp.concatenate([near, far], axis=1)
         block = jnp.concatenate([block[:32], block[32:]], axis=1).astype(jnp.bfloat16)
-        blocks[r] = block
+        blocks[r, 0:32, :] = block
+        first, last = sorted_skip[16 * r : 16 * r + 16], sorted_skip[64 + 16 * r : 80 + 16 * r]
+        blocks[r, 32:48, :] = jnp.where(marks[0] == 0, first, last).astype(jnp.bfloat16)
     for k in range(GROUP):
-        skip_outs[k][...] = blocks[ends[3] ^ k]
+        skip_outs[k][...] = blocks[marks[0] ^ k]
 
 
 def edge_slice(block, far):
@@ -194,17 +210,17 @@
     return jnp.maximum(total, 0.0)
 
 
-def by_rank(rank, near, blocks):
+def by_rank(marks, near, blocks):
     for k in range(GROUP):
-        blocks[rank[0] ^ k] = near[k][...]
-
-
-def edge_stage(place, *refs):
+        blocks[marks[0] ^ k] = near[k][...]
+
+
+def edge_stage(marks, *refs):
     near, (near_swap, far_swap, blocks) = refs[:GROUP], refs[GROUP:]
-    by_rank(place, near, blocks)
-    first = edge_slice(blocks[0], False)
-    last = edge_slice(blocks[GROUP - 1], True)
-    even = place[2] == 0
+    by_rank(marks, near, blocks)
+    first = edge_slice(blocks[0, 0:32, :], False)
+    last = edge_slice(blocks[GROUP - 1, 0:32, :], True)
+    even = marks[2] == 0
     near_swap[...] = jnp.where(even, last, first).astype(jnp.bfloat16)
     far_swap[...] = jnp.where(even, first, last).astype(jnp.bfloat16)
 
@@ -217,28 +233,48 @@
         out[dest] = deep
 
 
-def deeper_stage(deep, weights, *refs):
-    out = refs[-1]
+def deeper_stage(marks, deep, weights, *refs):
+    near, out, blocks = refs[:-2], refs[-2], refs[-1]
     n, chans, _ = out.shape
     voxels = deep.shape[1]
     deeper = spread_taps(weights, deep[...], ((1,), (0,)), chans, voxels)
     lane = lax.broadcasted_iota(jnp.int32, (chans, 128), 1)
     planes = n // GROUP
+    ride = len(near) == GROUP
+    if ride:
+        by_rank(marks, near, blocks)
+        edges = [blocks[r, 32:48, :].astype(jnp.float32) for r in (0, GROUP - 1)]
+        riders = [
+            [
+                jnp.concatenate(
+                    [
+                        pltpu.roll(edge[:, at // 128 * 128 : at // 128 * 128 + 128], (96 - at) % 128, 1)
+                        for at in (64 * r, 64 * r + 32)
+                    ],
+                    axis=0,
+                )
+                for r in range(GROUP)
+            ]
+            for edge in edges
+        ]
     for p in range(planes):
         part = pltpu.roll(deeper, (16 - 64 * p) % voxels, 1)[:, :128]
         if p == 0:
             part = jnp.where(lane < 16, 0.0, part)
         if p == planes - 1:
             part = jnp.where(lane >= 80, 0.0, part)
-        part = part.astype(jnp.bfloat16)
         for r in range(GROUP):
-            out[GROUP * p + r] = part
-
-
-def rise_stage(rank, chans, rise, out):
+            whole = part
+            if ride:
+                rider = jnp.where(marks[3] < p, riders[1][r], riders[0][r])
+                whole = jnp.where(lane < 96, part, rider)
+            out[GROUP * p + r] = whole.astype(jnp.bfloat16)
+
+
+def rise_stage(marks, chans, rise, out):
     lane = lax.broadcasted_iota(jnp.int32, (256, 64), 1)
     row = lax.broadcasted_iota(jnp.int32, (256, 64), 0)
-    source = (rank[0] + GROUP * (lane // chans)) * chans + lane % chans
+    source = (marks[0] + GROUP * (lane // chans)) * chans + lane % chans
     mine = jnp.where(row == source, 1.0, 0.0).astype(jnp.bfloat16)
     for pair in range(4):
         both = [dot(rise[2 * pair + k], mine) for k in range(2)]
@@ -246,17 +282,39 @@
         out[:, 128 * pair : 128 * pair + 128] = both
 
 
-def decode_stage(place, deeper, rise, near_swap, far_swap, *refs):
-    near, (*decode, out, framed, patches, risen, blocks) = refs[:GROUP], refs[GROUP:]
-    by_rank(place, near, blocks)
-    even = place[2] == 0
+def decode_stage(ride, marks, deeper, rise, *refs):
+    swaps = () if ride else refs[:2]
+    near, refs = refs[len(swaps) : len(swaps) + GROUP], refs[len(swaps) + GROUP :]
+    *decode, out, framed, patches, risen, blocks = refs
+    by_rank(marks, near, blocks)
+    n, chans, _ = deeper.shape
+    plane, planes = marks[3], n // GROUP
+    upper = lax.broadcasted_iota(jnp.int32, (64, 128), 1) >= 64
+
+    def edge(low):
+        if not ride:
+            even = marks[2] == 0
+            sides = [swap[...].astype(jnp.float32) for swap in swaps]
+            side = jnp.where(even, sides[low], sides[not low])
+            parts = []
+            for k in range(2):
+                half = side[:, 128 * k : 128 * k + 128]
+                parts += [pltpu.roll(half, 64, 1), half]
+            return jnp.concatenate(parts, axis=0)
+        other = jnp.maximum(plane - 1, 0) if low else jnp.minimum(plane + 1, planes - 1)
+        lane = lax.broadcasted_iota(jnp.int32, (16, 128), 1)
+        parts = []
+        for r in range(GROUP):
+            block = deeper[GROUP * other + r].astype(jnp.float32)
+            parts.append(jnp.where(lane < 96, pltpu.roll(block[:16], 96, 1), block[16:]))
+        return jnp.where(other == plane, 0.0, jnp.concatenate(parts, axis=0))
+
     framed[...] = jnp.zeros(framed.shape, jnp.float32)
-    spread = round_once(dot(deeper[...].astype(jnp.float32).T.astype(jnp.bfloat16), rise[...]))
+    spread = round_once(dot(deeper[...].reshape(n * chans, 128).astype(jnp.float32).T.astype(jnp.bfloat16), rise[...]))
     for pair in range(4):
         both = spread[:, 128 * pair : 128 * pair + 128]
         risen[2 * pair] = both
         risen[2 * pair + 1] = pltpu.roll(both, 64, 1)
-    upper = lax.broadcasted_iota(jnp.int32, (64, 128), 1) >= 64
     for s in range(10):
         d, a = (s + 1) // 2, (s + 1) % 2
         for h in range(4):
@@ -266,15 +324,9 @@
                         4 * a + 2 * b + c, 16 * d + 4 * h : 16 * d + 4 * h + 4, :
                     ]
         if s == 0 or s == 9:
-            sides = near_swap[...].astype(jnp.float32), far_swap[...].astype(jnp.float32)
-            edge = jnp.where(even, sides[s == 0], sides[s == 9])
-            parts = []
-            for k in range(2):
-                half = edge[:, 128 * k : 128 * k + 128]
-                parts += [pltpu.roll(half, 64, 1), half]
-            skip = jnp.concatenate(parts, axis=0)
+            skip = edge(s == 0)
         else:
-            both = blocks[(s - 1) // 2].astype(jnp.float32)
+            both = blocks[(s - 1) // 2, 0:32, :].astype(jnp.float32)
             skip = jnp.concatenate([both[:, :128], both[:, 128:]], axis=0)
             if (s - 1) % 2 == 0:
                 skip = pltpu.roll(skip, 64, 1)
@@ -308,8 +360,8 @@
     if len(decode) == 1:
         multiply(None)
     else:
-        pl.when(place[1] == 0)(lambda: multiply(0))
-        pl.when(place[1] == 1)(lambda: multiply(1))
+        pl.when(marks[1] == 0)(lambda: multiply(0))
+        pl.when(marks[1] == 1)(lambda: multiply(1))
 
 
 def final_stage(partials, weights, out, spaced):
@@ -353,29 +405,29 @@
     voxels = 16 * n
     bf16 = functools.partial(jax.ShapeDtypeStruct, dtype=jnp.bfloat16)
 
-    rep = lax.axis_index("rep")
-    marks = jnp.stack([rank, rep, lax.axis_index("z") % 2]).astype(jnp.int32)
-    odd = (place % 2).astype(jnp.int32)
-    off_chip, on_chip, volume = call(
-        front_stage,
-        (bf16((3, 16, 16, 128)), bf16((3, 16, 16, 128)), bf16((4, 16, 16, 128))),
-        [],
-        (odd.reshape(1), volume),
-        3 * 10**9,
-        16,
-        scalars=1,
-    )
+    rep, plane = lax.axis_index("rep"), lax.axis_index("z")
+    marks = jnp.stack([rank, rep, plane % 2, plane, place % 2, place, n - 1 - place])
+    marks = marks.astype(jnp.int32)
     decode_block = decode_kernel.reshape(27 * chans, 256)
     shared = lax.axis_size("rep") == 2 and chans == 32
-    if shared:
-        own_rows = lax.dynamic_slice_in_dim(decode_block, 528 * rep, 336, axis=0)
-        decode_block = jnp.concatenate([own_rows, decode_block[336:528]], axis=0)
-    line = lax.all_gather(decode_block, "z", axis=0)
-
+    ride = chans == 32
+    halo = bf16((3, 16, 16, 128))
+    off_chip, on_chip, *share = pl.pallas_call(
+        front_stage,
+        out_shape=(halo, halo) + ((bf16((528, 256)),) if shared else ()),
+        in_specs=[pl.BlockSpec(memory_space=pltpu.SMEM)] + [pl.BlockSpec(memory_space=pl.ANY)] * 2,
+        out_specs=(pl.BlockSpec(memory_space=pl.ANY),) * (3 if shared else 2),
+        scratch_shapes=[pltpu.SemaphoreType.DMA((4,))],
+        compiler_params=pltpu.CompilerParams(vmem_limit_bytes=60 * MIB),
+    )(marks, volume, decode_block)
     pairs = [(i, i + 1) for i in range(1, n - 1, 2)]
     off_chip = lax.ppermute(off_chip, ALL, pairs + [(j, i) for i, j in pairs])
     on_chip = lax.ppermute(on_chip, ALL, [(i, i ^ 1) for i in range(n)])
-
+    if shared:
+        decode_block = share[0]
+    line = lax.all_gather(decode_block, "z", axis=0)
+
+    pairs = [(i, i + 1) for i in range(1, n - 1, 2)]
     taps = first_kernel.reshape(3, 1152, 128)
     own = call(
         own_stage,
@@ -388,9 +440,8 @@
     lane = np.arange(256)
     source = (lane // 64 + GROUP * (lane % 64 // chans)) * chans + lane % chans
     order = jnp.asarray(np.arange(256)[:, None] == source[None, :], jnp.bfloat16)
-    ends = jnp.stack([place, n - 1 - place, odd, rank]).astype(jnp.int32)
     rise_part = call(
-        lambda rank_ref, *refs: rise_stage(rank_ref, chans, *refs),
+        lambda marks_ref, *refs: rise_stage(marks_ref, chans, *refs),
         bf16((n * chans, 512)),
         [],
         (marks, rise_kernel.reshape(8, n * chans, 256)),
@@ -400,16 +451,16 @@
     )
     pooled_two, *skips = call(
         stem_stage,
-        (bf16((n, 16, 256)),) + (bf16((32, 256)),) * GROUP,
+        (bf16((n, 16, 256)),) + (bf16((48, 256)),) * GROUP,
         [
             pltpu.VMEM((6, 18, 16, 384), jnp.bfloat16),
             pltpu.VMEM((128, 128), jnp.float32),
             pltpu.VMEM((4, 10, 24, 128), jnp.float32),
             pltpu.VMEM((256, 1152), jnp.bfloat16),
             pltpu.VMEM((2, 32, 128), jnp.float32),
-            pltpu.VMEM((GROUP, 32, 256), jnp.bfloat16),
+            pltpu.VMEM((GROUP, 48, 256), jnp.bfloat16),
         ],
-        (ends, off_chip, on_chip, own, taps, second_kernel.reshape(3, 1152, 256), order, rise_part),
+        (marks, off_chip, on_chip, own, taps, second_kernel.reshape(3, 1152, 256), order, rise_part),
         2 * 1024 * 2304 * 256,
         24,
         scalars=1,
@@ -419,7 +470,7 @@
     near = [skips[0]] + [
         lax.ppermute(skips[k], "r", [(r, r ^ k) for r in range(GROUP)]) for k in range(1, GROUP)
     ]
-    blocks = pltpu.VMEM((GROUP, 32, 256), jnp.bfloat16)
+    blocks = pltpu.VMEM((GROUP, 48, 256), jnp.bfloat16)
 
     deep = call(
         deep_stage,
@@ -441,39 +492,42 @@
         weights = (weights.reshape(1, 27 * 128, 256),)
     else:
         weights = (line,)
-    swaps = call(
-        edge_stage,
-        (bf16((16, 256)), bf16((16, 256))),
-        [blocks],
-        (marks, *near),
-        0,
-        16,
-        scalars=1,
-    )
-    near_pairs = [(p, p + 1) for p in range(0, planes - 1, 2)]
-    far_pairs = [(p, p + 1) for p in range(1, planes - 1, 2)]
-    near_swap = lax.ppermute(swaps[0], "z", near_pairs + [(j, i) for i, j in near_pairs])
-    far_swap = lax.ppermute(swaps[1], "z", far_pairs + [(j, i) for i, j in far_pairs])
+    swaps = ()
+    if not ride:
+        swaps = call(
+            edge_stage,
+            (bf16((16, 256)), bf16((16, 256))),
+            [blocks],
+            (marks, *near),
+            0,
+            16,
+            scalars=1,
+        )
+        near_pairs = [(p, p + 1) for p in range(0, planes - 1, 2)]
+        far_pairs = [(p, p + 1) for p in range(1, planes - 1, 2)]
+        near_swap = lax.ppermute(swaps[0], "z", near_pairs + [(j, i) for i, j in near_pairs])
+        far_swap = lax.ppermute(swaps[1], "z", far_pairs + [(j, i) for i, j in far_pairs])
+        swaps = (near_swap, far_swap)
     deep_whole = exchange(deep, ALL).reshape(n * chans, voxels)
 
     deeper = call(
         deeper_stage,
         bf16((n, chans, 128)),
-        [],
+        [blocks],
         (
+            marks,
             deep_whole,
             deeper_kernel.transpose(0, 1, 2, 4, 3).reshape(27 * chans, n * chans),
-            near_swap,
-            far_swap,
+            *(near if ride else ()),
         ),
         2 * 27 * chans * n * chans * voxels,
         16,
-        unread=2,
-    )
-    deeper_near = exchange(deeper, ALL).reshape(n * chans, 128)
+        scalars=1,
+    )
+    deeper_near = exchange(deeper, ALL)
 
     partial = call(
-        decode_stage,
+        functools.partial(decode_stage, ride),
         bf16((512, 256)),
         [
             pltpu.VMEM((10, 10, 24, 128), jnp.float32),
@@ -481,7 +535,7 @@
             pltpu.VMEM((8, 128, 128), jnp.float32),
             blocks,
         ],
-        (marks, deeper_near, rise_part, near_swap, far_swap, *near, *weights),
+        (marks, deeper_near, rise_part, *swaps, *near, *weights),
         2 * 512 * 3456 * 256,
         24,
         scalars=1,

time: 91.4 us -> 105 us (1.15)
  Pallas kernels: 14 us -> 34 us
  blocking collectives: 22.1 us -> 18.7 us
  starting transfers between devices: 21.2 us -> 18.8 us
    pallas_call x0 -> x1, Pallas kernels: none -> 22 us  [body(): pl.pallas_call(front_stage, out_shape=(halo, halo) + ((bf16((528, 256)),)...]
    all_to_all x2, waiting for transfers between devices: 6.25 us -> 9.74 us  [exchange(): lax.all_to_all(payload, axis, split_axis=0, concat_axis=0, tiled=True)]
    all_to_all x2, blocking collectives: 22.1 us -> 18.7 us  [exchange(): lax.all_to_all(payload, axis, split_axis=0, concat_axis=0, tiled=True)]
    pallas_call x9 -> x7, Pallas kernels: 14 us -> 12 us  [call(): pl.pallas_call(kernel, out_shape=outs, in_specs=[pl.BlockSpec(memory_spac...]
    ppermute x2 -> x0, starting transfers between devices: 2.02 us -> none  [the longest x1 1.37 us: body(): lax.ppermute(swaps[0], 'z', near_pairs + [(j, i) for i, j in near_pairs])]
    ppermute x1, waiting for transfers between devices: 1.98 us -> 0.01 us  [body(): off_chip = lax.ppermute(off_chip, ALL, pairs + [(j, i) for i, j in pairs])]
    ppermute x2 -> x0, waiting for transfers between devices: 1.12 us -> none  [the longest x1 1.12 us: body(): lax.ppermute(swaps[0], 'z', near_pairs + [(j, i) for i, j in near_pairs])]
  transfers between devices with their start and end apart: 11 -> 9, of which waited for: 6 -> 4; matrix products, arithmetic and copies ran while one was open for 3% -> 2% of each run, Pallas kernels for 11% -> 8%
where the time goes in v9:
time: 105 us; the launch traced here: 103 us
  Pallas kernels  34 us (32%)
  starting transfers between devices  18.8 us (18%)
  blocking collectives  18.7 us (18%)
  between operations  13.5 us (13%)
  waiting for transfers between devices  13.2 us (13%)
  local copies, waits for them, and re-layouts  5.11 us (5%)
    pallas_call x1, Pallas kernels, body(): pl.pallas_call(front_stage, out_shape=(halo, halo) + ((bf16((528, 256)),)...  22 us
    all_to_all x2, blocking collectives, exchange(): lax.all_to_all(payload, axis, split_axis=0, concat_axis=0, tiled=True)  18.7 us
    pallas_call x7, Pallas kernels, call(): pl.pallas_call(kernel, out_shape=outs, in_specs=[pl.BlockSpec(memory_spac...  12 us
    all_to_all x2, starting transfers between devices, exchange(): lax.all_to_all(payload, axis, split_axis=0, concat_axis=0, tiled=True)  10.7 us
    all_to_all x2, waiting for transfers between devices, exchange(): lax.all_to_all(payload, axis, split_axis=0, concat_axis=0, tiled=True)  9.74 us
    ppermute x1, starting transfers between devices, body(): off_chip = lax.ppermute(off_chip, ALL, pairs + [(j, i) for i, j in pairs])  4.57 us
    ppermute x3, waiting for transfers between devices, body(): lax.ppermute(skips[k], 'r', [(r, r ^ k) for r in range(GROUP)])  3.46 us
    unnamed x22, local copies, waits for them, and re-layouts  2.35 us
  transfers between devices with their start and end apart: 9, of which 4 were waited for; matrix products, arithmetic and copies ran while one was open for 2% of the time, Pallas kernels for 8%

profile of v9, /device:TPU:1, one launch (start us, length us, event | category | flops | bytes accessed | tf_op | source)
XLA Modules:
  0.0 103.4 jit_solution(6135138253755734396)
XLA Ops:
  6.5 0.7 stack.31.marks.marks_ref
  7.2 22.0 %shard_map.91 = (bf16[3,16,16,128]{3,2,1,0:T(8,128)(2,1)}, bf16[3,16,16,128]{3,2,1,0:T(8,128)(2,1)}, bf16[528,256]{1,0:T(8,128)(2,1)}) custom-call(s32[7]{0:T(128)} %stack.31.marks.marks_ref, bf16[4,16,16,128]{3,2,1,0:T(8,128)(2,1)} %volume.3, bf16[864,256]{1,0:T(8,128)(2,1)} %bitcast.35), custom_call_target="tpu_custom_call" | custom-call | tf_op jit(solution)/shard_map/pallas_call | solution.py:415
  29.2 0.0 all-gather.3.cloned.1.call-update
  29.3 4.6 %collective-permute-start = (bf16[3,16,16,128]{3,2,1,0:T(8,128)(2,1)}, bf16[3,16,16,128]{3,2,1,0:T(8,128)(2,1)S(1)}, u32[]{:S(2)}, u32[]{:S(2)}) collective-permute-start(bf16[3,16,16,128]{3,2,1,0:T(8,128)(2,1)} %get-tuple-element.13), channel_id=1, source_target_pairs={{1,2},{3,4},{5,6},{7,8},{9,10},{11,12},{13,14},{2,1},{4,3},{6,5},{... | collective-permute-start | bytes 589832 | tf_op jit(solution)/shard_map/ppermute | solution.py:424
  33.8 0.1 collective-permute-start.1
  33.9 0.0 copy-start
  33.9 1.6 %copy-done = bf16[2,2,2,512,256]{4,3,2,1,0:T(8,128)(2,1)S(1)} copy-done((bf16[2,2,2,512,256]{4,3,2,1,0:T(8,128)(2,1)S(1)}, bf16[2,2,2,512,256]{4,3,2,1,0:T(8,128)(2,1)}, u32[]{:S(2)}) %copy-start) | copy-done | bytes 2097176
  35.5 0.7 copy-done.9
  36.2 1.3 %shard_map.93._.rise = bf16[512,512]{1,0:T(8,128)(2,1)S(1)} custom-call(s32[7]{0:T(128)S(1)} %copy-done.9, bf16[8,512,256]{2,1,0:T(8,128)(2,1)S(1)} %bitcast.23), custom_call_target="tpu_custom_call" | custom-call | flops 134217728 | bytes 2097180 | tf_op jit(solution)/shard_map/pallas_call | solution.py:18
  37.5 0.0 copy-start.1
  37.5 0.0 copy-start.8
  37.6 1.4 %shard_map.92.own = f32[4,256,256]{2,1,0:T(8,128)S(1)} custom-call(bf16[4,16,16,128]{3,2,1,0:T(8,128)(2,1)S(1)} %copy-done.7, bf16[3,1152,128]{2,1,0:T(8,128)(2,1)S(1)} %bitcast.26), custom_call_target="tpu_custom_call" | custom-call | flops 1207959552 | bytes 1146880 | tf_op jit(solution)/shard_map/pallas_call | solution.py:18
  39.0 0.1 copy-done.1
  39.1 3.3 %shard_map.94 = (bf16[16,16,256]{2,1,0:T(8,128)(2,1)}, bf16[48,256]{1,0:T(8,128)(2,1)S(1)}, bf16[48,256]{1,0:T(8,128)(2,1)S(1)}, bf16[48,256]{1,0:T(8,128)(2,1)S(1)}, bf16[48,256]{1,0:T(8,128)(2,1)S(1)}) custom-call(s32[7]{0:T(128)S(1)} %copy-done.10, bf16[3,16,16,128]{3,2,1,0:T(8,128)(2,1)S(1)} %collective-permute-done.off_chip, ...), custom_call_target="tpu_custom_call" | custom-call | flops 1207959552 | bytes 4227100 | tf_op jit(solution)/shard_map/pallas_call | solution.py:18
  42.4 6.0 %all-to-all-start = ((bf16[16,16,256]{2,1,0:T(8,128)(2,1)}), bf16[16,16,256]{2,1,0:T(8,128)(2,1)S(1)}, u32[]{:S(2)}, u32[]{:S(2)}) async-start(bf16[16,16,256]{2,1,0:T(8,128)(2,1)} %get-tuple-element.15), calls=%async_computation | async-start | bytes 262144 | tf_op jit(solution)/shard_map/all_to_all | solution.py:387
  48.4 0.2 collective-permute-start.2
  48.6 1.6 %collective-permute-start.3 = (bf16[48,256]{1,0:T(8,128)(2,1)S(1)}, bf16[48,256]{1,0:T(8,128)(2,1)S(1)}, u32[]{:S(2)}, u32[]{:S(2)}) collective-permute-start(bf16[48,256]{1,0:T(8,128)(2,1)S(1)} %get-tuple-element.17), channel_id=1, source_target_pairs={{0,2},{1,3},{2,0},{3,1},{4,6},{5,7},{6,4},{7,5},{8,10},{9,11},{10,... | collective-permute-start | bytes 73736 | tf_op jit(solution)/shard_map/ppermute | solution.py:471
  50.2 0.4 collective-permute-start.4
  50.6 1.2 %collective-permute-done.3.refs_1_.refs_2_ = bf16[48,256]{1,0:T(8,128)(2,1)S(1)} collective-permute-done((bf16[48,256]{1,0:T(8,128)(2,1)S(1)}, bf16[48,256]{1,0:T(8,128)(2,1)S(1)}, u32[]{:S(2)}, u32[]{:S(2)}) %collective-permute-start.3) | collective-permute-done | bytes 24608 | tf_op jit(solution)/shard_map/ppermute | solution.py:471
  51.8 2.2 %collective-permute-done.4.refs_2_.refs_3_ = bf16[48,256]{1,0:T(8,128)(2,1)S(1)} collective-permute-done((bf16[48,256]{1,0:T(8,128)(2,1)S(1)}, bf16[48,256]{1,0:T(8,128)(2,1)S(1)}, u32[]{:S(2)}, u32[]{:S(2)}) %collective-permute-start.4) | collective-permute-done | bytes 24608 | tf_op jit(solution)/shard_map/ppermute | solution.py:471
  54.0 3.6 %all-to-all-done = bf16[16,16,256]{2,1,0:T(8,128)(2,1)S(1)} async-done(((bf16[16,16,256]{2,1,0:T(8,128)(2,1)}), bf16[16,16,256]{2,1,0:T(8,128)(2,1)S(1)}, u32[]{:S(2)}, u32[]{:S(2)}) %all-to-all-start) | async-done | bytes 131104 | tf_op jit(solution)/shard_map/all_to_all | solution.py:387
  57.7 1.3 %shard_map.95 = bf16[16,32,256]{2,1,0:T(8,128)(2,1)} custom-call(bf16[256,256]{1,0:T(8,128)(2,1)S(1)} %bitcast.29, bf16[864,256]{1,0:T(8,128)(2,1)S(1)} %bitcast.31, bf16[48,256]{1,0:T(8,128)(2,1)S(1)} %collective-permute-done.2.refs_0_.refs_1_, bf16[48,256]{1,0:T(8,128)(2,1)S(1)} %collective-permute-done.3.refs_1_.refs_2_, ...), custom_call_target="tpu_custom_call" | custom-call | flops 113246208 | bytes 573440 | tf_op jit(solution)/shard_map/pallas_call | solution.py:18
  58.9 4.7 %all-to-all-start.1 = ((bf16[16,32,256]{2,1,0:T(8,128)(2,1)}), bf16[16,32,256]{2,1,0:T(8,128)(2,1)S(1)}, u32[]{:S(2)}, u32[]{:S(2)}) async-start(bf16[16,32,256]{2,1,0:T(8,128)(2,1)} %shard_map.95), calls=%async_computation.1 | async-start | bytes 524288 | tf_op jit(solution)/shard_map/all_to_all | solution.py:387
  63.7 0.0 all-gather.3.cloned.1.call-done
  63.7 2.1 %slice.4 = bf16[4,336,256]{2,1,0:T(8,128)(2,1)} slice(bf16[4,528,256]{2,1,0:T(8,128)(2,1)} %bitcast.32), slice={[0:4], [0:336], [0:256]} | slice | bytes 1376256 | tf_op jit(solution)/shard_map/slice | solution.py:489
  65.8 1.3 %collective-permute-start.5 = (bf16[4,336,256]{2,1,0:T(8,128)(2,1)}, bf16[4,336,256]{2,1,0:T(8,128)(2,1)S(1)}, u32[]{:S(2)}, u32[]{:S(2)}) collective-permute-start(bf16[4,336,256]{2,1,0:T(8,128)(2,1)} %slice.4), channel_id=1, source_target_pairs={{0,16},{16,0},{1,17},{17,1},{2,18},{18,2},{3,19},{19,3},{4,20},{20... | collective-permute-start | bytes 2064392 | tf_op jit(solution)/shard_map/ppermute | solution.py:489
  67.1 6.1 %all-to-all-done.1 = bf16[16,32,256]{2,1,0:T(8,128)(2,1)S(1)} async-done(((bf16[16,32,256]{2,1,0:T(8,128)(2,1)}), bf16[16,32,256]{2,1,0:T(8,128)(2,1)S(1)}, u32[]{:S(2)}, u32[]{:S(2)}) %all-to-all-start.1) | async-done | bytes 262176 | tf_op jit(solution)/shard_map/all_to_all | solution.py:387
  73.2 1.3 %shard_map.96 = bf16[16,32,128]{2,1,0:T(8,128)(2,1)S(1)} custom-call(s32[7]{0:T(128)S(1)} %copy-done.10, bf16[512,256]{1,0:T(8,128)(2,1)S(1)} %bitcast.25, bf16[864,512]{1,0:T(8,128)(2,1)S(1)} %bitcast.28, bf16[48,256]{1,0:T(8,128)(2,1)S(1)} %get-tuple-element.19.refs_0_, bf16[48,256]{1,0:T(8,128)(2,1)S(1)} %collective-permute-done.2.refs_0_.refs_1_, ...), custom_call_target="tpu_custom_call" | custom-call | flops 226492416 | bytes 1245212 | tf_op jit(solution)/shard_map/pallas_call | solution.py:18
  74.4 10.2 %all_to_all.20.deeper = bf16[16,32,128]{2,1,0:T(8,128)(2,1)S(1)} all-to-all(bf16[16,32,128]{2,1,0:T(8,128)(2,1)S(1)} %shard_map.96), channel_id=1, replica_groups=mesh['rep'=2,'z'=4,'r'=4] {'z','r'}, dimensions={0} | all-to-all | bytes 262144 | tf_op jit(solution)/shard_map/all_to_all | solution.py:387
  84.7 2.3 %shard_map.97 = bf16[512,256]{1,0:T(8,128)(2,1)S(1)} custom-call(s32[7]{0:T(128)S(1)} %copy-done.10, bf16[16,32,128]{2,1,0:T(8,128)(2,1)S(1)} %all_to_all.20.deeper, bf16[512,512]{1,0:T(8,128)(2,1)S(1)} %shard_map.93._.rise, bf16[48,256]{1,0:T(8,128)(2,1)S(1)} %get-tuple-element.19.refs_0_, bf16[48,256]{1,0:T(8,128)(2,1)S(1)} %collective-permute-done.2.refs_0_.refs_1_, ...), custom_call_target="tpu_custom_call" | custom-call | flops 905969664 | bytes 2523164 | tf_op jit(solution)/shard_map/pallas_call | solution.py:18
  87.0 8.6 %all_to_all.21.partials = bf16[4,128,256]{2,1,0:T(8,128)(2,1)S(1)} all-to-all(bf16[4,128,256]{2,1,0:T(8,128)(2,1)S(1)} %bitcast.34), channel_id=1, replica_groups=mesh['rep'=2,'z'=4,'r'=4] {'r'}, dimensions={0} | all-to-all | bytes 524288 | tf_op jit(solution)/shard_map/all_to_all | solution.py:387
  95.5 1.1 %shard_map.98 = bf16[1024,128]{1,0:T(8,128)(2,1)} custom-call(bf16[4,128,256]{2,1,0:T(8,128)(2,1)S(1)} %all_to_all.21.partials, bf16[8,256,128]{2,1,0:T(8,128)(2,1)S(1)} %bitcast.30), custom_call_target="tpu_custom_call" | custom-call | flops 67108864 | bytes 786432 | tf_op jit(solution)/shard_map/pallas_call | solution.py:18
  (21 shorter events, 0.0 us)
Async XLA Ops:
  6.5 57.2 %all-gather.3.cloned.1.call-start = ((), (), s32[]{:S(2)}) async-start(), calls=%async_computation.4 | async-start | bytes 1351680 | tf_op jit(solution)/shard_map/all_gather | solution.py:428
  7.2 30.3 %copy-start.2 = (bf16[3,3,3,128,128]{4,3,2,1,0:T(8,128)(2,1)S(1)}, bf16[3,3,3,128,128]{4,3,2,1,0:T(8,128)(2,1)}, u32[]{:S(2)}) copy-start(bf16[3,3,3,128,128]{4,3,2,1,0:T(8,128)(2,1)} %param.10) | copy-start | bytes 2654212
  29.3 9.7 %collective-permute-start = (bf16[3,16,16,128]{3,2,1,0:T(8,128)(2,1)}, bf16[3,16,16,128]{3,2,1,0:T(8,128)(2,1)S(1)}, u32[]{:S(2)}, u32[]{:S(2)}) collective-permute-start(bf16[3,16,16,128]{3,2,1,0:T(8,128)(2,1)} %get-tuple-element.13), channel_id=1, source_target_pairs={{1,2},{3,4},{5,6},{7,8},{9,10},{11,12},{13,14},{2,1},{4,3},{6,5},{... | collective-permute-start | bytes 589832 | tf_op jit(solution)/shard_map/ppermute | solution.py:424
  33.8 5.2 %collective-permute-start.1 = (bf16[3,16,16,128]{3,2,1,0:T(8,128)(2,1)}, bf16[3,16,16,128]{3,2,1,0:T(8,128)(2,1)S(1)}, u32[]{:S(2)}, u32[]{:S(2)}) collective-permute-start(bf16[3,16,16,128]{3,2,1,0:T(8,128)(2,1)} %get-tuple-element.14), channel_id=1, source_target_pairs={{0,1},{1,0},{2,3},{3,2},{4,5},{5,4},{6,7},{7,6},{8,9},{9,8},{10,11... | collective-permute-start | bytes 589832 | tf_op jit(solution)/shard_map/ppermute | solution.py:425
  33.9 1.6 %copy-start = (bf16[2,2,2,512,256]{4,3,2,1,0:T(8,128)(2,1)S(1)}, bf16[2,2,2,512,256]{4,3,2,1,0:T(8,128)(2,1)}, u32[]{:S(2)}) copy-start(bf16[2,2,2,512,256]{4,3,2,1,0:T(8,128)(2,1)} %param.14) | copy-start | bytes 6291460
  35.5 0.7 copy-start.9
  36.2 1.3 %copy-start.7 = (bf16[4,16,16,128]{3,2,1,0:T(8,128)(2,1)S(1)}, bf16[4,16,16,128]{3,2,1,0:T(8,128)(2,1)}, u32[]{:S(2)}) copy-start(bf16[4,16,16,128]{3,2,1,0:T(8,128)(2,1)} %volume.3) | copy-start | bytes 786436
  37.5 1.5 %copy-start.1 = (bf16[3,3,3,128,256]{4,3,2,1,0:T(8,128)(2,1)S(1)}, bf16[3,3,3,128,256]{4,3,2,1,0:T(8,128)(2,1)}, u32[]{:S(2)}) copy-start(bf16[3,3,3,128,256]{4,3,2,1,0:T(8,128)(2,1)} %param.11) | copy-start | bytes 5308420
  37.5 1.5 %copy-start.8 = (bf16[256,256]{1,0:T(8,128)(2,1)S(1)}, bf16[256,256]{1,0:T(8,128)(2,1)}, u32[]{:S(2)}) copy-start(bf16[256,256]{1,0:T(8,128)(2,1)} %constant.36.clone.order) | copy-start | bytes 393220
  37.6 1.5 %copy-start.10 = (s32[7]{0:T(128)S(1)}, s32[7]{0:T(128)}, u32[]{:S(2)}) copy-start(s32[7]{0:T(128)} %stack.31.marks.marks_ref) | copy-start | bytes 88
  39.1 18.6 %copy-start.5 = (bf16[3,3,3,256,32]{3,4,2,1,0:T(8,128)(2,1)S(1)}, bf16[3,3,3,256,32]{3,4,2,1,0:T(8,128)(2,1)}, u32[]{:S(2)}) copy-start(bf16[3,3,3,256,32]{3,4,2,1,0:T(8,128)(2,1)} %param.12) | copy-start | bytes 1327108
  42.4 30.8 %copy-start.3 = (bf16[3,3,3,512,32]{3,4,2,1,0:T(8,128)(2,1)S(1)}, bf16[3,3,3,512,32]{3,4,2,1,0:T(8,128)(2,1)}, u32[]{:S(2)}) copy-start(bf16[3,3,3,512,32]{3,4,2,1,0:T(8,128)(2,1)} %param.13) | copy-start | bytes 2654212
  42.4 15.2 %all-to-all-start = ((bf16[16,16,256]{2,1,0:T(8,128)(2,1)}), bf16[16,16,256]{2,1,0:T(8,128)(2,1)S(1)}, u32[]{:S(2)}, u32[]{:S(2)}) async-start(bf16[16,16,256]{2,1,0:T(8,128)(2,1)} %get-tuple-element.15), calls=%async_computation | async-start | bytes 262144 | tf_op jit(solution)/shard_map/all_to_all | solution.py:387
  48.4 2.1 %collective-permute-start.2 = (bf16[48,256]{1,0:T(8,128)(2,1)S(1)}, bf16[48,256]{1,0:T(8,128)(2,1)S(1)}, u32[]{:S(2)}, u32[]{:S(2)}) collective-permute-start(bf16[48,256]{1,0:T(8,128)(2,1)S(1)} %get-tuple-element.16), channel_id=1, source_target_pairs={{0,1},{1,0},{2,3},{3,2},{4,5},{5,4},{6,7},{7,6},{8,9},{9,8},{10,11... | collective-permute-start | bytes 73736 | tf_op jit(solution)/shard_map/ppermute | solution.py:471
  48.6 3.2 %collective-permute-start.3 = (bf16[48,256]{1,0:T(8,128)(2,1)S(1)}, bf16[48,256]{1,0:T(8,128)(2,1)S(1)}, u32[]{:S(2)}, u32[]{:S(2)}) collective-permute-start(bf16[48,256]{1,0:T(8,128)(2,1)S(1)} %get-tuple-element.17), channel_id=1, source_target_pairs={{0,2},{1,3},{2,0},{3,1},{4,6},{5,7},{6,4},{7,5},{8,10},{9,11},{10,... | collective-permute-start | bytes 73736 | tf_op jit(solution)/shard_map/ppermute | solution.py:471
  50.2 3.9 %collective-permute-start.4 = (bf16[48,256]{1,0:T(8,128)(2,1)S(1)}, bf16[48,256]{1,0:T(8,128)(2,1)S(1)}, u32[]{:S(2)}, u32[]{:S(2)}) collective-permute-start(bf16[48,256]{1,0:T(8,128)(2,1)S(1)} %get-tuple-element.18), channel_id=1, source_target_pairs={{0,3},{1,2},{2,1},{3,0},{4,7},{5,6},{6,5},{7,4},{8,11},{9,10},{10,... | collective-permute-start | bytes 73736 | tf_op jit(solution)/shard_map/ppermute | solution.py:471
  58.9 14.2 %all-to-all-start.1 = ((bf16[16,32,256]{2,1,0:T(8,128)(2,1)}), bf16[16,32,256]{2,1,0:T(8,128)(2,1)S(1)}, u32[]{:S(2)}, u32[]{:S(2)}) async-start(bf16[16,32,256]{2,1,0:T(8,128)(2,1)} %shard_map.95), calls=%async_computation.1 | async-start | bytes 524288 | tf_op jit(solution)/shard_map/all_to_all | solution.py:387
  63.7 20.9 %copy-start.6 = (bf16[2112,256]{1,0:T(8,128)(2,1)S(1)}, bf16[2112,256]{1,0:T(8,128)(2,1)}, u32[]{:S(2)}) copy-start(bf16[2112,256]{1,0:T(8,128)(2,1)} %all-gather.3.cloned.1.call-done) | copy-start | bytes 3244036
  65.8 18.8 %collective-permute-start.5 = (bf16[4,336,256]{2,1,0:T(8,128)(2,1)}, bf16[4,336,256]{2,1,0:T(8,128)(2,1)S(1)}, u32[]{:S(2)}, u32[]{:S(2)}) collective-permute-start(bf16[4,336,256]{2,1,0:T(8,128)(2,1)} %slice.4), channel_id=1, source_target_pairs={{0,16},{16,0},{1,17},{17,1},{2,18},{18,2},{3,19},{19,3},{4,20},{20... | collective-permute-start | bytes 2064392 | tf_op jit(solution)/shard_map/ppermute | solution.py:489
  84.6 10.9 %copy-start.4 = (bf16[2,2,2,256,128]{4,3,2,1,0:T(8,128)(2,1)S(1)}, bf16[2,2,2,256,128]{4,3,2,1,0:T(8,128)(2,1)}, u32[]{:S(2)}) copy-start(bf16[2,2,2,256,128]{4,3,2,1,0:T(8,128)(2,1)} %param.16) | copy-start | bytes 1572868
Sparse Core Ops, SparseCore 0:
  29.4 33.8 all-gather.2

commit v10 on v9

--- a/solution.py
+++ b/solution.py
@@ -77,23 +77,23 @@
     return dot(left, weights)
 
 
-def front_stage(marks, volume, decode, off_chip, on_chip, *refs):
-    block, done = refs if len(refs) == 2 else (None, refs[0])
-    odd, rep = marks[4], marks[1]
-    pairs = [
-        (volume.at[pl.ds(odd, 3)], off_chip),
-        (volume.at[pl.ds(1 - odd, 3)], on_chip),
-    ]
-    if block is not None:
-        pairs += [
-            (decode.at[pl.ds(pl.multiple_of(528 * rep, 16), 336)], block.at[pl.ds(0, 336)]),
-            (decode.at[pl.ds(336, 192)], block.at[pl.ds(336, 192)]),
+def front_stage(odd, rep, volume, decode, off_chip, on_chip, whole, *refs):
+    copies = []
+    if len(refs) == 2:
+        block, done = refs
+        at = pl.multiple_of(528 * rep[0], 16)
+        copies = [
+            pltpu.make_async_copy(decode.at[pl.ds(at, 336)], block.at[pl.ds(0, 336)], done.at[0]),
+            pltpu.make_async_copy(
+                decode.at[pl.ds(336, 192)], block.at[pl.ds(336, 192)], done.at[1]
+            ),
         ]
-    copies = [
-        pltpu.make_async_copy(source, target, done.at[i]) for i, (source, target) in enumerate(pairs)
-    ]
     for copy in copies:
         copy.start()
+    for s in range(3):
+        off_chip[s] = jnp.where(odd[0] == 0, volume[s], volume[s + 1])
+        on_chip[s] = jnp.where(odd[0] == 0, volume[s + 1], volume[s])
+    whole[...] = volume[...]
     for copy in copies:
         copy.wait()
 
@@ -412,14 +412,22 @@
     shared = lax.axis_size("rep") == 2 and chans == 32
     ride = chans == 32
     halo = bf16((3, 16, 16, 128))
-    off_chip, on_chip, *share = pl.pallas_call(
+    in_spaces = [pltpu.SMEM, pltpu.SMEM, pltpu.VMEM, pl.ANY]
+    out_spaces = [pltpu.VMEM] * 3 + [pl.ANY] * shared
+    off_chip, on_chip, volume, *share = pl.pallas_call(
         front_stage,
-        out_shape=(halo, halo) + ((bf16((528, 256)),) if shared else ()),
-        in_specs=[pl.BlockSpec(memory_space=pltpu.SMEM)] + [pl.BlockSpec(memory_space=pl.ANY)] * 2,
-        out_specs=(pl.BlockSpec(memory_space=pl.ANY),) * (3 if shared else 2),
-        scratch_shapes=[pltpu.SemaphoreType.DMA((4,))],
-        compiler_params=pltpu.CompilerParams(vmem_limit_bytes=60 * MIB),
-    )(marks, volume, decode_block)
+        out_shape=(halo, halo, bf16(volume.shape)) + (bf16((528, 256)),) * shared,
+        in_specs=[pl.BlockSpec(memory_space=space) for space in in_spaces],
+        out_specs=tuple(pl.BlockSpec(memory_space=space) for space in out_spaces),
+        scratch_shapes=[pltpu.SemaphoreType.DMA((2,))],
+        compiler_params=pltpu.CompilerParams(vmem_limit_bytes=16 * MIB),
+        cost_estimate=pl.CostEstimate(flops=3 * 10**9, bytes_accessed=10**6, transcendentals=0),
+    )(
+        (place % 2).astype(jnp.int32).reshape(1),
+        rep.astype(jnp.int32).reshape(1),
+        volume,
+        decode_block,
+    )
     pairs = [(i, i + 1) for i in range(1, n - 1, 2)]
     off_chip = lax.ppermute(off_chip, ALL, pairs + [(j, i) for i, j in pairs])
     on_chip = lax.ppermute(on_chip, ALL, [(i, i ^ 1) for i in range(n)])

time: 105 us -> 88.3 us (0.84)
  Pallas kernels: 34 us -> 14.6 us
  waiting for transfers between devices: 13.2 us -> 15.5 us
    pallas_call x1, Pallas kernels: 22 us -> 1.46 us  [body(): pl.pallas_call(front_stage, out_shape=(halo, halo, bf16(volume.shape)) +...]
    ppermute x1, waiting for transfers between devices: 0.01 us -> 2.04 us  [body(): off_chip = lax.ppermute(off_chip, ALL, pairs + [(j, i) for i, j in pairs])]
    pallas_call x7, Pallas kernels: 12 us -> 13.1 us  [call(): pl.pallas_call(kernel, out_shape=outs, in_specs=[pl.BlockSpec(memory_spac...]
    unnamed x22 -> x24, local copies, waits for them, and re-layouts: 2.35 us -> 2.7 us
  transfers between devices with their start and end apart: 9 -> 9, of which waited for: 4 -> 5; matrix products, arithmetic and copies ran while one was open for 2% -> 3% of each run, Pallas kernels for 8% -> 11%
where the time goes in v10:
time: 88.3 us; the launch traced here: 86.8 us
  starting transfers between devices  19.5 us (22%)
  blocking collectives  18.7 us (21%)
  waiting for transfers between devices  15.5 us (18%)
  Pallas kernels  14.6 us (17%)
  between operations  13.5 us (15%)
  local copies, waits for them, and re-layouts  4.91 us (6%)
    all_to_all x2, blocking collectives, exchange(): lax.all_to_all(payload, axis, split_axis=0, concat_axis=0, tiled=True)  18.7 us
    pallas_call x7, Pallas kernels, call(): pl.pallas_call(kernel, out_shape=outs, in_specs=[pl.BlockSpec(memory_spac...  13.1 us
    all_to_all x2, starting transfers between devices, exchange(): lax.all_to_all(payload, axis, split_axis=0, concat_axis=0, tiled=True)  11.6 us
    all_to_all x2, waiting for transfers between devices, exchange(): lax.all_to_all(payload, axis, split_axis=0, concat_axis=0, tiled=True)  9.93 us
    ppermute x1, starting transfers between devices, body(): off_chip = lax.ppermute(off_chip, ALL, pairs + [(j, i) for i, j in pairs])  4.67 us
    ppermute x3, waiting for transfers between devices, body(): lax.ppermute(skips[k], 'r', [(r, r ^ k) for r in range(GROUP)])  3.48 us
    unnamed x24, local copies, waits for them, and re-layouts  2.7 us
    ppermute x3, starting transfers between devices, body(): lax.ppermute(skips[k], 'r', [(r, r ^ k) for r in range(GROUP)])  2.14 us
  transfers between devices with their start and end apart: 9, of which 5 were waited for; matrix products, arithmetic and copies ran while one was open for 3% of the time, Pallas kernels for 11%

profile of v10, /device:TPU:1, one launch (start us, length us, event | category | flops | bytes accessed | tf_op | source)
XLA Modules:
  0.0 86.8 jit_solution(7406336703008547613)
XLA Ops:
  6.5 1.0 %copy-done.8 = bf16[3,3,3,32,256]{4,3,2,1,0:T(8,128)(2,1)S(1)} copy-done((bf16[3,3,3,32,256]{4,3,2,1,0:T(8,128)(2,1)S(1)}, bf16[3,3,3,32,256]{4,3,2,1,0:T(8,128)(2,1)}, u32[]{:S(2)}) %copy-start.8) | copy-done | bytes 442392
  7.6 0.9 %copy-done.9 = bf16[4,16,16,128]{3,2,1,0:T(8,128)(2,1)S(1)} copy-done((bf16[4,16,16,128]{3,2,1,0:T(8,128)(2,1)S(1)}, bf16[4,16,16,128]{3,2,1,0:T(8,128)(2,1)}, u32[]{:S(2)}) %copy-start.9) | copy-done | bytes 262168
  8.5 1.5 %shard_map.91 = (bf16[3,16,16,128]{3,2,1,0:T(8,128)(2,1)}, bf16[3,16,16,128]{3,2,1,0:T(8,128)(2,1)}, bf16[4,16,16,128]{3,2,1,0:T(8,128)(2,1)S(1)}, bf16[528,256]{1,0:T(8,128)(2,1)}) custom-call(s32[1]{0:T(128)} %bitcast.4.odd, s32[1]{0:T(128)} %bitcast.1.rep, bf16[4,16,16,128]{3,2,1,0:T(8,128)(2,1)S(1)} %copy-done.9, bf16[864,256]{1,0:T(8,128)(2,1)S(1)} %bitcast.35), custom_call_target="tpu_custom_call" | custom-call | flops 3000000000 | bytes 1000000 | tf_op jit(solution)/shard_map/pallas_call | solution.py:417
  10.0 0.0 copy-start.10
  10.0 0.7 copy-done.10
  10.7 0.0 all-gather.3.cloned.1.call-update
  10.7 4.7 %collective-permute-start = (bf16[3,16,16,128]{3,2,1,0:T(8,128)(2,1)}, bf16[3,16,16,128]{3,2,1,0:T(8,128)(2,1)}, u32[]{:S(2)}, u32[]{:S(2)}) collective-permute-start(bf16[3,16,16,128]{3,2,1,0:T(8,128)(2,1)} %get-tuple-element.14), channel_id=1, source_target_pairs={{1,2},{3,4},{5,6},{7,8},{9,10},{11,12},{13,14},{2,1},{4,3},{6,5},{... | collective-permute-start | bytes 589832 | tf_op jit(solution)/shard_map/ppermute | solution.py:432
  15.4 0.1 collective-permute-start.1
  15.5 0.1 stack.31.marks_ref.marks
  15.6 1.3 %shard_map.93._.rise = bf16[512,512]{1,0:T(8,128)(2,1)S(1)} custom-call(s32[7]{0:T(128)S(1)} %stack.31.marks_ref.marks, bf16[8,512,256]{2,1,0:T(8,128)(2,1)S(1)} %bitcast.23), custom_call_target="tpu_custom_call" | custom-call | flops 134217728 | bytes 2097180 | tf_op jit(solution)/shard_map/pallas_call | solution.py:18
  16.9 0.0 copy-start.7
  16.9 1.4 %shard_map.92.own = f32[4,256,256]{2,1,0:T(8,128)S(1)} custom-call(bf16[4,16,16,128]{3,2,1,0:T(8,128)(2,1)S(1)} %copy-done.11, bf16[3,1152,128]{2,1,0:T(8,128)(2,1)S(1)} %bitcast.26), custom_call_target="tpu_custom_call" | custom-call | flops 1207959552 | bytes 1146880 | tf_op jit(solution)/shard_map/pallas_call | solution.py:18
  18.4 2.0 %collective-permute-done.off_chip = bf16[3,16,16,128]{3,2,1,0:T(8,128)(2,1)} collective-permute-done((bf16[3,16,16,128]{3,2,1,0:T(8,128)(2,1)}, bf16[3,16,16,128]{3,2,1,0:T(8,128)(2,1)}, u32[]{:S(2)}, u32[]{:S(2)}) %collective-permute-start) | collective-permute-done | bytes 196640 | tf_op jit(solution)/shard_map/ppermute | solution.py:432
  20.4 3.9 %shard_map.94 = (bf16[16,16,256]{2,1,0:T(8,128)(2,1)}, bf16[48,256]{1,0:T(8,128)(2,1)S(1)}, bf16[48,256]{1,0:T(8,128)(2,1)S(1)}, bf16[48,256]{1,0:T(8,128)(2,1)S(1)}, bf16[48,256]{1,0:T(8,128)(2,1)S(1)}) custom-call(s32[7]{0:T(128)S(1)} %stack.31.marks_ref.marks, bf16[3,16,16,128]{3,2,1,0:T(8,128)(2,1)} %collective-permute-done.off_chip, ...), custom_call_target="tpu_custom_call" | custom-call | flops 1207959552 | bytes 4227100 | tf_op jit(solution)/shard_map/pallas_call | solution.py:18
  24.3 6.3 %all-to-all-start = ((bf16[16,16,256]{2,1,0:T(8,128)(2,1)}), bf16[16,16,256]{2,1,0:T(8,128)(2,1)S(1)}, u32[]{:S(2)}, u32[]{:S(2)}) async-start(bf16[16,16,256]{2,1,0:T(8,128)(2,1)} %get-tuple-element.17), calls=%async_computation | async-start | bytes 262144 | tf_op jit(solution)/shard_map/all_to_all | solution.py:387
  30.6 0.2 collective-permute-start.2
  30.8 1.6 %collective-permute-start.3 = (bf16[48,256]{1,0:T(8,128)(2,1)S(1)}, bf16[48,256]{1,0:T(8,128)(2,1)S(1)}, u32[]{:S(2)}, u32[]{:S(2)}) collective-permute-start(bf16[48,256]{1,0:T(8,128)(2,1)S(1)} %get-tuple-element.19), channel_id=1, source_target_pairs={{0,2},{1,3},{2,0},{3,1},{4,6},{5,7},{6,4},{7,5},{8,10},{9,11},{10,... | collective-permute-start | bytes 73736 | tf_op jit(solution)/shard_map/ppermute | solution.py:479
  32.4 0.4 collective-permute-start.4
  32.7 1.2 %collective-permute-done.3.refs_1_.refs_2_ = bf16[48,256]{1,0:T(8,128)(2,1)S(1)} collective-permute-done((bf16[48,256]{1,0:T(8,128)(2,1)S(1)}, bf16[48,256]{1,0:T(8,128)(2,1)S(1)}, u32[]{:S(2)}, u32[]{:S(2)}) %collective-permute-start.3) | collective-permute-done | bytes 24608 | tf_op jit(solution)/shard_map/ppermute | solution.py:479
  34.0 2.2 %collective-permute-done.4.refs_2_.refs_3_ = bf16[48,256]{1,0:T(8,128)(2,1)S(1)} collective-permute-done((bf16[48,256]{1,0:T(8,128)(2,1)S(1)}, bf16[48,256]{1,0:T(8,128)(2,1)S(1)}, u32[]{:S(2)}, u32[]{:S(2)}) %collective-permute-start.4) | collective-permute-done | bytes 24608 | tf_op jit(solution)/shard_map/ppermute | solution.py:479
  36.2 3.6 %all-to-all-done = bf16[16,16,256]{2,1,0:T(8,128)(2,1)S(1)} async-done(((bf16[16,16,256]{2,1,0:T(8,128)(2,1)}), bf16[16,16,256]{2,1,0:T(8,128)(2,1)S(1)}, u32[]{:S(2)}, u32[]{:S(2)}) %all-to-all-start) | async-done | bytes 131104 | tf_op jit(solution)/shard_map/all_to_all | solution.py:387
  39.9 1.3 %shard_map.95 = bf16[16,32,256]{2,1,0:T(8,128)(2,1)} custom-call(bf16[256,256]{1,0:T(8,128)(2,1)S(1)} %bitcast.29, bf16[864,256]{1,0:T(8,128)(2,1)S(1)} %bitcast.31, bf16[48,256]{1,0:T(8,128)(2,1)S(1)} %collective-permute-done.2.refs_0_.refs_1_, bf16[48,256]{1,0:T(8,128)(2,1)S(1)} %collective-permute-done.3.refs_1_.refs_2_, ...), custom_call_target="tpu_custom_call" | custom-call | flops 113246208 | bytes 573440 | tf_op jit(solution)/shard_map/pallas_call | solution.py:18
  41.1 5.3 %all-to-all-start.1 = ((bf16[16,32,256]{2,1,0:T(8,128)(2,1)}), bf16[16,32,256]{2,1,0:T(8,128)(2,1)S(1)}, u32[]{:S(2)}, u32[]{:S(2)}) async-start(bf16[16,32,256]{2,1,0:T(8,128)(2,1)} %shard_map.95), calls=%async_computation.1 | async-start | bytes 524288 | tf_op jit(solution)/shard_map/all_to_all | solution.py:387
  46.4 0.0 all-gather.3.cloned.1.call-done
  46.5 2.1 %slice.4 = bf16[4,336,256]{2,1,0:T(8,128)(2,1)} slice(bf16[4,528,256]{2,1,0:T(8,128)(2,1)} %bitcast.32), slice={[0:4], [0:336], [0:256]} | slice | bytes 1376256 | tf_op jit(solution)/shard_map/slice | solution.py:497
  48.6 1.0 %collective-permute-start.5 = (bf16[4,336,256]{2,1,0:T(8,128)(2,1)}, bf16[4,336,256]{2,1,0:T(8,128)(2,1)}, u32[]{:S(2)}, u32[]{:S(2)}) collective-permute-start(bf16[4,336,256]{2,1,0:T(8,128)(2,1)} %slice.4), channel_id=1, source_target_pairs={{0,16},{16,0},{1,17},{17,1},{2,18},{18,2},{3,19},{19,3},{4,20},{20... | collective-permute-start | bytes 2064392 | tf_op jit(solution)/shard_map/ppermute | solution.py:497
  49.6 6.3 %all-to-all-done.1 = bf16[16,32,256]{2,1,0:T(8,128)(2,1)S(1)} async-done(((bf16[16,32,256]{2,1,0:T(8,128)(2,1)}), bf16[16,32,256]{2,1,0:T(8,128)(2,1)S(1)}, u32[]{:S(2)}, u32[]{:S(2)}) %all-to-all-start.1) | async-done | bytes 262176 | tf_op jit(solution)/shard_map/all_to_all | solution.py:387
  55.9 1.3 %shard_map.96 = bf16[16,32,128]{2,1,0:T(8,128)(2,1)S(1)} custom-call(s32[7]{0:T(128)S(1)} %stack.31.marks_ref.marks, bf16[512,256]{1,0:T(8,128)(2,1)S(1)} %bitcast.25, bf16[864,512]{1,0:T(8,128)(2,1)S(1)} %bitcast.28, bf16[48,256]{1,0:T(8,128)(2,1)S(1)} %get-tuple-element.21.refs_0_, bf16[48,256]{1,0:T(8,128)(2,1)S(1)} %collective-permute-done.2.refs_0_.refs_1_, ...), custom_call_target="tpu_custom_call" | custom-call | flops 226492416 | bytes 1245212 | tf_op jit(solution)/shard_map/pallas_call | solution.py:18
  57.2 10.2 %all_to_all.20.deeper = bf16[16,32,128]{2,1,0:T(8,128)(2,1)S(1)} all-to-all(bf16[16,32,128]{2,1,0:T(8,128)(2,1)S(1)} %shard_map.96), channel_id=1, replica_groups=mesh['rep'=2,'z'=4,'r'=4] {'z','r'}, dimensions={0} | all-to-all | bytes 262144 | tf_op jit(solution)/shard_map/all_to_all | solution.py:387
  67.4 2.9 %shard_map.97 = bf16[512,256]{1,0:T(8,128)(2,1)S(1)} custom-call(s32[7]{0:T(128)S(1)} %stack.31.marks_ref.marks, bf16[16,32,128]{2,1,0:T(8,128)(2,1)S(1)} %all_to_all.20.deeper, bf16[512,512]{1,0:T(8,128)(2,1)S(1)} %shard_map.93._.rise, bf16[48,256]{1,0:T(8,128)(2,1)S(1)} %get-tuple-element.21.refs_0_, ...), custom_call_target="tpu_custom_call" | custom-call | flops 905969664 | bytes 2523164 | tf_op jit(solution)/shard_map/pallas_call | solution.py:18
  70.3 8.6 %all_to_all.21.partials = bf16[4,128,256]{2,1,0:T(8,128)(2,1)S(1)} all-to-all(bf16[4,128,256]{2,1,0:T(8,128)(2,1)S(1)} %bitcast.34), channel_id=1, replica_groups=mesh['rep'=2,'z'=4,'r'=4] {'r'}, dimensions={0} | all-to-all | bytes 524288 | tf_op jit(solution)/shard_map/all_to_all | solution.py:387
  78.9 1.1 %shard_map.98 = bf16[1024,128]{1,0:T(8,128)(2,1)} custom-call(bf16[4,128,256]{2,1,0:T(8,128)(2,1)S(1)} %all_to_all.21.partials, bf16[8,256,128]{2,1,0:T(8,128)(2,1)S(1)} %bitcast.30), custom_call_target="tpu_custom_call" | custom-call | flops 67108864 | bytes 786432 | tf_op jit(solution)/shard_map/pallas_call | solution.py:18
  (23 shorter events, 0.0 us)
Async XLA Ops:
  6.5 39.9 %all-gather.3.cloned.1.call-start = ((), (), s32[]{:S(2)}) async-start(), calls=%async_computation.4 | async-start | bytes 1351680 | tf_op jit(solution)/shard_map/all_gather | solution.py:436
  6.5 1.0 %copy-start.8 = (bf16[3,3,3,32,256]{4,3,2,1,0:T(8,128)(2,1)S(1)}, bf16[3,3,3,32,256]{4,3,2,1,0:T(8,128)(2,1)}, u32[]{:S(2)}) copy-start(bf16[3,3,3,32,256]{4,3,2,1,0:T(8,128)(2,1)} %param.15) | copy-start | bytes 1327108
  7.6 0.9 %copy-start.9 = (bf16[4,16,16,128]{3,2,1,0:T(8,128)(2,1)S(1)}, bf16[4,16,16,128]{3,2,1,0:T(8,128)(2,1)}, u32[]{:S(2)}) copy-start(bf16[4,16,16,128]{3,2,1,0:T(8,128)(2,1)} %volume.1) | copy-start | bytes 786436
  8.5 7.1 %copy-start = (bf16[2,2,2,512,256]{4,3,2,1,0:T(8,128)(2,1)S(1)}, bf16[2,2,2,512,256]{4,3,2,1,0:T(8,128)(2,1)}, u32[]{:S(2)}) copy-start(bf16[2,2,2,512,256]{4,3,2,1,0:T(8,128)(2,1)} %param.14) | copy-start | bytes 6291460
  10.0 0.7 copy-start.10
  10.7 6.2 %copy-start.2 = (bf16[3,3,3,128,128]{4,3,2,1,0:T(8,128)(2,1)S(1)}, bf16[3,3,3,128,128]{4,3,2,1,0:T(8,128)(2,1)}, u32[]{:S(2)}) copy-start(bf16[3,3,3,128,128]{4,3,2,1,0:T(8,128)(2,1)} %param.10) | copy-start | bytes 2654212
  10.7 9.7 %collective-permute-start = (bf16[3,16,16,128]{3,2,1,0:T(8,128)(2,1)}, bf16[3,16,16,128]{3,2,1,0:T(8,128)(2,1)}, u32[]{:S(2)}, u32[]{:S(2)}) collective-permute-start(bf16[3,16,16,128]{3,2,1,0:T(8,128)(2,1)} %get-tuple-element.14), channel_id=1, source_target_pairs={{1,2},{3,4},{5,6},{7,8},{9,10},{11,12},{13,14},{2,1},{4,3},{6,5},{... | collective-permute-start | bytes 589832 | tf_op jit(solution)/shard_map/ppermute | solution.py:432
  15.4 5.0 %collective-permute-start.1 = (bf16[3,16,16,128]{3,2,1,0:T(8,128)(2,1)}, bf16[3,16,16,128]{3,2,1,0:T(8,128)(2,1)}, u32[]{:S(2)}, u32[]{:S(2)}) collective-permute-start(bf16[3,16,16,128]{3,2,1,0:T(8,128)(2,1)} %get-tuple-element.15), channel_id=1, source_target_pairs={{0,1},{1,0},{2,3},{3,2},{4,5},{5,4},{6,7},{7,6},{8,9},{9,8},{10,11... | collective-permute-start | bytes 589832 | tf_op jit(solution)/shard_map/ppermute | solution.py:433
  15.6 1.3 %copy-start.11 = (bf16[4,16,16,128]{3,2,1,0:T(8,128)(2,1)S(1)}, bf16[4,16,16,128]{3,2,1,0:T(8,128)(2,1)}, u32[]{:S(2)}) copy-start(bf16[4,16,16,128]{3,2,1,0:T(8,128)(2,1)} %copy-done.10) | copy-start | bytes 786436
  16.9 3.5 %copy-start.1 = (bf16[3,3,3,128,256]{4,3,2,1,0:T(8,128)(2,1)S(1)}, bf16[3,3,3,128,256]{4,3,2,1,0:T(8,128)(2,1)}, u32[]{:S(2)}) copy-start(bf16[3,3,3,128,256]{4,3,2,1,0:T(8,128)(2,1)} %param.11) | copy-start | bytes 5308420
  16.9 3.5 %copy-start.7 = (bf16[256,256]{1,0:T(8,128)(2,1)S(1)}, bf16[256,256]{1,0:T(8,128)(2,1)}, u32[]{:S(2)}) copy-start(bf16[256,256]{1,0:T(8,128)(2,1)} %constant.38.clone.order) | copy-start | bytes 393220
  20.4 19.4 %copy-start.5 = (bf16[3,3,3,256,32]{3,4,2,1,0:T(8,128)(2,1)S(1)}, bf16[3,3,3,256,32]{3,4,2,1,0:T(8,128)(2,1)}, u32[]{:S(2)}) copy-start(bf16[3,3,3,256,32]{3,4,2,1,0:T(8,128)(2,1)} %param.12) | copy-start | bytes 1327108
  24.3 31.6 %copy-start.3 = (bf16[3,3,3,512,32]{3,4,2,1,0:T(8,128)(2,1)S(1)}, bf16[3,3,3,512,32]{3,4,2,1,0:T(8,128)(2,1)}, u32[]{:S(2)}) copy-start(bf16[3,3,3,512,32]{3,4,2,1,0:T(8,128)(2,1)} %param.13) | copy-start | bytes 2654212
  24.3 15.6 %all-to-all-start = ((bf16[16,16,256]{2,1,0:T(8,128)(2,1)}), bf16[16,16,256]{2,1,0:T(8,128)(2,1)S(1)}, u32[]{:S(2)}, u32[]{:S(2)}) async-start(bf16[16,16,256]{2,1,0:T(8,128)(2,1)} %get-tuple-element.17), calls=%async_computation | async-start | bytes 262144 | tf_op jit(solution)/shard_map/all_to_all | solution.py:387
  30.6 2.1 %collective-permute-start.2 = (bf16[48,256]{1,0:T(8,128)(2,1)S(1)}, bf16[48,256]{1,0:T(8,128)(2,1)S(1)}, u32[]{:S(2)}, u32[]{:S(2)}) collective-permute-start(bf16[48,256]{1,0:T(8,128)(2,1)S(1)} %get-tuple-element.18), channel_id=1, source_target_pairs={{0,1},{1,0},{2,3},{3,2},{4,5},{5,4},{6,7},{7,6},{8,9},{9,8},{10,11... | collective-permute-start | bytes 73736 | tf_op jit(solution)/shard_map/ppermute | solution.py:479
  30.8 3.2 %collective-permute-start.3 = (bf16[48,256]{1,0:T(8,128)(2,1)S(1)}, bf16[48,256]{1,0:T(8,128)(2,1)S(1)}, u32[]{:S(2)}, u32[]{:S(2)}) collective-permute-start(bf16[48,256]{1,0:T(8,128)(2,1)S(1)} %get-tuple-element.19), channel_id=1, source_target_pairs={{0,2},{1,3},{2,0},{3,1},{4,6},{5,7},{6,4},{7,5},{8,10},{9,11},{10,... | collective-permute-start | bytes 73736 | tf_op jit(solution)/shard_map/ppermute | solution.py:479
  32.4 3.9 %collective-permute-start.4 = (bf16[48,256]{1,0:T(8,128)(2,1)S(1)}, bf16[48,256]{1,0:T(8,128)(2,1)S(1)}, u32[]{:S(2)}, u32[]{:S(2)}) collective-permute-start(bf16[48,256]{1,0:T(8,128)(2,1)S(1)} %get-tuple-element.20), channel_id=1, source_target_pairs={{0,3},{1,2},{2,1},{3,0},{4,7},{5,6},{6,5},{7,4},{8,11},{9,10},{10,... | collective-permute-start | bytes 73736 | tf_op jit(solution)/shard_map/ppermute | solution.py:479
  41.1 14.8 %all-to-all-start.1 = ((bf16[16,32,256]{2,1,0:T(8,128)(2,1)}), bf16[16,32,256]{2,1,0:T(8,128)(2,1)S(1)}, u32[]{:S(2)}, u32[]{:S(2)}) async-start(bf16[16,32,256]{2,1,0:T(8,128)(2,1)} %shard_map.95), calls=%async_computation.1 | async-start | bytes 524288 | tf_op jit(solution)/shard_map/all_to_all | solution.py:387
  46.4 20.9 %copy-start.6 = (bf16[2112,256]{1,0:T(8,128)(2,1)S(1)}, bf16[2112,256]{1,0:T(8,128)(2,1)}, u32[]{:S(2)}) copy-start(bf16[2112,256]{1,0:T(8,128)(2,1)} %all-gather.3.cloned.1.call-done) | copy-start | bytes 3244036
  48.6 18.8 %collective-permute-start.5 = (bf16[4,336,256]{2,1,0:T(8,128)(2,1)}, bf16[4,336,256]{2,1,0:T(8,128)(2,1)}, u32[]{:S(2)}, u32[]{:S(2)}) collective-permute-start(bf16[4,336,256]{2,1,0:T(8,128)(2,1)} %slice.4), channel_id=1, source_target_pairs={{0,16},{16,0},{1,17},{17,1},{2,18},{18,2},{3,19},{19,3},{4,20},{20... | collective-permute-start | bytes 2064392 | tf_op jit(solution)/shard_map/ppermute | solution.py:497
  67.4 11.5 %copy-start.4 = (bf16[2,2,2,256,128]{4,3,2,1,0:T(8,128)(2,1)S(1)}, bf16[2,2,2,256,128]{4,3,2,1,0:T(8,128)(2,1)}, u32[]{:S(2)}) copy-start(bf16[2,2,2,256,128]{4,3,2,1,0:T(8,128)(2,1)} %param.16) | copy-start | bytes 1572868
Sparse Core Ops, SparseCore 0:
  10.8 33.8 all-gather.2

commit v11 on v9

--- a/solution.py
+++ b/solution.py
@@ -77,16 +77,17 @@
     return dot(left, weights)
 
 
-def front_stage(marks, volume, decode, off_chip, on_chip, *refs):
-    block, done = refs if len(refs) == 2 else (None, refs[0])
-    odd, rep = marks[4], marks[1]
+def front_stage(odd, rep, volume, decode, off_chip, on_chip, *refs):
+    done = refs[-1]
     pairs = [
-        (volume.at[pl.ds(odd, 3)], off_chip),
-        (volume.at[pl.ds(1 - odd, 3)], on_chip),
+        (volume.at[pl.ds(odd[0], 3)], off_chip),
+        (volume.at[pl.ds(1 - odd[0], 3)], on_chip),
     ]
-    if block is not None:
+    if len(refs) == 2:
+        block = refs[0]
+        at = pl.multiple_of(528 * rep[0], 16)
         pairs += [
-            (decode.at[pl.ds(pl.multiple_of(528 * rep, 16), 336)], block.at[pl.ds(0, 336)]),
+            (decode.at[pl.ds(at, 336)], block.at[pl.ds(0, 336)]),
             (decode.at[pl.ds(336, 192)], block.at[pl.ds(336, 192)]),
         ]
     copies = [
@@ -225,8 +226,7 @@
     far_swap[...] = jnp.where(even, first, last).astype(jnp.bfloat16)
 
 
-def deep_stage(pooled, weights, *refs):
-    out = refs[-1]
+def deep_stage(pooled, weights, out):
     n, chans, voxels = out.shape
     deep = spread_taps(weights, pooled[...], ((1,), (1,)), chans, voxels).astype(jnp.bfloat16)
     for dest in range(n):
@@ -412,14 +412,21 @@
     shared = lax.axis_size("rep") == 2 and chans == 32
     ride = chans == 32
     halo = bf16((3, 16, 16, 128))
+    in_spaces = [pltpu.SMEM, pltpu.SMEM, pl.ANY, pl.ANY]
     off_chip, on_chip, *share = pl.pallas_call(
         front_stage,
-        out_shape=(halo, halo) + ((bf16((528, 256)),) if shared else ()),
-        in_specs=[pl.BlockSpec(memory_space=pltpu.SMEM)] + [pl.BlockSpec(memory_space=pl.ANY)] * 2,
-        out_specs=(pl.BlockSpec(memory_space=pl.ANY),) * (3 if shared else 2),
+        out_shape=(halo, halo) + (bf16((528, 256)),) * shared,
+        in_specs=[pl.BlockSpec(memory_space=space) for space in in_spaces],
+        out_specs=(pl.BlockSpec(memory_space=pltpu.VMEM),) * (2 + shared),
         scratch_shapes=[pltpu.SemaphoreType.DMA((4,))],
         compiler_params=pltpu.CompilerParams(vmem_limit_bytes=60 * MIB),
-    )(marks, volume, decode_block)
+        cost_estimate=pl.CostEstimate(flops=0, bytes_accessed=10**6, transcendentals=0),
+    )(
+        (place % 2).astype(jnp.int32).reshape(1),
+        rep.astype(jnp.int32).reshape(1),
+        volume,
+        decode_block,
+    )
     pairs = [(i, i + 1) for i in range(1, n - 1, 2)]
     off_chip = lax.ppermute(off_chip, ALL, pairs + [(j, i) for i, j in pairs])
     on_chip = lax.ppermute(on_chip, ALL, [(i, i ^ 1) for i in range(n)])
@@ -479,11 +486,9 @@
         (
             pooled_whole.reshape(voxels, 256),
             deep_kernel.transpose(0, 1, 2, 4, 3).reshape(27 * chans, 256),
-            *near[1:],
         ),
         2 * 27 * chans * 256 * voxels,
         16,
-        unread=GROUP - 1,
     )
     if shared:
         weights = (line, lax.ppermute(line[:, :336], "rep", [(0, 1), (1, 0)]))

time: 105 us -> 85.3 us (0.81)
  Pallas kernels: 34 us -> 14.2 us
  blocking collectives: 18.7 us -> 35.1 us
  waiting for transfers between devices: 13.2 us -> 4.31 us
  starting transfers between devices: 18.8 us -> 12.9 us
  local copies, waits for them, and re-layouts: 5.11 us -> 3.82 us
    pallas_call x1, Pallas kernels: 22 us -> 2.11 us  [body(): pl.pallas_call(front_stage, out_shape=(halo, halo) + (bf16((528, 256)),)...]
    all_to_all x2 -> x3, blocking collectives: 18.7 us -> 35.1 us  [exchange(): lax.all_to_all(payload, axis, split_axis=0, concat_axis=0, tiled=True)]
    all_to_all x2 -> x1, waiting for transfers between devices: 9.74 us -> 0.01 us  [exchange(): lax.all_to_all(payload, axis, split_axis=0, concat_axis=0, tiled=True)]
    all_to_all x2 -> x1, starting transfers between devices: 10.7 us -> 4.73 us  [exchange(): lax.all_to_all(payload, axis, split_axis=0, concat_axis=0, tiled=True)]
    unnamed x22 -> x20, local copies, waits for them, and re-layouts: 2.35 us -> 1.63 us
  transfers between devices with their start and end apart: 9 -> 8, of which waited for: 4 -> 3; matrix products, arithmetic and copies ran while one was open for 2% -> 3% of each run, Pallas kernels for 8% -> 10%
where the time goes in v11:
time: 85.3 us; the launch traced here: 83.8 us
  blocking collectives  35.1 us (41%)
  Pallas kernels  14.2 us (17%)
  between operations  13.5 us (16%)
  starting transfers between devices  12.9 us (15%)
  waiting for transfers between devices  4.31 us (5%)
  local copies, waits for them, and re-layouts  3.82 us (4%)
    all_to_all x3, blocking collectives, exchange(): lax.all_to_all(payload, axis, split_axis=0, concat_axis=0, tiled=True)  35.1 us
    pallas_call x7, Pallas kernels, call(): pl.pallas_call(kernel, out_shape=outs, in_specs=[pl.BlockSpec(memory_spac...  12.1 us
    all_to_all x1, starting transfers between devices, exchange(): lax.all_to_all(payload, axis, split_axis=0, concat_axis=0, tiled=True)  4.73 us
    ppermute x1, starting transfers between devices, body(): off_chip = lax.ppermute(off_chip, ALL, pairs + [(j, i) for i, j in pairs])  4.54 us
    ppermute x3, waiting for transfers between devices, body(): lax.ppermute(skips[k], 'r', [(r, r ^ k) for r in range(GROUP)])  3.83 us
    ppermute x3, starting transfers between devices, body(): lax.ppermute(skips[k], 'r', [(r, r ^ k) for r in range(GROUP)])  2.26 us
    pallas_call x1, Pallas kernels, body(): pl.pallas_call(front_stage, out_shape=(halo, halo) + (bf16((528, 256)),)...  2.11 us
    slice x1, local copies, waits for them, and re-layouts, body(): weights = (line, lax.ppermute(line[:, :336], 'rep', [(0, 1), (1, 0)]))  2.1 us
  transfers between devices with their start and end apart: 8, of which 3 were waited for; matrix products, arithmetic and copies ran while one was open for 3% of the time, Pallas kernels for 10%

profile of v11, /device:TPU:1, one launch (start us, length us, event | category | flops | bytes accessed | tf_op | source)
XLA Modules:
  0.0 83.8 jit_solution(2389451630344525772)
XLA Ops:
  6.5 2.1 %shard_map.91 = (bf16[3,16,16,128]{3,2,1,0:T(8,128)(2,1)}, bf16[3,16,16,128]{3,2,1,0:T(8,128)(2,1)}, bf16[528,256]{1,0:T(8,128)(2,1)}) custom-call(s32[1]{0:T(128)} %bitcast.4.odd, s32[1]{0:T(128)} %bitcast.1.rep, bf16[4,16,16,128]{3,2,1,0:T(8,128)(2,1)} %volume.3, bf16[864,256]{1,0:T(8,128)(2,1)} %bitcast.35), custom_call_target="tpu_custom_call" | custom-call | bytes 1000000 | tf_op jit(solution)/shard_map/pallas_call | solution.py:416
  8.7 0.0 all-gather.3.cloned.1.call-update
  8.7 4.5 %collective-permute-start = (bf16[3,16,16,128]{3,2,1,0:T(8,128)(2,1)}, bf16[3,16,16,128]{3,2,1,0:T(8,128)(2,1)S(1)}, u32[]{:S(2)}, u32[]{:S(2)}) collective-permute-start(bf16[3,16,16,128]{3,2,1,0:T(8,128)(2,1)} %get-tuple-element.13), channel_id=1, source_target_pairs={{1,2},{3,4},{5,6},{7,8},{9,10},{11,12},{13,14},{2,1},{4,3},{6,5},{... | collective-permute-start | bytes 589832 | tf_op jit(solution)/shard_map/ppermute | solution.py:431
  13.2 0.1 collective-permute-start.1
  13.3 0.1 stack.31.marks_ref.marks
  13.4 1.6 %copy-done = bf16[2,2,2,512,256]{4,3,2,1,0:T(8,128)(2,1)S(1)} copy-done((bf16[2,2,2,512,256]{4,3,2,1,0:T(8,128)(2,1)S(1)}, bf16[2,2,2,512,256]{4,3,2,1,0:T(8,128)(2,1)}, u32[]{:S(2)}) %copy-start) | copy-done | bytes 2097176
  15.0 1.3 %shard_map.93._.rise = bf16[512,512]{1,0:T(8,128)(2,1)S(1)} custom-call(s32[7]{0:T(128)S(1)} %stack.31.marks_ref.marks, bf16[8,512,256]{2,1,0:T(8,128)(2,1)S(1)} %bitcast.23), custom_call_target="tpu_custom_call" | custom-call | flops 134217728 | bytes 2097180 | tf_op jit(solution)/shard_map/pallas_call | solution.py:18
  16.4 0.0 copy-start.1
  16.4 0.0 copy-start.8
  16.4 1.4 %shard_map.92.own = f32[4,256,256]{2,1,0:T(8,128)S(1)} custom-call(bf16[4,16,16,128]{3,2,1,0:T(8,128)(2,1)S(1)} %copy-done.7, bf16[3,1152,128]{2,1,0:T(8,128)(2,1)S(1)} %bitcast.26), custom_call_target="tpu_custom_call" | custom-call | flops 1207959552 | bytes 1146880 | tf_op jit(solution)/shard_map/pallas_call | solution.py:18
  17.8 0.4 collective-permute-done.off_chip
  18.2 0.0 collective-permute-done.1.on_chip
  18.3 3.5 %shard_map.94 = (bf16[16,16,256]{2,1,0:T(8,128)(2,1)S(1)}, bf16[48,256]{1,0:T(8,128)(2,1)S(1)}, bf16[48,256]{1,0:T(8,128)(2,1)}, bf16[48,256]{1,0:T(8,128)(2,1)}, bf16[48,256]{1,0:T(8,128)(2,1)S(1)}) custom-call(s32[7]{0:T(128)S(1)} %stack.31.marks_ref.marks, bf16[3,16,16,128]{3,2,1,0:T(8,128)(2,1)S(1)} %collective-permute-done.off_chip, ...), custom_call_target="tpu_custom_call" | custom-call | flops 1207959552 | bytes 4227100 | tf_op jit(solution)/shard_map/pallas_call | solution.py:18
  21.7 15.3 %all_to_all.20 = bf16[16,16,256]{2,1,0:T(8,128)(2,1)S(1)} all-to-all(bf16[16,16,256]{2,1,0:T(8,128)(2,1)S(1)} %get-tuple-element.15), channel_id=1, replica_groups=mesh['rep'=2,'z'=4,'r'=4] {'z','r'}, dimensions={0} | all-to-all | bytes 262144 | tf_op jit(solution)/shard_map/all_to_all | solution.py:387
  37.1 1.3 %shard_map.95 = bf16[16,32,256]{2,1,0:T(8,128)(2,1)} custom-call(bf16[256,256]{1,0:T(8,128)(2,1)S(1)} %bitcast.29, bf16[864,256]{1,0:T(8,128)(2,1)S(1)} %bitcast.31), custom_call_target="tpu_custom_call" | custom-call | flops 113246208 | bytes 573440 | tf_op jit(solution)/shard_map/pallas_call | solution.py:18
  38.4 4.7 %all-to-all-start.1 = ((bf16[16,32,256]{2,1,0:T(8,128)(2,1)}), bf16[16,32,256]{2,1,0:T(8,128)(2,1)S(1)}, u32[]{:S(2)}, u32[]{:S(2)}) async-start(bf16[16,32,256]{2,1,0:T(8,128)(2,1)} %shard_map.95), calls=%async_computation.1 | async-start | bytes 524288 | tf_op jit(solution)/shard_map/all_to_all | solution.py:387
  43.1 0.0 all-gather.3.cloned.1.call-done
  43.1 2.1 %slice.4 = bf16[4,336,256]{2,1,0:T(8,128)(2,1)} slice(bf16[4,528,256]{2,1,0:T(8,128)(2,1)} %bitcast.32), slice={[0:4], [0:336], [0:256]} | slice | bytes 1376256 | tf_op jit(solution)/shard_map/slice | solution.py:494
  45.2 1.3 %collective-permute-start.5 = (bf16[4,336,256]{2,1,0:T(8,128)(2,1)}, bf16[4,336,256]{2,1,0:T(8,128)(2,1)S(1)}, u32[]{:S(2)}, u32[]{:S(2)}) collective-permute-start(bf16[4,336,256]{2,1,0:T(8,128)(2,1)} %slice.4), channel_id=1, source_target_pairs={{0,16},{16,0},{1,17},{17,1},{2,18},{18,2},{3,19},{19,3},{4,20},{20... | collective-permute-start | bytes 2064392 | tf_op jit(solution)/shard_map/ppermute | solution.py:494
  46.5 0.6 collective-permute-start.2
  47.1 1.4 %collective-permute-start.3 = (bf16[48,256]{1,0:T(8,128)(2,1)}, bf16[48,256]{1,0:T(8,128)(2,1)S(1)}, u32[]{:S(2)}, u32[]{:S(2)}) collective-permute-start(bf16[48,256]{1,0:T(8,128)(2,1)} %get-tuple-element.18), channel_id=1, source_target_pairs={{0,2},{1,3},{2,0},{3,1},{4,6},{5,7},{6,4},{7,5},{8,10},{9,11},{10,... | collective-permute-start | bytes 73736 | tf_op jit(solution)/shard_map/ppermute | solution.py:478
  48.5 0.2 collective-permute-start.4
  48.8 0.0 collective-permute-done.2.refs_1_
  48.8 1.7 %collective-permute-done.3.refs_2_ = bf16[48,256]{1,0:T(8,128)(2,1)S(1)} collective-permute-done((bf16[48,256]{1,0:T(8,128)(2,1)}, bf16[48,256]{1,0:T(8,128)(2,1)S(1)}, u32[]{:S(2)}, u32[]{:S(2)}) %collective-permute-start.3) | collective-permute-done | bytes 24608 | tf_op jit(solution)/shard_map/ppermute | solution.py:478
  50.4 2.2 %collective-permute-done.4.refs_3_ = bf16[48,256]{1,0:T(8,128)(2,1)S(1)} collective-permute-done((bf16[48,256]{1,0:T(8,128)(2,1)}, bf16[48,256]{1,0:T(8,128)(2,1)S(1)}, u32[]{:S(2)}, u32[]{:S(2)}) %collective-permute-start.4) | collective-permute-done | bytes 24608 | tf_op jit(solution)/shard_map/ppermute | solution.py:478
  52.6 0.0 all-to-all-done.1
  52.6 1.3 %shard_map.96 = bf16[16,32,128]{2,1,0:T(8,128)(2,1)S(1)} custom-call(s32[7]{0:T(128)S(1)} %stack.31.marks_ref.marks, bf16[512,256]{1,0:T(8,128)(2,1)S(1)} %bitcast.25, bf16[864,512]{1,0:T(8,128)(2,1)S(1)} %bitcast.28, bf16[48,256]{1,0:T(8,128)(2,1)S(1)} %get-tuple-element.16.refs_0_, bf16[48,256]{1,0:T(8,128)(2,1)S(1)} %collective-permute-done.2.refs_1_, ...), custom_call_target="tpu_custom_call" | custom-call | flops 226492416 | bytes 1245212 | tf_op jit(solution)/shard_map/pallas_call | solution.py:18
  53.9 11.2 %all_to_all.21.deeper = bf16[16,32,128]{2,1,0:T(8,128)(2,1)S(1)} all-to-all(bf16[16,32,128]{2,1,0:T(8,128)(2,1)S(1)} %shard_map.96), channel_id=1, replica_groups=mesh['rep'=2,'z'=4,'r'=4] {'z','r'}, dimensions={0} | all-to-all | bytes 262144 | tf_op jit(solution)/shard_map/all_to_all | solution.py:387
  65.0 0.0 collective-permute-done.5.refs_5_
  65.1 2.3 %shard_map.97 = bf16[512,256]{1,0:T(8,128)(2,1)S(1)} custom-call(s32[7]{0:T(128)S(1)} %stack.31.marks_ref.marks, bf16[16,32,128]{2,1,0:T(8,128)(2,1)S(1)} %all_to_all.21.deeper, bf16[512,512]{1,0:T(8,128)(2,1)S(1)} %shard_map.93._.rise, bf16[48,256]{1,0:T(8,128)(2,1)S(1)} %get-tuple-element.16.refs_0_, bf16[48,256]{1,0:T(8,128)(2,1)S(1)} %collective-permute-done.2.refs_1_, ...), custom_call_target="tpu_custom_call" | custom-call | flops 905969664 | bytes 2523164 | tf_op jit(solution)/shard_map/pallas_call | solution.py:18
  67.4 8.5 %all_to_all.22.partials = bf16[4,128,256]{2,1,0:T(8,128)(2,1)S(1)} all-to-all(bf16[4,128,256]{2,1,0:T(8,128)(2,1)S(1)} %bitcast.34), channel_id=1, replica_groups=mesh['rep'=2,'z'=4,'r'=4] {'r'}, dimensions={0} | all-to-all | bytes 524288 | tf_op jit(solution)/shard_map/all_to_all | solution.py:387
  75.9 1.1 %shard_map.98 = bf16[1024,128]{1,0:T(8,128)(2,1)} custom-call(bf16[4,128,256]{2,1,0:T(8,128)(2,1)S(1)} %all_to_all.22.partials, bf16[8,256,128]{2,1,0:T(8,128)(2,1)S(1)} %bitcast.30), custom_call_target="tpu_custom_call" | custom-call | flops 67108864 | bytes 786432 | tf_op jit(solution)/shard_map/pallas_call | solution.py:18
  (18 shorter events, 0.0 us)
Async XLA Ops:
  6.5 36.6 %all-gather.3.cloned.1.call-start = ((), (), s32[]{:S(2)}) async-start(), calls=%async_computation.4 | async-start | bytes 1351680 | tf_op jit(solution)/shard_map/all_gather | solution.py:435
  6.5 9.8 %copy-start.2 = (bf16[3,3,3,128,128]{4,3,2,1,0:T(8,128)(2,1)S(1)}, bf16[3,3,3,128,128]{4,3,2,1,0:T(8,128)(2,1)}, u32[]{:S(2)}) copy-start(bf16[3,3,3,128,128]{4,3,2,1,0:T(8,128)(2,1)} %param.10) | copy-start | bytes 2654212
  8.7 9.6 %collective-permute-start = (bf16[3,16,16,128]{3,2,1,0:T(8,128)(2,1)}, bf16[3,16,16,128]{3,2,1,0:T(8,128)(2,1)S(1)}, u32[]{:S(2)}, u32[]{:S(2)}) collective-permute-start(bf16[3,16,16,128]{3,2,1,0:T(8,128)(2,1)} %get-tuple-element.13), channel_id=1, source_target_pairs={{1,2},{3,4},{5,6},{7,8},{9,10},{11,12},{13,14},{2,1},{4,3},{6,5},{... | collective-permute-start | bytes 589832 | tf_op jit(solution)/shard_map/ppermute | solution.py:431
  13.2 5.0 %collective-permute-start.1 = (bf16[3,16,16,128]{3,2,1,0:T(8,128)(2,1)}, bf16[3,16,16,128]{3,2,1,0:T(8,128)(2,1)S(1)}, u32[]{:S(2)}, u32[]{:S(2)}) collective-permute-start(bf16[3,16,16,128]{3,2,1,0:T(8,128)(2,1)} %get-tuple-element.14), channel_id=1, source_target_pairs={{0,1},{1,0},{2,3},{3,2},{4,5},{5,4},{6,7},{7,6},{8,9},{9,8},{10,11... | collective-permute-start | bytes 589832 | tf_op jit(solution)/shard_map/ppermute | solution.py:432
  13.4 1.6 %copy-start = (bf16[2,2,2,512,256]{4,3,2,1,0:T(8,128)(2,1)S(1)}, bf16[2,2,2,512,256]{4,3,2,1,0:T(8,128)(2,1)}, u32[]{:S(2)}) copy-start(bf16[2,2,2,512,256]{4,3,2,1,0:T(8,128)(2,1)} %param.14) | copy-start | bytes 6291460
  15.0 1.3 %copy-start.7 = (bf16[4,16,16,128]{3,2,1,0:T(8,128)(2,1)S(1)}, bf16[4,16,16,128]{3,2,1,0:T(8,128)(2,1)}, u32[]{:S(2)}) copy-start(bf16[4,16,16,128]{3,2,1,0:T(8,128)(2,1)} %volume.3) | copy-start | bytes 786436
  16.4 1.9 %copy-start.1 = (bf16[3,3,3,128,256]{4,3,2,1,0:T(8,128)(2,1)S(1)}, bf16[3,3,3,128,256]{4,3,2,1,0:T(8,128)(2,1)}, u32[]{:S(2)}) copy-start(bf16[3,3,3,128,256]{4,3,2,1,0:T(8,128)(2,1)} %param.11) | copy-start | bytes 5308420
  16.4 1.9 %copy-start.8 = (bf16[256,256]{1,0:T(8,128)(2,1)S(1)}, bf16[256,256]{1,0:T(8,128)(2,1)}, u32[]{:S(2)}) copy-start(bf16[256,256]{1,0:T(8,128)(2,1)} %constant.38.clone.order) | copy-start | bytes 393220
  18.2 18.8 %copy-start.5 = (bf16[3,3,3,256,32]{3,4,2,1,0:T(8,128)(2,1)S(1)}, bf16[3,3,3,256,32]{3,4,2,1,0:T(8,128)(2,1)}, u32[]{:S(2)}) copy-start(bf16[3,3,3,256,32]{3,4,2,1,0:T(8,128)(2,1)} %param.12) | copy-start | bytes 1327108
  21.7 15.3 %copy-start.9 = (bf16[48,256]{1,0:T(8,128)(2,1)}, bf16[48,256]{1,0:T(8,128)(2,1)S(1)}, u32[]{:S(2)}) copy-start(bf16[48,256]{1,0:T(8,128)(2,1)S(1)} %get-tuple-element.19) | copy-start | bytes 73732
  21.7 30.9 %copy-start.3 = (bf16[3,3,3,512,32]{3,4,2,1,0:T(8,128)(2,1)S(1)}, bf16[3,3,3,512,32]{3,4,2,1,0:T(8,128)(2,1)}, u32[]{:S(2)}) copy-start(bf16[3,3,3,512,32]{3,4,2,1,0:T(8,128)(2,1)} %param.13) | copy-start | bytes 2654212
  38.4 14.2 %all-to-all-start.1 = ((bf16[16,32,256]{2,1,0:T(8,128)(2,1)}), bf16[16,32,256]{2,1,0:T(8,128)(2,1)S(1)}, u32[]{:S(2)}, u32[]{:S(2)}) async-start(bf16[16,32,256]{2,1,0:T(8,128)(2,1)} %shard_map.95), calls=%async_computation.1 | async-start | bytes 524288 | tf_op jit(solution)/shard_map/all_to_all | solution.py:387
  43.1 21.9 %copy-start.6 = (bf16[2112,256]{1,0:T(8,128)(2,1)S(1)}, bf16[2112,256]{1,0:T(8,128)(2,1)}, u32[]{:S(2)}) copy-start(bf16[2112,256]{1,0:T(8,128)(2,1)} %all-gather.3.cloned.1.call-done) | copy-start | bytes 3244036
  45.2 19.8 %collective-permute-start.5 = (bf16[4,336,256]{2,1,0:T(8,128)(2,1)}, bf16[4,336,256]{2,1,0:T(8,128)(2,1)S(1)}, u32[]{:S(2)}, u32[]{:S(2)}) collective-permute-start(bf16[4,336,256]{2,1,0:T(8,128)(2,1)} %slice.4), channel_id=1, source_target_pairs={{0,16},{16,0},{1,17},{17,1},{2,18},{18,2},{3,19},{19,3},{4,20},{20... | collective-permute-start | bytes 2064392 | tf_op jit(solution)/shard_map/ppermute | solution.py:494
  46.5 2.3 %collective-permute-start.2 = (bf16[48,256]{1,0:T(8,128)(2,1)}, bf16[48,256]{1,0:T(8,128)(2,1)S(1)}, u32[]{:S(2)}, u32[]{:S(2)}) collective-permute-start(bf16[48,256]{1,0:T(8,128)(2,1)} %get-tuple-element.17), channel_id=1, source_target_pairs={{0,1},{1,0},{2,3},{3,2},{4,5},{5,4},{6,7},{7,6},{8,9},{9,8},{10,11... | collective-permute-start | bytes 73736 | tf_op jit(solution)/shard_map/ppermute | solution.py:478
  47.1 3.3 %collective-permute-start.3 = (bf16[48,256]{1,0:T(8,128)(2,1)}, bf16[48,256]{1,0:T(8,128)(2,1)S(1)}, u32[]{:S(2)}, u32[]{:S(2)}) collective-permute-start(bf16[48,256]{1,0:T(8,128)(2,1)} %get-tuple-element.18), channel_id=1, source_target_pairs={{0,2},{1,3},{2,0},{3,1},{4,6},{5,7},{6,4},{7,5},{8,10},{9,11},{10,... | collective-permute-start | bytes 73736 | tf_op jit(solution)/shard_map/ppermute | solution.py:478
  48.5 4.1 %collective-permute-start.4 = (bf16[48,256]{1,0:T(8,128)(2,1)}, bf16[48,256]{1,0:T(8,128)(2,1)S(1)}, u32[]{:S(2)}, u32[]{:S(2)}) collective-permute-start(bf16[48,256]{1,0:T(8,128)(2,1)} %copy-done.9), channel_id=1, source_target_pairs={{0,3},{1,2},{2,1},{3,0},{4,7},{5,6},{6,5},{7,4},{8,11},{9,10},{10,... | collective-permute-start | bytes 73736 | tf_op jit(solution)/shard_map/ppermute | solution.py:478
  65.0 10.9 %copy-start.4 = (bf16[2,2,2,256,128]{4,3,2,1,0:T(8,128)(2,1)S(1)}, bf16[2,2,2,256,128]{4,3,2,1,0:T(8,128)(2,1)}, u32[]{:S(2)}) copy-start(bf16[2,2,2,256,128]{4,3,2,1,0:T(8,128)(2,1)} %param.16) | copy-start | bytes 1572868
Sparse Core Ops, SparseCore 0:
  8.9 33.8 all-gather.2

commit v12 on v11

--- a/solution.py
+++ b/solution.py
@@ -285,7 +285,8 @@
 def decode_stage(ride, marks, deeper, rise, *refs):
     swaps = () if ride else refs[:2]
     near, refs = refs[len(swaps) : len(swaps) + GROUP], refs[len(swaps) + GROUP :]
-    *decode, out, framed, patches, risen, blocks = refs
+    decode, outs = refs[: -5 - GROUP], refs[-5 - GROUP : -5]
+    framed, patches, risen, blocks, parts = refs[-5:]
     by_rank(marks, near, blocks)
     n, chans, _ = deeper.shape
     plane, planes = marks[3], n // GROUP
@@ -355,19 +356,22 @@
             ]
             term = dot(patches[64 * a : 64 * a + 512], jnp.concatenate(right, axis=0))
             partial = term if partial is None else partial + term
-        out[...] = partial.astype(jnp.bfloat16)
+        parts[...] = partial.astype(jnp.bfloat16).reshape(GROUP, 128, 256)
 
     if len(decode) == 1:
         multiply(None)
     else:
         pl.when(marks[1] == 0)(lambda: multiply(0))
         pl.when(marks[1] == 1)(lambda: multiply(1))
-
-
-def final_stage(partials, weights, out, spaced):
-    decoded = partials[0].astype(jnp.float32)
-    for g in range(1, GROUP):
-        decoded += partials[g].astype(jnp.float32)
+    for k in range(GROUP):
+        outs[k][...] = parts[marks[0] ^ k]
+
+
+def final_stage(*refs):
+    partials, (weights, out, spaced) = refs[:GROUP], refs[GROUP:]
+    decoded = partials[0][...].astype(jnp.float32)
+    for partial in partials[1:]:
+        decoded += partial[...].astype(jnp.float32)
     decoded = jnp.maximum(decoded, 0.0).astype(jnp.bfloat16)
     for a in range(2):
         for b in range(2):
@@ -385,6 +389,11 @@
 
 def exchange(payload, axis):
     return lax.all_to_all(payload, axis, split_axis=0, concat_axis=0, tiled=True)
+
+
+def by_xor(blocks):
+    swaps = [[(r, r ^ k) for r in range(GROUP)] for k in range(GROUP)]
+    return [blocks[0]] + [lax.ppermute(blocks[k], "r", swaps[k]) for k in range(1, GROUP)]
 
 
 def body(
@@ -474,9 +483,7 @@
         unread=1,
     )
     pooled_whole = exchange(pooled_two, ALL)
-    near = [skips[0]] + [
-        lax.ppermute(skips[k], "r", [(r, r ^ k) for r in range(GROUP)]) for k in range(1, GROUP)
-    ]
+    near = by_xor(skips)
     blocks = pltpu.VMEM((GROUP, 48, 256), jnp.bfloat16)
 
     deep = call(
@@ -531,26 +538,27 @@
     )
     deeper_near = exchange(deeper, ALL)
 
-    partial = call(
+    partials = call(
         functools.partial(decode_stage, ride),
-        bf16((512, 256)),
+        (bf16((128, 256)),) * GROUP,
         [
             pltpu.VMEM((10, 10, 24, 128), jnp.float32),
             pltpu.VMEM((640, 1152), jnp.bfloat16),
             pltpu.VMEM((8, 128, 128), jnp.float32),
             blocks,
+            pltpu.VMEM((GROUP, 128, 256), jnp.bfloat16),
         ],
         (marks, deeper_near, rise_part, *swaps, *near, *weights),
         2 * 512 * 3456 * 256,
         24,
         scalars=1,
     )
-    partials = exchange(partial.reshape(GROUP, 128, 256), "r")
+    partials = by_xor(partials)
     out = call(
         final_stage,
         bf16((1024, 128)),
         [pltpu.VMEM((1024, 128), jnp.float32)],
-        (partials, final_kernel.reshape(8, 256, 128)),
+        (*partials, final_kernel.reshape(8, 256, 128)),
         2 * 128 * 256 * 1024,
         16,
     )

time: 85.3 us -> 82.5 us (0.967); the launches traced: 83.8 us -> 81.9 us
  blocking collectives: 35.1 us -> 26.6 us
  waiting for transfers between devices: 4.31 us -> 7.82 us
  starting transfers between devices: 12.9 us -> 15.9 us
    all_to_all x3 -> x2, blocking collectives: 35.1 us -> 26.6 us  [exchange(): lax.all_to_all(payload, axis, split_axis=0, concat_axis=0, tiled=True)]
    ppermute x3 -> x6, waiting for transfers between devices: 3.83 us -> 7.33 us  [by_xor(): lax.ppermute(blocks[k], 'r', swaps[k])]
    ppermute x3 -> x6, starting transfers between devices: 2.26 us -> 5.22 us  [by_xor(): lax.ppermute(blocks[k], 'r', swaps[k])]
  transfers between devices with their start and end apart: 8 -> 11, of which waited for: 3 -> 5; matrix products, arithmetic and copies ran while one was open for 3% -> 3% of each run, Pallas kernels for 10% -> 11%
where the time goes in v12:
time: 82.5 us; the launch traced here: 81.9 us
  blocking collectives  26.6 us (32%)
  starting transfers between devices  15.9 us (19%)
  Pallas kernels  14.2 us (17%)
  between operations  13.5 us (16%)
  waiting for transfers between devices  7.82 us (9%)
  local copies, waits for them, and re-layouts  3.82 us (5%)
    all_to_all x2, blocking collectives, exchange(): lax.all_to_all(payload, axis, split_axis=0, concat_axis=0, tiled=True)  26.6 us
    pallas_call x7, Pallas kernels, call(): pl.pallas_call(kernel, out_shape=outs, in_specs=[pl.BlockSpec(memory_spac...  12.1 us
    ppermute x6, waiting for transfers between devices, by_xor(): lax.ppermute(blocks[k], 'r', swaps[k])  7.33 us
    ppermute x6, starting transfers between devices, by_xor(): lax.ppermute(blocks[k], 'r', swaps[k])  5.22 us
    all_to_all x1, starting transfers between devices, exchange(): lax.all_to_all(payload, axis, split_axis=0, concat_axis=0, tiled=True)  4.76 us
    ppermute x1, starting transfers between devices, body(): off_chip = lax.ppermute(off_chip, ALL, pairs + [(j, i) for i, j in pairs])  4.54 us
    pallas_call x1, Pallas kernels, body(): pl.pallas_call(front_stage, out_shape=(halo, halo) + (bf16((528, 256)),)...  2.11 us
    slice x1, local copies, waits for them, and re-layouts, body(): weights = (line, lax.ppermute(line[:, :336], 'rep', [(0, 1), (1, 0)]))  2.1 us
  transfers between devices with their start and end apart: 11, of which 5 were waited for; matrix products, arithmetic and copies ran while one was open for 3% of the time, Pallas kernels for 11%

profile of v12, /device:TPU:1, one launch (start us, length us, event | category | flops | bytes accessed | tf_op | source)
XLA Modules:
  0.0 81.9 jit_solution(6181971417423218671)
XLA Ops:
  6.5 2.1 %shard_map.91 = (bf16[3,16,16,128]{3,2,1,0:T(8,128)(2,1)}, bf16[3,16,16,128]{3,2,1,0:T(8,128)(2,1)}, bf16[528,256]{1,0:T(8,128)(2,1)}) custom-call(s32[1]{0:T(128)} %bitcast.4.odd, s32[1]{0:T(128)} %bitcast.1.rep, bf16[4,16,16,128]{3,2,1,0:T(8,128)(2,1)} %volume.3, bf16[864,256]{1,0:T(8,128)(2,1)} %bitcast.33), custom_call_target="tpu_custom_call" | custom-call | bytes 1000000 | tf_op jit(solution)/shard_map/pallas_call | solution.py:425
  8.7 0.0 all-gather.3.cloned.1.call-update
  8.7 4.5 %collective-permute-start = (bf16[3,16,16,128]{3,2,1,0:T(8,128)(2,1)}, bf16[3,16,16,128]{3,2,1,0:T(8,128)(2,1)S(1)}, u32[]{:S(2)}, u32[]{:S(2)}) collective-permute-start(bf16[3,16,16,128]{3,2,1,0:T(8,128)(2,1)} %get-tuple-element.17), channel_id=1, source_target_pairs={{1,2},{3,4},{5,6},{7,8},{9,10},{11,12},{13,14},{2,1},{4,3},{6,5},{... | collective-permute-start | bytes 589832 | tf_op jit(solution)/shard_map/ppermute | solution.py:440
  13.2 0.1 collective-permute-start.1
  13.3 0.1 stack.31.marks_ref.marks
  13.4 1.6 %copy-done = bf16[2,2,2,512,256]{4,3,2,1,0:T(8,128)(2,1)S(1)} copy-done((bf16[2,2,2,512,256]{4,3,2,1,0:T(8,128)(2,1)S(1)}, bf16[2,2,2,512,256]{4,3,2,1,0:T(8,128)(2,1)}, u32[]{:S(2)}) %copy-start) | copy-done | bytes 2097176
  15.0 1.3 %shard_map.93._.rise = bf16[512,512]{1,0:T(8,128)(2,1)S(1)} custom-call(s32[7]{0:T(128)S(1)} %stack.31.marks_ref.marks, bf16[8,512,256]{2,1,0:T(8,128)(2,1)S(1)} %bitcast.22), custom_call_target="tpu_custom_call" | custom-call | flops 134217728 | bytes 2097180 | tf_op jit(solution)/shard_map/pallas_call | solution.py:18
  16.4 0.0 copy-start.1
  16.4 0.0 copy-start.8
  16.4 1.4 %shard_map.92.own = f32[4,256,256]{2,1,0:T(8,128)S(1)} custom-call(bf16[4,16,16,128]{3,2,1,0:T(8,128)(2,1)S(1)} %copy-done.7, bf16[3,1152,128]{2,1,0:T(8,128)(2,1)S(1)} %bitcast.25), custom_call_target="tpu_custom_call" | custom-call | flops 1207959552 | bytes 1146880 | tf_op jit(solution)/shard_map/pallas_call | solution.py:18
  17.8 0.4 collective-permute-done.off_chip
  18.3 3.5 %shard_map.94 = (bf16[16,16,256]{2,1,0:T(8,128)(2,1)S(1)}, bf16[48,256]{1,0:T(8,128)(2,1)S(1)}, bf16[48,256]{1,0:T(8,128)(2,1)}, bf16[48,256]{1,0:T(8,128)(2,1)}, bf16[48,256]{1,0:T(8,128)(2,1)S(1)}) custom-call(s32[7]{0:T(128)S(1)} %stack.31.marks_ref.marks, bf16[3,16,16,128]{3,2,1,0:T(8,128)(2,1)S(1)} %collective-permute-done.off_chip, ...), custom_call_target="tpu_custom_call" | custom-call | flops 1207959552 | bytes 4227100 | tf_op jit(solution)/shard_map/pallas_call | solution.py:18
  21.7 15.3 %all_to_all.15 = bf16[16,16,256]{2,1,0:T(8,128)(2,1)S(1)} all-to-all(bf16[16,16,256]{2,1,0:T(8,128)(2,1)S(1)} %get-tuple-element.19), channel_id=1, replica_groups=mesh['rep'=2,'z'=4,'r'=4] {'z','r'}, dimensions={0} | all-to-all | bytes 262144 | tf_op jit(solution)/shard_map/all_to_all | solution.py:391
  37.0 1.3 %shard_map.95 = bf16[16,32,256]{2,1,0:T(8,128)(2,1)} custom-call(bf16[256,256]{1,0:T(8,128)(2,1)S(1)} %bitcast.28, bf16[864,256]{1,0:T(8,128)(2,1)S(1)} %bitcast.30), custom_call_target="tpu_custom_call" | custom-call | flops 113246208 | bytes 573440 | tf_op jit(solution)/shard_map/pallas_call | solution.py:18
  38.3 4.8 %all-to-all-start.1 = ((bf16[16,32,256]{2,1,0:T(8,128)(2,1)}), bf16[16,32,256]{2,1,0:T(8,128)(2,1)S(1)}, u32[]{:S(2)}, u32[]{:S(2)}) async-start(bf16[16,32,256]{2,1,0:T(8,128)(2,1)} %shard_map.95), calls=%async_computation.1 | async-start | bytes 524288 | tf_op jit(solution)/shard_map/all_to_all | solution.py:391
  43.1 0.0 all-gather.3.cloned.1.call-done
  43.1 2.1 %slice.4 = bf16[4,336,256]{2,1,0:T(8,128)(2,1)} slice(bf16[4,528,256]{2,1,0:T(8,128)(2,1)} %bitcast.31), slice={[0:4], [0:336], [0:256]} | slice | bytes 1376256 | tf_op jit(solution)/shard_map/slice | solution.py:501
  45.2 1.3 %collective-permute-start.5 = (bf16[4,336,256]{2,1,0:T(8,128)(2,1)}, bf16[4,336,256]{2,1,0:T(8,128)(2,1)S(1)}, u32[]{:S(2)}, u32[]{:S(2)}) collective-permute-start(bf16[4,336,256]{2,1,0:T(8,128)(2,1)} %slice.4), channel_id=1, source_target_pairs={{0,16},{16,0},{1,17},{17,1},{2,18},{18,2},{3,19},{19,3},{4,20},{20... | collective-permute-start | bytes 2064392 | tf_op jit(solution)/shard_map/ppermute | solution.py:501
  46.5 0.6 collective-permute-start.2
  47.1 1.4 %collective-permute-start.3 = (bf16[48,256]{1,0:T(8,128)(2,1)}, bf16[48,256]{1,0:T(8,128)(2,1)S(1)}, u32[]{:S(2)}, u32[]{:S(2)}) collective-permute-start(bf16[48,256]{1,0:T(8,128)(2,1)} %get-tuple-element.22), channel_id=1, source_target_pairs={{0,2},{1,3},{2,0},{3,1},{4,6},{5,7},{6,4},{7,5},{8,10},{9,11},{10,... | collective-permute-start | bytes 73736 | tf_op jit(solution)/shard_map/ppermute | solution.py:396
  48.5 0.3 collective-permute-start.4
  48.8 1.7 %collective-permute-done.3.refs_2_ = bf16[48,256]{1,0:T(8,128)(2,1)S(1)} collective-permute-done((bf16[48,256]{1,0:T(8,128)(2,1)}, bf16[48,256]{1,0:T(8,128)(2,1)S(1)}, u32[]{:S(2)}, u32[]{:S(2)}) %collective-permute-start.3) | collective-permute-done | bytes 24608 | tf_op jit(solution)/shard_map/ppermute | solution.py:396
  50.4 2.1 %collective-permute-done.4.refs_3_ = bf16[48,256]{1,0:T(8,128)(2,1)S(1)} collective-permute-done((bf16[48,256]{1,0:T(8,128)(2,1)}, bf16[48,256]{1,0:T(8,128)(2,1)S(1)}, u32[]{:S(2)}, u32[]{:S(2)}) %collective-permute-start.4) | collective-permute-done | bytes 24608 | tf_op jit(solution)/shard_map/ppermute | solution.py:396
  52.6 1.3 %shard_map.96 = bf16[16,32,128]{2,1,0:T(8,128)(2,1)S(1)} custom-call(s32[7]{0:T(128)S(1)} %stack.31.marks_ref.marks, bf16[512,256]{1,0:T(8,128)(2,1)S(1)} %bitcast.24, bf16[864,512]{1,0:T(8,128)(2,1)S(1)} %bitcast.27, bf16[48,256]{1,0:T(8,128)(2,1)S(1)} %get-tuple-element.20.refs_0_, bf16[48,256]{1,0:T(8,128)(2,1)S(1)} %collective-permute-done.2.refs_1_, ...), custom_call_target="tpu_custom_call" | custom-call | flops 226492416 | bytes 1245212 | tf_op jit(solution)/shard_map/pallas_call | solution.py:18
  53.8 0.0 copy-start.4
  53.9 11.3 %all_to_all.16.deeper = bf16[16,32,128]{2,1,0:T(8,128)(2,1)S(1)} all-to-all(bf16[16,32,128]{2,1,0:T(8,128)(2,1)S(1)} %shard_map.96), channel_id=1, replica_groups=mesh['rep'=2,'z'=4,'r'=4] {'z','r'}, dimensions={0} | all-to-all | bytes 262144 | tf_op jit(solution)/shard_map/all_to_all | solution.py:391
  65.2 2.3 %shard_map.97 = (bf16[128,256]{1,0:T(8,128)(2,1)S(1)}, bf16[128,256]{1,0:T(8,128)(2,1)S(1)}, bf16[128,256]{1,0:T(8,128)(2,1)S(1)}, bf16[128,256]{1,0:T(8,128)(2,1)S(1)}) custom-call(s32[7]{0:T(128)S(1)} %stack.31.marks_ref.marks, bf16[16,32,128]{2,1,0:T(8,128)(2,1)S(1)} %all_to_all.16.deeper, bf16[512,512]{1,0:T(8,128)(2,1)S(1)} %shard_map.93._.rise, ...), custom_call_target="tpu_custom_call" | custom-call | flops 905969664 | bytes 2523164 | tf_op jit(solution)/shard_map/pallas_call | solution.py:18
  67.5 1.2 %collective-permute-start.6 = (bf16[128,256]{1,0:T(8,128)(2,1)S(1)}, bf16[128,256]{1,0:T(8,128)(2,1)S(1)}, u32[]{:S(2)}, u32[]{:S(2)}) collective-permute-start(bf16[128,256]{1,0:T(8,128)(2,1)S(1)} %get-tuple-element.26), channel_id=1, source_target_pairs={{0,1},{1,0},{2,3},{3,2},{4,5},{5,4},{6,7},{7,6},{8,9},{9,8},{10,11... | collective-permute-start | bytes 196616 | tf_op jit(solution)/shard_map/ppermute | solution.py:396
  68.8 1.7 %collective-permute-start.8 = (bf16[128,256]{1,0:T(8,128)(2,1)S(1)}, bf16[128,256]{1,0:T(8,128)(2,1)S(1)}, u32[]{:S(2)}, u32[]{:S(2)}) collective-permute-start(bf16[128,256]{1,0:T(8,128)(2,1)S(1)} %get-tuple-element.28), channel_id=1, source_target_pairs={{0,3},{1,2},{2,1},{3,0},{4,7},{5,6},{6,5},{7,4},{8,11},{9,10},{10,... | collective-permute-start | bytes 196616 | tf_op jit(solution)/shard_map/ppermute | solution.py:396
  70.5 2.0 %collective-permute-done.7.refs_2_ = bf16[128,256]{1,0:T(8,128)(2,1)S(1)} collective-permute-done((bf16[128,256]{1,0:T(8,128)(2,1)S(1)}, bf16[128,256]{1,0:T(8,128)(2,1)S(1)}, u32[]{:S(2)}, u32[]{:S(2)}) %collective-permute-start.7) | collective-permute-done | bytes 65568 | tf_op jit(solution)/shard_map/ppermute | solution.py:396
  72.4 1.6 %collective-permute-done.8.refs_3_ = bf16[128,256]{1,0:T(8,128)(2,1)S(1)} collective-permute-done((bf16[128,256]{1,0:T(8,128)(2,1)S(1)}, bf16[128,256]{1,0:T(8,128)(2,1)S(1)}, u32[]{:S(2)}, u32[]{:S(2)}) %collective-permute-start.8) | collective-permute-done | bytes 65568 | tf_op jit(solution)/shard_map/ppermute | solution.py:396
  74.0 1.1 %shard_map.98 = bf16[1024,128]{1,0:T(8,128)(2,1)} custom-call(bf16[128,256]{1,0:T(8,128)(2,1)S(1)} %get-tuple-element.25.refs_0_, bf16[128,256]{1,0:T(8,128)(2,1)S(1)} %collective-permute-done.6.refs_1_, bf16[128,256]{1,0:T(8,128)(2,1)S(1)} %collective-permute-done.7.refs_2_, bf16[128,256]{1,0:T(8,128)(2,1)S(1)} %collective-permute-done.8.refs_3_, ...), custom_call_target="tpu_custom_call" | custom-call | flops 67108864 | bytes 786432 | tf_op jit(solution)/shard_map/pallas_call | solution.py:18
  (23 shorter events, 0.0 us)
Async XLA Ops:
  6.5 36.6 %all-gather.3.cloned.1.call-start = ((), (), s32[]{:S(2)}) async-start(), calls=%async_computation.3 | async-start | bytes 1351680 | tf_op jit(solution)/shard_map/all_gather | solution.py:444
  6.5 9.8 %copy-start.2 = (bf16[3,3,3,128,128]{4,3,2,1,0:T(8,128)(2,1)S(1)}, bf16[3,3,3,128,128]{4,3,2,1,0:T(8,128)(2,1)}, u32[]{:S(2)}) copy-start(bf16[3,3,3,128,128]{4,3,2,1,0:T(8,128)(2,1)} %param.10) | copy-start | bytes 2654212
  8.7 9.6 %collective-permute-start = (bf16[3,16,16,128]{3,2,1,0:T(8,128)(2,1)}, bf16[3,16,16,128]{3,2,1,0:T(8,128)(2,1)S(1)}, u32[]{:S(2)}, u32[]{:S(2)}) collective-permute-start(bf16[3,16,16,128]{3,2,1,0:T(8,128)(2,1)} %get-tuple-element.17), channel_id=1, source_target_pairs={{1,2},{3,4},{5,6},{7,8},{9,10},{11,12},{13,14},{2,1},{4,3},{6,5},{... | collective-permute-start | bytes 589832 | tf_op jit(solution)/shard_map/ppermute | solution.py:440
  13.2 5.0 %collective-permute-start.1 = (bf16[3,16,16,128]{3,2,1,0:T(8,128)(2,1)}, bf16[3,16,16,128]{3,2,1,0:T(8,128)(2,1)S(1)}, u32[]{:S(2)}, u32[]{:S(2)}) collective-permute-start(bf16[3,16,16,128]{3,2,1,0:T(8,128)(2,1)} %get-tuple-element.18), channel_id=1, source_target_pairs={{0,1},{1,0},{2,3},{3,2},{4,5},{5,4},{6,7},{7,6},{8,9},{9,8},{10,11... | collective-permute-start | bytes 589832 | tf_op jit(solution)/shard_map/ppermute | solution.py:441
  13.4 1.6 %copy-start = (bf16[2,2,2,512,256]{4,3,2,1,0:T(8,128)(2,1)S(1)}, bf16[2,2,2,512,256]{4,3,2,1,0:T(8,128)(2,1)}, u32[]{:S(2)}) copy-start(bf16[2,2,2,512,256]{4,3,2,1,0:T(8,128)(2,1)} %param.14) | copy-start | bytes 6291460
  15.0 1.3 %copy-start.7 = (bf16[4,16,16,128]{3,2,1,0:T(8,128)(2,1)S(1)}, bf16[4,16,16,128]{3,2,1,0:T(8,128)(2,1)}, u32[]{:S(2)}) copy-start(bf16[4,16,16,128]{3,2,1,0:T(8,128)(2,1)} %volume.3) | copy-start | bytes 786436
  16.4 1.9 %copy-start.1 = (bf16[3,3,3,128,256]{4,3,2,1,0:T(8,128)(2,1)S(1)}, bf16[3,3,3,128,256]{4,3,2,1,0:T(8,128)(2,1)}, u32[]{:S(2)}) copy-start(bf16[3,3,3,128,256]{4,3,2,1,0:T(8,128)(2,1)} %param.11) | copy-start | bytes 5308420
  16.4 1.9 %copy-start.8 = (bf16[256,256]{1,0:T(8,128)(2,1)S(1)}, bf16[256,256]{1,0:T(8,128)(2,1)}, u32[]{:S(2)}) copy-start(bf16[256,256]{1,0:T(8,128)(2,1)} %constant.38.clone.order) | copy-start | bytes 393220
  18.2 18.8 %copy-start.5 = (bf16[3,3,3,256,32]{3,4,2,1,0:T(8,128)(2,1)S(1)}, bf16[3,3,3,256,32]{3,4,2,1,0:T(8,128)(2,1)}, u32[]{:S(2)}) copy-start(bf16[3,3,3,256,32]{3,4,2,1,0:T(8,128)(2,1)} %param.12) | copy-start | bytes 1327108
  21.7 15.3 %copy-start.9 = (bf16[48,256]{1,0:T(8,128)(2,1)}, bf16[48,256]{1,0:T(8,128)(2,1)S(1)}, u32[]{:S(2)}) copy-start(bf16[48,256]{1,0:T(8,128)(2,1)S(1)} %get-tuple-element.23) | copy-start | bytes 73732
  21.7 30.9 %copy-start.3 = (bf16[3,3,3,512,32]{3,4,2,1,0:T(8,128)(2,1)S(1)}, bf16[3,3,3,512,32]{3,4,2,1,0:T(8,128)(2,1)}, u32[]{:S(2)}) copy-start(bf16[3,3,3,512,32]{3,4,2,1,0:T(8,128)(2,1)} %param.13) | copy-start | bytes 2654212
  38.3 14.3 %all-to-all-start.1 = ((bf16[16,32,256]{2,1,0:T(8,128)(2,1)}), bf16[16,32,256]{2,1,0:T(8,128)(2,1)S(1)}, u32[]{:S(2)}, u32[]{:S(2)}) async-start(bf16[16,32,256]{2,1,0:T(8,128)(2,1)} %shard_map.95), calls=%async_computation.1 | async-start | bytes 524288 | tf_op jit(solution)/shard_map/all_to_all | solution.py:391
  43.1 22.1 %copy-start.6 = (bf16[2112,256]{1,0:T(8,128)(2,1)S(1)}, bf16[2112,256]{1,0:T(8,128)(2,1)}, u32[]{:S(2)}) copy-start(bf16[2112,256]{1,0:T(8,128)(2,1)} %all-gather.3.cloned.1.call-done) | copy-start | bytes 3244036
  45.2 20.0 %collective-permute-start.5 = (bf16[4,336,256]{2,1,0:T(8,128)(2,1)}, bf16[4,336,256]{2,1,0:T(8,128)(2,1)S(1)}, u32[]{:S(2)}, u32[]{:S(2)}) collective-permute-start(bf16[4,336,256]{2,1,0:T(8,128)(2,1)} %slice.4), channel_id=1, source_target_pairs={{0,16},{16,0},{1,17},{17,1},{2,18},{18,2},{3,19},{19,3},{4,20},{20... | collective-permute-start | bytes 2064392 | tf_op jit(solution)/shard_map/ppermute | solution.py:501
  46.5 2.3 %collective-permute-start.2 = (bf16[48,256]{1,0:T(8,128)(2,1)}, bf16[48,256]{1,0:T(8,128)(2,1)S(1)}, u32[]{:S(2)}, u32[]{:S(2)}) collective-permute-start(bf16[48,256]{1,0:T(8,128)(2,1)} %get-tuple-element.21), channel_id=1, source_target_pairs={{0,1},{1,0},{2,3},{3,2},{4,5},{5,4},{6,7},{7,6},{8,9},{9,8},{10,11... | collective-permute-start | bytes 73736 | tf_op jit(solution)/shard_map/ppermute | solution.py:396
  47.1 3.3 %collective-permute-start.3 = (bf16[48,256]{1,0:T(8,128)(2,1)}, bf16[48,256]{1,0:T(8,128)(2,1)S(1)}, u32[]{:S(2)}, u32[]{:S(2)}) collective-permute-start(bf16[48,256]{1,0:T(8,128)(2,1)} %get-tuple-element.22), channel_id=1, source_target_pairs={{0,2},{1,3},{2,0},{3,1},{4,6},{5,7},{6,4},{7,5},{8,10},{9,11},{10,... | collective-permute-start | bytes 73736 | tf_op jit(solution)/shard_map/ppermute | solution.py:396
  48.5 4.1 %collective-permute-start.4 = (bf16[48,256]{1,0:T(8,128)(2,1)}, bf16[48,256]{1,0:T(8,128)(2,1)S(1)}, u32[]{:S(2)}, u32[]{:S(2)}) collective-permute-start(bf16[48,256]{1,0:T(8,128)(2,1)} %copy-done.9), channel_id=1, source_target_pairs={{0,3},{1,2},{2,1},{3,0},{4,7},{5,6},{6,5},{7,4},{8,11},{9,10},{10,... | collective-permute-start | bytes 73736 | tf_op jit(solution)/shard_map/ppermute | solution.py:396
  53.8 20.2 %copy-start.4 = (bf16[2,2,2,256,128]{4,3,2,1,0:T(8,128)(2,1)S(1)}, bf16[2,2,2,256,128]{4,3,2,1,0:T(8,128)(2,1)}, u32[]{:S(2)}) copy-start(bf16[2,2,2,256,128]{4,3,2,1,0:T(8,128)(2,1)} %param.16) | copy-start | bytes 1572868
  67.5 2.9 %collective-permute-start.6 = (bf16[128,256]{1,0:T(8,128)(2,1)S(1)}, bf16[128,256]{1,0:T(8,128)(2,1)S(1)}, u32[]{:S(2)}, u32[]{:S(2)}) collective-permute-start(bf16[128,256]{1,0:T(8,128)(2,1)S(1)} %get-tuple-element.26), channel_id=1, source_target_pairs={{0,1},{1,0},{2,3},{3,2},{4,5},{5,4},{6,7},{7,6},{8,9},{9,8},{10,11... | collective-permute-start | bytes 196616 | tf_op jit(solution)/shard_map/ppermute | solution.py:396
  68.8 3.7 %collective-permute-start.7 = (bf16[128,256]{1,0:T(8,128)(2,1)S(1)}, bf16[128,256]{1,0:T(8,128)(2,1)S(1)}, u32[]{:S(2)}, u32[]{:S(2)}) collective-permute-start(bf16[128,256]{1,0:T(8,128)(2,1)S(1)} %get-tuple-element.27), channel_id=1, source_target_pairs={{0,2},{1,3},{2,0},{3,1},{4,6},{5,7},{6,4},{7,5},{8,10},{9,11},{10,... | collective-permute-start | bytes 196616 | tf_op jit(solution)/shard_map/ppermute | solution.py:396
  68.8 5.2 %collective-permute-start.8 = (bf16[128,256]{1,0:T(8,128)(2,1)S(1)}, bf16[128,256]{1,0:T(8,128)(2,1)S(1)}, u32[]{:S(2)}, u32[]{:S(2)}) collective-permute-start(bf16[128,256]{1,0:T(8,128)(2,1)S(1)} %get-tuple-element.28), channel_id=1, source_target_pairs={{0,3},{1,2},{2,1},{3,0},{4,7},{5,6},{6,5},{7,4},{8,11},{9,10},{10,... | collective-permute-start | bytes 196616 | tf_op jit(solution)/shard_map/ppermute | solution.py:396
Sparse Core Ops, SparseCore 0:
  8.9 33.8 all-gather.2
